TPU v7x, 32 devices: a whole 2x2x4 slice. The times are simulated.
32 devices in a mesh: freq: 2 (over y), src: 4 (over z), rcv: 4 (over x, core).
Axes of the slice: x: 2, y: 2, z: 4, core: 2. Of those that a mesh axis runs over, the one named last changes fastest.
Arguments:
- primaries: bfloat16 [4, 2, 1024, 3072], P('freq', None, 'src', 'rcv'), parts along dimension 0, may hold values from -0.078125 to 0.078125
- data: bfloat16 [4, 2, 1024, 1024], P('freq', None, 'src', 'rcv'), parts along dimension 0, may hold values from -6 to 6
- aperture: int32 [4, 12], replicated, may hold values from 0 to 3, as said below
Outputs:
- multiples: float32 [4, 2, 1024, 1024], P('freq', None, 'src', 'rcv'), parts along dimension 0
There are 2 independent parts, one for each index of `freq`. A program takes and returns all parts, laid end to end along the dimension named above; an argument that names none is the same for every part. Nothing has to cross between parts.
Inputs may be any that keep to these rules, and one draw needn't show every extreme that they name: aperture[b, a] lies within 6 blocks of b; entries of a row may repeat; in every draw some row names both b - 6 and b + 6, where these exist.
All inputs are finite; a program needn't handle non-finite values.
Results may differ from a plain program's by a relative error of at most 0.0003.
Values may be sent and summed in bfloat16 or wider, within the bound.
No kernel may reach another device: no remote copies, remote signals or barrier semaphores. Data moves between devices by JAX's collectives and lax.ppermute only.
A program may use at most 128 MiB of HBM per device.

v0:
```python
import jax
import jax.numpy as jnp
from jax import lax
from jax.sharding import PartitionSpec as P

BLK = 256
APER = 12
HW = 6


def from_behind(x, axis, by):
    peers = lax.axis_size(axis)
    pairs = [(i, i + by) for i in range(peers) if 0 <= i + by < peers]
    return lax.ppermute(x, axis, pairs)


def fetch_piece(values, offset, axis_count):
    if offset == 0:
        return values
    if abs(offset) >= axis_count:
        return jnp.zeros_like(values)
    return from_behind(values, "src", offset)


def body(primaries, data, aperture):
    row_count = data.shape[2]
    per_block = BLK // row_count
    reach_dev = HW * per_block + per_block - 1
    axis_count = lax.axis_size("src")
    src_index = lax.axis_index("src")
    own_block = src_index // per_block
    pieces = [fetch_piece(data, -offset, axis_count) for offset in range(-reach_dev, reach_dev + 1)]
    window = jnp.concatenate(pieces, axis=2)
    aperture_row = lax.dynamic_index_in_dim(aperture, own_block, 0, keepdims=False)
    first_row = (src_index - reach_dev) * row_count
    picked_list = []
    for slot in range(APER):
        begin_row = aperture_row[slot] * BLK - first_row
        picked_list.append(lax.dynamic_slice_in_dim(window, begin_row, BLK, 2))
    selected = jnp.concatenate(picked_list, axis=2)
    panel_piece = lax.all_gather(primaries, "rcv", axis=3, tiled=True)
    real_part = jnp.einsum(
        "sxc,scr->sxr", panel_piece[:, 0], selected[:, 0], preferred_element_type=jnp.float32
    )
    real_part = real_part - jnp.einsum(
        "sxc,scr->sxr", panel_piece[:, 1], selected[:, 1], preferred_element_type=jnp.float32
    )
    imag_part = jnp.einsum(
        "sxc,scr->sxr", panel_piece[:, 0], selected[:, 1], preferred_element_type=jnp.float32
    )
    imag_part = imag_part + jnp.einsum(
        "sxc,scr->sxr", panel_piece[:, 1], selected[:, 0], preferred_element_type=jnp.float32
    )
    return jnp.stack([real_part, imag_part], axis=1)


def solution(mesh):
    placed = (P("freq", None, "src", "rcv"), P("freq", None, "src", "rcv"), P())
    return jax.shard_map(
        body, mesh=mesh, in_specs=placed, out_specs=P("freq", None, "src", "rcv"), check_vma=False
    )
```

profile of v0, /device:TPU:0, one launch (start us, length us, event | category | flops | bytes accessed | tf_op | source)
XLA Modules:
  0.0 118.4 jit_solution(11537282170126539830)
XLA Ops:
  6.5 0.0 copy-start
  6.5 0.0 all-gather.2.cloned.1.call-start
  6.5 2.7 %copy.11 = bf16[2,2,256,768]{3,2,0,1:T(8,128)(2,1)} copy(bf16[2,2,256,768]{3,2,1,0:T(8,128)(2,1)} %param.3) | data formatting | bytes 3145728 | tf_op args[0]
  9.2 0.0 all-gather.2.cloned.1.call-update
  9.2 1.2 %copy.4 = bf16[2,2,256,256]{2,3,0,1:T(8,128)(2,1)S(1)} copy(bf16[2,2,256,256]{3,2,1,0:T(8,128)(2,1)} %param.4) | data formatting | bytes 1048576 | tf_op args[1]
  10.5 7.0 %collective-permute-start = (bf16[2,2,256,256]{2,3,0,1:T(8,128)(2,1)S(1)}, bf16[2,2,256,256]{2,3,0,1:T(8,128)(2,1)S(1)}, u32[]{:S(2)}, u32[]{:S(2)}) collective-permute-start(bf16[2,2,256,256]{2,3,0,1:T(8,128)(2,1)S(1)} %copy.4), channel_id=1, source_target_pairs={{0,12},{1,13},{2,14},{3,15},{16,28},{17,29},{18,30},{19,31}} | collective-permute-start | bytes 1572872 | tf_op jit(solution)/shard_map/ppermute | solution.py:14
  17.5 1.3 %collective-permute-start.1 = (bf16[2,2,256,256]{2,3,0,1:T(8,128)(2,1)S(1)}, bf16[2,2,256,256]{2,3,0,1:T(8,128)(2,1)S(1)}, u32[]{:S(2)}, u32[]{:S(2)}) collective-permute-start(bf16[2,2,256,256]{2,3,0,1:T(8,128)(2,1)S(1)} %copy.4), channel_id=1, source_target_pairs={{0,8},{4,12},{1,9},{5,13},{2,10},{6,14},{3,11},{7,15},{16,24},{20,... | collective-permute-start | bytes 1572872 | tf_op jit(solution)/shard_map/ppermute | solution.py:14
  18.8 2.5 %collective-permute-start.2 = (bf16[2,2,256,256]{2,3,0,1:T(8,128)(2,1)S(1)}, bf16[2,2,256,256]{2,3,0,1:T(8,128)(2,1)S(1)}, u32[]{:S(2)}, u32[]{:S(2)}) collective-permute-start(bf16[2,2,256,256]{2,3,0,1:T(8,128)(2,1)S(1)} %copy.4), channel_id=1, source_target_pairs={{0,4},{4,8},{8,12},{1,5},{5,9},{9,13},{2,6},{6,10},{10,14},{3,7},{... | collective-permute-start | bytes 1572872 | tf_op jit(solution)/shard_map/ppermute | solution.py:14
  21.3 1.3 %collective-permute-start.3 = (bf16[2,2,256,256]{2,3,0,1:T(8,128)(2,1)S(1)}, bf16[2,2,256,256]{2,3,0,1:T(8,128)(2,1)S(1)}, u32[]{:S(2)}, u32[]{:S(2)}) collective-permute-start(bf16[2,2,256,256]{2,3,0,1:T(8,128)(2,1)S(1)} %copy.4), channel_id=1, source_target_pairs={{4,0},{8,4},{12,8},{5,1},{9,5},{13,9},{6,2},{10,6},{14,10},{7,3},{... | collective-permute-start | bytes 1572872 | tf_op jit(solution)/shard_map/ppermute | solution.py:14
  22.6 1.3 %collective-permute-start.4 = (bf16[2,2,256,256]{2,3,0,1:T(8,128)(2,1)S(1)}, bf16[2,2,256,256]{2,3,0,1:T(8,128)(2,1)S(1)}, u32[]{:S(2)}, u32[]{:S(2)}) collective-permute-start(bf16[2,2,256,256]{2,3,0,1:T(8,128)(2,1)S(1)} %copy.4), channel_id=1, source_target_pairs={{8,0},{12,4},{9,1},{13,5},{10,2},{14,6},{11,3},{15,7},{24,16},{28,... | collective-permute-start | bytes 1572872 | tf_op jit(solution)/shard_map/ppermute | solution.py:14
  23.9 0.9 broadcast_dynamic-update-slice_fusion.2
  24.8 0.0 copy-done
  24.8 1.2 broadcast_dynamic-update-slice_fusion
  25.9 0.7 fusion.8
  34.3 0.0 collective-permute-done
  34.3 1.3 %collective-permute-start.5 = (bf16[2,2,256,256]{2,3,0,1:T(8,128)(2,1)S(1)}, bf16[2,2,256,256]{2,3,0,1:T(8,128)(2,1)S(1)}, u32[]{:S(2)}, u32[]{:S(2)}) collective-permute-start(bf16[2,2,256,256]{2,3,0,1:T(8,128)(2,1)S(1)} %copy.4), channel_id=1, source_target_pairs={{12,0},{13,1},{14,2},{15,3},{28,16},{29,17},{30,18},{31,19}} | collective-permute-start | bytes 1572872 | tf_op jit(solution)/shard_map/ppermute | solution.py:14
  35.6 0.9 constant_dynamic-update-slice_fusion.6
  36.4 4.6 %collective-permute-done.1 = bf16[2,2,256,256]{2,3,0,1:T(8,128)(2,1)S(1)} collective-permute-done((bf16[2,2,256,256]{2,3,0,1:T(8,128)(2,1)S(1)}, bf16[2,2,256,256]{2,3,0,1:T(8,128)(2,1)S(1)}, u32[]{:S(2)}, u32[]{:S(2)}) %collective-permute-start.1) | collective-permute-done | bytes 524320 | tf_op jit(solution)/shard_map/ppermute | solution.py:14
  41.1 0.8 constant_dynamic-update-slice_fusion.5
  41.9 9.2 %collective-permute-done.2 = bf16[2,2,256,256]{2,3,0,1:T(8,128)(2,1)S(1)} collective-permute-done((bf16[2,2,256,256]{2,3,0,1:T(8,128)(2,1)S(1)}, bf16[2,2,256,256]{2,3,0,1:T(8,128)(2,1)S(1)}, u32[]{:S(2)}, u32[]{:S(2)}) %collective-permute-start.2) | collective-permute-done | bytes 524320 | tf_op jit(solution)/shard_map/ppermute | solution.py:14
  51.2 0.9 constant_dynamic-update-slice_fusion.4
  52.1 0.9 constant_dynamic-update-slice_fusion.3
  53.0 0.0 collective-permute-done.3
  53.0 0.9 constant_dynamic-update-slice_fusion.2
  53.9 15.8 %collective-permute-done.4 = bf16[2,2,256,256]{2,3,0,1:T(8,128)(2,1)S(1)} collective-permute-done((bf16[2,2,256,256]{2,3,0,1:T(8,128)(2,1)S(1)}, bf16[2,2,256,256]{2,3,0,1:T(8,128)(2,1)S(1)}, u32[]{:S(2)}, u32[]{:S(2)}) %collective-permute-start.4) | collective-permute-done | bytes 524320 | tf_op jit(solution)/shard_map/ppermute | solution.py:14
  69.7 0.9 constant_dynamic-update-slice_fusion.1
  70.6 0.0 collective-permute-done.5
  70.6 0.9 constant_dynamic-update-slice_fusion
  71.5 0.9 broadcast_dynamic-update-slice_fusion.3
  72.3 1.1 broadcast_dynamic-update-slice_fusion.1
  73.4 1.9 %dynamic-slice_dynamic-update-slice_fusion.11 = bf16[2,2,3072,256]{2,3,0,1:T(8,128)(2,1)} fusion(bf16[2,2,3328,256]{2,3,0,1:T(8,128)(2,1)} %broadcast_dynamic-update-slice_fusion.1, s32[]{:T(128)S(6)} %select_n.44), kind=kLoop, calls=%fused_computation.24 | loop fusion | bytes 1048580
  75.4 1.9 %dynamic-slice_dynamic-update-slice_fusion.10 = bf16[2,2,3072,256]{2,3,0,1:T(8,128)(2,1)} fusion(bf16[2,2,3072,256]{2,3,0,1:T(8,128)(2,1)} %dynamic-slice_dynamic-update-slice_fusion.11, bf16[2,2,3328,256]{2,3,0,1:T(8,128)(2,1)} %broadcast_dynamic-update-slice_fusion.1, s32[]{:T(128)S(6)} %select_n.45), kind=kLoop, calls=%fused_computation.23 | loop fusion | bytes 1048580
  77.3 1.9 %dynamic-slice_dynamic-update-slice_fusion.9 = bf16[2,2,3072,256]{2,3,0,1:T(8,128)(2,1)} fusion(bf16[2,2,3072,256]{2,3,0,1:T(8,128)(2,1)} %dynamic-slice_dynamic-update-slice_fusion.10, bf16[2,2,3328,256]{2,3,0,1:T(8,128)(2,1)} %broadcast_dynamic-update-slice_fusion.1, s32[]{:T(128)S(6)} %select_n.46), kind=kLoop, calls=%fused_computation.22 | loop fusion | bytes 1048580
  79.2 2.0 %dynamic-slice_dynamic-update-slice_fusion.8 = bf16[2,2,3072,256]{2,3,0,1:T(8,128)(2,1)} fusion(bf16[2,2,3072,256]{2,3,0,1:T(8,128)(2,1)} %dynamic-slice_dynamic-update-slice_fusion.9, bf16[2,2,3328,256]{2,3,0,1:T(8,128)(2,1)} %broadcast_dynamic-update-slice_fusion.1, s32[]{:T(128)S(6)} %select_n.47), kind=kLoop, calls=%fused_computation.21 | loop fusion | bytes 1048580
  81.2 1.9 %dynamic-slice_dynamic-update-slice_fusion.7 = bf16[2,2,3072,256]{2,3,0,1:T(8,128)(2,1)} fusion(bf16[2,2,3072,256]{2,3,0,1:T(8,128)(2,1)} %dynamic-slice_dynamic-update-slice_fusion.8, bf16[2,2,3328,256]{2,3,0,1:T(8,128)(2,1)} %broadcast_dynamic-update-slice_fusion.1, s32[]{:T(128)S(6)} %select_n.48), kind=kLoop, calls=%fused_computation.20 | loop fusion | bytes 1048580
  83.1 1.9 %dynamic-slice_dynamic-update-slice_fusion.6 = bf16[2,2,3072,256]{2,3,0,1:T(8,128)(2,1)} fusion(bf16[2,2,3072,256]{2,3,0,1:T(8,128)(2,1)} %dynamic-slice_dynamic-update-slice_fusion.7, bf16[2,2,3328,256]{2,3,0,1:T(8,128)(2,1)} %broadcast_dynamic-update-slice_fusion.1, s32[]{:T(128)S(6)} %select_n.49), kind=kLoop, calls=%fused_computation.19 | loop fusion | bytes 1048580
  85.0 2.0 %dynamic-slice_dynamic-update-slice_fusion.5 = bf16[2,2,3072,256]{2,3,0,1:T(8,128)(2,1)} fusion(bf16[2,2,3072,256]{2,3,0,1:T(8,128)(2,1)} %dynamic-slice_dynamic-update-slice_fusion.6, bf16[2,2,3328,256]{2,3,0,1:T(8,128)(2,1)} %broadcast_dynamic-update-slice_fusion.1, s32[]{:T(128)S(6)} %select_n.50), kind=kLoop, calls=%fused_computation.18 | loop fusion | bytes 1048580
  87.0 2.0 %dynamic-slice_dynamic-update-slice_fusion.4 = bf16[2,2,3072,256]{2,3,0,1:T(8,128)(2,1)} fusion(bf16[2,2,3072,256]{2,3,0,1:T(8,128)(2,1)} %dynamic-slice_dynamic-update-slice_fusion.5, bf16[2,2,3328,256]{2,3,0,1:T(8,128)(2,1)} %broadcast_dynamic-update-slice_fusion.1, s32[]{:T(128)S(6)} %select_n.51), kind=kLoop, calls=%fused_computation.17 | loop fusion | bytes 1048580
  89.0 2.0 %dynamic-slice_dynamic-update-slice_fusion.3 = bf16[2,2,3072,256]{2,3,0,1:T(8,128)(2,1)} fusion(bf16[2,2,3072,256]{2,3,0,1:T(8,128)(2,1)} %dynamic-slice_dynamic-update-slice_fusion.4, bf16[2,2,3328,256]{2,3,0,1:T(8,128)(2,1)} %broadcast_dynamic-update-slice_fusion.1, s32[]{:T(128)S(6)} %select_n.52), kind=kLoop, calls=%fused_computation.16 | loop fusion | bytes 1048580
  91.0 2.0 %dynamic-slice_dynamic-update-slice_fusion.2 = bf16[2,2,3072,256]{2,3,0,1:T(8,128)(2,1)} fusion(bf16[2,2,3072,256]{2,3,0,1:T(8,128)(2,1)} %dynamic-slice_dynamic-update-slice_fusion.3, bf16[2,2,3328,256]{2,3,0,1:T(8,128)(2,1)} %broadcast_dynamic-update-slice_fusion.1, s32[]{:T(128)S(6)} %select_n.53), kind=kLoop, calls=%fused_computation.15 | loop fusion | bytes 1048580
  92.9 2.0 %dynamic-slice_dynamic-update-slice_fusion.1 = bf16[2,2,3072,256]{2,3,0,1:T(8,128)(2,1)} fusion(bf16[2,2,3072,256]{2,3,0,1:T(8,128)(2,1)} %dynamic-slice_dynamic-update-slice_fusion.2, bf16[2,2,3328,256]{2,3,0,1:T(8,128)(2,1)} %broadcast_dynamic-update-slice_fusion.1, s32[]{:T(128)S(6)} %select_n.54), kind=kLoop, calls=%fused_computation.14 | loop fusion | bytes 1048580
  94.9 1.9 %dynamic-slice_dynamic-update-slice_fusion = bf16[2,2,3072,256]{2,3,0,1:T(8,128)(2,1)} fusion(bf16[2,2,3072,256]{2,3,0,1:T(8,128)(2,1)} %dynamic-slice_dynamic-update-slice_fusion.1, bf16[2,2,3328,256]{2,3,0,1:T(8,128)(2,1)} %broadcast_dynamic-update-slice_fusion.1, s32[]{:T(128)S(6)} %select_n.55), kind=kLoop, calls=%fused_computation.13 | loop fusion | bytes 1048580 | tf_op jit(solution)/shard_map/concatenate | solution.py:40
  96.8 0.0 all-gather.2.cloned.1.call-done
  96.8 0.0 copy-start.1
  96.8 4.0 %fusion.1 = f32[2,256,256]{2,1,0:T(8,128)S(1)} fusion(bf16[2,2,3072,256]{2,3,0,1:T(8,128)(2,1)} %dynamic-slice_dynamic-update-slice_fusion, bf16[2,2,256,3072]{3,2,0,1:T(8,128)(2,1)} %all-gather.2.cloned.1.call-done), kind=kOutput, calls=%fused_computation.5 | convolution fusion | flops 805306368 | bytes 6815744 | tf_op jit(solution)/shard_map/sxc,scr->sxr/dot_general | solution.py:42
  100.8 0.6 copy-done.1
  101.4 2.9 %fusion = f32[2,256,256]{2,1,0:T(8,128)S(1)} fusion(bf16[2,2,3072,256]{2,3,0,1:T(8,128)(2,1)} %dynamic-slice_dynamic-update-slice_fusion, bf16[2,2,256,3072]{3,2,0,1:T(8,128)(2,1)S(1)} %copy-done.1), kind=kOutput, calls=%fused_computation.4 | convolution fusion | flops 805306368 | bytes 6815744 | tf_op jit(solution)/shard_map/sxc,scr->sxr/dot_general | solution.py:51
  104.4 2.9 %fusion.5 = f32[2,1,256,256]{2,3,0,1:T(8,128)S(1)} fusion(f32[2,256,256]{2,1,0:T(8,128)S(1)} %fusion.1, bf16[2,2,256,3072]{3,2,0,1:T(8,128)(2,1)S(1)} %copy-done.1, bf16[2,2,3072,256]{2,3,0,1:T(8,128)(2,1)} %dynamic-slice_dynamic-update-slice_fusion), kind=kOutput, calls=%fused_computation.9 | convolution fusion | flops 805437440 | bytes 7340032 | tf_op jit(solution)/shard_map/sxc,scr->sxr/dot_general | solution.py:45
  107.3 2.9 %fusion.7 = f32[2,1,256,256]{2,3,0,1:T(8,128)S(1)} fusion(f32[2,256,256]{2,1,0:T(8,128)S(1)} %fusion, bf16[2,2,256,3072]{3,2,0,1:T(8,128)(2,1)S(1)} %copy-done.1, bf16[2,2,3072,256]{2,3,0,1:T(8,128)(2,1)} %dynamic-slice_dynamic-update-slice_fusion), kind=kOutput, calls=%fused_computation.11 | convolution fusion | flops 805437440 | bytes 7340032 | tf_op jit(solution)/shard_map/sxc,scr->sxr/dot_general | solution.py:48
  110.2 0.1 pad_maximum_fusion
  110.3 1.3 %copy.12 = f32[2,2,256,256]{3,2,1,0:T(8,128)} copy(f32[2,2,256,256]{2,3,0,1:T(8,128)S(1)} %pad_maximum_fusion) | data formatting | bytes 2097152 | tf_op jit(solution)/shard_map/stack | solution.py:54
  (1 shorter events, 0.0 us)
Async XLA Ops:
  6.5 18.3 %copy-start = (s32[4,12]{1,0:T(4,128)S(1)}, s32[4,12]{1,0:T(4,128)}, u32[]{:S(2)}) copy-start(s32[4,12]{1,0:T(4,128)} %param.5) | copy-start | bytes 580
  6.5 90.3 %all-gather.2.cloned.1.call-start = ((), (), s32[]{:S(2)}) async-start(), calls=%async_computation | async-start | bytes 7864320 | tf_op jit(solution)/shard_map/all_gather | solution.py:41
  10.5 23.8 %collective-permute-start = (bf16[2,2,256,256]{2,3,0,1:T(8,128)(2,1)S(1)}, bf16[2,2,256,256]{2,3,0,1:T(8,128)(2,1)S(1)}, u32[]{:S(2)}, u32[]{:S(2)}) collective-permute-start(bf16[2,2,256,256]{2,3,0,1:T(8,128)(2,1)S(1)} %copy.4), channel_id=1, source_target_pairs={{0,12},{1,13},{2,14},{3,15},{16,28},{17,29},{18,30},{19,31}} | collective-permute-start | bytes 1572872 | tf_op jit(solution)/shard_map/ppermute | solution.py:14
  17.5 23.6 %collective-permute-start.1 = (bf16[2,2,256,256]{2,3,0,1:T(8,128)(2,1)S(1)}, bf16[2,2,256,256]{2,3,0,1:T(8,128)(2,1)S(1)}, u32[]{:S(2)}, u32[]{:S(2)}) collective-permute-start(bf16[2,2,256,256]{2,3,0,1:T(8,128)(2,1)S(1)} %copy.4), channel_id=1, source_target_pairs={{0,8},{4,12},{1,9},{5,13},{2,10},{6,14},{3,11},{7,15},{16,24},{20,... | collective-permute-start | bytes 1572872 | tf_op jit(solution)/shard_map/ppermute | solution.py:14
  18.8 32.4 %collective-permute-start.2 = (bf16[2,2,256,256]{2,3,0,1:T(8,128)(2,1)S(1)}, bf16[2,2,256,256]{2,3,0,1:T(8,128)(2,1)S(1)}, u32[]{:S(2)}, u32[]{:S(2)}) collective-permute-start(bf16[2,2,256,256]{2,3,0,1:T(8,128)(2,1)S(1)} %copy.4), channel_id=1, source_target_pairs={{0,4},{4,8},{8,12},{1,5},{5,9},{9,13},{2,6},{6,10},{10,14},{3,7},{... | collective-permute-start | bytes 1572872 | tf_op jit(solution)/shard_map/ppermute | solution.py:14
  21.3 31.7 %collective-permute-start.3 = (bf16[2,2,256,256]{2,3,0,1:T(8,128)(2,1)S(1)}, bf16[2,2,256,256]{2,3,0,1:T(8,128)(2,1)S(1)}, u32[]{:S(2)}, u32[]{:S(2)}) collective-permute-start(bf16[2,2,256,256]{2,3,0,1:T(8,128)(2,1)S(1)} %copy.4), channel_id=1, source_target_pairs={{4,0},{8,4},{12,8},{5,1},{9,5},{13,9},{6,2},{10,6},{14,10},{7,3},{... | collective-permute-start | bytes 1572872 | tf_op jit(solution)/shard_map/ppermute | solution.py:14
  22.6 47.1 %collective-permute-start.4 = (bf16[2,2,256,256]{2,3,0,1:T(8,128)(2,1)S(1)}, bf16[2,2,256,256]{2,3,0,1:T(8,128)(2,1)S(1)}, u32[]{:S(2)}, u32[]{:S(2)}) collective-permute-start(bf16[2,2,256,256]{2,3,0,1:T(8,128)(2,1)S(1)} %copy.4), channel_id=1, source_target_pairs={{8,0},{12,4},{9,1},{13,5},{10,2},{14,6},{11,3},{15,7},{24,16},{28,... | collective-permute-start | bytes 1572872 | tf_op jit(solution)/shard_map/ppermute | solution.py:14
  34.3 36.3 %collective-permute-start.5 = (bf16[2,2,256,256]{2,3,0,1:T(8,128)(2,1)S(1)}, bf16[2,2,256,256]{2,3,0,1:T(8,128)(2,1)S(1)}, u32[]{:S(2)}, u32[]{:S(2)}) collective-permute-start(bf16[2,2,256,256]{2,3,0,1:T(8,128)(2,1)S(1)} %copy.4), channel_id=1, source_target_pairs={{12,0},{13,1},{14,2},{15,3},{28,16},{29,17},{30,18},{31,19}} | collective-permute-start | bytes 1572872 | tf_op jit(solution)/shard_map/ppermute | solution.py:14
  96.8 4.6 %copy-start.1 = (bf16[2,2,256,3072]{3,2,0,1:T(8,128)(2,1)S(1)}, bf16[2,2,256,3072]{3,2,0,1:T(8,128)(2,1)}, u32[]{:S(2)}) copy-start(bf16[2,2,256,3072]{3,2,0,1:T(8,128)(2,1)} %all-gather.2.cloned.1.call-done) | copy-start | bytes 18874372
Sparse Core Ops, SparseCore 0:
  9.4 49.0 all-gather.1
where the time goes:
time: 120 us; the launch traced here: 118 us
  local copies, waits for them, and re-layouts  40.1 us (33%)
  waiting for transfers between devices  29.7 us (25%)
  between operations  21.1 us (18%)
  starting transfers between devices  14.7 us (12%)
  matrix products  12.7 us (11%)
    unnamed x27, local copies, waits for them, and re-layouts  35.2 us
    ppermute x6, waiting for transfers between devices, from_behind(): return lax.ppermute(x, axis, pairs)  29.7 us
    ppermute x6, starting transfers between devices, from_behind(): return lax.ppermute(x, axis, pairs)  14.7 us
    dot_general x1, matrix products, body(): jnp.einsum('sxc,scr->sxr', panel_piece[:, 0], selected[:, 0], preferred_e...  3.99 us
    dot_general x1, matrix products, body(): jnp.einsum('sxc,scr->sxr', panel_piece[:, 1], selected[:, 1], preferred_e...  2.91 us
    dot_general x1, matrix products, body(): jnp.einsum('sxc,scr->sxr', panel_piece[:, 0], selected[:, 1], preferred_e...  2.9 us
    dot_general x1, matrix products, body(): jnp.einsum('sxc,scr->sxr', panel_piece[:, 1], selected[:, 0], preferred_e...  2.9 us
  transfers between devices with their start and end apart: 7, of which 3 were waited for; matrix products, arithmetic and copies ran while one was open for 30% of the time, Pallas kernels for 0%

commit v1 on v0

v1 whole, which is shorter than its diff:
```python
import functools

import jax
import jax.numpy as jnp
from jax import lax
from jax.experimental import pallas as pl
from jax.experimental.pallas import tpu as pltpu
from jax.sharding import PartitionSpec as P

BLK = 256
APER = 12
HW = 6


def from_behind(x, axis, by):
    peers = lax.axis_size(axis)
    pairs = [(i, i + by) for i in range(peers) if 0 <= i + by < peers]
    return lax.ppermute(x, axis, pairs)


def swap(x, axis, bit):
    peers = lax.axis_size(axis)
    return lax.ppermute(x, axis, [(i, i ^ bit) for i in range(peers)])


def gather_window(data):
    axis_count = lax.axis_size("src")
    if axis_count <= 2 * HW + 1:
        return lax.all_gather(data, "src", axis=0, tiled=False), False
    pieces = [data if off == 0 else from_behind(data, "src", -off) for off in range(-HW, HW + 1)]
    return jnp.stack(pieces, axis=0), True


def gather_panels(primaries):
    peers = lax.axis_size("rcv")
    panels = {0: primaries}
    bit = peers // 2
    while bit >= 1:
        for m in list(panels):
            panels[m ^ bit] = swap(panels[m], "rcv", bit)
        bit //= 2
    return [panels[m] for m in range(peers)]


def kernel(relative, per_shard, aperture_ref, *refs):
    *panel_refs, window_ref, out_ref = refs
    block = lax.axis_index("src")
    me = lax.axis_index("rcv")
    first = block - HW if relative else 0
    real = None
    imag = None
    for m, panel_ref in enumerate(panel_refs):
        shard = lax.bitwise_xor(me, m)
        rows = [aperture_ref[block, shard * per_shard + q] - first for q in range(per_shard)]
        data_re = jnp.concatenate([window_ref[row, 0, 0] for row in rows], axis=0)
        data_im = jnp.concatenate([window_ref[row, 0, 1] for row in rows], axis=0)
        panel_re = panel_ref[0, 0]
        panel_im = panel_ref[0, 1]
        dot = functools.partial(jnp.dot, preferred_element_type=jnp.float32)
        re = dot(panel_re, data_re) - dot(panel_im, data_im)
        im = dot(panel_re, data_im) + dot(panel_im, data_re)
        real = re if real is None else real + re
        imag = im if imag is None else imag + im
    out_ref[0, 0] = real
    out_ref[0, 1] = imag


def body(primaries, data, aperture):
    surveys = primaries.shape[0]
    columns = primaries.shape[3]
    width = data.shape[3]
    window, relative = gather_window(data)
    panels = gather_panels(primaries)
    depth = window.shape[0]
    return pl.pallas_call(
        functools.partial(kernel, relative, columns // BLK),
        grid=(surveys,),
        out_shape=jax.ShapeDtypeStruct((surveys, 2, BLK, width), jnp.float32),
        in_specs=[pl.BlockSpec(memory_space=pltpu.SMEM)]
        + [pl.BlockSpec((1, 2, BLK, columns), lambda v: (v, 0, 0, 0)) for _ in panels]
        + [pl.BlockSpec((depth, 1, 2, BLK, width), lambda v: (0, v, 0, 0, 0))],
        out_specs=pl.BlockSpec((1, 2, BLK, width), lambda v: (v, 0, 0, 0)),
        compiler_params=pltpu.CompilerParams(vmem_limit_bytes=40 * 1024 * 1024),
        cost_estimate=pl.CostEstimate(
            flops=8 * surveys * BLK * BLK * APER * width, bytes_accessed=9 << 20, transcendentals=0
        ),
    )(aperture, *panels, window)


def solution(mesh):
    placed = (P("freq", None, "src", "rcv"), P("freq", None, "src", "rcv"), P())
    return jax.shard_map(
        body, mesh=mesh, in_specs=placed, out_specs=P("freq", None, "src", "rcv"), check_vma=False
    )
```

time: 120 us -> 73.9 us (0.62); the launches traced: 118 us -> 73.7 us
  local copies, waits for them, and re-layouts: 40.1 us -> 3.68 us
  waiting for transfers between devices: 29.7 us -> 48 us
  matrix products: 12.7 us -> 0 us
  starting transfers between devices: 14.7 us -> 3.01 us
  between operations: 21.1 us -> 13.4 us
  Pallas kernels: 0 us -> 5.59 us
    unnamed x27 -> x6, local copies, waits for them, and re-layouts: 35.2 us -> 3.68 us
    all_gather x1, waiting for transfers between devices: 0.01 us -> 12.7 us  [gather_window(): return (lax.all_gather(data, 'src', axis=0, tiled=False), False)]
    dot_general x4 -> x0, matrix products: 12.7 us -> none  [the longest x1 3.99 us: body(): jnp.einsum('sxc,scr->sxr', panel_piece[:, 0], selected[:, 0], preferred_e...]
    ppermute x6 -> x3, starting transfers between devices: 14.7 us -> 3.01 us  [swap(): return lax.ppermute(x, axis, [(i, i ^ bit) for i in range(peers)])]
    pallas_call x0 -> x1, Pallas kernels: none -> 5.59 us  [body(): pl.pallas_call(functools.partial(kernel, relative, columns // BLK), grid=...]
    ppermute x6 -> x3, waiting for transfers between devices: 29.7 us -> 34.6 us  [swap(): return lax.ppermute(x, axis, [(i, i ^ bit) for i in range(peers)])]
    concatenate x2 -> x0, local copies, waits for them, and re-layouts: 2.97 us -> none  [the longest x1 1.89 us: body(): selected = jnp.concatenate(picked_list, axis=2)]
    another operation x1 -> x0, local copies, waits for them, and re-layouts: 1.31 us -> none  [body(): return jnp.stack([real_part, imag_part], axis=1)]
  transfers between devices with their start and end apart: 7 -> 4, of which waited for: 3 -> 2; matrix products, arithmetic and copies ran while one was open for 30% -> 0% of each run, Pallas kernels for 0% -> 0%
where the time goes in v1:
time: 73.9 us; the launch traced here: 73.7 us
  waiting for transfers between devices  48 us (65%)
  between operations  13.4 us (18%)
  Pallas kernels  5.59 us (8%)
  local copies, waits for them, and re-layouts  3.68 us (5%)
  starting transfers between devices  3.01 us (4%)
    ppermute x3, waiting for transfers between devices, swap(): return lax.ppermute(x, axis, [(i, i ^ bit) for i in range(peers)])  34.6 us
    all_gather x1, waiting for transfers between devices, gather_window(): return (lax.all_gather(data, 'src', axis=0, tiled=False), False)  12.7 us
    pallas_call x1, Pallas kernels, body(): pl.pallas_call(functools.partial(kernel, relative, columns // BLK), grid=...  5.59 us
    unnamed x6, local copies, waits for them, and re-layouts  3.68 us
    ppermute x3, starting transfers between devices, swap(): return lax.ppermute(x, axis, [(i, i ^ bit) for i in range(peers)])  3.01 us
  transfers between devices with their start and end apart: 4, of which 2 were waited for; matrix products, arithmetic and copies ran while one was open for 0% of the time, Pallas kernels for 0%

profile of v1, /device:TPU:0, one launch (start us, length us, event | category | flops | bytes accessed | tf_op | source)
XLA Modules:
  0.0 73.7 jit_solution(15519046654457732772)
XLA Ops:
  6.5 0.0 all-gather.3.cloned.1.call-start
  6.5 0.7 all-gather.3.cloned.1.call-update
  7.3 3.0 %collective-permute-start.1 = (bf16[2,2,256,768]{3,2,1,0:T(8,128)(2,1)}, bf16[2,2,256,768]{3,2,1,0:T(8,128)(2,1)S(1)}, u32[]{:S(2)}, u32[]{:S(2)}) collective-permute-start(bf16[2,2,256,768]{3,2,1,0:T(8,128)(2,1)} %refs_0_.1), channel_id=1, source_target_pairs={{0,2},{1,3},{2,0},{3,1},{4,6},{5,7},{6,4},{7,5},{8,10},{9,11},{10,... | collective-permute-start | bytes 4718600 | tf_op jit(solution)/shard_map/ppermute | solution.py:23
  10.3 0.0 collective-permute-start
  10.3 34.6 %collective-permute-done.1.refs_2_ = bf16[2,2,256,768]{3,2,1,0:T(8,128)(2,1)S(1)} collective-permute-done((bf16[2,2,256,768]{3,2,1,0:T(8,128)(2,1)}, bf16[2,2,256,768]{3,2,1,0:T(8,128)(2,1)S(1)}, u32[]{:S(2)}, u32[]{:S(2)}) %collective-permute-start.1) | collective-permute-done | bytes 1572896 | tf_op jit(solution)/shard_map/ppermute | solution.py:23
  44.9 0.0 collective-permute-start.2
  44.9 0.0 collective-permute-done.refs_1_
  44.9 12.7 %all-gather.3.cloned.1.call-done = bf16[8,2,256,256]{3,2,1,0:T(8,128)(2,1)} async-done(((bf16[2,2,256,256]{3,2,1,0:T(8,128)(2,1)}), bf16[8,2,256,256]{3,2,1,0:T(8,128)(2,1)}) %all-gather.3.cloned.1.call-update) | async-done | bytes 2097168 | tf_op jit(solution)/shard_map/all_gather | solution.py:29
  57.6 0.0 collective-permute-done.2.refs_3_
  57.6 0.0 copy-start
  57.6 1.6 %copy-done = bf16[8,2,256,256]{3,2,1,0:T(8,128)(2,1)S(1)} copy-done((bf16[8,2,256,256]{3,2,1,0:T(8,128)(2,1)S(1)}, bf16[8,2,256,256]{3,2,1,0:T(8,128)(2,1)}, u32[]{:S(2)}) %copy-start) | copy-done | bytes 2097176
  59.2 0.0 copy-start.1
  59.2 1.4 %copy-done.1 = bf16[2,2,256,768]{3,2,1,0:T(8,128)(2,1)S(1)} copy-done((bf16[2,2,256,768]{3,2,1,0:T(8,128)(2,1)S(1)}, bf16[2,2,256,768]{3,2,1,0:T(8,128)(2,1)}, u32[]{:S(2)}) %copy-start.1) | copy-done | bytes 1572888
  60.6 0.0 copy-start.2
  60.6 0.7 copy-done.2
  61.3 5.6 %shard_map.37 = f32[2,2,256,256]{3,2,1,0:T(8,128)} custom-call(s32[4,12]{1,0:T(4,128)S(1)} %copy-done.2, bf16[2,2,256,768]{3,2,1,0:T(8,128)(2,1)S(1)} %copy-done.1, bf16[2,2,256,768]{3,2,1,0:T(8,128)(2,1)S(1)} %collective-permute-done.refs_1_, bf16[2,2,256,768]{3,2,1,0:T(8,128)(2,1)S(1)} %collective-permute-done.1.refs_2_, ...), custom_call_target="tpu_custom_call" | custom-call | flops 3221225472 | bytes 9437184 | tf_op jit(solution)/shard_map/pallas_call | solution.py:75
Async XLA Ops:
  6.5 51.1 %all-gather.3.cloned.1.call-start = ((), (), s32[]{:S(2)}) async-start(), calls=%async_computation | async-start | bytes 2621440 | tf_op jit(solution)/shard_map/all_gather | solution.py:29
  7.3 37.6 %collective-permute-start.1 = (bf16[2,2,256,768]{3,2,1,0:T(8,128)(2,1)}, bf16[2,2,256,768]{3,2,1,0:T(8,128)(2,1)S(1)}, u32[]{:S(2)}, u32[]{:S(2)}) collective-permute-start(bf16[2,2,256,768]{3,2,1,0:T(8,128)(2,1)} %refs_0_.1), channel_id=1, source_target_pairs={{0,2},{1,3},{2,0},{3,1},{4,6},{5,7},{6,4},{7,5},{8,10},{9,11},{10,... | collective-permute-start | bytes 4718600 | tf_op jit(solution)/shard_map/ppermute | solution.py:23
  10.3 34.6 %collective-permute-start = (bf16[2,2,256,768]{3,2,1,0:T(8,128)(2,1)}, bf16[2,2,256,768]{3,2,1,0:T(8,128)(2,1)S(1)}, u32[]{:S(2)}, u32[]{:S(2)}) collective-permute-start(bf16[2,2,256,768]{3,2,1,0:T(8,128)(2,1)} %refs_0_.1), channel_id=1, source_target_pairs={{0,1},{1,0},{2,3},{3,2},{4,5},{5,4},{6,7},{7,6},{8,9},{9,8},{10,11... | collective-permute-start | bytes 4718600 | tf_op jit(solution)/shard_map/ppermute | solution.py:23
  44.9 12.7 %collective-permute-start.2 = (bf16[2,2,256,768]{3,2,1,0:T(8,128)(2,1)S(1)}, bf16[2,2,256,768]{3,2,1,0:T(8,128)(2,1)}, u32[]{:S(2)}, u32[]{:S(2)}) collective-permute-start(bf16[2,2,256,768]{3,2,1,0:T(8,128)(2,1)S(1)} %collective-permute-done.1.refs_2_), channel_id=1, source_target_pairs={{0,1},{1,0},{2,3},{3,2},{4,5},{5,4},{6,7},{7,6},{8,9},{9,8},{10,11... | collective-permute-start | bytes 4718600 | tf_op jit(solution)/shard_map/ppermute | solution.py:23
  57.6 1.6 %copy-start = (bf16[8,2,256,256]{3,2,1,0:T(8,128)(2,1)S(1)}, bf16[8,2,256,256]{3,2,1,0:T(8,128)(2,1)}, u32[]{:S(2)}) copy-start(bf16[8,2,256,256]{3,2,1,0:T(8,128)(2,1)} %all-gather.3.cloned.1.call-done) | copy-start | bytes 6291460
  59.2 1.4 %copy-start.1 = (bf16[2,2,256,768]{3,2,1,0:T(8,128)(2,1)S(1)}, bf16[2,2,256,768]{3,2,1,0:T(8,128)(2,1)}, u32[]{:S(2)}) copy-start(bf16[2,2,256,768]{3,2,1,0:T(8,128)(2,1)} %refs_0_.1) | copy-start | bytes 4718596
  60.6 0.7 copy-start.2
Sparse Core Ops, SparseCore 0:
  8.9 48.6 all-gather.2

commit v2 on v1

v2 whole, which is shorter than its diff:
```python
import functools

import jax
import jax.numpy as jnp
from jax import lax
from jax.experimental import pallas as pl
from jax.experimental.pallas import tpu as pltpu
from jax.sharding import PartitionSpec as P

BLK = 256
APER = 12
HW = 6


def from_behind(x, axis, by):
    peers = lax.axis_size(axis)
    pairs = [(i, i + by) for i in range(peers) if 0 <= i + by < peers]
    return lax.ppermute(x, axis, pairs)


def swap(x, axis, bit):
    peers = lax.axis_size(axis)
    return lax.ppermute(x, axis, [(i, i ^ bit) for i in range(peers)])


def gather_window(parts):
    reach = min(HW, lax.axis_size("src") - 1)
    windows = [{0: part} for part in parts]
    for hop in range(1, reach + 1):
        for window in windows:
            window[-hop] = from_behind(window[1 - hop], "src", 1)
            window[hop] = from_behind(window[hop - 1], "src", -1)
    return [[window[distance] for distance in range(-reach, reach + 1)] for window in windows]


def gather_panels(parts):
    peers = lax.axis_size("rcv")
    gathered = [{0: part} for part in parts]
    bit = peers // 2
    while bit >= 1:
        for panels in gathered:
            for m in list(panels):
                panels[m ^ bit] = swap(panels[m], "rcv", bit)
        bit //= 2
    return [[panels[m] for m in range(peers)] for panels in gathered]


def kernel(survey, panel_count, piece_count, aperture_ref, *refs):
    panel_refs = refs[:panel_count]
    piece_refs = refs[panel_count : panel_count + piece_count]
    out_ref, panels, window, result, panel_sems, piece_sems, out_sem = refs[-7:]
    reach = piece_count // 2
    block = lax.axis_index("src")
    me = lax.axis_index("rcv")
    per_shard = panels.shape[-1] // BLK
    piece_copies = [
        pltpu.make_async_copy(ref, window.at[k], piece_sems.at[k]) for k, ref in enumerate(piece_refs)
    ]
    panel_copies = [
        pltpu.make_async_copy(ref, panels.at[m], panel_sems.at[m]) for m, ref in enumerate(panel_refs)
    ]
    for copy in piece_copies:
        copy.start()
    for copy in panel_copies:
        copy.start()
    for copy in piece_copies:
        copy.wait()
    dot = functools.partial(jnp.dot, preferred_element_type=jnp.float32)
    real = None
    imag = None
    for m in range(panel_count):
        shard = lax.bitwise_xor(me, m)
        rows = [aperture_ref[block, shard * per_shard + q] - block + reach for q in range(per_shard)]
        data_re = jnp.concatenate([window[row, 0, 0] for row in rows], axis=0)
        data_im = jnp.concatenate([window[row, 0, 1] for row in rows], axis=0)
        panel_copies[m].wait()
        panel_re = panels[m, 0, 0]
        panel_im = panels[m, 0, 1]
        re = dot(panel_re, data_re) - dot(panel_im, data_im)
        im = dot(panel_re, data_im) + dot(panel_im, data_re)
        real = re if real is None else real + re
        imag = im if imag is None else imag + im
    result[0] = real
    result[1] = imag
    out_copy = pltpu.make_async_copy(result, out_ref.at[survey], out_sem)
    out_copy.start()
    out_copy.wait()


def products(survey, surveys, aperture, panels, pieces, out):
    columns = panels[0].shape[-1]
    width = pieces[0].shape[-1]
    anywhere = pl.BlockSpec(memory_space=pl.ANY)
    operands = [aperture, *panels, *pieces]
    in_specs = [pl.BlockSpec(memory_space=pltpu.SMEM)] + [anywhere] * (len(panels) + len(pieces))
    aliases = {}
    if out is not None:
        aliases = {len(operands): 0}
        operands.append(out)
        in_specs.append(anywhere)
    return pl.pallas_call(
        functools.partial(kernel, survey, len(panels), len(pieces)),
        out_shape=jax.ShapeDtypeStruct((surveys, 2, BLK, width), jnp.float32),
        in_specs=in_specs,
        out_specs=anywhere,
        scratch_shapes=[
            pltpu.VMEM((len(panels), 1, 2, BLK, columns), jnp.bfloat16),
            pltpu.VMEM((len(pieces), 1, 2, BLK, width), jnp.bfloat16),
            pltpu.VMEM((2, BLK, width), jnp.float32),
            pltpu.SemaphoreType.DMA((len(panels),)),
            pltpu.SemaphoreType.DMA((len(pieces),)),
            pltpu.SemaphoreType.DMA,
        ],
        input_output_aliases=aliases,
        compiler_params=pltpu.CompilerParams(vmem_limit_bytes=24 * 1024 * 1024),
        cost_estimate=pl.CostEstimate(
            flops=8 * BLK * BLK * APER * width, bytes_accessed=5 << 20, transcendentals=0
        ),
    )(*operands)


def body(primaries, data, aperture):
    surveys = primaries.shape[0]
    panels = gather_panels([primaries[v : v + 1] for v in range(surveys)])
    windows = gather_window([data[v : v + 1] for v in range(surveys)])
    out = None
    for v in range(surveys):
        out = products(v, surveys, aperture, panels[v], windows[v], out)
    return out


def solution(mesh):
    placed = (P("freq", None, "src", "rcv"), P("freq", None, "src", "rcv"), P())
    return jax.shard_map(
        body, mesh=mesh, in_specs=placed, out_specs=P("freq", None, "src", "rcv"), check_vma=False
    )
```

time: 73.9 us -> 66.4 us (0.90)
  starting transfers between devices: 3.01 us -> 35.2 us
  waiting for transfers between devices: 48 us -> 20.7 us
  between operations: 13.4 us -> 0.18 us
  Pallas kernels: 5.59 us -> 8.37 us
  local copies, waits for them, and re-layouts: 3.68 us -> 1.57 us
    ppermute x0 -> x12, starting transfers between devices: none -> 31 us  [from_behind(): return lax.ppermute(x, axis, pairs)]
    ppermute x3 -> x6, waiting for transfers between devices: 34.6 us -> 3.77 us  [swap(): return lax.ppermute(x, axis, [(i, i ^ bit) for i in range(peers)])]
    ppermute x0 -> x12, waiting for transfers between devices: none -> 16.9 us  [from_behind(): return lax.ppermute(x, axis, pairs)]
    all_gather x1 -> x0, waiting for transfers between devices: 12.7 us -> none  [gather_window(): return (lax.all_gather(data, 'src', axis=0, tiled=False), False)]
    unnamed x6 -> x4, local copies, waits for them, and re-layouts: 3.68 us -> 0.01 us
    pallas_call x1 -> x2, Pallas kernels: 5.59 us -> 8.37 us  [products(): pl.pallas_call(functools.partial(kernel, survey, len(panels), len(pieces)...]
    slice x0 -> x2, local copies, waits for them, and re-layouts: none -> 1.56 us  [the longest x1 1.53 us: body(): panels = gather_panels([primaries[v:v + 1] for v in range(surveys)])]
    ppermute x3 -> x6, starting transfers between devices: 3.01 us -> 4.18 us  [swap(): return lax.ppermute(x, axis, [(i, i ^ bit) for i in range(peers)])]
  transfers between devices with their start and end apart: 4 -> 18, of which waited for: 2 -> 8; matrix products, arithmetic and copies ran while one was open for 0% -> 0% of each run, Pallas kernels for 0% -> 6%
where the time goes in v2:
time: 66.4 us; the launch traced here: 66 us
  starting transfers between devices  35.2 us (53%)
  waiting for transfers between devices  20.7 us (31%)
  Pallas kernels  8.37 us (13%)
  local copies, waits for them, and re-layouts  1.57 us (2%)
    ppermute x12, starting transfers between devices, from_behind(): return lax.ppermute(x, axis, pairs)  31 us
    ppermute x12, waiting for transfers between devices, from_behind(): return lax.ppermute(x, axis, pairs)  16.9 us
    pallas_call x2, Pallas kernels, products(): pl.pallas_call(functools.partial(kernel, survey, len(panels), len(pieces)...  8.37 us
    ppermute x6, starting transfers between devices, swap(): return lax.ppermute(x, axis, [(i, i ^ bit) for i in range(peers)])  4.18 us
    ppermute x6, waiting for transfers between devices, swap(): return lax.ppermute(x, axis, [(i, i ^ bit) for i in range(peers)])  3.77 us
    slice x1, local copies, waits for them, and re-layouts, body(): panels = gather_panels([primaries[v:v + 1] for v in range(surveys)])  1.53 us
  transfers between devices with their start and end apart: 18, of which 8 were waited for; matrix products, arithmetic and copies ran while one was open for 0% of the time, Pallas kernels for 6%

profile of v2, /device:TPU:0, one launch (start us, length us, event | category | flops | bytes accessed | tf_op | source)
XLA Modules:
  0.0 66.0 jit_solution(1625306889811290273)
XLA Ops:
  0.0 0.0 copy-start.1
  0.0 0.0 copy-start
  0.0 1.5 %fusion = (bf16[1,2,256,768]{3,2,1,0:T(8,128)(2,1)S(1)}, bf16[1,2,256,768]{3,2,1,0:T(8,128)(2,1)S(1)}) fusion(bf16[2,2,256,768]{3,2,1,0:T(8,128)(2,1)} %param.3), kind=kLoop, calls=%fused_computation | loop fusion | bytes 3145728 | tf_op jit(solution)/shard_map/slice | solution.py:124
  1.5 3.0 %collective-permute-start.10 = (bf16[1,2,256,768]{3,2,1,0:T(8,128)(2,1)S(1)}, bf16[1,2,256,768]{3,2,1,0:T(8,128)(2,1)S(1)}, u32[]{:S(2)}, u32[]{:S(2)}) collective-permute-start(bf16[1,2,256,768]{3,2,1,0:T(8,128)(2,1)S(1)} %get-tuple-element.5.refs_0_), channel_id=1, source_target_pairs={{0,2},{1,3},{2,0},{3,1},{4,6},{5,7},{6,4},{7,5},{8,10},{9,11},{10,... | collective-permute-start | bytes 2359304 | tf_op jit(solution)/shard_map/ppermute | solution.py:23
  4.5 0.0 copy-done.1
  4.6 3.5 %collective-permute-start.12 = (bf16[1,2,256,256]{3,2,1,0:T(8,128)(2,1)S(1)}, bf16[1,2,256,256]{3,2,1,0:T(8,128)(2,1)S(1)}, u32[]{:S(2)}, u32[]{:S(2)}) collective-permute-start(bf16[1,2,256,256]{3,2,1,0:T(8,128)(2,1)S(1)} %get-tuple-element.7.refs_7_), channel_id=1, source_target_pairs={{0,4},{4,8},{8,12},{1,5},{5,9},{9,13},{2,6},{6,10},{10,14},{3,7},{... | collective-permute-start | bytes 786440 | tf_op jit(solution)/shard_map/ppermute | solution.py:18
  8.1 1.3 %collective-permute-start.15 = (bf16[1,2,256,256]{3,2,1,0:T(8,128)(2,1)S(1)}, bf16[1,2,256,256]{3,2,1,0:T(8,128)(2,1)S(1)}, u32[]{:S(2)}, u32[]{:S(2)}) collective-permute-start(bf16[1,2,256,256]{3,2,1,0:T(8,128)(2,1)S(1)} %get-tuple-element.7.refs_7_), channel_id=1, source_target_pairs={{4,0},{8,4},{12,8},{5,1},{9,5},{13,9},{6,2},{10,6},{14,10},{7,3},{... | collective-permute-start | bytes 786440 | tf_op jit(solution)/shard_map/ppermute | solution.py:18
  9.4 4.6 %collective-permute-start.3 = (bf16[1,2,256,256]{3,2,1,0:T(8,128)(2,1)S(1)}, bf16[1,2,256,256]{3,2,1,0:T(8,128)(2,1)S(1)}, u32[]{:S(2)}, u32[]{:S(2)}) collective-permute-start(bf16[1,2,256,256]{3,2,1,0:T(8,128)(2,1)S(1)} %get-tuple-element.8.refs_7_), channel_id=1, source_target_pairs={{0,4},{4,8},{8,12},{1,5},{5,9},{9,13},{2,6},{6,10},{10,14},{3,7},{... | collective-permute-start | bytes 786440 | tf_op jit(solution)/shard_map/ppermute | solution.py:18
  14.0 0.6 collective-permute-start.1
  14.6 0.0 collective-permute-done.12.refs_6_
  14.6 1.3 %collective-permute-start.6 = (bf16[1,2,256,256]{3,2,1,0:T(8,128)(2,1)S(1)}, bf16[1,2,256,256]{3,2,1,0:T(8,128)(2,1)S(1)}, u32[]{:S(2)}, u32[]{:S(2)}) collective-permute-start(bf16[1,2,256,256]{3,2,1,0:T(8,128)(2,1)S(1)} %get-tuple-element.8.refs_7_), channel_id=1, source_target_pairs={{4,0},{8,4},{12,8},{5,1},{9,5},{13,9},{6,2},{10,6},{14,10},{7,3},{... | collective-permute-start | bytes 786440 | tf_op jit(solution)/shard_map/ppermute | solution.py:18
  15.8 1.6 %collective-permute-done.15.refs_8_ = bf16[1,2,256,256]{3,2,1,0:T(8,128)(2,1)S(1)} collective-permute-done((bf16[1,2,256,256]{3,2,1,0:T(8,128)(2,1)S(1)}, bf16[1,2,256,256]{3,2,1,0:T(8,128)(2,1)S(1)}, u32[]{:S(2)}, u32[]{:S(2)}) %collective-permute-start.15) | collective-permute-done | bytes 262176 | tf_op jit(solution)/shard_map/ppermute | solution.py:18
  17.5 3.5 %collective-permute-start.13 = (bf16[1,2,256,256]{3,2,1,0:T(8,128)(2,1)S(1)}, bf16[1,2,256,256]{3,2,1,0:T(8,128)(2,1)S(1)}, u32[]{:S(2)}, u32[]{:S(2)}) collective-permute-start(bf16[1,2,256,256]{3,2,1,0:T(8,128)(2,1)S(1)} %collective-permute-done.12.refs_6_), channel_id=1, source_target_pairs={{0,4},{4,8},{8,12},{1,5},{5,9},{9,13},{2,6},{6,10},{10,14},{3,7},{... | collective-permute-start | bytes 786440 | tf_op jit(solution)/shard_map/ppermute | solution.py:18
  20.9 0.0 collective-permute-done.3.refs_6_
  21.0 1.3 %collective-permute-start.16 = (bf16[1,2,256,256]{3,2,1,0:T(8,128)(2,1)S(1)}, bf16[1,2,256,256]{3,2,1,0:T(8,128)(2,1)S(1)}, u32[]{:S(2)}, u32[]{:S(2)}) collective-permute-start(bf16[1,2,256,256]{3,2,1,0:T(8,128)(2,1)S(1)} %collective-permute-done.15.refs_8_), channel_id=1, source_target_pairs={{4,0},{8,4},{12,8},{5,1},{9,5},{13,9},{6,2},{10,6},{14,10},{7,3},{... | collective-permute-start | bytes 786440 | tf_op jit(solution)/shard_map/ppermute | solution.py:18
  22.3 0.8 %collective-permute-done.6.refs_8_ = bf16[1,2,256,256]{3,2,1,0:T(8,128)(2,1)S(1)} collective-permute-done((bf16[1,2,256,256]{3,2,1,0:T(8,128)(2,1)S(1)}, bf16[1,2,256,256]{3,2,1,0:T(8,128)(2,1)S(1)}, u32[]{:S(2)}, u32[]{:S(2)}) %collective-permute-start.6) | collective-permute-done | bytes 262176 | tf_op jit(solution)/shard_map/ppermute | solution.py:18
  23.1 3.7 %collective-permute-start.4 = (bf16[1,2,256,256]{3,2,1,0:T(8,128)(2,1)S(1)}, bf16[1,2,256,256]{3,2,1,0:T(8,128)(2,1)S(1)}, u32[]{:S(2)}, u32[]{:S(2)}) collective-permute-start(bf16[1,2,256,256]{3,2,1,0:T(8,128)(2,1)S(1)} %collective-permute-done.3.refs_6_), channel_id=1, source_target_pairs={{0,4},{4,8},{8,12},{1,5},{5,9},{9,13},{2,6},{6,10},{10,14},{3,7},{... | collective-permute-start | bytes 786440 | tf_op jit(solution)/shard_map/ppermute | solution.py:18
  26.8 0.0 collective-permute-done.13.refs_5_
  26.8 1.3 %collective-permute-start.7 = (bf16[1,2,256,256]{3,2,1,0:T(8,128)(2,1)S(1)}, bf16[1,2,256,256]{3,2,1,0:T(8,128)(2,1)S(1)}, u32[]{:S(2)}, u32[]{:S(2)}) collective-permute-start(bf16[1,2,256,256]{3,2,1,0:T(8,128)(2,1)S(1)} %collective-permute-done.6.refs_8_), channel_id=1, source_target_pairs={{4,0},{8,4},{12,8},{5,1},{9,5},{13,9},{6,2},{10,6},{14,10},{7,3},{... | collective-permute-start | bytes 786440 | tf_op jit(solution)/shard_map/ppermute | solution.py:18
  28.1 1.4 %collective-permute-done.16.refs_9_ = bf16[1,2,256,256]{3,2,1,0:T(8,128)(2,1)S(1)} collective-permute-done((bf16[1,2,256,256]{3,2,1,0:T(8,128)(2,1)S(1)}, bf16[1,2,256,256]{3,2,1,0:T(8,128)(2,1)S(1)}, u32[]{:S(2)}, u32[]{:S(2)}) %collective-permute-start.16) | collective-permute-done | bytes 262176 | tf_op jit(solution)/shard_map/ppermute | solution.py:18
  29.5 0.0 collective-permute-start.9
  29.5 0.0 collective-permute-done.10.refs_2_
  29.5 0.5 collective-permute-start.11
  30.1 0.6 collective-permute-done.4.refs_5_
  30.7 4.4 %collective-permute-start.14 = (bf16[1,2,256,256]{3,2,1,0:T(8,128)(2,1)S(1)}, bf16[1,2,256,256]{3,2,1,0:T(8,128)(2,1)S(1)}, u32[]{:S(2)}, u32[]{:S(2)}) collective-permute-start(bf16[1,2,256,256]{3,2,1,0:T(8,128)(2,1)S(1)} %collective-permute-done.13.refs_5_), channel_id=1, source_target_pairs={{0,4},{4,8},{8,12},{1,5},{5,9},{9,13},{2,6},{6,10},{10,14},{3,7},{... | collective-permute-start | bytes 786440 | tf_op jit(solution)/shard_map/ppermute | solution.py:18
  35.1 0.0 collective-permute-done.7.refs_9_
  35.1 0.1 collective-permute-start
  35.2 3.8 %collective-permute-done.1.refs_2_ = bf16[1,2,256,768]{3,2,1,0:T(8,128)(2,1)S(1)} collective-permute-done((bf16[1,2,256,768]{3,2,1,0:T(8,128)(2,1)S(1)}, bf16[1,2,256,768]{3,2,1,0:T(8,128)(2,1)S(1)}, u32[]{:S(2)}, u32[]{:S(2)}) %collective-permute-start.1) | collective-permute-done | bytes 786464 | tf_op jit(solution)/shard_map/ppermute | solution.py:23
  38.9 0.0 collective-permute-start.2
  38.9 0.3 collective-permute-done.14.refs_4_
  39.3 1.3 %collective-permute-start.17 = (bf16[1,2,256,256]{3,2,1,0:T(8,128)(2,1)S(1)}, bf16[1,2,256,256]{3,2,1,0:T(8,128)(2,1)S(1)}, u32[]{:S(2)}, u32[]{:S(2)}) collective-permute-start(bf16[1,2,256,256]{3,2,1,0:T(8,128)(2,1)S(1)} %collective-permute-done.16.refs_9_), channel_id=1, source_target_pairs={{4,0},{8,4},{12,8},{5,1},{9,5},{13,9},{6,2},{10,6},{14,10},{7,3},{... | collective-permute-start | bytes 786440 | tf_op jit(solution)/shard_map/ppermute | solution.py:18
  40.5 9.1 %collective-permute-done.17.refs_10_ = bf16[1,2,256,256]{3,2,1,0:T(8,128)(2,1)S(1)} collective-permute-done((bf16[1,2,256,256]{3,2,1,0:T(8,128)(2,1)S(1)}, bf16[1,2,256,256]{3,2,1,0:T(8,128)(2,1)S(1)}, u32[]{:S(2)}, u32[]{:S(2)}) %collective-permute-start.17) | collective-permute-done | bytes 262176 | tf_op jit(solution)/shard_map/ppermute | solution.py:18
  49.6 3.6 %collective-permute-start.5 = (bf16[1,2,256,256]{3,2,1,0:T(8,128)(2,1)S(1)}, bf16[1,2,256,256]{3,2,1,0:T(8,128)(2,1)S(1)}, u32[]{:S(2)}, u32[]{:S(2)}) collective-permute-start(bf16[1,2,256,256]{3,2,1,0:T(8,128)(2,1)S(1)} %collective-permute-done.4.refs_5_), channel_id=1, source_target_pairs={{0,4},{4,8},{8,12},{1,5},{5,9},{9,13},{2,6},{6,10},{10,14},{3,7},{... | collective-permute-start | bytes 786440 | tf_op jit(solution)/shard_map/ppermute | solution.py:18
  53.3 0.0 collective-permute-done.9.refs_1_
  53.3 1.3 %collective-permute-start.8 = (bf16[1,2,256,256]{3,2,1,0:T(8,128)(2,1)S(1)}, bf16[1,2,256,256]{3,2,1,0:T(8,128)(2,1)S(1)}, u32[]{:S(2)}, u32[]{:S(2)}) collective-permute-start(bf16[1,2,256,256]{3,2,1,0:T(8,128)(2,1)S(1)} %collective-permute-done.7.refs_9_), channel_id=1, source_target_pairs={{4,0},{8,4},{12,8},{5,1},{9,5},{13,9},{6,2},{10,6},{14,10},{7,3},{... | collective-permute-start | bytes 786440 | tf_op jit(solution)/shard_map/ppermute | solution.py:18
  54.6 0.0 collective-permute-done.11.refs_3_
  54.6 0.0 copy-done
  54.6 4.2 %shard_map.37.refs_11_ = f32[2,2,256,256]{3,2,1,0:T(8,128)} custom-call(s32[4,12]{1,0:T(4,128)S(1)} %copy-done, bf16[1,2,256,768]{3,2,1,0:T(8,128)(2,1)S(1)} %get-tuple-element.5.refs_0_, bf16[1,2,256,768]{3,2,1,0:T(8,128)(2,1)S(1)} %collective-permute-done.9.refs_1_, bf16[1,2,256,768]{3,2,1,0:T(8,128)(2,1)S(1)} %collective-permute-done.10.refs_2_, ...), custom_call_target="tpu_custom_call" | custom-call | flops 1610612736 | bytes 5242880 | tf_op jit(solution)/shard_map/pallas_call | solution.py:101
  58.8 0.0 collective-permute-done.5.refs_4_
  58.8 3.0 %collective-permute-done.8.refs_10_ = bf16[1,2,256,256]{3,2,1,0:T(8,128)(2,1)S(1)} collective-permute-done((bf16[1,2,256,256]{3,2,1,0:T(8,128)(2,1)S(1)}, bf16[1,2,256,256]{3,2,1,0:T(8,128)(2,1)S(1)}, u32[]{:S(2)}, u32[]{:S(2)}) %collective-permute-start.8) | collective-permute-done | bytes 262176 | tf_op jit(solution)/shard_map/ppermute | solution.py:18
  61.8 0.0 collective-permute-done.refs_1_
  61.8 0.0 collective-permute-done.2.refs_3_
  61.8 4.2 %shard_map.38 = f32[2,2,256,256]{3,2,1,0:T(8,128)} custom-call(s32[4,12]{1,0:T(4,128)S(1)} %copy-done, bf16[1,2,256,768]{3,2,1,0:T(8,128)(2,1)S(1)} %get-tuple-element.6.refs_0_, bf16[1,2,256,768]{3,2,1,0:T(8,128)(2,1)S(1)} %collective-permute-done.refs_1_, ...), custom_call_target="tpu_custom_call", output_to_operand_aliasing={{}: (12, {})} | custom-call | flops 1610612736 | bytes 5242880 | tf_op jit(solution)/shard_map/pallas_call | solution.py:101
  (1 shorter events, 0.0 us)
Async XLA Ops:
  0.0 4.5 %copy-start.1 = (bf16[2,2,256,256]{3,2,1,0:T(8,128)(2,1)S(1)}, bf16[2,2,256,256]{3,2,1,0:T(8,128)(2,1)}, u32[]{:S(2)}) copy-start(bf16[2,2,256,256]{3,2,1,0:T(8,128)(2,1)} %param.4) | copy-start | bytes 1572868
  0.0 54.6 %copy-start = (s32[4,12]{1,0:T(4,128)S(1)}, s32[4,12]{1,0:T(4,128)}, u32[]{:S(2)}) copy-start(s32[4,12]{1,0:T(4,128)} %aperture_ref.3) | copy-start | bytes 580
  1.5 28.0 %collective-permute-start.10 = (bf16[1,2,256,768]{3,2,1,0:T(8,128)(2,1)S(1)}, bf16[1,2,256,768]{3,2,1,0:T(8,128)(2,1)S(1)}, u32[]{:S(2)}, u32[]{:S(2)}) collective-permute-start(bf16[1,2,256,768]{3,2,1,0:T(8,128)(2,1)S(1)} %get-tuple-element.5.refs_0_), channel_id=1, source_target_pairs={{0,2},{1,3},{2,0},{3,1},{4,6},{5,7},{6,4},{7,5},{8,10},{9,11},{10,... | collective-permute-start | bytes 2359304 | tf_op jit(solution)/shard_map/ppermute | solution.py:23
  4.6 10.0 %collective-permute-start.12 = (bf16[1,2,256,256]{3,2,1,0:T(8,128)(2,1)S(1)}, bf16[1,2,256,256]{3,2,1,0:T(8,128)(2,1)S(1)}, u32[]{:S(2)}, u32[]{:S(2)}) collective-permute-start(bf16[1,2,256,256]{3,2,1,0:T(8,128)(2,1)S(1)} %get-tuple-element.7.refs_7_), channel_id=1, source_target_pairs={{0,4},{4,8},{8,12},{1,5},{5,9},{9,13},{2,6},{6,10},{10,14},{3,7},{... | collective-permute-start | bytes 786440 | tf_op jit(solution)/shard_map/ppermute | solution.py:18
  8.1 9.4 %collective-permute-start.15 = (bf16[1,2,256,256]{3,2,1,0:T(8,128)(2,1)S(1)}, bf16[1,2,256,256]{3,2,1,0:T(8,128)(2,1)S(1)}, u32[]{:S(2)}, u32[]{:S(2)}) collective-permute-start(bf16[1,2,256,256]{3,2,1,0:T(8,128)(2,1)S(1)} %get-tuple-element.7.refs_7_), channel_id=1, source_target_pairs={{4,0},{8,4},{12,8},{5,1},{9,5},{13,9},{6,2},{10,6},{14,10},{7,3},{... | collective-permute-start | bytes 786440 | tf_op jit(solution)/shard_map/ppermute | solution.py:18
  9.4 11.6 %collective-permute-start.3 = (bf16[1,2,256,256]{3,2,1,0:T(8,128)(2,1)S(1)}, bf16[1,2,256,256]{3,2,1,0:T(8,128)(2,1)S(1)}, u32[]{:S(2)}, u32[]{:S(2)}) collective-permute-start(bf16[1,2,256,256]{3,2,1,0:T(8,128)(2,1)S(1)} %get-tuple-element.8.refs_7_), channel_id=1, source_target_pairs={{0,4},{4,8},{8,12},{1,5},{5,9},{9,13},{2,6},{6,10},{10,14},{3,7},{... | collective-permute-start | bytes 786440 | tf_op jit(solution)/shard_map/ppermute | solution.py:18
  14.0 25.0 %collective-permute-start.1 = (bf16[1,2,256,768]{3,2,1,0:T(8,128)(2,1)S(1)}, bf16[1,2,256,768]{3,2,1,0:T(8,128)(2,1)S(1)}, u32[]{:S(2)}, u32[]{:S(2)}) collective-permute-start(bf16[1,2,256,768]{3,2,1,0:T(8,128)(2,1)S(1)} %get-tuple-element.6.refs_0_), channel_id=1, source_target_pairs={{0,2},{1,3},{2,0},{3,1},{4,6},{5,7},{6,4},{7,5},{8,10},{9,11},{10,... | collective-permute-start | bytes 2359304 | tf_op jit(solution)/shard_map/ppermute | solution.py:23
  14.6 8.5 %collective-permute-start.6 = (bf16[1,2,256,256]{3,2,1,0:T(8,128)(2,1)S(1)}, bf16[1,2,256,256]{3,2,1,0:T(8,128)(2,1)S(1)}, u32[]{:S(2)}, u32[]{:S(2)}) collective-permute-start(bf16[1,2,256,256]{3,2,1,0:T(8,128)(2,1)S(1)} %get-tuple-element.8.refs_7_), channel_id=1, source_target_pairs={{4,0},{8,4},{12,8},{5,1},{9,5},{13,9},{6,2},{10,6},{14,10},{7,3},{... | collective-permute-start | bytes 786440 | tf_op jit(solution)/shard_map/ppermute | solution.py:18
  17.5 9.4 %collective-permute-start.13 = (bf16[1,2,256,256]{3,2,1,0:T(8,128)(2,1)S(1)}, bf16[1,2,256,256]{3,2,1,0:T(8,128)(2,1)S(1)}, u32[]{:S(2)}, u32[]{:S(2)}) collective-permute-start(bf16[1,2,256,256]{3,2,1,0:T(8,128)(2,1)S(1)} %collective-permute-done.12.refs_6_), channel_id=1, source_target_pairs={{0,4},{4,8},{8,12},{1,5},{5,9},{9,13},{2,6},{6,10},{10,14},{3,7},{... | collective-permute-start | bytes 786440 | tf_op jit(solution)/shard_map/ppermute | solution.py:18
  21.0 8.6 %collective-permute-start.16 = (bf16[1,2,256,256]{3,2,1,0:T(8,128)(2,1)S(1)}, bf16[1,2,256,256]{3,2,1,0:T(8,128)(2,1)S(1)}, u32[]{:S(2)}, u32[]{:S(2)}) collective-permute-start(bf16[1,2,256,256]{3,2,1,0:T(8,128)(2,1)S(1)} %collective-permute-done.15.refs_8_), channel_id=1, source_target_pairs={{4,0},{8,4},{12,8},{5,1},{9,5},{13,9},{6,2},{10,6},{14,10},{7,3},{... | collective-permute-start | bytes 786440 | tf_op jit(solution)/shard_map/ppermute | solution.py:18
  23.1 7.6 %collective-permute-start.4 = (bf16[1,2,256,256]{3,2,1,0:T(8,128)(2,1)S(1)}, bf16[1,2,256,256]{3,2,1,0:T(8,128)(2,1)S(1)}, u32[]{:S(2)}, u32[]{:S(2)}) collective-permute-start(bf16[1,2,256,256]{3,2,1,0:T(8,128)(2,1)S(1)} %collective-permute-done.3.refs_6_), channel_id=1, source_target_pairs={{0,4},{4,8},{8,12},{1,5},{5,9},{9,13},{2,6},{6,10},{10,14},{3,7},{... | collective-permute-start | bytes 786440 | tf_op jit(solution)/shard_map/ppermute | solution.py:18
  26.8 8.3 %collective-permute-start.7 = (bf16[1,2,256,256]{3,2,1,0:T(8,128)(2,1)S(1)}, bf16[1,2,256,256]{3,2,1,0:T(8,128)(2,1)S(1)}, u32[]{:S(2)}, u32[]{:S(2)}) collective-permute-start(bf16[1,2,256,256]{3,2,1,0:T(8,128)(2,1)S(1)} %collective-permute-done.6.refs_8_), channel_id=1, source_target_pairs={{4,0},{8,4},{12,8},{5,1},{9,5},{13,9},{6,2},{10,6},{14,10},{7,3},{... | collective-permute-start | bytes 786440 | tf_op jit(solution)/shard_map/ppermute | solution.py:18
  29.5 23.8 %collective-permute-start.9 = (bf16[1,2,256,768]{3,2,1,0:T(8,128)(2,1)S(1)}, bf16[1,2,256,768]{3,2,1,0:T(8,128)(2,1)S(1)}, u32[]{:S(2)}, u32[]{:S(2)}) collective-permute-start(bf16[1,2,256,768]{3,2,1,0:T(8,128)(2,1)S(1)} %get-tuple-element.5.refs_0_), channel_id=1, source_target_pairs={{0,1},{1,0},{2,3},{3,2},{4,5},{5,4},{6,7},{7,6},{8,9},{9,8},{10,11... | collective-permute-start | bytes 2359304 | tf_op jit(solution)/shard_map/ppermute | solution.py:23
  29.5 25.1 %collective-permute-start.11 = (bf16[1,2,256,768]{3,2,1,0:T(8,128)(2,1)S(1)}, bf16[1,2,256,768]{3,2,1,0:T(8,128)(2,1)S(1)}, u32[]{:S(2)}, u32[]{:S(2)}) collective-permute-start(bf16[1,2,256,768]{3,2,1,0:T(8,128)(2,1)S(1)} %collective-permute-done.10.refs_2_), channel_id=1, source_target_pairs={{0,1},{1,0},{2,3},{3,2},{4,5},{5,4},{6,7},{7,6},{8,9},{9,8},{10,11... | collective-permute-start | bytes 2359304 | tf_op jit(solution)/shard_map/ppermute | solution.py:23
  30.7 8.6 %collective-permute-start.14 = (bf16[1,2,256,256]{3,2,1,0:T(8,128)(2,1)S(1)}, bf16[1,2,256,256]{3,2,1,0:T(8,128)(2,1)S(1)}, u32[]{:S(2)}, u32[]{:S(2)}) collective-permute-start(bf16[1,2,256,256]{3,2,1,0:T(8,128)(2,1)S(1)} %collective-permute-done.13.refs_5_), channel_id=1, source_target_pairs={{0,4},{4,8},{8,12},{1,5},{5,9},{9,13},{2,6},{6,10},{10,14},{3,7},{... | collective-permute-start | bytes 786440 | tf_op jit(solution)/shard_map/ppermute | solution.py:18
  35.1 26.7 %collective-permute-start = (bf16[1,2,256,768]{3,2,1,0:T(8,128)(2,1)S(1)}, bf16[1,2,256,768]{3,2,1,0:T(8,128)(2,1)S(1)}, u32[]{:S(2)}, u32[]{:S(2)}) collective-permute-start(bf16[1,2,256,768]{3,2,1,0:T(8,128)(2,1)S(1)} %get-tuple-element.6.refs_0_), channel_id=1, source_target_pairs={{0,1},{1,0},{2,3},{3,2},{4,5},{5,4},{6,7},{7,6},{8,9},{9,8},{10,11... | collective-permute-start | bytes 2359304 | tf_op jit(solution)/shard_map/ppermute | solution.py:23
  38.9 22.9 %collective-permute-start.2 = (bf16[1,2,256,768]{3,2,1,0:T(8,128)(2,1)S(1)}, bf16[1,2,256,768]{3,2,1,0:T(8,128)(2,1)S(1)}, u32[]{:S(2)}, u32[]{:S(2)}) collective-permute-start(bf16[1,2,256,768]{3,2,1,0:T(8,128)(2,1)S(1)} %collective-permute-done.1.refs_2_), channel_id=1, source_target_pairs={{0,1},{1,0},{2,3},{3,2},{4,5},{5,4},{6,7},{7,6},{8,9},{9,8},{10,11... | collective-permute-start | bytes 2359304 | tf_op jit(solution)/shard_map/ppermute | solution.py:23
  39.3 10.4 %collective-permute-start.17 = (bf16[1,2,256,256]{3,2,1,0:T(8,128)(2,1)S(1)}, bf16[1,2,256,256]{3,2,1,0:T(8,128)(2,1)S(1)}, u32[]{:S(2)}, u32[]{:S(2)}) collective-permute-start(bf16[1,2,256,256]{3,2,1,0:T(8,128)(2,1)S(1)} %collective-permute-done.16.refs_9_), channel_id=1, source_target_pairs={{4,0},{8,4},{12,8},{5,1},{9,5},{13,9},{6,2},{10,6},{14,10},{7,3},{... | collective-permute-start | bytes 786440 | tf_op jit(solution)/shard_map/ppermute | solution.py:18
  49.6 9.2 %collective-permute-start.5 = (bf16[1,2,256,256]{3,2,1,0:T(8,128)(2,1)S(1)}, bf16[1,2,256,256]{3,2,1,0:T(8,128)(2,1)S(1)}, u32[]{:S(2)}, u32[]{:S(2)}) collective-permute-start(bf16[1,2,256,256]{3,2,1,0:T(8,128)(2,1)S(1)} %collective-permute-done.4.refs_5_), channel_id=1, source_target_pairs={{0,4},{4,8},{8,12},{1,5},{5,9},{9,13},{2,6},{6,10},{10,14},{3,7},{... | collective-permute-start | bytes 786440 | tf_op jit(solution)/shard_map/ppermute | solution.py:18
  53.3 8.5 %collective-permute-start.8 = (bf16[1,2,256,256]{3,2,1,0:T(8,128)(2,1)S(1)}, bf16[1,2,256,256]{3,2,1,0:T(8,128)(2,1)S(1)}, u32[]{:S(2)}, u32[]{:S(2)}) collective-permute-start(bf16[1,2,256,256]{3,2,1,0:T(8,128)(2,1)S(1)} %collective-permute-done.7.refs_9_), channel_id=1, source_target_pairs={{4,0},{8,4},{12,8},{5,1},{9,5},{13,9},{6,2},{10,6},{14,10},{7,3},{... | collective-permute-start | bytes 786440 | tf_op jit(solution)/shard_map/ppermute | solution.py:18

commit v3 on v2

v3 whole, which is shorter than its diff:
```python
import functools

import jax
import jax.numpy as jnp
from jax import lax
from jax.experimental import pallas as pl
from jax.experimental.pallas import tpu as pltpu
from jax.sharding import PartitionSpec as P

BLK = 256
APER = 12
HW = 6


def from_behind(x, axis, by):
    peers = lax.axis_size(axis)
    pairs = [(i, i + by) for i in range(peers) if 0 <= i + by < peers]
    return lax.ppermute(x, axis, pairs)


def swap(x, axis, bit):
    peers = lax.axis_size(axis)
    return lax.ppermute(x, axis, [(i, i ^ bit) for i in range(peers)])


def after(value, *earlier):
    return lax.optimization_barrier((value, *earlier))[0]


def line_window(data):
    peers = lax.axis_size("src")
    at_end = (lax.axis_index("src") + 1) % peers < 2
    far = lax.ppermute(data, "src", [(0, 3), (1, 2), (2, 1), (3, 0)])
    near = lax.ppermute(data, "src", [(0, 1), (1, 0), (2, 3), (3, 2)])
    onward = jnp.where(at_end, data, far)
    return [
        [(data, v), (near, v), (lax.ppermute(onward[v : v + 1], "src", [(0, 2), (2, 3), (3, 1), (1, 0)]), 0), (far, v)]
        for v in range(data.shape[0])
    ]


def hop_window(data):
    reach = min(HW, lax.axis_size("src") - 1)
    window = {0: data}
    for hop in range(1, reach + 1):
        window[-hop] = from_behind(window[1 - hop], "src", 1)
        window[hop] = from_behind(window[hop - 1], "src", -1)
    return [[(window[distance], v) for distance in range(-reach, reach + 1)] for v in range(data.shape[0])]


def gather_panels(primaries, windows):
    peers = lax.axis_size("rcv")
    whole = {0: primaries}
    bit = 1
    while bit < peers // 2:
        for m in list(whole):
            whole[m ^ bit] = swap(whole[m], "rcv", bit)
        bit *= 2
    panels = []
    for v in range(primaries.shape[0]):
        own = primaries[v : v + 1]
        if v > 0:
            own = after(primaries, whole[1])[v : v + 1]
        found = {bit: swap(own, "rcv", bit)}
        handed = found[bit]
        if v > 0:
            handed = after(handed, *[piece for window in windows for piece, _ in window])
        for lower in range(1, bit):
            last = lower & (lower - 1)
            found[bit ^ lower] = swap(found[bit ^ last] if last else handed, "rcv", lower & -lower)
        panels.append([(whole[m], v) for m in range(bit)] + [(found[m], 0) for m in range(bit, peers)])
    return panels


def window_slot(block, wanted, peers, reach):
    return lax.bitwise_xor(block, wanted) if peers == 4 else wanted - block + reach


def kernel(survey, panel_at, piece_at, aperture_ref, *refs):
    panel_count, piece_count = len(panel_at), len(piece_at)
    panel_refs = [ref.at[v] for ref, v in zip(refs, panel_at)]
    piece_refs = [ref.at[v] for ref, v in zip(refs[panel_count:], piece_at)]
    out_ref, window, result, piece_sems, out_sems = refs[-5:]
    block = lax.axis_index("src")
    me = lax.axis_index("rcv")
    per_shard = panel_refs[0].shape[-1] // BLK
    copies = [
        pltpu.make_async_copy(ref, window.at[k], piece_sems.at[k]) for k, ref in enumerate(piece_refs)
    ]
    for copy in copies:
        copy.start()
    slots = []
    for m in range(panel_count):
        shard = lax.bitwise_xor(me, m)
        wanted = [aperture_ref[block, shard * per_shard + q] for q in range(per_shard)]
        slots.append([window_slot(block, w, lax.axis_size("src"), piece_count // 2) for w in wanted])
    for copy in copies:
        copy.wait()
    dot = functools.partial(jnp.dot, preferred_element_type=jnp.float32)

    def total(panel_part, data_part):
        terms = [
            dot(ref[panel_part], jnp.concatenate([window[k, data_part] for k in rows], axis=0))
            for ref, rows in zip(panel_refs, slots)
        ]
        return sum(terms[1:], terms[0])

    outs = [pltpu.make_async_copy(result.at[part], out_ref.at[survey, part], out_sems.at[part]) for part in range(2)]
    result[0] = total(0, 0) - total(1, 1)
    outs[0].start()
    result[1] = total(0, 1) + total(1, 0)
    outs[1].start()
    for copy in outs:
        copy.wait()


def products(survey, surveys, aperture, panels, pieces, out):
    panels, panel_at = zip(*panels)
    pieces, piece_at = zip(*pieces)
    width = pieces[0].shape[-1]
    anywhere = pl.BlockSpec(memory_space=pl.ANY)
    operands = [aperture, *panels, *pieces]
    in_specs = [pl.BlockSpec(memory_space=pltpu.SMEM)]
    in_specs += [pl.BlockSpec(memory_space=pltpu.VMEM)] * len(panels) + [anywhere] * len(pieces)
    aliases = {}
    if out is not None:
        aliases = {len(operands): 0}
        operands.append(out)
        in_specs.append(anywhere)
    return pl.pallas_call(
        functools.partial(kernel, survey, panel_at, piece_at),
        out_shape=jax.ShapeDtypeStruct((surveys, 2, BLK, width), jnp.float32),
        in_specs=in_specs,
        out_specs=anywhere,
        scratch_shapes=[
            pltpu.VMEM((len(pieces), 2, BLK, width), jnp.bfloat16),
            pltpu.VMEM((2, BLK, width), jnp.float32),
            pltpu.SemaphoreType.DMA((len(pieces),)),
            pltpu.SemaphoreType.DMA((2,)),
        ],
        input_output_aliases=aliases,
        compiler_params=pltpu.CompilerParams(vmem_limit_bytes=24 * 1024 * 1024),
        cost_estimate=pl.CostEstimate(
            flops=8 * BLK * BLK * APER * width, bytes_accessed=5 << 20, transcendentals=0
        ),
    )(*operands)


def body(primaries, data, aperture):
    surveys = primaries.shape[0]
    windows = (line_window if lax.axis_size("src") == 4 else hop_window)(data)
    panels = gather_panels(primaries, windows)
    out = None
    for v in range(surveys):
        out = products(v, surveys, aperture, panels[v], windows[v], out)
    return out


def solution(mesh):
    placed = (P("freq", None, "src", "rcv"), P("freq", None, "src", "rcv"), P())
    return jax.shard_map(
        body, mesh=mesh, in_specs=placed, out_specs=P("freq", None, "src", "rcv"), check_vma=False
    )
```

time: 66.4 us -> 54.2 us (0.82)
  starting transfers between devices: 35.2 us -> 18.9 us
  local copies, waits for them, and re-layouts: 1.57 us -> 3.07 us
  Pallas kernels: 8.37 us -> 9.78 us
  other arithmetic: 0 us -> 1.1 us
    ppermute x12 -> x4, starting transfers between devices: 31 us -> 16.4 us  [the longest x2 11.7 us: line_window(): lax.ppermute(onward[v:v + 1], 'src', [(0, 2), (2, 3), (3, 1), (1, 0)])]
    ppermute x12 -> x4, waiting for transfers between devices: 16.9 us -> 19.1 us  [the longest x2 10.9 us: line_window(): lax.ppermute(onward[v:v + 1], 'src', [(0, 2), (2, 3), (3, 1), (1, 0)])]
    ppermute x6 -> x5, waiting for transfers between devices: 3.77 us -> 1.87 us  [swap(): return lax.ppermute(x, axis, [(i, i ^ bit) for i in range(peers)])]
    ppermute x6 -> x5, starting transfers between devices: 4.18 us -> 2.48 us  [swap(): return lax.ppermute(x, axis, [(i, i ^ bit) for i in range(peers)])]
    slice x2 -> x3, local copies, waits for them, and re-layouts: 1.56 us -> 3.06 us  [the longest x1 2.09 us: gather_panels(): own = primaries[v:v + 1]]
    pallas_call x2, Pallas kernels: 8.37 us -> 9.78 us  [products(): pl.pallas_call(functools.partial(kernel, survey, panel_at, piece_at), out...]
    select_n x0 -> x1, other arithmetic: none -> 1.1 us  [line_window(): onward = jnp.where(at_end, data, far)]
  transfers between devices with their start and end apart: 18 -> 9, of which waited for: 8 -> 4; matrix products, arithmetic and copies ran while one was open for 0% -> 8% of each run, Pallas kernels for 6% -> 9%
where the time goes in v3:
time: 54.2 us; the launch traced here: 53.8 us
  waiting for transfers between devices  20.9 us (39%)
  starting transfers between devices  18.9 us (35%)
  Pallas kernels  9.78 us (18%)
  local copies, waits for them, and re-layouts  3.07 us (6%)
  other arithmetic  1.1 us (2%)
    ppermute x2, starting transfers between devices, line_window(): lax.ppermute(onward[v:v + 1], 'src', [(0, 2), (2, 3), (3, 1), (1, 0)])  11.7 us
    ppermute x2, waiting for transfers between devices, line_window(): lax.ppermute(onward[v:v + 1], 'src', [(0, 2), (2, 3), (3, 1), (1, 0)])  10.9 us
    pallas_call x2, Pallas kernels, products(): pl.pallas_call(functools.partial(kernel, survey, panel_at, piece_at), out...  9.78 us
    ppermute x1, waiting for transfers between devices, line_window(): far = lax.ppermute(data, 'src', [(0, 3), (1, 2), (2, 1), (3, 0)])  8.12 us
    ppermute x1, starting transfers between devices, line_window(): far = lax.ppermute(data, 'src', [(0, 3), (1, 2), (2, 1), (3, 0)])  4.66 us
    ppermute x5, starting transfers between devices, swap(): return lax.ppermute(x, axis, [(i, i ^ bit) for i in range(peers)])  2.48 us
    slice x1, local copies, waits for them, and re-layouts, gather_panels(): own = primaries[v:v + 1]  2.09 us
    ppermute x5, waiting for transfers between devices, swap(): return lax.ppermute(x, axis, [(i, i ^ bit) for i in range(peers)])  1.87 us
  transfers between devices with their start and end apart: 9, of which 4 were waited for; matrix products, arithmetic and copies ran while one was open for 8% of the time, Pallas kernels for 9%

profile of v3, /device:TPU:0, one launch (start us, length us, event | category | flops | bytes accessed | tf_op | source)
XLA Modules:
  0.0 53.8 jit_solution(3026118240176136231)
XLA Ops:
  0.0 0.0 copy-start
  0.0 0.5 collective-permute-start
  0.5 4.7 %collective-permute-start.3 = (bf16[2,2,256,256]{3,2,1,0:T(8,128)(2,1)}, bf16[2,2,256,256]{3,2,1,0:T(8,128)(2,1)}, u32[]{:S(2)}, u32[]{:S(2)}) collective-permute-start(bf16[2,2,256,256]{3,2,1,0:T(8,128)(2,1)} %refs_4_.3), channel_id=1, source_target_pairs={{0,12},{4,8},{8,4},{12,0},{1,13},{5,9},{9,5},{13,1},{2,14},{6,10},... | collective-permute-start | bytes 1572872 | tf_op jit(solution)/shard_map/ppermute | solution.py:33
  5.1 2.1 %slice.15 = bf16[1,2,256,768]{3,2,1,0:T(8,128)(2,1)} slice(bf16[2,2,256,768]{3,2,1,0:T(8,128)(2,1)} %refs_0_.3), slice={[0:1], [0:2], [0:256], [0:768]} | slice | bytes 1572864 | tf_op jit(solution)/shard_map/slice | solution.py:61
  7.2 1.5 %collective-permute-start.7 = (bf16[1,2,256,768]{3,2,1,0:T(8,128)(2,1)}, bf16[1,2,256,768]{3,2,1,0:T(8,128)(2,1)}, u32[]{:S(2)}, u32[]{:S(2)}) collective-permute-start(bf16[1,2,256,768]{3,2,1,0:T(8,128)(2,1)} %slice.15), channel_id=1, source_target_pairs={{0,2},{1,3},{2,0},{3,1},{4,6},{5,7},{6,4},{7,5},{8,10},{9,11},{10,... | collective-permute-start | bytes 2359304 | tf_op jit(solution)/shard_map/ppermute | solution.py:23
  8.7 0.0 collective-permute-done.refs_1_
  8.7 0.0 copy-done
  8.7 0.9 %slice.12 = bf16[1,2,256,768]{3,2,1,0:T(8,128)(2,1)} slice(bf16[2,2,256,768]{3,2,1,0:T(8,128)(2,1)S(1)} %copy-done), slice={[1:2], [0:2], [0:256], [0:768]} | slice | bytes 1572864 | tf_op jit(solution)/shard_map/slice | solution.py:63
  9.6 0.0 copy-start.1
  9.6 0.5 collective-permute-start.1
  10.2 0.0 collective-permute-start.2
  10.2 8.1 %collective-permute-done.3.refs_7_ = bf16[2,2,256,256]{3,2,1,0:T(8,128)(2,1)} collective-permute-done((bf16[2,2,256,256]{3,2,1,0:T(8,128)(2,1)}, bf16[2,2,256,256]{3,2,1,0:T(8,128)(2,1)}, u32[]{:S(2)}, u32[]{:S(2)}) %collective-permute-start.3) | collective-permute-done | bytes 524320 | tf_op jit(solution)/shard_map/ppermute | solution.py:33
  18.3 1.1 %broadcast_select_fusion = bf16[2,2,256,256]{3,2,1,0:T(8,128)(2,1)S(1)} fusion(bf16[2,2,256,256]{3,2,1,0:T(8,128)(2,1)} %refs_4_.3, bf16[2,2,256,256]{3,2,1,0:T(8,128)(2,1)} %collective-permute-done.3.refs_7_, pred[]{:T(512)S(6)} %lt.10), kind=kLoop, calls=%fused_computation | loop fusion | flops 262144 | bytes 1572865 | tf_op jit(solution)/shard_map/jit(_where)/select_n | solution.py:35
  19.5 11.7 %collective-permute-start.5 = (bf16[1,2,256,256]{3,2,1,0:T(8,128)(2,1)S(1)}, bf16[1,2,256,256]{3,2,1,0:T(8,128)(2,1)S(1)}, u32[]{:S(2)}, u32[]{:S(2)}) collective-permute-start(bf16[1,2,256,256]{3,2,1,0:T(8,128)(2,1)S(1)} %get-tuple-element.9), channel_id=1, source_target_pairs={{0,8},{8,12},{12,4},{4,0},{1,9},{9,13},{13,5},{5,1},{2,10},{10,14}... | collective-permute-start | bytes 786440 | tf_op jit(solution)/shard_map/ppermute | solution.py:37
  31.1 0.1 collective-permute-start.4
  31.2 0.0 collective-permute-done.7.refs_2_
  31.2 0.0 collective-permute-start.8
  31.2 0.0 collective-permute-done.2.refs_5_
  31.2 6.7 %collective-permute-done.5.refs_6_ = bf16[1,2,256,256]{3,2,1,0:T(8,128)(2,1)S(1)} collective-permute-done((bf16[1,2,256,256]{3,2,1,0:T(8,128)(2,1)S(1)}, bf16[1,2,256,256]{3,2,1,0:T(8,128)(2,1)S(1)}, u32[]{:S(2)}, u32[]{:S(2)}) %collective-permute-start.5) | collective-permute-done | bytes 262176 | tf_op jit(solution)/shard_map/ppermute | solution.py:37
  37.9 4.3 %collective-permute-done.4.refs_6_ = bf16[1,2,256,256]{3,2,1,0:T(8,128)(2,1)S(1)} collective-permute-done((bf16[1,2,256,256]{3,2,1,0:T(8,128)(2,1)S(1)}, bf16[1,2,256,256]{3,2,1,0:T(8,128)(2,1)S(1)}, u32[]{:S(2)}, u32[]{:S(2)}) %collective-permute-start.4) | collective-permute-done | bytes 262176 | tf_op jit(solution)/shard_map/ppermute | solution.py:37
  42.1 1.9 %collective-permute-done.1.refs_2_ = bf16[1,2,256,768]{3,2,1,0:T(8,128)(2,1)} collective-permute-done((bf16[1,2,256,768]{3,2,1,0:T(8,128)(2,1)}, bf16[1,2,256,768]{3,2,1,0:T(8,128)(2,1)}, u32[]{:S(2)}, u32[]{:S(2)}) %collective-permute-start.1) | collective-permute-done | bytes 786464 | tf_op jit(solution)/shard_map/ppermute | solution.py:23
  44.0 0.0 collective-permute-start.6
  44.0 0.0 collective-permute-done.8.refs_3_
  44.0 0.0 copy-done.1
  44.0 4.9 %shard_map.37.refs_8_ = f32[2,2,256,256]{3,2,1,0:T(8,128)} custom-call(s32[4,12]{1,0:T(4,128)S(1)} %copy-done.1, bf16[2,2,256,768]{3,2,1,0:T(8,128)(2,1)S(1)} %copy-done, bf16[2,2,256,768]{3,2,1,0:T(8,128)(2,1)S(1)} %collective-permute-done.refs_1_, bf16[1,2,256,768]{3,2,1,0:T(8,128)(2,1)} %collective-permute-done.7.refs_2_, ...), custom_call_target="tpu_custom_call" | custom-call | flops 1610612736 | bytes 5242880 | tf_op jit(solution)/shard_map/pallas_call | solution.py:130
  48.9 0.0 collective-permute-done.6.refs_3_
  48.9 4.9 %shard_map.38 = f32[2,2,256,256]{3,2,1,0:T(8,128)} custom-call(s32[4,12]{1,0:T(4,128)S(1)} %copy-done.1, bf16[2,2,256,768]{3,2,1,0:T(8,128)(2,1)S(1)} %copy-done, bf16[2,2,256,768]{3,2,1,0:T(8,128)(2,1)S(1)} %collective-permute-done.refs_1_, bf16[1,2,256,768]{3,2,1,0:T(8,128)(2,1)} %collective-permute-done.1.refs_2_, ...), custom_call_target="tpu_custom_call", output_to_operand_aliasing={{}: (9, {})} | custom-call | flops 1610612736 | bytes 5242880 | tf_op jit(solution)/shard_map/pallas_call | solution.py:130
  (1 shorter events, 0.0 us)
Async XLA Ops:
  0.0 8.7 %copy-start = (bf16[2,2,256,768]{3,2,1,0:T(8,128)(2,1)S(1)}, bf16[2,2,256,768]{3,2,1,0:T(8,128)(2,1)}, u32[]{:S(2)}) copy-start(bf16[2,2,256,768]{3,2,1,0:T(8,128)(2,1)} %refs_0_.3) | copy-start | bytes 4718596
  0.0 8.7 %collective-permute-start = (bf16[2,2,256,768]{3,2,1,0:T(8,128)(2,1)}, bf16[2,2,256,768]{3,2,1,0:T(8,128)(2,1)S(1)}, u32[]{:S(2)}, u32[]{:S(2)}) collective-permute-start(bf16[2,2,256,768]{3,2,1,0:T(8,128)(2,1)} %refs_0_.3), channel_id=1, source_target_pairs={{0,1},{1,0},{2,3},{3,2},{4,5},{5,4},{6,7},{7,6},{8,9},{9,8},{10,11... | collective-permute-start | bytes 4718600 | tf_op jit(solution)/shard_map/ppermute | solution.py:23
  0.5 17.8 %collective-permute-start.3 = (bf16[2,2,256,256]{3,2,1,0:T(8,128)(2,1)}, bf16[2,2,256,256]{3,2,1,0:T(8,128)(2,1)}, u32[]{:S(2)}, u32[]{:S(2)}) collective-permute-start(bf16[2,2,256,256]{3,2,1,0:T(8,128)(2,1)} %refs_4_.3), channel_id=1, source_target_pairs={{0,12},{4,8},{8,4},{12,0},{1,13},{5,9},{9,5},{13,1},{2,14},{6,10},... | collective-permute-start | bytes 1572872 | tf_op jit(solution)/shard_map/ppermute | solution.py:33
  7.2 24.0 %collective-permute-start.7 = (bf16[1,2,256,768]{3,2,1,0:T(8,128)(2,1)}, bf16[1,2,256,768]{3,2,1,0:T(8,128)(2,1)}, u32[]{:S(2)}, u32[]{:S(2)}) collective-permute-start(bf16[1,2,256,768]{3,2,1,0:T(8,128)(2,1)} %slice.15), channel_id=1, source_target_pairs={{0,2},{1,3},{2,0},{3,1},{4,6},{5,7},{6,4},{7,5},{8,10},{9,11},{10,... | collective-permute-start | bytes 2359304 | tf_op jit(solution)/shard_map/ppermute | solution.py:23
  9.6 34.4 %copy-start.1 = (s32[4,12]{1,0:T(4,128)S(1)}, s32[4,12]{1,0:T(4,128)}, u32[]{:S(2)}) copy-start(s32[4,12]{1,0:T(4,128)} %aperture_ref.3) | copy-start | bytes 580
  9.6 34.4 %collective-permute-start.1 = (bf16[1,2,256,768]{3,2,1,0:T(8,128)(2,1)}, bf16[1,2,256,768]{3,2,1,0:T(8,128)(2,1)}, u32[]{:S(2)}, u32[]{:S(2)}) collective-permute-start(bf16[1,2,256,768]{3,2,1,0:T(8,128)(2,1)} %slice.12), channel_id=1, source_target_pairs={{0,2},{1,3},{2,0},{3,1},{4,6},{5,7},{6,4},{7,5},{8,10},{9,11},{10,... | collective-permute-start | bytes 2359304 | tf_op jit(solution)/shard_map/ppermute | solution.py:23
  10.2 21.0 %collective-permute-start.2 = (bf16[2,2,256,256]{3,2,1,0:T(8,128)(2,1)}, bf16[2,2,256,256]{3,2,1,0:T(8,128)(2,1)}, u32[]{:S(2)}, u32[]{:S(2)}) collective-permute-start(bf16[2,2,256,256]{3,2,1,0:T(8,128)(2,1)} %refs_4_.3), channel_id=1, source_target_pairs={{0,4},{4,0},{8,12},{12,8},{1,5},{5,1},{9,13},{13,9},{2,6},{6,2},{1... | collective-permute-start | bytes 1572872 | tf_op jit(solution)/shard_map/ppermute | solution.py:34
  19.5 18.4 %collective-permute-start.5 = (bf16[1,2,256,256]{3,2,1,0:T(8,128)(2,1)S(1)}, bf16[1,2,256,256]{3,2,1,0:T(8,128)(2,1)S(1)}, u32[]{:S(2)}, u32[]{:S(2)}) collective-permute-start(bf16[1,2,256,256]{3,2,1,0:T(8,128)(2,1)S(1)} %get-tuple-element.9), channel_id=1, source_target_pairs={{0,8},{8,12},{12,4},{4,0},{1,9},{9,13},{13,5},{5,1},{2,10},{10,14}... | collective-permute-start | bytes 786440 | tf_op jit(solution)/shard_map/ppermute | solution.py:37
  31.1 11.0 %collective-permute-start.4 = (bf16[1,2,256,256]{3,2,1,0:T(8,128)(2,1)S(1)}, bf16[1,2,256,256]{3,2,1,0:T(8,128)(2,1)S(1)}, u32[]{:S(2)}, u32[]{:S(2)}) collective-permute-start(bf16[1,2,256,256]{3,2,1,0:T(8,128)(2,1)S(1)} %get-tuple-element.10), channel_id=1, source_target_pairs={{0,8},{8,12},{12,4},{4,0},{1,9},{9,13},{13,5},{5,1},{2,10},{10,14}... | collective-permute-start | bytes 786440 | tf_op jit(solution)/shard_map/ppermute | solution.py:37
  31.2 12.8 %collective-permute-start.8 = (bf16[1,2,256,768]{3,2,1,0:T(8,128)(2,1)}, bf16[1,2,256,768]{3,2,1,0:T(8,128)(2,1)S(1)}, u32[]{:S(2)}, u32[]{:S(2)}) collective-permute-start(bf16[1,2,256,768]{3,2,1,0:T(8,128)(2,1)} %collective-permute-done.7.refs_2_), channel_id=1, source_target_pairs={{0,1},{1,0},{2,3},{3,2},{4,5},{5,4},{6,7},{7,6},{8,9},{9,8},{10,11... | collective-permute-start | bytes 2359304 | tf_op jit(solution)/shard_map/ppermute | solution.py:23
  44.0 4.9 %collective-permute-start.6 = (bf16[1,2,256,768]{3,2,1,0:T(8,128)(2,1)}, bf16[1,2,256,768]{3,2,1,0:T(8,128)(2,1)S(1)}, u32[]{:S(2)}, u32[]{:S(2)}) collective-permute-start(bf16[1,2,256,768]{3,2,1,0:T(8,128)(2,1)} %collective-permute-done.1.refs_2_), channel_id=1, source_target_pairs={{0,1},{1,0},{2,3},{3,2},{4,5},{5,4},{6,7},{7,6},{8,9},{9,8},{10,11... | collective-permute-start | bytes 2359304 | tf_op jit(solution)/shard_map/ppermute | solution.py:23

commit v4 on v3

v4 whole, which is shorter than its diff:
```python
import functools

import jax
import jax.numpy as jnp
from jax import lax
from jax.experimental import pallas as pl
from jax.experimental.pallas import tpu as pltpu
from jax.sharding import PartitionSpec as P

BLK = 256
APER = 12
HW = 6


def from_behind(x, axis, by):
    peers = lax.axis_size(axis)
    pairs = [(i, i + by) for i in range(peers) if 0 <= i + by < peers]
    return lax.ppermute(x, axis, pairs)


def swap(x, axis, bit):
    peers = lax.axis_size(axis)
    return lax.ppermute(x, axis, [(i, i ^ bit) for i in range(peers)])


def after(value, *earlier):
    return lax.optimization_barrier((value, *earlier))[0]


def line_window(data):
    peers = lax.axis_size("src")
    at_end = (lax.axis_index("src") + 1) % peers < 2
    windows = []
    for v, own in enumerate(lax.optimization_barrier([data[v : v + 1] for v in range(data.shape[0])])):
        far = lax.ppermute(own, "src", [(0, 3), (1, 2), (2, 1), (3, 0)])
        near = lax.ppermute(own, "src", [(0, 1), (1, 0), (2, 3), (3, 2)])
        middle = lax.ppermute(jnp.where(at_end, own, far), "src", [(0, 2), (2, 3), (3, 1), (1, 0)])
        windows.append([(data, v), (near, 0), (middle, 0), (far, 0)])
    return windows


def hop_window(data):
    reach = min(HW, lax.axis_size("src") - 1)
    window = {0: data}
    for hop in range(1, reach + 1):
        window[-hop] = from_behind(window[1 - hop], "src", 1)
        window[hop] = from_behind(window[hop - 1], "src", -1)
    return [[(window[distance], v) for distance in range(-reach, reach + 1)] for v in range(data.shape[0])]


def gather_panels(first, primaries, windows):
    bit = lax.axis_size("rcv") // 2
    panels = []
    for v in range(primaries.shape[0]):
        own = first if v == 0 else after(primaries, windows[v - 1][1][0])[v : v + 1]
        found = {0: own, bit: swap(own, "rcv", bit)}
        ready = after((found[0], found[bit]), *[piece for piece, _ in windows[v]])
        for lower in range(1, bit):
            last = lower & (lower - 1)
            for half, first in zip((0, bit), ready):
                found[half ^ lower] = swap(found[half ^ last] if last else first, "rcv", lower & -lower)
        panels.append([(found[m], 0) for m in range(2 * bit)])
    return panels


def window_slot(block, wanted, peers, reach):
    return lax.bitwise_xor(block, wanted) if peers == 4 else wanted - block + reach


def kernel(survey, panel_at, piece_at, aperture_ref, *refs):
    panel_refs = [ref.at[v] for ref, v in zip(refs, panel_at)]
    piece_refs = [ref.at[v] for ref, v in zip(refs[len(panel_at) :], piece_at)]
    out_ref, window, result, out_sems = refs[-4:]
    block = lax.axis_index("src")
    me = lax.axis_index("rcv")
    columns = panel_refs[0].shape[-1]
    per_shard = columns // BLK
    width = result.shape[-1]
    for k, ref in enumerate(piece_refs):
        window[k, :, :width] = ref[0]
        window[k, :, width:] = ref[1]
    panels = []
    blocks = []
    for m, ref in enumerate(panel_refs):
        shard = lax.bitwise_xor(me, m)
        panels.append(ref[...].reshape(2 * BLK, columns))
        for q in range(per_shard):
            wanted = aperture_ref[block, shard * per_shard + q]
            blocks.append(window[window_slot(block, wanted, lax.axis_size("src"), len(piece_refs) // 2)])
    products = jnp.dot(
        jnp.concatenate(panels, axis=1), jnp.concatenate(blocks, axis=0), preferred_element_type=jnp.float32
    )
    outs = [pltpu.make_async_copy(result.at[part], out_ref.at[survey, part], out_sems.at[part]) for part in range(2)]
    result[0] = products[:BLK, :width] - products[BLK:, width:]
    outs[0].start()
    result[1] = products[:BLK, width:] + products[BLK:, :width]
    outs[1].start()
    for copy in outs:
        copy.wait()


def multiply(survey, surveys, aperture, panels, pieces, out):
    panels, panel_at = zip(*panels)
    pieces, piece_at = zip(*pieces)
    width = pieces[0].shape[-1]
    anywhere = pl.BlockSpec(memory_space=pl.ANY)
    operands = [aperture, *panels, *pieces]
    in_specs = [pl.BlockSpec(memory_space=pltpu.SMEM)]
    in_specs += [pl.BlockSpec(memory_space=pltpu.VMEM)] * (len(panels) + len(pieces))
    aliases = {}
    weight = 1 if survey + 1 == surveys else 2
    if out is not None:
        aliases = {len(operands): 0}
        operands.append(out)
        in_specs.append(anywhere)
    return pl.pallas_call(
        functools.partial(kernel, survey, panel_at, piece_at),
        out_shape=jax.ShapeDtypeStruct((surveys, 2, BLK, width), jnp.float32),
        in_specs=in_specs,
        out_specs=anywhere,
        scratch_shapes=[
            pltpu.VMEM((len(pieces), BLK, 2 * width), jnp.bfloat16),
            pltpu.VMEM((2, BLK, width), jnp.float32),
            pltpu.SemaphoreType.DMA((2,)),
        ],
        input_output_aliases=aliases,
        compiler_params=pltpu.CompilerParams(vmem_limit_bytes=24 * 1024 * 1024),
        cost_estimate=pl.CostEstimate(
            flops=int(weight * 8 * BLK * BLK * APER * width), bytes_accessed=5 << 20, transcendentals=0
        ),
    )(*operands)


def body(primaries, data, aperture):
    surveys = primaries.shape[0]
    first = primaries[:1]
    windows = (line_window if lax.axis_size("src") == 4 else hop_window)(after(data, first))
    panels = gather_panels(first, primaries, windows)
    out = None
    for v in range(surveys):
        out = multiply(v, surveys, aperture, panels[v], windows[v], out)
    return out


def solution(mesh):
    placed = (P("freq", None, "src", "rcv"), P("freq", None, "src", "rcv"), P())
    return jax.shard_map(
        body, mesh=mesh, in_specs=placed, out_specs=P("freq", None, "src", "rcv"), check_vma=False
    )
```

time: 54.2 us -> 52.2 us (0.963)
  waiting for transfers between devices: 20.9 us -> 25.5 us
  Pallas kernels: 9.78 us -> 6.46 us
  starting transfers between devices: 18.9 us -> 17.4 us
  other arithmetic: 1.1 us -> 0.07 us
  local copies, waits for them, and re-layouts: 3.07 us -> 2.47 us
    ppermute x4 -> x6, waiting for transfers between devices: 19.1 us -> 25.5 us  [the longest x2 14.9 us: line_window(): lax.ppermute(jnp.where(at_end, own, far), 'src', [(0, 2), (2, 3), (3, 1),...]
    ppermute x4 -> x6, starting transfers between devices: 16.4 us -> 12.8 us  [the longest x2 6.04 us: line_window(): lax.ppermute(jnp.where(at_end, own, far), 'src', [(0, 2), (2, 3), (3, 1),...]
    pallas_call x2, Pallas kernels: 9.78 us -> 6.46 us  [multiply(): pl.pallas_call(functools.partial(kernel, survey, panel_at, piece_at), out...]
    ppermute x5 -> x6, starting transfers between devices: 2.48 us -> 4.63 us  [swap(): return lax.ppermute(x, axis, [(i, i ^ bit) for i in range(peers)])]
    ppermute x5 -> x6, waiting for transfers between devices: 1.87 us -> 0.02 us  [swap(): return lax.ppermute(x, axis, [(i, i ^ bit) for i in range(peers)])]
    select_n x1 -> x2, other arithmetic: 1.1 us -> 0.07 us  [line_window(): jnp.where(at_end, own, far)]
    slice x3, local copies, waits for them, and re-layouts: 3.06 us -> 2.46 us  [the longest x1 1.24 us: body(): first = primaries[:1]]
  transfers between devices with their start and end apart: 9 -> 12, of which waited for: 4 -> 5; matrix products, arithmetic and copies ran while one was open for 8% -> 2% of each run, Pallas kernels for 9% -> 6%
where the time goes in v4:
time: 52.2 us; the launch traced here: 52 us
  waiting for transfers between devices  25.5 us (49%)
  starting transfers between devices  17.4 us (33%)
  Pallas kernels  6.46 us (12%)
  local copies, waits for them, and re-layouts  2.47 us (5%)
    ppermute x2, waiting for transfers between devices, line_window(): lax.ppermute(jnp.where(at_end, own, far), 'src', [(0, 2), (2, 3), (3, 1),...  14.9 us
    pallas_call x2, Pallas kernels, multiply(): pl.pallas_call(functools.partial(kernel, survey, panel_at, piece_at), out...  6.46 us
    ppermute x2, waiting for transfers between devices, line_window(): far = lax.ppermute(own, 'src', [(0, 3), (1, 2), (2, 1), (3, 0)])  6.36 us
    ppermute x2, starting transfers between devices, line_window(): lax.ppermute(jnp.where(at_end, own, far), 'src', [(0, 2), (2, 3), (3, 1),...  6.04 us
    ppermute x6, starting transfers between devices, swap(): return lax.ppermute(x, axis, [(i, i ^ bit) for i in range(peers)])  4.63 us
    ppermute x2, waiting for transfers between devices, line_window(): near = lax.ppermute(own, 'src', [(0, 1), (1, 0), (2, 3), (3, 2)])  4.27 us
    ppermute x2, starting transfers between devices, line_window(): far = lax.ppermute(own, 'src', [(0, 3), (1, 2), (2, 1), (3, 0)])  4.06 us
    ppermute x2, starting transfers between devices, line_window(): near = lax.ppermute(own, 'src', [(0, 1), (1, 0), (2, 3), (3, 2)])  2.69 us
  transfers between devices with their start and end apart: 12, of which 5 were waited for; matrix products, arithmetic and copies ran while one was open for 2% of the time, Pallas kernels for 6%

profile of v4, /device:TPU:0, one launch (start us, length us, event | category | flops | bytes accessed | tf_op | source)
XLA Modules:
  0.0 52.0 jit_solution(2413687412919266586)
XLA Ops:
  0.0 0.0 copy-start
  0.0 1.2 %slice.12.refs_0_ = bf16[1,2,256,768]{3,2,1,0:T(8,128)(2,1)S(1)} slice(bf16[2,2,256,768]{3,2,1,0:T(8,128)(2,1)} %param.3), slice={[0:1], [0:2], [0:256], [0:768]} | slice | bytes 1572864 | tf_op jit(solution)/shard_map/slice | solution.py:136
  1.2 3.0 %collective-permute-start.7 = (bf16[1,2,256,768]{3,2,1,0:T(8,128)(2,1)S(1)}, bf16[1,2,256,768]{3,2,1,0:T(8,128)(2,1)S(1)}, u32[]{:S(2)}, u32[]{:S(2)}) collective-permute-start(bf16[1,2,256,768]{3,2,1,0:T(8,128)(2,1)S(1)} %slice.12.refs_0_), channel_id=1, source_target_pairs={{0,2},{1,3},{2,0},{3,1},{4,6},{5,7},{6,4},{7,5},{8,10},{9,11},{10,... | collective-permute-start | bytes 2359304 | tf_op jit(solution)/shard_map/ppermute | solution.py:23
  4.3 0.0 copy-done
  4.3 1.6 %collective-permute-start = (bf16[1,2,256,256]{3,2,1,0:T(8,128)(2,1)S(1)}, bf16[1,2,256,256]{3,2,1,0:T(8,128)(2,1)S(1)}, u32[]{:S(2)}, u32[]{:S(2)}) collective-permute-start(bf16[1,2,256,256]{3,2,1,0:T(8,128)(2,1)S(1)} %get-tuple-element.14), channel_id=1, source_target_pairs={{0,4},{4,0},{8,12},{12,8},{1,5},{5,1},{9,13},{13,9},{2,6},{6,2},{1... | collective-permute-start | bytes 786440 | tf_op jit(solution)/shard_map/ppermute | solution.py:36
  5.9 2.5 %collective-permute-start.8 = (bf16[1,2,256,256]{3,2,1,0:T(8,128)(2,1)S(1)}, bf16[1,2,256,256]{3,2,1,0:T(8,128)(2,1)S(1)}, u32[]{:S(2)}, u32[]{:S(2)}) collective-permute-start(bf16[1,2,256,256]{3,2,1,0:T(8,128)(2,1)S(1)} %get-tuple-element.14), channel_id=1, source_target_pairs={{0,12},{4,8},{8,4},{12,0},{1,13},{5,9},{9,5},{13,1},{2,14},{6,10},... | collective-permute-start | bytes 786440 | tf_op jit(solution)/shard_map/ppermute | solution.py:35
  8.4 0.0 copy-start.1
  8.4 4.3 %collective-permute-done.refs_5_ = bf16[1,2,256,256]{3,2,1,0:T(8,128)(2,1)S(1)} collective-permute-done((bf16[1,2,256,256]{3,2,1,0:T(8,128)(2,1)S(1)}, bf16[1,2,256,256]{3,2,1,0:T(8,128)(2,1)S(1)}, u32[]{:S(2)}, u32[]{:S(2)}) %collective-permute-start) | collective-permute-done | bytes 262176 | tf_op jit(solution)/shard_map/ppermute | solution.py:36
  12.7 1.2 %slice.15.refs_0_ = bf16[1,2,256,768]{3,2,1,0:T(8,128)(2,1)S(1)} slice(bf16[2,2,256,768]{3,2,1,0:T(8,128)(2,1)} %param.3), slice={[1:2], [0:2], [0:256], [0:768]} | slice | bytes 1572864 | tf_op jit(solution)/shard_map/slice | solution.py:55
  13.9 0.6 %collective-permute-start.1 = (bf16[1,2,256,768]{3,2,1,0:T(8,128)(2,1)S(1)}, bf16[1,2,256,768]{3,2,1,0:T(8,128)(2,1)S(1)}, u32[]{:S(2)}, u32[]{:S(2)}) collective-permute-start(bf16[1,2,256,768]{3,2,1,0:T(8,128)(2,1)S(1)} %slice.15.refs_0_), channel_id=1, source_target_pairs={{0,2},{1,3},{2,0},{3,1},{4,6},{5,7},{6,4},{7,5},{8,10},{9,11},{10,... | collective-permute-start | bytes 2359304 | tf_op jit(solution)/shard_map/ppermute | solution.py:23
  14.5 5.4 %collective-permute-done.8.refs_7_ = bf16[1,2,256,256]{3,2,1,0:T(8,128)(2,1)S(1)} collective-permute-done((bf16[1,2,256,256]{3,2,1,0:T(8,128)(2,1)S(1)}, bf16[1,2,256,256]{3,2,1,0:T(8,128)(2,1)S(1)}, u32[]{:S(2)}, u32[]{:S(2)}) %collective-permute-start.8) | collective-permute-done | bytes 262176 | tf_op jit(solution)/shard_map/ppermute | solution.py:35
  19.9 1.8 %collective-permute-start.9 = (bf16[1,2,256,256]{3,2,1,0:T(8,128)(2,1)S(1)}, bf16[1,2,256,256]{3,2,1,0:T(8,128)(2,1)S(1)}, u32[]{:S(2)}, u32[]{:S(2)}) collective-permute-start(bf16[1,2,256,256]{3,2,1,0:T(8,128)(2,1)S(1)} %broadcast_select_fusion), channel_id=1, source_target_pairs={{0,8},{8,12},{12,4},{4,0},{1,9},{9,13},{13,5},{5,1},{2,10},{10,14}... | collective-permute-start | bytes 786440 | tf_op jit(solution)/shard_map/ppermute | solution.py:37
  21.7 1.6 %collective-permute-start.3 = (bf16[1,2,256,256]{3,2,1,0:T(8,128)(2,1)S(1)}, bf16[1,2,256,256]{3,2,1,0:T(8,128)(2,1)S(1)}, u32[]{:S(2)}, u32[]{:S(2)}) collective-permute-start(bf16[1,2,256,256]{3,2,1,0:T(8,128)(2,1)S(1)} %get-tuple-element.16), channel_id=1, source_target_pairs={{0,12},{4,8},{8,4},{12,0},{1,13},{5,9},{9,5},{13,1},{2,14},{6,10},... | collective-permute-start | bytes 786440 | tf_op jit(solution)/shard_map/ppermute | solution.py:35
  23.3 1.0 %collective-permute-start.2 = (bf16[1,2,256,256]{3,2,1,0:T(8,128)(2,1)S(1)}, bf16[1,2,256,256]{3,2,1,0:T(8,128)(2,1)S(1)}, u32[]{:S(2)}, u32[]{:S(2)}) collective-permute-start(bf16[1,2,256,256]{3,2,1,0:T(8,128)(2,1)S(1)} %get-tuple-element.16), channel_id=1, source_target_pairs={{0,4},{4,0},{8,12},{12,8},{1,5},{5,1},{9,13},{13,9},{2,6},{6,2},{1... | collective-permute-start | bytes 786440 | tf_op jit(solution)/shard_map/ppermute | solution.py:36
  24.4 9.2 %collective-permute-done.9.refs_6_ = bf16[1,2,256,256]{3,2,1,0:T(8,128)(2,1)S(1)} collective-permute-done((bf16[1,2,256,256]{3,2,1,0:T(8,128)(2,1)S(1)}, bf16[1,2,256,256]{3,2,1,0:T(8,128)(2,1)S(1)}, u32[]{:S(2)}, u32[]{:S(2)}) %collective-permute-start.9) | collective-permute-done | bytes 262176 | tf_op jit(solution)/shard_map/ppermute | solution.py:37
  33.5 0.0 collective-permute-done.7.refs_2_
  33.5 0.0 collective-permute-start.10
  33.5 0.5 collective-permute-start.11
  34.0 1.0 %collective-permute-done.3.refs_7_ = bf16[1,2,256,256]{3,2,1,0:T(8,128)(2,1)S(1)} collective-permute-done((bf16[1,2,256,256]{3,2,1,0:T(8,128)(2,1)S(1)}, bf16[1,2,256,256]{3,2,1,0:T(8,128)(2,1)S(1)}, u32[]{:S(2)}, u32[]{:S(2)}) %collective-permute-start.3) | collective-permute-done | bytes 262176 | tf_op jit(solution)/shard_map/ppermute | solution.py:35
  35.0 4.2 %collective-permute-start.4 = (bf16[1,2,256,256]{3,2,1,0:T(8,128)(2,1)S(1)}, bf16[1,2,256,256]{3,2,1,0:T(8,128)(2,1)S(1)}, u32[]{:S(2)}, u32[]{:S(2)}) collective-permute-start(bf16[1,2,256,256]{3,2,1,0:T(8,128)(2,1)S(1)} %broadcast_select_fusion.1), channel_id=1, source_target_pairs={{0,8},{8,12},{12,4},{4,0},{1,9},{9,13},{13,5},{5,1},{2,10},{10,14}... | collective-permute-start | bytes 786440 | tf_op jit(solution)/shard_map/ppermute | solution.py:37
  39.3 0.0 collective-permute-done.2.refs_5_
  39.3 5.7 %collective-permute-done.4.refs_6_ = bf16[1,2,256,256]{3,2,1,0:T(8,128)(2,1)S(1)} collective-permute-done((bf16[1,2,256,256]{3,2,1,0:T(8,128)(2,1)S(1)}, bf16[1,2,256,256]{3,2,1,0:T(8,128)(2,1)S(1)}, u32[]{:S(2)}, u32[]{:S(2)}) %collective-permute-start.4) | collective-permute-done | bytes 262176 | tf_op jit(solution)/shard_map/ppermute | solution.py:37
  45.0 0.0 collective-permute-done.1.refs_2_
  45.0 0.0 collective-permute-start.5
  45.0 0.5 collective-permute-start.6
  45.5 0.0 collective-permute-done.10.refs_1_
  45.5 0.0 collective-permute-done.11.refs_3_
  45.5 0.0 copy-done.1
  45.5 3.2 %shard_map.37.refs_8_ = f32[2,2,256,256]{3,2,1,0:T(8,128)} custom-call(s32[4,12]{1,0:T(4,128)S(1)} %copy-done.1, bf16[1,2,256,768]{3,2,1,0:T(8,128)(2,1)S(1)} %slice.12.refs_0_, bf16[1,2,256,768]{3,2,1,0:T(8,128)(2,1)S(1)} %collective-permute-done.10.refs_1_, bf16[1,2,256,768]{3,2,1,0:T(8,128)(2,1)S(1)} %collective-permute-done.7.refs_2_, ...), custom_call_target="tpu_custom_call" | custom-call | flops 3221225472 | bytes 5242880 | tf_op jit(solution)/shard_map/pallas_call | solution.py:116
  48.7 0.0 collective-permute-done.5.refs_1_
  48.7 0.0 collective-permute-done.6.refs_3_
  48.8 3.2 %shard_map.38 = f32[2,2,256,256]{3,2,1,0:T(8,128)} custom-call(s32[4,12]{1,0:T(4,128)S(1)} %copy-done.1, bf16[1,2,256,768]{3,2,1,0:T(8,128)(2,1)S(1)} %slice.15.refs_0_, bf16[1,2,256,768]{3,2,1,0:T(8,128)(2,1)S(1)} %collective-permute-done.5.refs_1_, bf16[1,2,256,768]{3,2,1,0:T(8,128)(2,1)S(1)} %collective-permute-done.1.refs_2_, ...), custom_call_target="tpu_custom_call", output_to_operand_aliasing={{}: (9, {})} | custom-call | flops 1610612736 | bytes 5242880 | tf_op jit(solution)/shard_map/pallas_call | solution.py:116
  (3 shorter events, 0.1 us)
Async XLA Ops:
  0.0 4.3 %copy-start = (bf16[2,2,256,256]{3,2,1,0:T(8,128)(2,1)S(1)}, bf16[2,2,256,256]{3,2,1,0:T(8,128)(2,1)}, u32[]{:S(2)}) copy-start(bf16[2,2,256,256]{3,2,1,0:T(8,128)(2,1)} %refs_4_.1) | copy-start | bytes 1572868
  1.2 32.3 %collective-permute-start.7 = (bf16[1,2,256,768]{3,2,1,0:T(8,128)(2,1)S(1)}, bf16[1,2,256,768]{3,2,1,0:T(8,128)(2,1)S(1)}, u32[]{:S(2)}, u32[]{:S(2)}) collective-permute-start(bf16[1,2,256,768]{3,2,1,0:T(8,128)(2,1)S(1)} %slice.12.refs_0_), channel_id=1, source_target_pairs={{0,2},{1,3},{2,0},{3,1},{4,6},{5,7},{6,4},{7,5},{8,10},{9,11},{10,... | collective-permute-start | bytes 2359304 | tf_op jit(solution)/shard_map/ppermute | solution.py:23
  4.3 8.4 %collective-permute-start = (bf16[1,2,256,256]{3,2,1,0:T(8,128)(2,1)S(1)}, bf16[1,2,256,256]{3,2,1,0:T(8,128)(2,1)S(1)}, u32[]{:S(2)}, u32[]{:S(2)}) collective-permute-start(bf16[1,2,256,256]{3,2,1,0:T(8,128)(2,1)S(1)} %get-tuple-element.14), channel_id=1, source_target_pairs={{0,4},{4,0},{8,12},{12,8},{1,5},{5,1},{9,13},{13,9},{2,6},{6,2},{1... | collective-permute-start | bytes 786440 | tf_op jit(solution)/shard_map/ppermute | solution.py:36
  5.9 13.9 %collective-permute-start.8 = (bf16[1,2,256,256]{3,2,1,0:T(8,128)(2,1)S(1)}, bf16[1,2,256,256]{3,2,1,0:T(8,128)(2,1)S(1)}, u32[]{:S(2)}, u32[]{:S(2)}) collective-permute-start(bf16[1,2,256,256]{3,2,1,0:T(8,128)(2,1)S(1)} %get-tuple-element.14), channel_id=1, source_target_pairs={{0,12},{4,8},{8,4},{12,0},{1,13},{5,9},{9,5},{13,1},{2,14},{6,10},... | collective-permute-start | bytes 786440 | tf_op jit(solution)/shard_map/ppermute | solution.py:35
  8.4 37.1 %copy-start.1 = (s32[4,12]{1,0:T(4,128)S(1)}, s32[4,12]{1,0:T(4,128)}, u32[]{:S(2)}) copy-start(s32[4,12]{1,0:T(4,128)} %aperture_ref.3) | copy-start | bytes 580
  13.9 31.1 %collective-permute-start.1 = (bf16[1,2,256,768]{3,2,1,0:T(8,128)(2,1)S(1)}, bf16[1,2,256,768]{3,2,1,0:T(8,128)(2,1)S(1)}, u32[]{:S(2)}, u32[]{:S(2)}) collective-permute-start(bf16[1,2,256,768]{3,2,1,0:T(8,128)(2,1)S(1)} %slice.15.refs_0_), channel_id=1, source_target_pairs={{0,2},{1,3},{2,0},{3,1},{4,6},{5,7},{6,4},{7,5},{8,10},{9,11},{10,... | collective-permute-start | bytes 2359304 | tf_op jit(solution)/shard_map/ppermute | solution.py:23
  19.9 13.6 %collective-permute-start.9 = (bf16[1,2,256,256]{3,2,1,0:T(8,128)(2,1)S(1)}, bf16[1,2,256,256]{3,2,1,0:T(8,128)(2,1)S(1)}, u32[]{:S(2)}, u32[]{:S(2)}) collective-permute-start(bf16[1,2,256,256]{3,2,1,0:T(8,128)(2,1)S(1)} %broadcast_select_fusion), channel_id=1, source_target_pairs={{0,8},{8,12},{12,4},{4,0},{1,9},{9,13},{13,5},{5,1},{2,10},{10,14}... | collective-permute-start | bytes 786440 | tf_op jit(solution)/shard_map/ppermute | solution.py:37
  21.7 13.3 %collective-permute-start.3 = (bf16[1,2,256,256]{3,2,1,0:T(8,128)(2,1)S(1)}, bf16[1,2,256,256]{3,2,1,0:T(8,128)(2,1)S(1)}, u32[]{:S(2)}, u32[]{:S(2)}) collective-permute-start(bf16[1,2,256,256]{3,2,1,0:T(8,128)(2,1)S(1)} %get-tuple-element.16), channel_id=1, source_target_pairs={{0,12},{4,8},{8,4},{12,0},{1,13},{5,9},{9,5},{13,1},{2,14},{6,10},... | collective-permute-start | bytes 786440 | tf_op jit(solution)/shard_map/ppermute | solution.py:35
  23.3 16.0 %collective-permute-start.2 = (bf16[1,2,256,256]{3,2,1,0:T(8,128)(2,1)S(1)}, bf16[1,2,256,256]{3,2,1,0:T(8,128)(2,1)S(1)}, u32[]{:S(2)}, u32[]{:S(2)}) collective-permute-start(bf16[1,2,256,256]{3,2,1,0:T(8,128)(2,1)S(1)} %get-tuple-element.16), channel_id=1, source_target_pairs={{0,4},{4,0},{8,12},{12,8},{1,5},{5,1},{9,13},{13,9},{2,6},{6,2},{1... | collective-permute-start | bytes 786440 | tf_op jit(solution)/shard_map/ppermute | solution.py:36
  33.5 12.0 %collective-permute-start.10 = (bf16[1,2,256,768]{3,2,1,0:T(8,128)(2,1)S(1)}, bf16[1,2,256,768]{3,2,1,0:T(8,128)(2,1)S(1)}, u32[]{:S(2)}, u32[]{:S(2)}) collective-permute-start(bf16[1,2,256,768]{3,2,1,0:T(8,128)(2,1)S(1)} %slice.12.refs_0_), channel_id=1, source_target_pairs={{0,1},{1,0},{2,3},{3,2},{4,5},{5,4},{6,7},{7,6},{8,9},{9,8},{10,11... | collective-permute-start | bytes 2359304 | tf_op jit(solution)/shard_map/ppermute | solution.py:23
  33.5 12.0 %collective-permute-start.11 = (bf16[1,2,256,768]{3,2,1,0:T(8,128)(2,1)S(1)}, bf16[1,2,256,768]{3,2,1,0:T(8,128)(2,1)S(1)}, u32[]{:S(2)}, u32[]{:S(2)}) collective-permute-start(bf16[1,2,256,768]{3,2,1,0:T(8,128)(2,1)S(1)} %collective-permute-done.7.refs_2_), channel_id=1, source_target_pairs={{0,1},{1,0},{2,3},{3,2},{4,5},{5,4},{6,7},{7,6},{8,9},{9,8},{10,11... | collective-permute-start | bytes 2359304 | tf_op jit(solution)/shard_map/ppermute | solution.py:23
  35.0 9.9 %collective-permute-start.4 = (bf16[1,2,256,256]{3,2,1,0:T(8,128)(2,1)S(1)}, bf16[1,2,256,256]{3,2,1,0:T(8,128)(2,1)S(1)}, u32[]{:S(2)}, u32[]{:S(2)}) collective-permute-start(bf16[1,2,256,256]{3,2,1,0:T(8,128)(2,1)S(1)} %broadcast_select_fusion.1), channel_id=1, source_target_pairs={{0,8},{8,12},{12,4},{4,0},{1,9},{9,13},{13,5},{5,1},{2,10},{10,14}... | collective-permute-start | bytes 786440 | tf_op jit(solution)/shard_map/ppermute | solution.py:37
  45.0 3.8 %collective-permute-start.5 = (bf16[1,2,256,768]{3,2,1,0:T(8,128)(2,1)S(1)}, bf16[1,2,256,768]{3,2,1,0:T(8,128)(2,1)S(1)}, u32[]{:S(2)}, u32[]{:S(2)}) collective-permute-start(bf16[1,2,256,768]{3,2,1,0:T(8,128)(2,1)S(1)} %slice.15.refs_0_), channel_id=1, source_target_pairs={{0,1},{1,0},{2,3},{3,2},{4,5},{5,4},{6,7},{7,6},{8,9},{9,8},{10,11... | collective-permute-start | bytes 2359304 | tf_op jit(solution)/shard_map/ppermute | solution.py:23
  45.0 3.8 %collective-permute-start.6 = (bf16[1,2,256,768]{3,2,1,0:T(8,128)(2,1)S(1)}, bf16[1,2,256,768]{3,2,1,0:T(8,128)(2,1)S(1)}, u32[]{:S(2)}, u32[]{:S(2)}) collective-permute-start(bf16[1,2,256,768]{3,2,1,0:T(8,128)(2,1)S(1)} %collective-permute-done.1.refs_2_), channel_id=1, source_target_pairs={{0,1},{1,0},{2,3},{3,2},{4,5},{5,4},{6,7},{7,6},{8,9},{9,8},{10,11... | collective-permute-start | bytes 2359304 | tf_op jit(solution)/shard_map/ppermute | solution.py:23

commit v5 on v4

v5 whole, which is shorter than its diff:
```python
import functools

import jax
import jax.numpy as jnp
from jax import lax
from jax.experimental import pallas as pl
from jax.experimental.pallas import tpu as pltpu
from jax.sharding import PartitionSpec as P

BLK = 256
APER = 12
HW = 6


def from_behind(x, axis, by):
    peers = lax.axis_size(axis)
    pairs = [(i, i + by) for i in range(peers) if 0 <= i + by < peers]
    return lax.ppermute(x, axis, pairs)


def swap(x, axis, bit):
    peers = lax.axis_size(axis)
    return lax.ppermute(x, axis, [(i, i ^ bit) for i in range(peers)])


def after(value, *earlier):
    return lax.optimization_barrier((value, *earlier))[0]


def line_window(data):
    peers = lax.axis_size("src")
    at_end = (lax.axis_index("src") + 1) % peers < 2
    windows = []
    for v, own in enumerate(lax.optimization_barrier([data[v : v + 1] for v in range(data.shape[0])])):
        far = lax.ppermute(own, "src", [(0, 3), (1, 2), (2, 1), (3, 0)])
        near = lax.ppermute(own, "src", [(0, 1), (1, 0), (2, 3), (3, 2)])
        onward = jnp.where(at_end, own, far)
        middle = lax.ppermute(onward, "src", [(0, 2), (2, 3), (3, 1), (1, 0)])
        windows.append([(own, 0), (near, 0), (middle, 0), (far, 0)])
    return windows


def hop_window(data):
    reach = min(HW, lax.axis_size("src") - 1)
    window = {0: data}
    for hop in range(1, reach + 1):
        window[-hop] = from_behind(window[1 - hop], "src", 1)
        window[hop] = from_behind(window[hop - 1], "src", -1)
    return [[(window[distance], v) for distance in range(-reach, reach + 1)] for v in range(data.shape[0])]


def gather_panels(primaries, windows):
    bit = lax.axis_size("rcv") // 2
    awaited = [piece for piece, _ in windows[0]] + [piece for window in windows[1:] for piece, _ in (window[1], window[-1])]
    panels = []
    for v in range(primaries.shape[0]):
        own = primaries[v : v + 1]
        found = {0: own, bit: swap(own, "rcv", bit)}
        ready = after((own, found[bit]), *awaited) if v == 0 else (own, found[bit])
        for half, origin in zip((0, bit), ready):
            for lower in range(1, bit):
                last = lower & (lower - 1)
                found[half ^ lower] = swap(found[half ^ last] if last else origin, "rcv", lower & -lower)
        panels.append([(found[m], 0) for m in range(2 * bit)])
    return panels


def window_slot(block, wanted, peers, reach):
    return lax.bitwise_xor(block, wanted) if peers == 4 else wanted - block + reach


def window_kernel(piece_at, *refs):
    window = refs[-1]
    width = window.shape[-1] // 2
    for k, (ref, v) in enumerate(zip(refs, piece_at)):
        window[k, :, :width] = ref[v, 0]
        window[k, :, width:] = ref[v, 1]


def assemble(pieces, weight):
    pieces, piece_at = zip(*pieces)
    width = pieces[0].shape[-1]
    return pl.pallas_call(
        functools.partial(window_kernel, piece_at),
        out_shape=jax.ShapeDtypeStruct((len(pieces), BLK, 2 * width), jnp.bfloat16),
        in_specs=[pl.BlockSpec(memory_space=pltpu.VMEM)] * len(pieces),
        out_specs=pl.BlockSpec(memory_space=pltpu.VMEM),
        compiler_params=pltpu.CompilerParams(vmem_limit_bytes=16 * 1024 * 1024),
        cost_estimate=pl.CostEstimate(
            flops=int(weight * 8 * BLK * BLK * APER * width), bytes_accessed=1 << 20, transcendentals=0
        ),
    )(*pieces)


def kernel(survey, panel_at, aperture_ref, *refs):
    panel_refs = [ref.at[v] for ref, v in zip(refs, panel_at)]
    window = refs[len(panel_at)]
    out_ref, result, out_sems = refs[-3:]
    block = lax.axis_index("src")
    me = lax.axis_index("rcv")
    columns = panel_refs[0].shape[-1]
    per_shard = columns // BLK
    width = result.shape[-1]
    panels = []
    blocks = []
    for m, ref in enumerate(panel_refs):
        shard = lax.bitwise_xor(me, m)
        panels.append(ref[...].reshape(2 * BLK, columns))
        for q in range(per_shard):
            wanted = aperture_ref[block, shard * per_shard + q]
            blocks.append(window[window_slot(block, wanted, lax.axis_size("src"), window.shape[0] // 2)])
    products = jnp.dot(
        jnp.concatenate(panels, axis=1), jnp.concatenate(blocks, axis=0), preferred_element_type=jnp.float32
    )
    outs = [pltpu.make_async_copy(result.at[part], out_ref.at[survey, part], out_sems.at[part]) for part in range(2)]
    result[0] = products[:BLK, :width] - products[BLK:, width:]
    outs[0].start()
    result[1] = products[:BLK, width:] + products[BLK:, :width]
    outs[1].start()
    for copy in outs:
        copy.wait()


def multiply(survey, surveys, aperture, panels, window, out, weight):
    panels, panel_at = zip(*panels)
    width = window.shape[-1] // 2
    anywhere = pl.BlockSpec(memory_space=pl.ANY)
    operands = [aperture, *panels, window]
    in_specs = [pl.BlockSpec(memory_space=pltpu.SMEM)]
    in_specs += [pl.BlockSpec(memory_space=pltpu.VMEM)] * (len(panels) + 1)
    aliases = {}
    if out is not None:
        aliases = {len(operands): 0}
        operands.append(out)
        in_specs.append(anywhere)
    return pl.pallas_call(
        functools.partial(kernel, survey, panel_at),
        out_shape=jax.ShapeDtypeStruct((surveys, 2, BLK, width), jnp.float32),
        in_specs=in_specs,
        out_specs=anywhere,
        scratch_shapes=[pltpu.VMEM((2, BLK, width), jnp.float32), pltpu.SemaphoreType.DMA((2,))],
        input_output_aliases=aliases,
        compiler_params=pltpu.CompilerParams(vmem_limit_bytes=24 * 1024 * 1024),
        cost_estimate=pl.CostEstimate(
            flops=int(weight * 8 * BLK * BLK * APER * width), bytes_accessed=1 << 20, transcendentals=0
        ),
    )(*operands)


def body(primaries, data, aperture):
    surveys = primaries.shape[0]
    windows = (line_window if lax.axis_size("src") == 4 else hop_window)(data)
    panels = gather_panels(primaries, windows)
    out = None
    for v in range(surveys):
        pieces = windows[v]
        if out is not None:
            pieces = [(after(piece, out), at) for piece, at in pieces]
        window = assemble(pieces, 4 if v else 0.1)
        out = multiply(v, surveys, aperture, panels[v], window, out, 1 if v else 0.3)
    return out


def solution(mesh):
    placed = (P("freq", None, "src", "rcv"), P("freq", None, "src", "rcv"), P())
    return jax.shard_map(
        body, mesh=mesh, in_specs=placed, out_specs=P("freq", None, "src", "rcv"), check_vma=False
    )
```

time: 52.2 us -> 50.2 us (0.962)
  waiting for transfers between devices: 25.5 us -> 20.1 us
  starting transfers between devices: 17.4 us -> 19.8 us
  Pallas kernels: 6.46 us -> 8.39 us
  local copies, waits for them, and re-layouts: 2.47 us -> 1.57 us
    ppermute x2, waiting for transfers between devices: 14.9 us -> 5.69 us  [line_window(): middle = lax.ppermute(onward, 'src', [(0, 2), (2, 3), (3, 1), (1, 0)])]
    ppermute x2, starting transfers between devices: 6.04 us -> 10 us  [line_window(): middle = lax.ppermute(onward, 'src', [(0, 2), (2, 3), (3, 1), (1, 0)])]
    ppermute x2, waiting for transfers between devices: 6.36 us -> 8.79 us  [line_window(): far = lax.ppermute(own, 'src', [(0, 3), (1, 2), (2, 1), (3, 0)])]
    pallas_call x2 -> x4, Pallas kernels: 6.46 us -> 8.39 us  [the longest x2 6.35 us: multiply(): pl.pallas_call(functools.partial(kernel, survey, panel_at), out_shape=jax...]
    ppermute x2, starting transfers between devices: 2.69 us -> 1.13 us  [line_window(): near = lax.ppermute(own, 'src', [(0, 1), (1, 0), (2, 3), (3, 2)])]
    slice x2 -> x1, local copies, waits for them, and re-layouts: 2.43 us -> 1.53 us  [gather_panels(): own = primaries[v:v + 1]]
    ppermute x6, waiting for transfers between devices: 0.02 us -> 0.76 us  [swap(): return lax.ppermute(x, axis, [(i, i ^ bit) for i in range(peers)])]
    ppermute x2, waiting for transfers between devices: 4.27 us -> 4.9 us  [line_window(): near = lax.ppermute(own, 'src', [(0, 1), (1, 0), (2, 3), (3, 2)])]
  transfers between devices with their start and end apart: 12 -> 12, of which waited for: 5 -> 6; matrix products, arithmetic and copies ran while one was open for 2% -> 0% of each run, Pallas kernels for 6% -> 10%
where the time goes in v5:
time: 50.2 us; the launch traced here: 50 us
  waiting for transfers between devices  20.1 us (40%)
  starting transfers between devices  19.8 us (39%)
  Pallas kernels  8.39 us (17%)
  local copies, waits for them, and re-layouts  1.57 us (3%)
    ppermute x2, starting transfers between devices, line_window(): middle = lax.ppermute(onward, 'src', [(0, 2), (2, 3), (3, 1), (1, 0)])  10 us
    ppermute x2, waiting for transfers between devices, line_window(): far = lax.ppermute(own, 'src', [(0, 3), (1, 2), (2, 1), (3, 0)])  8.79 us
    pallas_call x2, Pallas kernels, multiply(): pl.pallas_call(functools.partial(kernel, survey, panel_at), out_shape=jax...  6.35 us
    ppermute x2, waiting for transfers between devices, line_window(): middle = lax.ppermute(onward, 'src', [(0, 2), (2, 3), (3, 1), (1, 0)])  5.69 us
    ppermute x2, waiting for transfers between devices, line_window(): near = lax.ppermute(own, 'src', [(0, 1), (1, 0), (2, 3), (3, 2)])  4.9 us
    ppermute x2, starting transfers between devices, line_window(): far = lax.ppermute(own, 'src', [(0, 3), (1, 2), (2, 1), (3, 0)])  4.56 us
    ppermute x6, starting transfers between devices, swap(): return lax.ppermute(x, axis, [(i, i ^ bit) for i in range(peers)])  4.06 us
    pallas_call x2, Pallas kernels, assemble(): pl.pallas_call(functools.partial(window_kernel, piece_at), out_shape=jax....  2.04 us
  transfers between devices with their start and end apart: 12, of which 6 were waited for; matrix products, arithmetic and copies ran while one was open for 0% of the time, Pallas kernels for 10%

profile of v5, /device:TPU:0, one launch (start us, length us, event | category | flops | bytes accessed | tf_op | source)
XLA Modules:
  0.0 50.0 jit_solution(1121591610551513141)
XLA Ops:
  0.0 0.0 copy-start.1
  0.0 1.5 %fusion = (bf16[1,2,256,768]{3,2,1,0:T(8,128)(2,1)S(1)}, bf16[1,2,256,768]{3,2,1,0:T(8,128)(2,1)S(1)}) fusion(bf16[2,2,256,768]{3,2,1,0:T(8,128)(2,1)} %param.3), kind=kLoop, calls=%fused_computation.2 | loop fusion | bytes 3145728 | tf_op jit(solution)/shard_map/slice | solution.py:57
  1.5 3.0 %collective-permute-start.3 = (bf16[1,2,256,768]{3,2,1,0:T(8,128)(2,1)S(1)}, bf16[1,2,256,768]{3,2,1,0:T(8,128)(2,1)S(1)}, u32[]{:S(2)}, u32[]{:S(2)}) collective-permute-start(bf16[1,2,256,768]{3,2,1,0:T(8,128)(2,1)S(1)} %get-tuple-element.15.refs_0_), channel_id=1, source_target_pairs={{0,2},{1,3},{2,0},{3,1},{4,6},{5,7},{6,4},{7,5},{8,10},{9,11},{10,... | collective-permute-start | bytes 2359304 | tf_op jit(solution)/shard_map/ppermute | solution.py:23
  4.5 0.0 copy-done.1
  4.6 3.7 %collective-permute-start.5 = (bf16[1,2,256,256]{3,2,1,0:T(8,128)(2,1)S(1)}, bf16[1,2,256,256]{3,2,1,0:T(8,128)(2,1)S(1)}, u32[]{:S(2)}, u32[]{:S(2)}) collective-permute-start(bf16[1,2,256,256]{3,2,1,0:T(8,128)(2,1)S(1)} %get-tuple-element.14.refs_0_), channel_id=1, source_target_pairs={{0,12},{4,8},{8,4},{12,0},{1,13},{5,9},{9,5},{13,1},{2,14},{6,10},... | collective-permute-start | bytes 786440 | tf_op jit(solution)/shard_map/ppermute | solution.py:35
  8.2 0.0 collective-permute-start.4
  8.3 0.9 %collective-permute-start.8 = (bf16[1,2,256,256]{3,2,1,0:T(8,128)(2,1)S(1)}, bf16[1,2,256,256]{3,2,1,0:T(8,128)(2,1)S(1)}, u32[]{:S(2)}, u32[]{:S(2)}) collective-permute-start(bf16[1,2,256,256]{3,2,1,0:T(8,128)(2,1)S(1)} %get-tuple-element.17.refs_0_), channel_id=1, source_target_pairs={{0,12},{4,8},{8,4},{12,0},{1,13},{5,9},{9,5},{13,1},{2,14},{6,10},... | collective-permute-start | bytes 786440 | tf_op jit(solution)/shard_map/ppermute | solution.py:35
  9.1 1.1 %collective-permute-start.7 = (bf16[1,2,256,256]{3,2,1,0:T(8,128)(2,1)S(1)}, bf16[1,2,256,256]{3,2,1,0:T(8,128)(2,1)}, u32[]{:S(2)}, u32[]{:S(2)}) collective-permute-start(bf16[1,2,256,256]{3,2,1,0:T(8,128)(2,1)S(1)} %get-tuple-element.17.refs_0_), channel_id=1, source_target_pairs={{0,4},{4,0},{8,12},{12,8},{1,5},{5,1},{9,13},{13,9},{2,6},{6,2},{1... | collective-permute-start | bytes 786440 | tf_op jit(solution)/shard_map/ppermute | solution.py:36
  10.3 5.4 %collective-permute-done.5.refs_3_ = bf16[1,2,256,256]{3,2,1,0:T(8,128)(2,1)S(1)} collective-permute-done((bf16[1,2,256,256]{3,2,1,0:T(8,128)(2,1)S(1)}, bf16[1,2,256,256]{3,2,1,0:T(8,128)(2,1)S(1)}, u32[]{:S(2)}, u32[]{:S(2)}) %collective-permute-start.5) | collective-permute-done | bytes 262176 | tf_op jit(solution)/shard_map/ppermute | solution.py:35
  15.8 0.0 copy-start
  15.8 7.3 %collective-permute-start.6 = (bf16[1,2,256,256]{3,2,1,0:T(8,128)(2,1)S(1)}, bf16[1,2,256,256]{3,2,1,0:T(8,128)(2,1)S(1)}, u32[]{:S(2)}, u32[]{:S(2)}) collective-permute-start(bf16[1,2,256,256]{3,2,1,0:T(8,128)(2,1)S(1)} %broadcast_select_fusion.1), channel_id=1, source_target_pairs={{0,8},{8,12},{12,4},{4,0},{1,9},{9,13},{13,5},{5,1},{2,10},{10,14}... | collective-permute-start | bytes 786440 | tf_op jit(solution)/shard_map/ppermute | solution.py:38
  23.1 0.0 collective-permute-done.4.refs_1_
  23.1 0.5 %collective-permute-start.1 = (bf16[1,2,256,768]{3,2,1,0:T(8,128)(2,1)S(1)}, bf16[1,2,256,768]{3,2,1,0:T(8,128)(2,1)S(1)}, u32[]{:S(2)}, u32[]{:S(2)}) collective-permute-start(bf16[1,2,256,768]{3,2,1,0:T(8,128)(2,1)S(1)} %get-tuple-element.22.refs_0_), channel_id=1, source_target_pairs={{0,2},{1,3},{2,0},{3,1},{4,6},{5,7},{6,4},{7,5},{8,10},{9,11},{10,... | collective-permute-start | bytes 2359304 | tf_op jit(solution)/shard_map/ppermute | solution.py:23
  23.6 3.3 %collective-permute-done.8.refs_3_ = bf16[1,2,256,256]{3,2,1,0:T(8,128)(2,1)S(1)} collective-permute-done((bf16[1,2,256,256]{3,2,1,0:T(8,128)(2,1)S(1)}, bf16[1,2,256,256]{3,2,1,0:T(8,128)(2,1)S(1)}, u32[]{:S(2)}, u32[]{:S(2)}) %collective-permute-start.8) | collective-permute-done | bytes 262176 | tf_op jit(solution)/shard_map/ppermute | solution.py:35
  27.0 4.9 %collective-permute-done.7.refs_1_ = bf16[1,2,256,256]{3,2,1,0:T(8,128)(2,1)} collective-permute-done((bf16[1,2,256,256]{3,2,1,0:T(8,128)(2,1)S(1)}, bf16[1,2,256,256]{3,2,1,0:T(8,128)(2,1)}, u32[]{:S(2)}, u32[]{:S(2)}) %collective-permute-start.7) | collective-permute-done | bytes 262176 | tf_op jit(solution)/shard_map/ppermute | solution.py:36
  31.9 4.9 %collective-permute-done.6.refs_2_ = bf16[1,2,256,256]{3,2,1,0:T(8,128)(2,1)S(1)} collective-permute-done((bf16[1,2,256,256]{3,2,1,0:T(8,128)(2,1)S(1)}, bf16[1,2,256,256]{3,2,1,0:T(8,128)(2,1)S(1)}, u32[]{:S(2)}, u32[]{:S(2)}) %collective-permute-start.6) | collective-permute-done | bytes 262176 | tf_op jit(solution)/shard_map/ppermute | solution.py:38
  36.8 0.0 collective-permute-done.3.refs_2_
  36.8 0.0 collective-permute-start.10
  36.9 0.5 collective-permute-start.9
  37.4 2.7 %collective-permute-start.11 = (bf16[1,2,256,256]{3,2,1,0:T(8,128)(2,1)S(1)}, bf16[1,2,256,256]{3,2,1,0:T(8,128)(2,1)S(1)}, u32[]{:S(2)}, u32[]{:S(2)}) collective-permute-start(bf16[1,2,256,256]{3,2,1,0:T(8,128)(2,1)S(1)} %broadcast_select_fusion), channel_id=1, source_target_pairs={{0,8},{8,12},{12,4},{4,0},{1,9},{9,13},{13,5},{5,1},{2,10},{10,14}... | collective-permute-start | bytes 786440 | tf_op jit(solution)/shard_map/ppermute | solution.py:38
  40.1 0.0 collective-permute-start
  40.1 0.7 %collective-permute-done.1.refs_2_ = bf16[1,2,256,768]{3,2,1,0:T(8,128)(2,1)S(1)} collective-permute-done((bf16[1,2,256,768]{3,2,1,0:T(8,128)(2,1)S(1)}, bf16[1,2,256,768]{3,2,1,0:T(8,128)(2,1)S(1)}, u32[]{:S(2)}, u32[]{:S(2)}) %collective-permute-start.1) | collective-permute-done | bytes 786464 | tf_op jit(solution)/shard_map/ppermute | solution.py:23
  40.8 0.0 collective-permute-start.2
  40.8 1.0 %shard_map.37.refs_4_ = bf16[4,256,512]{2,1,0:T(8,128)(2,1)S(1)} custom-call(bf16[1,2,256,256]{3,2,1,0:T(8,128)(2,1)S(1)} %get-tuple-element.14.refs_0_, bf16[1,2,256,256]{3,2,1,0:T(8,128)(2,1)} %collective-permute-done.4.refs_1_, bf16[1,2,256,256]{3,2,1,0:T(8,128)(2,1)S(1)} %collective-permute-done.6.refs_2_, ...), custom_call_target="tpu_custom_call" | custom-call | flops 161061280 | bytes 1048576 | tf_op jit(solution)/shard_map/pallas_call | solution.py:83
  41.9 0.0 collective-permute-done.10.refs_3_
  41.9 0.0 collective-permute-done.9.refs_1_
  41.9 0.0 copy-done
  41.9 3.2 %shard_map.38.refs_5_ = f32[2,2,256,256]{3,2,1,0:T(8,128)} custom-call(s32[4,12]{1,0:T(4,128)S(1)} %copy-done, bf16[1,2,256,768]{3,2,1,0:T(8,128)(2,1)S(1)} %get-tuple-element.15.refs_0_, bf16[1,2,256,768]{3,2,1,0:T(8,128)(2,1)S(1)} %collective-permute-done.9.refs_1_, bf16[1,2,256,768]{3,2,1,0:T(8,128)(2,1)S(1)} %collective-permute-done.3.refs_2_, ...), custom_call_target="tpu_custom_call" | custom-call | flops 483183808 | bytes 1048576 | tf_op jit(solution)/shard_map/pallas_call | solution.py:136
  45.1 0.7 %collective-permute-done.11.refs_2_ = bf16[1,2,256,256]{3,2,1,0:T(8,128)(2,1)S(1)} collective-permute-done((bf16[1,2,256,256]{3,2,1,0:T(8,128)(2,1)S(1)}, bf16[1,2,256,256]{3,2,1,0:T(8,128)(2,1)S(1)}, u32[]{:S(2)}, u32[]{:S(2)}) %collective-permute-start.11) | collective-permute-done | bytes 262176 | tf_op jit(solution)/shard_map/ppermute | solution.py:38
  45.8 1.0 %shard_map.39.refs_4_ = bf16[4,256,512]{2,1,0:T(8,128)(2,1)S(1)} custom-call(bf16[1,2,256,256]{3,2,1,0:T(8,128)(2,1)S(1)} %get-tuple-element.17.refs_0_, bf16[1,2,256,256]{3,2,1,0:T(8,128)(2,1)} %collective-permute-done.7.refs_1_, bf16[1,2,256,256]{3,2,1,0:T(8,128)(2,1)S(1)} %collective-permute-done.11.refs_2_, ...), custom_call_target="tpu_custom_call" | custom-call | flops 6442450944 | bytes 1048576 | tf_op jit(solution)/shard_map/pallas_call | solution.py:83
  46.8 0.0 collective-permute-done.refs_1_
  46.8 0.0 collective-permute-done.2.refs_3_
  46.9 3.2 %shard_map.40 = f32[2,2,256,256]{3,2,1,0:T(8,128)} custom-call(s32[4,12]{1,0:T(4,128)S(1)} %copy-done, bf16[1,2,256,768]{3,2,1,0:T(8,128)(2,1)S(1)} %get-tuple-element.22.refs_0_, bf16[1,2,256,768]{3,2,1,0:T(8,128)(2,1)S(1)} %collective-permute-done.refs_1_, ...), custom_call_target="tpu_custom_call", output_to_operand_aliasing={{}: (6, {})} | custom-call | flops 1610612736 | bytes 1048576 | tf_op jit(solution)/shard_map/pallas_call | solution.py:136
  (3 shorter events, 0.1 us)
Async XLA Ops:
  0.0 4.5 %copy-start.1 = (bf16[2,2,256,256]{3,2,1,0:T(8,128)(2,1)S(1)}, bf16[2,2,256,256]{3,2,1,0:T(8,128)(2,1)}, u32[]{:S(2)}) copy-start(bf16[2,2,256,256]{3,2,1,0:T(8,128)(2,1)} %param.4) | copy-start | bytes 1572868
  1.5 35.3 %collective-permute-start.3 = (bf16[1,2,256,768]{3,2,1,0:T(8,128)(2,1)S(1)}, bf16[1,2,256,768]{3,2,1,0:T(8,128)(2,1)S(1)}, u32[]{:S(2)}, u32[]{:S(2)}) collective-permute-start(bf16[1,2,256,768]{3,2,1,0:T(8,128)(2,1)S(1)} %get-tuple-element.15.refs_0_), channel_id=1, source_target_pairs={{0,2},{1,3},{2,0},{3,1},{4,6},{5,7},{6,4},{7,5},{8,10},{9,11},{10,... | collective-permute-start | bytes 2359304 | tf_op jit(solution)/shard_map/ppermute | solution.py:23
  4.6 11.1 %collective-permute-start.5 = (bf16[1,2,256,256]{3,2,1,0:T(8,128)(2,1)S(1)}, bf16[1,2,256,256]{3,2,1,0:T(8,128)(2,1)S(1)}, u32[]{:S(2)}, u32[]{:S(2)}) collective-permute-start(bf16[1,2,256,256]{3,2,1,0:T(8,128)(2,1)S(1)} %get-tuple-element.14.refs_0_), channel_id=1, source_target_pairs={{0,12},{4,8},{8,4},{12,0},{1,13},{5,9},{9,5},{13,1},{2,14},{6,10},... | collective-permute-start | bytes 786440 | tf_op jit(solution)/shard_map/ppermute | solution.py:35
  8.2 14.9 %collective-permute-start.4 = (bf16[1,2,256,256]{3,2,1,0:T(8,128)(2,1)S(1)}, bf16[1,2,256,256]{3,2,1,0:T(8,128)(2,1)}, u32[]{:S(2)}, u32[]{:S(2)}) collective-permute-start(bf16[1,2,256,256]{3,2,1,0:T(8,128)(2,1)S(1)} %get-tuple-element.14.refs_0_), channel_id=1, source_target_pairs={{0,4},{4,0},{8,12},{12,8},{1,5},{5,1},{9,13},{13,9},{2,6},{6,2},{1... | collective-permute-start | bytes 786440 | tf_op jit(solution)/shard_map/ppermute | solution.py:36
  8.3 18.7 %collective-permute-start.8 = (bf16[1,2,256,256]{3,2,1,0:T(8,128)(2,1)S(1)}, bf16[1,2,256,256]{3,2,1,0:T(8,128)(2,1)S(1)}, u32[]{:S(2)}, u32[]{:S(2)}) collective-permute-start(bf16[1,2,256,256]{3,2,1,0:T(8,128)(2,1)S(1)} %get-tuple-element.17.refs_0_), channel_id=1, source_target_pairs={{0,12},{4,8},{8,4},{12,0},{1,13},{5,9},{9,5},{13,1},{2,14},{6,10},... | collective-permute-start | bytes 786440 | tf_op jit(solution)/shard_map/ppermute | solution.py:35
  9.1 22.7 %collective-permute-start.7 = (bf16[1,2,256,256]{3,2,1,0:T(8,128)(2,1)S(1)}, bf16[1,2,256,256]{3,2,1,0:T(8,128)(2,1)}, u32[]{:S(2)}, u32[]{:S(2)}) collective-permute-start(bf16[1,2,256,256]{3,2,1,0:T(8,128)(2,1)S(1)} %get-tuple-element.17.refs_0_), channel_id=1, source_target_pairs={{0,4},{4,0},{8,12},{12,8},{1,5},{5,1},{9,13},{13,9},{2,6},{6,2},{1... | collective-permute-start | bytes 786440 | tf_op jit(solution)/shard_map/ppermute | solution.py:36
  15.8 26.1 %copy-start = (s32[4,12]{1,0:T(4,128)S(1)}, s32[4,12]{1,0:T(4,128)}, u32[]{:S(2)}) copy-start(s32[4,12]{1,0:T(4,128)} %aperture_ref.3) | copy-start | bytes 580
  15.8 21.1 %collective-permute-start.6 = (bf16[1,2,256,256]{3,2,1,0:T(8,128)(2,1)S(1)}, bf16[1,2,256,256]{3,2,1,0:T(8,128)(2,1)S(1)}, u32[]{:S(2)}, u32[]{:S(2)}) collective-permute-start(bf16[1,2,256,256]{3,2,1,0:T(8,128)(2,1)S(1)} %broadcast_select_fusion.1), channel_id=1, source_target_pairs={{0,8},{8,12},{12,4},{4,0},{1,9},{9,13},{13,5},{5,1},{2,10},{10,14}... | collective-permute-start | bytes 786440 | tf_op jit(solution)/shard_map/ppermute | solution.py:38
  23.1 17.7 %collective-permute-start.1 = (bf16[1,2,256,768]{3,2,1,0:T(8,128)(2,1)S(1)}, bf16[1,2,256,768]{3,2,1,0:T(8,128)(2,1)S(1)}, u32[]{:S(2)}, u32[]{:S(2)}) collective-permute-start(bf16[1,2,256,768]{3,2,1,0:T(8,128)(2,1)S(1)} %get-tuple-element.22.refs_0_), channel_id=1, source_target_pairs={{0,2},{1,3},{2,0},{3,1},{4,6},{5,7},{6,4},{7,5},{8,10},{9,11},{10,... | collective-permute-start | bytes 2359304 | tf_op jit(solution)/shard_map/ppermute | solution.py:23
  36.8 5.0 %collective-permute-start.10 = (bf16[1,2,256,768]{3,2,1,0:T(8,128)(2,1)S(1)}, bf16[1,2,256,768]{3,2,1,0:T(8,128)(2,1)S(1)}, u32[]{:S(2)}, u32[]{:S(2)}) collective-permute-start(bf16[1,2,256,768]{3,2,1,0:T(8,128)(2,1)S(1)} %collective-permute-done.3.refs_2_), channel_id=1, source_target_pairs={{0,1},{1,0},{2,3},{3,2},{4,5},{5,4},{6,7},{7,6},{8,9},{9,8},{10,11... | collective-permute-start | bytes 2359304 | tf_op jit(solution)/shard_map/ppermute | solution.py:23
  36.9 5.0 %collective-permute-start.9 = (bf16[1,2,256,768]{3,2,1,0:T(8,128)(2,1)S(1)}, bf16[1,2,256,768]{3,2,1,0:T(8,128)(2,1)S(1)}, u32[]{:S(2)}, u32[]{:S(2)}) collective-permute-start(bf16[1,2,256,768]{3,2,1,0:T(8,128)(2,1)S(1)} %get-tuple-element.15.refs_0_), channel_id=1, source_target_pairs={{0,1},{1,0},{2,3},{3,2},{4,5},{5,4},{6,7},{7,6},{8,9},{9,8},{10,11... | collective-permute-start | bytes 2359304 | tf_op jit(solution)/shard_map/ppermute | solution.py:23
  37.4 8.4 %collective-permute-start.11 = (bf16[1,2,256,256]{3,2,1,0:T(8,128)(2,1)S(1)}, bf16[1,2,256,256]{3,2,1,0:T(8,128)(2,1)S(1)}, u32[]{:S(2)}, u32[]{:S(2)}) collective-permute-start(bf16[1,2,256,256]{3,2,1,0:T(8,128)(2,1)S(1)} %broadcast_select_fusion), channel_id=1, source_target_pairs={{0,8},{8,12},{12,4},{4,0},{1,9},{9,13},{13,5},{5,1},{2,10},{10,14}... | collective-permute-start | bytes 786440 | tf_op jit(solution)/shard_map/ppermute | solution.py:38
  40.1 6.8 %collective-permute-start = (bf16[1,2,256,768]{3,2,1,0:T(8,128)(2,1)S(1)}, bf16[1,2,256,768]{3,2,1,0:T(8,128)(2,1)S(1)}, u32[]{:S(2)}, u32[]{:S(2)}) collective-permute-start(bf16[1,2,256,768]{3,2,1,0:T(8,128)(2,1)S(1)} %get-tuple-element.22.refs_0_), channel_id=1, source_target_pairs={{0,1},{1,0},{2,3},{3,2},{4,5},{5,4},{6,7},{7,6},{8,9},{9,8},{10,11... | collective-permute-start | bytes 2359304 | tf_op jit(solution)/shard_map/ppermute | solution.py:23
  40.8 6.0 %collective-permute-start.2 = (bf16[1,2,256,768]{3,2,1,0:T(8,128)(2,1)S(1)}, bf16[1,2,256,768]{3,2,1,0:T(8,128)(2,1)S(1)}, u32[]{:S(2)}, u32[]{:S(2)}) collective-permute-start(bf16[1,2,256,768]{3,2,1,0:T(8,128)(2,1)S(1)} %collective-permute-done.1.refs_2_), channel_id=1, source_target_pairs={{0,1},{1,0},{2,3},{3,2},{4,5},{5,4},{6,7},{7,6},{8,9},{9,8},{10,11... | collective-permute-start | bytes 2359304 | tf_op jit(solution)/shard_map/ppermute | solution.py:23

commit v6 on v4

--- a/solution.py
+++ b/solution.py
@@ -30,12 +30,13 @@
 def line_window(data):
     peers = lax.axis_size("src")
     at_end = (lax.axis_index("src") + 1) % peers < 2
+    near = lax.ppermute(data, "src", [(0, 1), (1, 0), (2, 3), (3, 2)])
     windows = []
     for v, own in enumerate(lax.optimization_barrier([data[v : v + 1] for v in range(data.shape[0])])):
         far = lax.ppermute(own, "src", [(0, 3), (1, 2), (2, 1), (3, 0)])
-        near = lax.ppermute(own, "src", [(0, 1), (1, 0), (2, 3), (3, 2)])
-        middle = lax.ppermute(jnp.where(at_end, own, far), "src", [(0, 2), (2, 3), (3, 1), (1, 0)])
-        windows.append([(data, v), (near, 0), (middle, 0), (far, 0)])
+        onward = jnp.where(at_end, own, far)
+        middle = lax.ppermute(onward, "src", [(0, 2), (2, 3), (3, 1), (1, 0)])
+        windows.append([(data, v), (near, v), (middle, 0), (far, 0)])
     return windows
 
 
@@ -48,19 +49,22 @@
     return [[(window[distance], v) for distance in range(-reach, reach + 1)] for v in range(data.shape[0])]
 
 
-def gather_panels(first, primaries, windows):
+def exchange(primaries):
     bit = lax.axis_size("rcv") // 2
-    panels = []
+    halves = []
     for v in range(primaries.shape[0]):
-        own = first if v == 0 else after(primaries, windows[v - 1][1][0])[v : v + 1]
-        found = {0: own, bit: swap(own, "rcv", bit)}
-        ready = after((found[0], found[bit]), *[piece for piece, _ in windows[v]])
-        for lower in range(1, bit):
-            last = lower & (lower - 1)
-            for half, first in zip((0, bit), ready):
-                found[half ^ lower] = swap(found[half ^ last] if last else first, "rcv", lower & -lower)
-        panels.append([(found[m], 0) for m in range(2 * bit)])
-    return panels
+        own = primaries[v : v + 1]
+        primaries = after(primaries, own)
+        halves.append((own, swap(own, "rcv", bit)))
+    return halves
+
+
+def hand_on(halves):
+    bit = lax.axis_size("rcv") // 2
+    panels = list(halves)
+    for lower in range(1, bit):
+        panels += [swap(panels[2 * (lower & (lower - 1)) + half], "rcv", lower & -lower) for half in range(2)]
+    return panels[::2] + panels[1::2]
 
 
 def window_slot(block, wanted, peers, reach):
@@ -108,7 +112,7 @@
     in_specs = [pl.BlockSpec(memory_space=pltpu.SMEM)]
     in_specs += [pl.BlockSpec(memory_space=pltpu.VMEM)] * (len(panels) + len(pieces))
     aliases = {}
-    weight = 1 if survey + 1 == surveys else 2
+    weight = 1 if survey + 1 == surveys else 1.6
     if out is not None:
         aliases = {len(operands): 0}
         operands.append(out)
@@ -133,12 +137,13 @@
 
 def body(primaries, data, aperture):
     surveys = primaries.shape[0]
-    first = primaries[:1]
-    windows = (line_window if lax.axis_size("src") == 4 else hop_window)(after(data, first))
-    panels = gather_panels(first, primaries, windows)
+    halves = exchange(primaries)
+    windows = (line_window if lax.axis_size("src") == 4 else hop_window)(after(data, halves[0][0]))
+    under_way = [window[k][0] for window in windows[1:] for k in (1, -1)]
     out = None
     for v in range(surveys):
-        out = multiply(v, surveys, aperture, panels[v], windows[v], out)
+        ready = after(halves[v], [piece for piece, _ in windows[v]], under_way)
+        out = multiply(v, surveys, aperture, [(panel, 0) for panel in hand_on(ready)], windows[v], out)
     return out
 
 

time: 52.2 us -> 51.7 us (level)
  waiting for transfers between devices: 25.5 us -> 17.1 us
  starting transfers between devices: 17.4 us -> 22.4 us
  other arithmetic: 0.07 us -> 1.96 us
  Pallas kernels: 6.46 us -> 7.67 us
    ppermute x4 -> x3, waiting for transfers between devices: 19.1 us -> 10 us  [the longest x2 10 us: line_window(): middle = lax.ppermute(onward, 'src', [(0, 2), (2, 3), (3, 1), (1, 0)])]
    ppermute x4 -> x3, starting transfers between devices: 8.74 us -> 14.1 us  [the longest x2 14.1 us: line_window(): middle = lax.ppermute(onward, 'src', [(0, 2), (2, 3), (3, 1), (1, 0)])]
    select_n x2, other arithmetic: 0.07 us -> 1.96 us  [line_window(): onward = jnp.where(at_end, own, far)]
    pallas_call x2, Pallas kernels: 6.46 us -> 7.67 us  [multiply(): pl.pallas_call(functools.partial(kernel, survey, panel_at, piece_at), out...]
    slice x2, local copies, waits for them, and re-layouts: 2.43 us -> 1.38 us  [exchange(): own = primaries[v:v + 1]]
    slice x1, local copies, waits for them, and re-layouts: 0.03 us -> 0.83 us  [line_window(): data[v:v + 1]]
    ppermute x2, waiting for transfers between devices: 6.36 us -> 7.12 us  [line_window(): far = lax.ppermute(own, 'src', [(0, 3), (1, 2), (2, 1), (3, 0)])]
  transfers between devices with their start and end apart: 12 -> 11, of which waited for: 5 -> 3; matrix products, arithmetic and copies ran while one was open for 2% -> 6% of each run, Pallas kernels for 6% -> 8%
where the time goes in v6:
time: 51.7 us; the launch traced here: 51.4 us
  starting transfers between devices  22.4 us (43%)
  waiting for transfers between devices  17.1 us (33%)
  Pallas kernels  7.67 us (15%)
  local copies, waits for them, and re-layouts  2.23 us (4%)
  other arithmetic  1.96 us (4%)
    ppermute x2, starting transfers between devices, line_window(): middle = lax.ppermute(onward, 'src', [(0, 2), (2, 3), (3, 1), (1, 0)])  14.1 us
    ppermute x2, waiting for transfers between devices, line_window(): middle = lax.ppermute(onward, 'src', [(0, 2), (2, 3), (3, 1), (1, 0)])  10 us
    pallas_call x2, Pallas kernels, multiply(): pl.pallas_call(functools.partial(kernel, survey, panel_at, piece_at), out...  7.67 us
    ppermute x2, waiting for transfers between devices, line_window(): far = lax.ppermute(own, 'src', [(0, 3), (1, 2), (2, 1), (3, 0)])  7.12 us
    ppermute x6, starting transfers between devices, swap(): return lax.ppermute(x, axis, [(i, i ^ bit) for i in range(peers)])  4.62 us
    ppermute x2, starting transfers between devices, line_window(): far = lax.ppermute(own, 'src', [(0, 3), (1, 2), (2, 1), (3, 0)])  3.61 us
    select_n x2, other arithmetic, line_window(): onward = jnp.where(at_end, own, far)  1.96 us
    slice x2, local copies, waits for them, and re-layouts, exchange(): own = primaries[v:v + 1]  1.38 us
  transfers between devices with their start and end apart: 11, of which 3 were waited for; matrix products, arithmetic and copies ran while one was open for 6% of the time, Pallas kernels for 8%

profile of v6, /device:TPU:0, one launch (start us, length us, event | category | flops | bytes accessed | tf_op | source)
XLA Modules:
  0.0 51.4 jit_solution(13510655583628957138)
XLA Ops:
  0.0 0.0 copy-start
  0.0 0.0 copy-start.2
  0.0 1.3 %slice.12.refs_0_ = bf16[1,2,256,768]{3,2,1,0:T(8,128)(2,1)S(1)} slice(bf16[2,2,256,768]{3,2,1,0:T(8,128)(2,1)} %param.3), slice={[0:1], [0:2], [0:256], [0:768]} | slice | bytes 1572864 | tf_op jit(solution)/shard_map/slice | solution.py:56
  1.3 3.0 %collective-permute-start.6 = (bf16[1,2,256,768]{3,2,1,0:T(8,128)(2,1)S(1)}, bf16[1,2,256,768]{3,2,1,0:T(8,128)(2,1)}, u32[]{:S(2)}, u32[]{:S(2)}) collective-permute-start(bf16[1,2,256,768]{3,2,1,0:T(8,128)(2,1)S(1)} %slice.12.refs_0_), channel_id=1, source_target_pairs={{0,2},{1,3},{2,0},{3,1},{4,6},{5,7},{6,4},{7,5},{8,10},{9,11},{10,... | collective-permute-start | bytes 2359304 | tf_op jit(solution)/shard_map/ppermute | solution.py:23
  4.3 0.0 copy-done
  4.3 0.8 %fusion = (bf16[1,2,256,256]{3,2,1,0:T(8,128)(2,1)}, bf16[1,2,256,256]{3,2,1,0:T(8,128)(2,1)}) fusion(bf16[2,2,256,256]{3,2,1,0:T(8,128)(2,1)S(1)} %copy-done), kind=kLoop, calls=%fused_computation.2 | loop fusion | bytes 1048576 | tf_op jit(solution)/shard_map/slice | solution.py:35
  5.2 0.0 copy-start.1
  5.2 3.6 %collective-permute-start.7 = (bf16[1,2,256,256]{3,2,1,0:T(8,128)(2,1)}, bf16[1,2,256,256]{3,2,1,0:T(8,128)(2,1)S(1)}, u32[]{:S(2)}, u32[]{:S(2)}) collective-permute-start(bf16[1,2,256,256]{3,2,1,0:T(8,128)(2,1)} %get-tuple-element.18), channel_id=1, source_target_pairs={{0,12},{4,8},{8,4},{12,0},{1,13},{5,9},{9,5},{13,1},{2,14},{6,10},... | collective-permute-start | bytes 786440 | tf_op jit(solution)/shard_map/ppermute | solution.py:36
  8.8 0.0 copy-done.2
  8.8 0.1 slice.13.refs_0_
  8.8 0.6 %collective-permute-start = (bf16[1,2,256,768]{3,2,1,0:T(8,128)(2,1)S(1)}, bf16[1,2,256,768]{3,2,1,0:T(8,128)(2,1)S(1)}, u32[]{:S(2)}, u32[]{:S(2)}) collective-permute-start(bf16[1,2,256,768]{3,2,1,0:T(8,128)(2,1)S(1)} %slice.13.refs_0_), channel_id=1, source_target_pairs={{0,2},{1,3},{2,0},{3,1},{4,6},{5,7},{6,4},{7,5},{8,10},{9,11},{10,... | collective-permute-start | bytes 2359304 | tf_op jit(solution)/shard_map/ppermute | solution.py:23
  9.4 0.0 collective-permute-start.2
  9.5 0.0 collective-permute-start.1
  9.5 7.1 %collective-permute-done.7.refs_7_ = bf16[1,2,256,256]{3,2,1,0:T(8,128)(2,1)S(1)} collective-permute-done((bf16[1,2,256,256]{3,2,1,0:T(8,128)(2,1)}, bf16[1,2,256,256]{3,2,1,0:T(8,128)(2,1)S(1)}, u32[]{:S(2)}, u32[]{:S(2)}) %collective-permute-start.7) | collective-permute-done | bytes 262176 | tf_op jit(solution)/shard_map/ppermute | solution.py:36
  16.6 1.0 %broadcast_select_fusion = bf16[1,2,256,256]{3,2,1,0:T(8,128)(2,1)S(1)} fusion(bf16[1,2,256,256]{3,2,1,0:T(8,128)(2,1)} %get-tuple-element.18, bf16[1,2,256,256]{3,2,1,0:T(8,128)(2,1)S(1)} %collective-permute-done.7.refs_7_, pred[]{:T(512)S(6)} %lt.10), kind=kLoop, calls=%fused_computation | loop fusion | flops 131072 | bytes 786433 | tf_op jit(solution)/shard_map/jit(_where)/select_n | solution.py:37
  17.6 11.0 %collective-permute-start.8 = (bf16[1,2,256,256]{3,2,1,0:T(8,128)(2,1)S(1)}, bf16[1,2,256,256]{3,2,1,0:T(8,128)(2,1)S(1)}, u32[]{:S(2)}, u32[]{:S(2)}) collective-permute-start(bf16[1,2,256,256]{3,2,1,0:T(8,128)(2,1)S(1)} %broadcast_select_fusion), channel_id=1, source_target_pairs={{0,8},{8,12},{12,4},{4,0},{1,9},{9,13},{13,5},{5,1},{2,10},{10,14}... | collective-permute-start | bytes 786440 | tf_op jit(solution)/shard_map/ppermute | solution.py:38
  28.5 0.0 collective-permute-done.2.refs_7_
  28.5 1.0 %broadcast_select_fusion.1 = bf16[1,2,256,256]{3,2,1,0:T(8,128)(2,1)S(1)} fusion(bf16[1,2,256,256]{3,2,1,0:T(8,128)(2,1)} %get-tuple-element.15, bf16[1,2,256,256]{3,2,1,0:T(8,128)(2,1)S(1)} %collective-permute-done.2.refs_7_, pred[]{:T(512)S(6)} %lt.10), kind=kLoop, calls=%fused_computation.1 | loop fusion | flops 131072 | bytes 786433 | tf_op jit(solution)/shard_map/jit(_where)/select_n | solution.py:37
  29.5 3.2 %collective-permute-start.3 = (bf16[1,2,256,256]{3,2,1,0:T(8,128)(2,1)S(1)}, bf16[1,2,256,256]{3,2,1,0:T(8,128)(2,1)S(1)}, u32[]{:S(2)}, u32[]{:S(2)}) collective-permute-start(bf16[1,2,256,256]{3,2,1,0:T(8,128)(2,1)S(1)} %broadcast_select_fusion.1), channel_id=1, source_target_pairs={{0,8},{8,12},{12,4},{4,0},{1,9},{9,13},{13,5},{5,1},{2,10},{10,14}... | collective-permute-start | bytes 786440 | tf_op jit(solution)/shard_map/ppermute | solution.py:38
  32.7 5.6 %collective-permute-done.8.refs_6_ = bf16[1,2,256,256]{3,2,1,0:T(8,128)(2,1)S(1)} collective-permute-done((bf16[1,2,256,256]{3,2,1,0:T(8,128)(2,1)S(1)}, bf16[1,2,256,256]{3,2,1,0:T(8,128)(2,1)S(1)}, u32[]{:S(2)}, u32[]{:S(2)}) %collective-permute-start.8) | collective-permute-done | bytes 262176 | tf_op jit(solution)/shard_map/ppermute | solution.py:38
  38.3 0.0 collective-permute-done.1.refs_5_
  38.3 0.0 collective-permute-done.6.refs_2_
  38.3 0.0 collective-permute-start.10
  38.3 0.5 collective-permute-start.9
  38.8 4.4 %collective-permute-done.3.refs_6_ = bf16[1,2,256,256]{3,2,1,0:T(8,128)(2,1)S(1)} collective-permute-done((bf16[1,2,256,256]{3,2,1,0:T(8,128)(2,1)S(1)}, bf16[1,2,256,256]{3,2,1,0:T(8,128)(2,1)S(1)}, u32[]{:S(2)}, u32[]{:S(2)}) %collective-permute-start.3) | collective-permute-done | bytes 262176 | tf_op jit(solution)/shard_map/ppermute | solution.py:38
  43.2 0.0 collective-permute-done.refs_2_
  43.2 0.0 collective-permute-start.4
  43.2 0.5 collective-permute-start.5
  43.7 0.0 collective-permute-done.10.refs_3_
  43.7 0.0 collective-permute-done.9.refs_1_
  43.7 0.0 copy-done.1
  43.7 4.0 %shard_map.37.refs_8_ = f32[2,2,256,256]{3,2,1,0:T(8,128)} custom-call(s32[4,12]{1,0:T(4,128)S(1)} %copy-done.1, bf16[1,2,256,768]{3,2,1,0:T(8,128)(2,1)S(1)} %slice.12.refs_0_, bf16[1,2,256,768]{3,2,1,0:T(8,128)(2,1)S(1)} %collective-permute-done.9.refs_1_, bf16[1,2,256,768]{3,2,1,0:T(8,128)(2,1)} %collective-permute-done.6.refs_2_, ...), custom_call_target="tpu_custom_call" | custom-call | flops 2576980480 | bytes 5242880 | tf_op jit(solution)/shard_map/pallas_call | solution.py:120
  47.7 0.0 collective-permute-done.4.refs_1_
  47.7 0.0 collective-permute-done.5.refs_3_
  47.7 3.7 %shard_map.38 = f32[2,2,256,256]{3,2,1,0:T(8,128)} custom-call(s32[4,12]{1,0:T(4,128)S(1)} %copy-done.1, bf16[1,2,256,768]{3,2,1,0:T(8,128)(2,1)S(1)} %slice.13.refs_0_, bf16[1,2,256,768]{3,2,1,0:T(8,128)(2,1)S(1)} %collective-permute-done.4.refs_1_, bf16[1,2,256,768]{3,2,1,0:T(8,128)(2,1)S(1)} %collective-permute-done.refs_2_, ...), custom_call_target="tpu_custom_call", output_to_operand_aliasing={{}: (9, {})} | custom-call | flops 1610612736 | bytes 5242880 | tf_op jit(solution)/shard_map/pallas_call | solution.py:120
Async XLA Ops:
  0.0 4.3 %copy-start = (bf16[2,2,256,256]{3,2,1,0:T(8,128)(2,1)S(1)}, bf16[2,2,256,256]{3,2,1,0:T(8,128)(2,1)}, u32[]{:S(2)}) copy-start(bf16[2,2,256,256]{3,2,1,0:T(8,128)(2,1)} %refs_4_.1) | copy-start | bytes 1572868
  0.0 8.8 %copy-start.2 = (bf16[2,2,256,768]{3,2,1,0:T(8,128)(2,1)S(1)}, bf16[2,2,256,768]{3,2,1,0:T(8,128)(2,1)}, u32[]{:S(2)}) copy-start(bf16[2,2,256,768]{3,2,1,0:T(8,128)(2,1)} %param.3) | copy-start | bytes 4718596
  1.3 36.9 %collective-permute-start.6 = (bf16[1,2,256,768]{3,2,1,0:T(8,128)(2,1)S(1)}, bf16[1,2,256,768]{3,2,1,0:T(8,128)(2,1)}, u32[]{:S(2)}, u32[]{:S(2)}) collective-permute-start(bf16[1,2,256,768]{3,2,1,0:T(8,128)(2,1)S(1)} %slice.12.refs_0_), channel_id=1, source_target_pairs={{0,2},{1,3},{2,0},{3,1},{4,6},{5,7},{6,4},{7,5},{8,10},{9,11},{10,... | collective-permute-start | bytes 2359304 | tf_op jit(solution)/shard_map/ppermute | solution.py:23
  5.2 38.6 %copy-start.1 = (s32[4,12]{1,0:T(4,128)S(1)}, s32[4,12]{1,0:T(4,128)}, u32[]{:S(2)}) copy-start(s32[4,12]{1,0:T(4,128)} %aperture_ref.3) | copy-start | bytes 580
  5.2 11.4 %collective-permute-start.7 = (bf16[1,2,256,256]{3,2,1,0:T(8,128)(2,1)}, bf16[1,2,256,256]{3,2,1,0:T(8,128)(2,1)S(1)}, u32[]{:S(2)}, u32[]{:S(2)}) collective-permute-start(bf16[1,2,256,256]{3,2,1,0:T(8,128)(2,1)} %get-tuple-element.18), channel_id=1, source_target_pairs={{0,12},{4,8},{8,4},{12,0},{1,13},{5,9},{9,5},{13,1},{2,14},{6,10},... | collective-permute-start | bytes 786440 | tf_op jit(solution)/shard_map/ppermute | solution.py:36
  8.8 34.4 %collective-permute-start = (bf16[1,2,256,768]{3,2,1,0:T(8,128)(2,1)S(1)}, bf16[1,2,256,768]{3,2,1,0:T(8,128)(2,1)S(1)}, u32[]{:S(2)}, u32[]{:S(2)}) collective-permute-start(bf16[1,2,256,768]{3,2,1,0:T(8,128)(2,1)S(1)} %slice.13.refs_0_), channel_id=1, source_target_pairs={{0,2},{1,3},{2,0},{3,1},{4,6},{5,7},{6,4},{7,5},{8,10},{9,11},{10,... | collective-permute-start | bytes 2359304 | tf_op jit(solution)/shard_map/ppermute | solution.py:23
  9.4 19.1 %collective-permute-start.2 = (bf16[1,2,256,256]{3,2,1,0:T(8,128)(2,1)}, bf16[1,2,256,256]{3,2,1,0:T(8,128)(2,1)S(1)}, u32[]{:S(2)}, u32[]{:S(2)}) collective-permute-start(bf16[1,2,256,256]{3,2,1,0:T(8,128)(2,1)} %get-tuple-element.15), channel_id=1, source_target_pairs={{0,12},{4,8},{8,4},{12,0},{1,13},{5,9},{9,5},{13,1},{2,14},{6,10},... | collective-permute-start | bytes 786440 | tf_op jit(solution)/shard_map/ppermute | solution.py:36
  9.5 28.8 %collective-permute-start.1 = (bf16[2,2,256,256]{3,2,1,0:T(8,128)(2,1)S(1)}, bf16[2,2,256,256]{3,2,1,0:T(8,128)(2,1)}, u32[]{:S(2)}, u32[]{:S(2)}) collective-permute-start(bf16[2,2,256,256]{3,2,1,0:T(8,128)(2,1)S(1)} %copy-done), channel_id=1, source_target_pairs={{0,4},{4,0},{8,12},{12,8},{1,5},{5,1},{9,13},{13,9},{2,6},{6,2},{1... | collective-permute-start | bytes 1572872 | tf_op jit(solution)/shard_map/ppermute | solution.py:33
  17.6 20.7 %collective-permute-start.8 = (bf16[1,2,256,256]{3,2,1,0:T(8,128)(2,1)S(1)}, bf16[1,2,256,256]{3,2,1,0:T(8,128)(2,1)S(1)}, u32[]{:S(2)}, u32[]{:S(2)}) collective-permute-start(bf16[1,2,256,256]{3,2,1,0:T(8,128)(2,1)S(1)} %broadcast_select_fusion), channel_id=1, source_target_pairs={{0,8},{8,12},{12,4},{4,0},{1,9},{9,13},{13,5},{5,1},{2,10},{10,14}... | collective-permute-start | bytes 786440 | tf_op jit(solution)/shard_map/ppermute | solution.py:38
  29.5 13.7 %collective-permute-start.3 = (bf16[1,2,256,256]{3,2,1,0:T(8,128)(2,1)S(1)}, bf16[1,2,256,256]{3,2,1,0:T(8,128)(2,1)S(1)}, u32[]{:S(2)}, u32[]{:S(2)}) collective-permute-start(bf16[1,2,256,256]{3,2,1,0:T(8,128)(2,1)S(1)} %broadcast_select_fusion.1), channel_id=1, source_target_pairs={{0,8},{8,12},{12,4},{4,0},{1,9},{9,13},{13,5},{5,1},{2,10},{10,14}... | collective-permute-start | bytes 786440 | tf_op jit(solution)/shard_map/ppermute | solution.py:38
  38.3 5.5 %collective-permute-start.10 = (bf16[1,2,256,768]{3,2,1,0:T(8,128)(2,1)}, bf16[1,2,256,768]{3,2,1,0:T(8,128)(2,1)S(1)}, u32[]{:S(2)}, u32[]{:S(2)}) collective-permute-start(bf16[1,2,256,768]{3,2,1,0:T(8,128)(2,1)} %collective-permute-done.6.refs_2_), channel_id=1, source_target_pairs={{0,1},{1,0},{2,3},{3,2},{4,5},{5,4},{6,7},{7,6},{8,9},{9,8},{10,11... | collective-permute-start | bytes 2359304 | tf_op jit(solution)/shard_map/ppermute | solution.py:23
  38.3 5.5 %collective-permute-start.9 = (bf16[1,2,256,768]{3,2,1,0:T(8,128)(2,1)S(1)}, bf16[1,2,256,768]{3,2,1,0:T(8,128)(2,1)S(1)}, u32[]{:S(2)}, u32[]{:S(2)}) collective-permute-start(bf16[1,2,256,768]{3,2,1,0:T(8,128)(2,1)S(1)} %slice.12.refs_0_), channel_id=1, source_target_pairs={{0,1},{1,0},{2,3},{3,2},{4,5},{5,4},{6,7},{7,6},{8,9},{9,8},{10,11... | collective-permute-start | bytes 2359304 | tf_op jit(solution)/shard_map/ppermute | solution.py:23
  43.2 4.5 %collective-permute-start.4 = (bf16[1,2,256,768]{3,2,1,0:T(8,128)(2,1)S(1)}, bf16[1,2,256,768]{3,2,1,0:T(8,128)(2,1)S(1)}, u32[]{:S(2)}, u32[]{:S(2)}) collective-permute-start(bf16[1,2,256,768]{3,2,1,0:T(8,128)(2,1)S(1)} %slice.13.refs_0_), channel_id=1, source_target_pairs={{0,1},{1,0},{2,3},{3,2},{4,5},{5,4},{6,7},{7,6},{8,9},{9,8},{10,11... | collective-permute-start | bytes 2359304 | tf_op jit(solution)/shard_map/ppermute | solution.py:23
  43.2 4.5 %collective-permute-start.5 = (bf16[1,2,256,768]{3,2,1,0:T(8,128)(2,1)S(1)}, bf16[1,2,256,768]{3,2,1,0:T(8,128)(2,1)S(1)}, u32[]{:S(2)}, u32[]{:S(2)}) collective-permute-start(bf16[1,2,256,768]{3,2,1,0:T(8,128)(2,1)S(1)} %collective-permute-done.refs_2_), channel_id=1, source_target_pairs={{0,1},{1,0},{2,3},{3,2},{4,5},{5,4},{6,7},{7,6},{8,9},{9,8},{10,11... | collective-permute-start | bytes 2359304 | tf_op jit(solution)/shard_map/ppermute | solution.py:23

commit v7 on v0

v7 whole, which is shorter than its diff:
```python
import functools

import jax
import jax.numpy as jnp
from jax import lax
from jax.experimental import pallas as pl
from jax.experimental.pallas import tpu as pltpu
from jax.sharding import PartitionSpec as P

BLK = 256
APER = 12
HW = 6
LANES = 128


def after(value, *earlier):
    return lax.optimization_barrier((value, *earlier))[0]


def from_behind(x, axis, by):
    peers = lax.axis_size(axis)
    pairs = [(i, i + by) for i in range(peers) if 0 <= i + by < peers]
    return lax.ppermute(x, axis, pairs)


def swap(x, axis, bit):
    peers = lax.axis_size(axis)
    return lax.ppermute(x, axis, [(i, i ^ bit) for i in range(peers)])


def at_end():
    return (lax.axis_index("src") + 1) % lax.axis_size("src") < 2


def line_window(data):
    middle = lax.ppermute(data, "src", [(1, 2), (2, 1)])
    near = lax.ppermute(data, "src", [(0, 1), (1, 0), (2, 3), (3, 2)])
    ends = lax.ppermute(data, "src", [(0, 3), (3, 0)])
    onward = jnp.where(at_end(), data, middle)
    windows = []
    for v in range(data.shape[0]):
        onward = onward if v == 0 else after(onward, near)
        across = lax.ppermute(onward[v : v + 1], "src", [(0, 2), (2, 3), (3, 1), (1, 0)])
        windows.append([(data, v), (near, v), (middle, v), (ends, v), (across, 0)])
    return windows


def hop_window(data):
    reach = min(HW, lax.axis_size("src") - 1)
    window = {0: data}
    for hop in range(1, reach + 1):
        window[-hop] = from_behind(window[1 - hop], "src", 1)
        window[hop] = from_behind(window[hop - 1], "src", -1)
    return [[(window[distance], v) for distance in range(-reach, reach + 1)] for v in range(data.shape[0])]


def gather_panels(primaries):
    bit = lax.axis_size("rcv") // 2
    panels = {0: primaries, bit: swap(primaries, "rcv", bit)}
    for lower in range(1, bit):
        for half in (0, bit):
            panels[half ^ lower] = swap(panels[half ^ (lower & (lower - 1))], "rcv", lower & -lower)
    return [panels[m] for m in range(2 * bit)]


def fill_window(window, refs, piece_at):
    pieces = [ref.at[v] for ref, v in zip(refs, piece_at)]
    line = lax.axis_size("src") == 4
    for h in range(window.shape[0]):
        lanes = pl.ds(h * LANES, LANES)
        for part in range(2):
            blocks = [piece[part, :, lanes] for piece in pieces]
            if line:
                own, near, middle, ends, across = blocks
                blocks = [own, near, across, jnp.where(at_end(), ends, middle)]
            for k, block in enumerate(blocks):
                window[h, k, :, pl.ds(part * LANES, LANES)] = block


def product(window, h, aperture_ref, panels):
    src = lax.axis_index("src")
    me = lax.axis_index("rcv")
    blocks = []
    for m, panel in panels:
        shard = lax.bitwise_xor(me, m)
        per_shard = panel.shape[-1] // BLK
        for q in range(per_shard):
            wanted = aperture_ref[src, shard * per_shard + q]
            k = lax.bitwise_xor(src, wanted) if lax.axis_size("src") == 4 else wanted - src + window.shape[1] // 2
            blocks.append(window[h, k])
    values = jnp.concatenate([panel[...].reshape(2 * BLK, panel.shape[-1]) for _, panel in panels], axis=1)
    both = jnp.dot(values, jnp.concatenate(blocks, axis=0), preferred_element_type=jnp.float32)
    return both[:BLK, :LANES] - both[BLK:, LANES:], both[:BLK, LANES:] + both[BLK:, :LANES]


def first_kernel(split, piece_at, aperture_ref, *refs):
    panel_refs = refs[:split]
    window, partial = refs[-2:]
    fill_window(window, refs[split:-2], piece_at)

    @pl.loop(0, window.shape[0])
    def _(h):
        partial[h, 0], partial[h, 1] = product(
            window, h, aperture_ref, [(m, ref.at[0]) for m, ref in enumerate(panel_refs)]
        )


def last_kernel(split, piece_at, aperture_ref, first_window, partial, *refs):
    panel_count = len(refs) - len(piece_at) - 4
    panel_refs = refs[:panel_count]
    out_ref, window, result, sems = refs[-4:]
    fill_window(window, refs[panel_count:-4], piece_at)
    halves = window.shape[0]

    def copies(h):
        return [
            pltpu.make_async_copy(
                result.at[h, v, part], out_ref.at[v, part, :, pl.ds(h * LANES, LANES)], sems.at[h, v, part]
            )
            for v in range(2)
            for part in range(2)
        ]

    @pl.loop(0, halves)
    def _(h):
        panels = [(m, ref.at[0]) for m, ref in enumerate(panel_refs)]
        real, imag = product(window=first_window, h=h, aperture_ref=aperture_ref, panels=panels[split:])
        result[h, 0, 0] = partial[h, 0] + real
        result[h, 0, 1] = partial[h, 1] + imag
        panels = [(m, ref.at[1]) for m, ref in enumerate(panel_refs)]
        result[h, 1, 0], result[h, 1, 1] = product(window, h, aperture_ref, panels)
        for copy in copies(h):
            copy.start()

    for h in range(halves):
        for copy in copies(h):
            copy.wait()


def spec(space):
    return pl.BlockSpec(memory_space=space)


def cost(share):
    return pl.CostEstimate(flops=int(share * (8 * BLK * BLK * APER * BLK)), bytes_accessed=1 << 20, transcendentals=0)


def held(piece, token):
    return pl.pallas_call(
        lambda piece_ref, token_ref, out_ref: None,
        out_shape=jax.ShapeDtypeStruct(piece.shape, piece.dtype),
        in_specs=[spec(pl.ANY)] * 2,
        out_specs=spec(pl.ANY),
        input_output_aliases={0: 0},
        cost_estimate=cost(12),
    )(piece, token)


def body(primaries, data, aperture):
    width = data.shape[3]
    halves = width // LANES
    first, last = (line_window if lax.axis_size("src") == 4 else hop_window)(data)
    panels = gather_panels(primaries)
    depth = 4 if lax.axis_size("src") == 4 else len(first)
    split = len(panels) - 1
    window_shape = (halves, depth, BLK, 2 * LANES)
    params = pltpu.CompilerParams(vmem_limit_bytes=24 * 1024 * 1024)

    pieces, piece_at = zip(*first)
    window, partial = pl.pallas_call(
        functools.partial(first_kernel, split, piece_at),
        out_shape=[
            jax.ShapeDtypeStruct(window_shape, jnp.bfloat16),
            jax.ShapeDtypeStruct((halves, 2, BLK, LANES), jnp.float32),
        ],
        in_specs=[spec(pltpu.SMEM)] + [spec(pltpu.VMEM)] * (split + len(pieces)),
        out_specs=[spec(pltpu.VMEM)] * 2,
        compiler_params=params,
        cost_estimate=cost(0.3),
    )(aperture, *panels[:split], *pieces)

    pieces, piece_at = zip(*last)
    pieces = [*pieces[:-1], held(pieces[-1], partial)]
    return pl.pallas_call(
        functools.partial(last_kernel, split, piece_at),
        out_shape=jax.ShapeDtypeStruct((2, 2, BLK, width), jnp.float32),
        in_specs=[spec(pltpu.SMEM)] + [spec(pltpu.VMEM)] * (2 + len(panels) + len(pieces)),
        out_specs=spec(pl.ANY),
        scratch_shapes=[
            pltpu.VMEM(window_shape, jnp.bfloat16),
            pltpu.VMEM((halves, 2, 2, BLK, LANES), jnp.float32),
            pltpu.SemaphoreType.DMA((halves, 2, 2)),
        ],
        compiler_params=params,
        cost_estimate=cost(1.25),
    )(aperture, window, partial, *panels, *pieces)


def solution(mesh):
    placed = (P("freq", None, "src", "rcv"), P("freq", None, "src", "rcv"), P())
    return jax.shard_map(
        body, mesh=mesh, in_specs=placed, out_specs=P("freq", None, "src", "rcv"), check_vma=False
    )
```

time: 120 us -> 55.3 us (0.46)
  local copies, waits for them, and re-layouts: 40.1 us -> 6.82 us
  between operations: 21.1 us -> 0.1 us
  waiting for transfers between devices: 29.7 us -> 15.4 us
  matrix products: 12.7 us -> 0 us
  Pallas kernels: 0 us -> 9.39 us
  starting transfers between devices: 14.7 us -> 22.1 us
    unnamed x27 -> x20, local copies, waits for them, and re-layouts: 35.2 us -> 6.78 us
    ppermute x6 -> x8, waiting for transfers between devices: 29.7 us -> 15.4 us  [the longest x3 14.3 us: swap(): return lax.ppermute(x, axis, [(i, i ^ bit) for i in range(peers)])]
    dot_general x4 -> x0, matrix products: 12.7 us -> none  [the longest x1 3.99 us: body(): jnp.einsum('sxc,scr->sxr', panel_piece[:, 0], selected[:, 0], preferred_e...]
    pallas_call x0 -> x3, Pallas kernels: none -> 9.39 us  [the longest x1 5.78 us: body(): pl.pallas_call(functools.partial(last_kernel, split, piece_at), out_shape...]
    ppermute x6 -> x8, starting transfers between devices: 14.7 us -> 22.1 us  [the longest x2 10.8 us: line_window(): lax.ppermute(onward[v:v + 1], 'src', [(0, 2), (2, 3), (3, 1), (1, 0)])]
    concatenate x2 -> x0, local copies, waits for them, and re-layouts: 2.97 us -> none  [the longest x1 1.89 us: body(): selected = jnp.concatenate(picked_list, axis=2)]
    another operation x1 -> x0, local copies, waits for them, and re-layouts: 1.31 us -> none  [body(): return jnp.stack([real_part, imag_part], axis=1)]
  transfers between devices with their start and end apart: 7 -> 8, of which waited for: 3 -> 3; matrix products, arithmetic and copies ran while one was open for 30% -> 2% of each run, Pallas kernels for 0% -> 7%
where the time goes in v7:
time: 55.3 us; the launch traced here: 54.9 us
  starting transfers between devices  22.1 us (40%)
  waiting for transfers between devices  15.4 us (28%)
  Pallas kernels  9.39 us (17%)
  local copies, waits for them, and re-layouts  6.82 us (12%)
  other arithmetic  1.19 us (2%)
    ppermute x3, waiting for transfers between devices, swap(): return lax.ppermute(x, axis, [(i, i ^ bit) for i in range(peers)])  14.3 us
    ppermute x2, starting transfers between devices, line_window(): lax.ppermute(onward[v:v + 1], 'src', [(0, 2), (2, 3), (3, 1), (1, 0)])  10.8 us
    unnamed x20, local copies, waits for them, and re-layouts  6.78 us
    pallas_call x1, Pallas kernels, body(): pl.pallas_call(functools.partial(last_kernel, split, piece_at), out_shape...  5.78 us
    ppermute x1, starting transfers between devices, line_window(): near = lax.ppermute(data, 'src', [(0, 1), (1, 0), (2, 3), (3, 2)])  3.67 us
    pallas_call x1, Pallas kernels, body(): pl.pallas_call(functools.partial(first_kernel, split, piece_at), out_shap...  3.61 us
    ppermute x1, starting transfers between devices, line_window(): ends = lax.ppermute(data, 'src', [(0, 3), (3, 0)])  3.25 us
    ppermute x3, starting transfers between devices, swap(): return lax.ppermute(x, axis, [(i, i ^ bit) for i in range(peers)])  2.94 us
  transfers between devices with their start and end apart: 8, of which 3 were waited for; matrix products, arithmetic and copies ran while one was open for 2% of the time, Pallas kernels for 7%

profile of v7, /device:TPU:0, one launch (start us, length us, event | category | flops | bytes accessed | tf_op | source)
XLA Modules:
  0.0 54.9 jit_solution(17230559723521778189)
XLA Ops:
  0.0 0.0 copy-start
  0.0 0.0 copy-start.9
  0.0 2.9 %collective-permute-start.1 = (bf16[2,2,256,768]{3,2,1,0:T(8,128)(2,1)}, bf16[2,2,256,768]{3,2,1,0:T(8,128)(2,1)S(1)}, u32[]{:S(2)}, u32[]{:S(2)}) collective-permute-start(bf16[2,2,256,768]{3,2,1,0:T(8,128)(2,1)} %refs_0_.3), channel_id=1, source_target_pairs={{0,2},{1,3},{2,0},{3,1},{4,6},{5,7},{6,4},{7,5},{8,10},{9,11},{10,... | collective-permute-start | bytes 4718600 | tf_op jit(solution)/shard_map/ppermute | solution.py:28
  2.9 0.0 collective-permute-start
  2.9 1.5 %collective-permute-start.3 = (bf16[2,2,256,256]{3,2,1,0:T(8,128)(2,1)}, bf16[2,2,256,256]{3,2,1,0:T(8,128)(2,1)}, u32[]{:S(2)}, u32[]{:S(2)}) collective-permute-start(bf16[2,2,256,256]{3,2,1,0:T(8,128)(2,1)} %refs_4_.1), channel_id=1, source_target_pairs={{4,8},{8,4},{5,9},{9,5},{6,10},{10,6},{7,11},{11,7},{20,24},{24,20... | collective-permute-start | bytes 1572872 | tf_op jit(solution)/shard_map/ppermute | solution.py:36
  4.4 3.7 %collective-permute-start.2 = (bf16[2,2,256,256]{3,2,1,0:T(8,128)(2,1)}, bf16[2,2,256,256]{3,2,1,0:T(8,128)(2,1)}, u32[]{:S(2)}, u32[]{:S(2)}) collective-permute-start(bf16[2,2,256,256]{3,2,1,0:T(8,128)(2,1)} %refs_4_.1), channel_id=1, source_target_pairs={{0,4},{4,0},{8,12},{12,8},{1,5},{5,1},{9,13},{13,9},{2,6},{6,2},{1... | collective-permute-start | bytes 1572872 | tf_op jit(solution)/shard_map/ppermute | solution.py:37
  8.1 3.2 %collective-permute-start.4 = (bf16[2,2,256,256]{3,2,1,0:T(8,128)(2,1)}, bf16[2,2,256,256]{3,2,1,0:T(8,128)(2,1)}, u32[]{:S(2)}, u32[]{:S(2)}) collective-permute-start(bf16[2,2,256,256]{3,2,1,0:T(8,128)(2,1)} %refs_4_.1), channel_id=1, source_target_pairs={{0,12},{12,0},{1,13},{13,1},{2,14},{14,2},{3,15},{15,3},{16,28},{2... | collective-permute-start | bytes 1572872 | tf_op jit(solution)/shard_map/ppermute | solution.py:38
  11.3 0.0 copy-start.1
  11.4 0.0 collective-permute-done.3.refs_5_.refs_6_
  11.4 1.2 %broadcast_select_fusion = bf16[2,2,256,256]{3,2,1,0:T(8,128)(2,1)S(1)} fusion(bf16[2,2,256,256]{3,2,1,0:T(8,128)(2,1)} %refs_4_.1, bf16[2,2,256,256]{3,2,1,0:T(8,128)(2,1)} %collective-permute-done.3.refs_5_.refs_6_, pred[]{:T(512)S(6)} %lt.10), kind=kLoop, calls=%fused_computation | loop fusion | flops 262144 | bytes 1572865 | tf_op jit(solution)/shard_map/jit(_where)/select_n | solution.py:39
  12.6 10.7 %collective-permute-start.5 = (bf16[1,2,256,256]{3,2,1,0:T(8,128)(2,1)S(1)}, bf16[1,2,256,256]{3,2,1,0:T(8,128)(2,1)S(1)}, u32[]{:S(2)}, u32[]{:S(2)}) collective-permute-start(bf16[1,2,256,256]{3,2,1,0:T(8,128)(2,1)S(1)} %slice.8), channel_id=1, source_target_pairs={{0,8},{8,12},{12,4},{4,0},{1,9},{9,13},{13,5},{5,1},{2,10},{10,14}... | collective-permute-start | bytes 786440 | tf_op jit(solution)/shard_map/ppermute | solution.py:43
  23.3 0.0 collective-permute-done.2.refs_4_.refs_5_
  23.3 0.1 collective-permute-start.7
  23.4 14.3 %collective-permute-done.1.refs_2_ = bf16[2,2,256,768]{3,2,1,0:T(8,128)(2,1)S(1)} collective-permute-done((bf16[2,2,256,768]{3,2,1,0:T(8,128)(2,1)}, bf16[2,2,256,768]{3,2,1,0:T(8,128)(2,1)S(1)}, u32[]{:S(2)}, u32[]{:S(2)}) %collective-permute-start.1) | collective-permute-done | bytes 1572896 | tf_op jit(solution)/shard_map/ppermute | solution.py:28
  37.6 0.0 collective-permute-start.6
  37.6 0.0 collective-permute-done.4.refs_6_.refs_7_
  37.6 1.0 %collective-permute-done.5.refs_7_ = bf16[1,2,256,256]{3,2,1,0:T(8,128)(2,1)S(1)} collective-permute-done((bf16[1,2,256,256]{3,2,1,0:T(8,128)(2,1)S(1)}, bf16[1,2,256,256]{3,2,1,0:T(8,128)(2,1)S(1)}, u32[]{:S(2)}, u32[]{:S(2)}) %collective-permute-start.5) | collective-permute-done | bytes 262176 | tf_op jit(solution)/shard_map/ppermute | solution.py:43
  38.6 0.0 collective-permute-done.refs_1_
  38.6 0.0 copy-done
  38.6 0.0 copy-done.9
  38.6 0.0 copy-done.1
  38.6 3.6 %shard_map.37 = (bf16[2,4,256,256]{3,2,1,0:T(8,128)(2,1)S(1)}, f32[2,2,256,128]{3,2,1,0:T(8,128)S(1)}) custom-call(s32[4,12]{1,0:T(4,128)S(1)} %copy-done.9, bf16[2,2,256,768]{3,2,1,0:T(8,128)(2,1)S(1)} %copy-done, bf16[2,2,256,768]{3,2,1,0:T(8,128)(2,1)} %collective-permute-done.refs_1_, bf16[2,2,256,768]{3,2,1,0:T(8,128)(2,1)S(1)} %collective-permute-done.1.refs_2_, ...), custom_call_target="tpu_custom_call" | custom-call | flops 483183808 | bytes 1048576 | tf_op jit(solution)/shard_map/pallas_call | solution.py:170
  42.2 0.0 copy-start.3
  42.3 1.0 %copy-done.3 = bf16[2,4,256,256]{3,2,1,0:T(8,128)(2,1)} copy-done((bf16[2,4,256,256]{3,2,1,0:T(8,128)(2,1)}, bf16[2,4,256,256]{3,2,1,0:T(8,128)(2,1)S(1)}, u32[]{:S(2)}) %copy-start.3) | copy-done | bytes 1048600
  43.2 0.0 copy-start.5
  43.2 0.8 %copy-done.5 = f32[2,2,256,128]{3,2,1,0:T(8,128)} copy-done((f32[2,2,256,128]{3,2,1,0:T(8,128)}, f32[2,2,256,128]{3,2,1,0:T(8,128)S(1)}, u32[]{:S(2)}) %copy-start.5) | copy-done | bytes 524312
  44.0 0.1 collective-permute-done.7.piece_ref
  44.1 0.0 copy-start.7
  44.1 0.7 %copy-done.7 = bf16[1,2,256,256]{3,2,1,0:T(8,128)(2,1)} copy-done((bf16[1,2,256,256]{3,2,1,0:T(8,128)(2,1)}, bf16[1,2,256,256]{3,2,1,0:T(8,128)(2,1)S(1)}, u32[]{:S(2)}) %copy-start.7) | copy-done | bytes 262168
  44.9 0.0 collective-permute-done.6.refs_3_
  44.9 0.0 copy-start.2
  44.9 1.0 %copy-done.2 = bf16[2,2,256,256]{3,2,1,0:T(8,128)(2,1)S(1)} copy-done((bf16[2,2,256,256]{3,2,1,0:T(8,128)(2,1)S(1)}, bf16[2,2,256,256]{3,2,1,0:T(8,128)(2,1)}, u32[]{:S(2)}) %copy-start.2) | copy-done | bytes 524312
  45.9 0.0 copy-start.4
  45.9 1.2 %copy-done.4 = bf16[2,4,256,256]{3,2,1,0:T(8,128)(2,1)S(1)} copy-done((bf16[2,4,256,256]{3,2,1,0:T(8,128)(2,1)S(1)}, bf16[2,4,256,256]{3,2,1,0:T(8,128)(2,1)}, u32[]{:S(2)}) %copy-start.4) | copy-done | bytes 1048600
  47.1 0.0 copy-start.6
  47.1 1.0 %copy-done.6 = f32[2,2,256,128]{3,2,1,0:T(8,128)S(1)} copy-done((f32[2,2,256,128]{3,2,1,0:T(8,128)S(1)}, f32[2,2,256,128]{3,2,1,0:T(8,128)}, u32[]{:S(2)}) %copy-start.6) | copy-done | bytes 524312
  48.2 0.0 copy-start.8
  48.2 0.9 %copy-done.8 = bf16[1,2,256,256]{3,2,1,0:T(8,128)(2,1)S(1)} copy-done((bf16[1,2,256,256]{3,2,1,0:T(8,128)(2,1)S(1)}, bf16[1,2,256,256]{3,2,1,0:T(8,128)(2,1)}, u32[]{:S(2)}) %copy-start.8) | copy-done | bytes 262168
  49.1 5.8 %shard_map.39 = f32[2,2,256,256]{3,2,1,0:T(8,128)} custom-call(s32[4,12]{1,0:T(4,128)S(1)} %copy-done.9, bf16[2,4,256,256]{3,2,1,0:T(8,128)(2,1)S(1)} %copy-done.4, f32[2,2,256,128]{3,2,1,0:T(8,128)S(1)} %copy-done.6, bf16[2,2,256,768]{3,2,1,0:T(8,128)(2,1)S(1)} %copy-done, bf16[2,2,256,768]{3,2,1,0:T(8,128)(2,1)} %collective-permute-done.refs_1_, ...), custom_call_target="tpu_custom_call" | custom-call | flops 2013265920 | bytes 1048576 | tf_op jit(solution)/shard_map/pallas_call | solution.py:184
  (3 shorter events, 0.0 us)
Async XLA Ops:
  0.0 38.6 %copy-start = (bf16[2,2,256,768]{3,2,1,0:T(8,128)(2,1)S(1)}, bf16[2,2,256,768]{3,2,1,0:T(8,128)(2,1)}, u32[]{:S(2)}) copy-start(bf16[2,2,256,768]{3,2,1,0:T(8,128)(2,1)} %refs_0_.3) | copy-start | bytes 4718596
  0.0 38.6 %copy-start.9 = (s32[4,12]{1,0:T(4,128)S(1)}, s32[4,12]{1,0:T(4,128)}, u32[]{:S(2)}) copy-start(s32[4,12]{1,0:T(4,128)} %aperture_ref.3) | copy-start | bytes 580
  0.0 37.6 %collective-permute-start.1 = (bf16[2,2,256,768]{3,2,1,0:T(8,128)(2,1)}, bf16[2,2,256,768]{3,2,1,0:T(8,128)(2,1)S(1)}, u32[]{:S(2)}, u32[]{:S(2)}) collective-permute-start(bf16[2,2,256,768]{3,2,1,0:T(8,128)(2,1)} %refs_0_.3), channel_id=1, source_target_pairs={{0,2},{1,3},{2,0},{3,1},{4,6},{5,7},{6,4},{7,5},{8,10},{9,11},{10,... | collective-permute-start | bytes 4718600 | tf_op jit(solution)/shard_map/ppermute | solution.py:28
  2.9 35.7 %collective-permute-start = (bf16[2,2,256,768]{3,2,1,0:T(8,128)(2,1)}, bf16[2,2,256,768]{3,2,1,0:T(8,128)(2,1)}, u32[]{:S(2)}, u32[]{:S(2)}) collective-permute-start(bf16[2,2,256,768]{3,2,1,0:T(8,128)(2,1)} %refs_0_.3), channel_id=1, source_target_pairs={{0,1},{1,0},{2,3},{3,2},{4,5},{5,4},{6,7},{7,6},{8,9},{9,8},{10,11... | collective-permute-start | bytes 4718600 | tf_op jit(solution)/shard_map/ppermute | solution.py:28
  2.9 8.4 %collective-permute-start.3 = (bf16[2,2,256,256]{3,2,1,0:T(8,128)(2,1)}, bf16[2,2,256,256]{3,2,1,0:T(8,128)(2,1)}, u32[]{:S(2)}, u32[]{:S(2)}) collective-permute-start(bf16[2,2,256,256]{3,2,1,0:T(8,128)(2,1)} %refs_4_.1), channel_id=1, source_target_pairs={{4,8},{8,4},{5,9},{9,5},{6,10},{10,6},{7,11},{11,7},{20,24},{24,20... | collective-permute-start | bytes 1572872 | tf_op jit(solution)/shard_map/ppermute | solution.py:36
  4.4 18.9 %collective-permute-start.2 = (bf16[2,2,256,256]{3,2,1,0:T(8,128)(2,1)}, bf16[2,2,256,256]{3,2,1,0:T(8,128)(2,1)}, u32[]{:S(2)}, u32[]{:S(2)}) collective-permute-start(bf16[2,2,256,256]{3,2,1,0:T(8,128)(2,1)} %refs_4_.1), channel_id=1, source_target_pairs={{0,4},{4,0},{8,12},{12,8},{1,5},{5,1},{9,13},{13,9},{2,6},{6,2},{1... | collective-permute-start | bytes 1572872 | tf_op jit(solution)/shard_map/ppermute | solution.py:37
  8.1 29.5 %collective-permute-start.4 = (bf16[2,2,256,256]{3,2,1,0:T(8,128)(2,1)}, bf16[2,2,256,256]{3,2,1,0:T(8,128)(2,1)}, u32[]{:S(2)}, u32[]{:S(2)}) collective-permute-start(bf16[2,2,256,256]{3,2,1,0:T(8,128)(2,1)} %refs_4_.1), channel_id=1, source_target_pairs={{0,12},{12,0},{1,13},{13,1},{2,14},{14,2},{3,15},{15,3},{16,28},{2... | collective-permute-start | bytes 1572872 | tf_op jit(solution)/shard_map/ppermute | solution.py:38
  11.3 27.3 %copy-start.1 = (bf16[2,2,256,256]{3,2,1,0:T(8,128)(2,1)S(1)}, bf16[2,2,256,256]{3,2,1,0:T(8,128)(2,1)}, u32[]{:S(2)}) copy-start(bf16[2,2,256,256]{3,2,1,0:T(8,128)(2,1)} %refs_4_.1) | copy-start | bytes 1572868
  12.6 26.0 %collective-permute-start.5 = (bf16[1,2,256,256]{3,2,1,0:T(8,128)(2,1)S(1)}, bf16[1,2,256,256]{3,2,1,0:T(8,128)(2,1)S(1)}, u32[]{:S(2)}, u32[]{:S(2)}) collective-permute-start(bf16[1,2,256,256]{3,2,1,0:T(8,128)(2,1)S(1)} %slice.8), channel_id=1, source_target_pairs={{0,8},{8,12},{12,4},{4,0},{1,9},{9,13},{13,5},{5,1},{2,10},{10,14}... | collective-permute-start | bytes 786440 | tf_op jit(solution)/shard_map/ppermute | solution.py:43
  23.3 20.9 %collective-permute-start.7 = (bf16[1,2,256,256]{3,2,1,0:T(8,128)(2,1)S(1)}, bf16[1,2,256,256]{3,2,1,0:T(8,128)(2,1)S(1)}, u32[]{:S(2)}, u32[]{:S(2)}) collective-permute-start(bf16[1,2,256,256]{3,2,1,0:T(8,128)(2,1)S(1)} %slice.7), channel_id=1, source_target_pairs={{0,8},{8,12},{12,4},{4,0},{1,9},{9,13},{13,5},{5,1},{2,10},{10,14}... | collective-permute-start | bytes 786440 | tf_op jit(solution)/shard_map/ppermute | solution.py:43
  37.6 7.3 %collective-permute-start.6 = (bf16[2,2,256,768]{3,2,1,0:T(8,128)(2,1)S(1)}, bf16[2,2,256,768]{3,2,1,0:T(8,128)(2,1)}, u32[]{:S(2)}, u32[]{:S(2)}) collective-permute-start(bf16[2,2,256,768]{3,2,1,0:T(8,128)(2,1)S(1)} %collective-permute-done.1.refs_2_), channel_id=1, source_target_pairs={{0,1},{1,0},{2,3},{3,2},{4,5},{5,4},{6,7},{7,6},{8,9},{9,8},{10,11... | collective-permute-start | bytes 4718600 | tf_op jit(solution)/shard_map/ppermute | solution.py:28
  42.2 1.0 %copy-start.3 = (bf16[2,4,256,256]{3,2,1,0:T(8,128)(2,1)}, bf16[2,4,256,256]{3,2,1,0:T(8,128)(2,1)S(1)}, u32[]{:S(2)}) copy-start(bf16[2,4,256,256]{3,2,1,0:T(8,128)(2,1)S(1)} %get-tuple-element.8.first_window) | copy-start | bytes 3145732
  43.2 0.8 %copy-start.5 = (f32[2,2,256,128]{3,2,1,0:T(8,128)}, f32[2,2,256,128]{3,2,1,0:T(8,128)S(1)}, u32[]{:S(2)}) copy-start(f32[2,2,256,128]{3,2,1,0:T(8,128)S(1)} %get-tuple-element.9.token_ref.partial) | copy-start | bytes 1572868
  44.1 0.7 %copy-start.7 = (bf16[1,2,256,256]{3,2,1,0:T(8,128)(2,1)}, bf16[1,2,256,256]{3,2,1,0:T(8,128)(2,1)S(1)}, u32[]{:S(2)}) copy-start(bf16[1,2,256,256]{3,2,1,0:T(8,128)(2,1)S(1)} %collective-permute-done.7.piece_ref) | copy-start | bytes 786436
  44.9 1.0 %copy-start.2 = (bf16[2,2,256,256]{3,2,1,0:T(8,128)(2,1)S(1)}, bf16[2,2,256,256]{3,2,1,0:T(8,128)(2,1)}, u32[]{:S(2)}) copy-start(bf16[2,2,256,256]{3,2,1,0:T(8,128)(2,1)} %refs_4_.1) | copy-start | bytes 1572868
  45.9 1.2 %copy-start.4 = (bf16[2,4,256,256]{3,2,1,0:T(8,128)(2,1)S(1)}, bf16[2,4,256,256]{3,2,1,0:T(8,128)(2,1)}, u32[]{:S(2)}) copy-start(bf16[2,4,256,256]{3,2,1,0:T(8,128)(2,1)} %copy-done.3) | copy-start | bytes 3145732
  47.1 1.0 %copy-start.6 = (f32[2,2,256,128]{3,2,1,0:T(8,128)S(1)}, f32[2,2,256,128]{3,2,1,0:T(8,128)}, u32[]{:S(2)}) copy-start(f32[2,2,256,128]{3,2,1,0:T(8,128)} %copy-done.5) | copy-start | bytes 1572868
  48.2 0.9 %copy-start.8 = (bf16[1,2,256,256]{3,2,1,0:T(8,128)(2,1)S(1)}, bf16[1,2,256,256]{3,2,1,0:T(8,128)(2,1)}, u32[]{:S(2)}) copy-start(bf16[1,2,256,256]{3,2,1,0:T(8,128)(2,1)} %shard_map.38.refs_8_) | copy-start | bytes 786436

commit v8 on v7

v8 whole, which is shorter than its diff:
```python
import functools

import jax
import jax.numpy as jnp
from jax import lax
from jax.experimental import pallas as pl
from jax.experimental.pallas import tpu as pltpu
from jax.sharding import PartitionSpec as P

BLK = 256
APER = 12
HW = 6


def after(value, *earlier):
    return lax.optimization_barrier((value, *earlier))[0]


def from_behind(x, axis, by):
    peers = lax.axis_size(axis)
    pairs = [(i, i + by) for i in range(peers) if 0 <= i + by < peers]
    return lax.ppermute(x, axis, pairs)


def swap(x, axis, bit):
    peers = lax.axis_size(axis)
    return lax.ppermute(x, axis, [(i, i ^ bit) for i in range(peers)])


def at_end():
    return (lax.axis_index("src") + 1) % lax.axis_size("src") < 2


def line_window(data):
    near = lax.ppermute(data, "src", [(0, 1), (1, 0), (2, 3), (3, 2)])
    windows = []
    for v, own in enumerate(lax.optimization_barrier([data[v : v + 1] for v in range(data.shape[0])])):
        far = lax.ppermute(own, "src", [(0, 3), (1, 2), (2, 1), (3, 0)])
        onward = jnp.where(at_end(), own, far if v == 0 else after(far, near))
        across = lax.ppermute(onward, "src", [(0, 2), (2, 3), (3, 1), (1, 0)])
        windows.append([(data, v), (near, v), (across, 0), (far, 0)])
    return windows


def hop_window(data):
    reach = min(HW, lax.axis_size("src") - 1)
    window = {0: data}
    for hop in range(1, reach + 1):
        window[-hop] = from_behind(window[1 - hop], "src", 1)
        window[hop] = from_behind(window[hop - 1], "src", -1)
    return [[(window[distance], v) for distance in range(-reach, reach + 1)] for v in range(data.shape[0])]


def gather_panels(primaries):
    bit = lax.axis_size("rcv") // 2
    panels = {0: primaries, bit: swap(primaries, "rcv", bit)}
    for lower in range(1, bit):
        for half in (0, bit):
            panels[half ^ lower] = swap(panels[half ^ (lower & (lower - 1))], "rcv", lower & -lower)
    return [panels[m] for m in range(2 * bit)]


def fill_window(window, pieces):
    width = window.shape[-1] // 2
    for k, piece in pieces.items():
        window[k, :, :width] = piece[0]
        window[k, :, width:] = piece[1]


def product(window, aperture_ref, panels):
    src = lax.axis_index("src")
    me = lax.axis_index("rcv")
    width = window.shape[-1] // 2
    blocks = []
    for m, panel in panels.items():
        shard = lax.bitwise_xor(me, m)
        per_shard = panel.shape[-1] // BLK
        for q in range(per_shard):
            wanted = aperture_ref[src, shard * per_shard + q]
            blocks.append(window[lax.bitwise_xor(src, wanted) if lax.axis_size("src") == 4 else wanted - src + window.shape[0] // 2])
    values = jnp.concatenate([panel[...].reshape(2 * BLK, panel.shape[-1]) for panel in panels.values()], axis=1)
    both = jnp.dot(values, jnp.concatenate(blocks, axis=0), preferred_element_type=jnp.float32)
    return both[:BLK, :width] - both[BLK:, width:], both[:BLK, width:] + both[BLK:, :width]


def first_kernel(split, first_at, last_at, aperture_ref, *refs):
    panel_refs = refs[:split]
    first_refs = refs[split : split + len(first_at)]
    last_refs = refs[split + len(first_at) : -3]
    first_window, last_window, partial = refs[-3:]
    fill_window(first_window, {k: ref.at[v] for k, (ref, v) in enumerate(zip(first_refs, first_at))})
    fill_window(last_window, {k: ref.at[v] for ref, (k, v) in zip(last_refs, last_at.items())})
    partial[0], partial[1] = product(first_window, aperture_ref, {m: ref.at[0] for m, ref in enumerate(panel_refs)})


def last_kernel(split, late, aperture_ref, partial, first_window, _, late_ref, *refs):
    panel_refs = refs[:-4]
    out_ref, window, result, sems = refs[-4:]

    def finish(v, real, imag):
        result[v, 0] = real
        result[v, 1] = imag
        copies = [pltpu.make_async_copy(result.at[v, part], out_ref.at[v, part], sems.at[v, part]) for part in range(2)]
        for copy in copies:
            copy.start()
        return copies

    real, imag = product(first_window, aperture_ref, {m: ref.at[0] for m, ref in enumerate(panel_refs) if m >= split})
    copies = finish(0, partial[0] + real, partial[1] + imag)
    fill_window(window, {late: late_ref.at[0]})
    copies += finish(1, *product(window, aperture_ref, {m: ref.at[1] for m, ref in enumerate(panel_refs)}))
    for copy in copies:
        copy.wait()


def spec(space):
    return pl.BlockSpec(memory_space=space)


def cost(share):
    return pl.CostEstimate(flops=int(share * (8 * BLK * BLK * APER * BLK)), bytes_accessed=1 << 20, transcendentals=0)


def limit(megabytes):
    return pltpu.CompilerParams(vmem_limit_bytes=megabytes << 20)


def held(piece, token):
    return pl.pallas_call(
        lambda piece_ref, token_ref, out_ref: None,
        out_shape=jax.ShapeDtypeStruct(piece.shape, piece.dtype),
        in_specs=[spec(pl.ANY)] * 2,
        out_specs=spec(pl.ANY),
        input_output_aliases={0: 0},
        compiler_params=limit(1),
        cost_estimate=cost(12),
    )(piece, token)


def body(primaries, data, aperture):
    width = data.shape[3]
    line = lax.axis_size("src") == 4
    first, last = (line_window if line else hop_window)(data)
    panels = gather_panels(primaries)
    split = len(panels) - 1
    late = 2 if line else len(last) - 1
    late_piece, late_at = last[late]
    late_piece = late_piece[late_at : late_at + 1]
    window_shape = (len(first), BLK, 2 * width)
    early = {k: piece for k, piece in enumerate(last) if k != late}

    first_window, window, partial = pl.pallas_call(
        functools.partial(first_kernel, split, [v for _, v in first], {k: v for k, (_, v) in early.items()}),
        out_shape=[jax.ShapeDtypeStruct(window_shape, jnp.bfloat16)] * 2
        + [jax.ShapeDtypeStruct((2, BLK, width), jnp.float32)],
        in_specs=[spec(pltpu.SMEM)] + [spec(pltpu.VMEM)] * (split + len(first) + len(early)),
        out_specs=[spec(pltpu.VMEM)] * 3,
        compiler_params=limit(16),
        cost_estimate=cost(0.3),
    )(aperture, *panels[:split], *[piece for piece, _ in first], *[piece for piece, _ in early.values()])

    return pl.pallas_call(
        functools.partial(last_kernel, split, late),
        out_shape=[
            jax.ShapeDtypeStruct((2, 2, BLK, width), jnp.float32),
            jax.ShapeDtypeStruct(window_shape, jnp.bfloat16),
        ],
        in_specs=[spec(pltpu.SMEM)] + [spec(pltpu.VMEM)] * (4 + len(panels)),
        out_specs=[spec(pl.ANY), spec(pltpu.VMEM)],
        scratch_shapes=[pltpu.VMEM((2, 2, BLK, width), jnp.float32), pltpu.SemaphoreType.DMA((2, 2))],
        input_output_aliases={3: 1},
        compiler_params=limit(16),
        cost_estimate=cost(1.25),
    )(aperture, partial, first_window, window, held(late_piece, partial), *panels)[0]


def solution(mesh):
    placed = (P("freq", None, "src", "rcv"), P("freq", None, "src", "rcv"), P())
    return jax.shard_map(
        body, mesh=mesh, in_specs=placed, out_specs=P("freq", None, "src", "rcv"), check_vma=False
    )
```

time: 55.3 us -> 51.1 us (0.924)
  waiting for transfers between devices: 15.4 us -> 22 us
  local copies, waits for them, and re-layouts: 6.82 us -> 1.85 us
  starting transfers between devices: 22.1 us -> 17.2 us
  Pallas kernels: 9.39 us -> 7.73 us
  other arithmetic: 1.19 us -> 1.96 us
    ppermute x4, waiting for transfers between devices: 1.09 us -> 22 us  [the longest x2 20.1 us: line_window(): far = lax.ppermute(own, 'src', [(0, 3), (1, 2), (2, 1), (3, 0)])]
    ppermute x3, waiting for transfers between devices: 14.3 us -> 0.01 us  [swap(): return lax.ppermute(x, axis, [(i, i ^ bit) for i in range(peers)])]
    unnamed x20 -> x6, local copies, waits for them, and re-layouts: 6.78 us -> 0.01 us
    ppermute x4, starting transfers between devices: 15.5 us -> 12.7 us  [the longest x2 8.9 us: line_window(): across = lax.ppermute(onward, 'src', [(0, 2), (2, 3), (3, 1), (1, 0)])]
    ppermute x1, starting transfers between devices: 3.67 us -> 1.58 us  [line_window(): near = lax.ppermute(data, 'src', [(0, 1), (1, 0), (2, 3), (3, 2)])]
    slice x2 -> x1, local copies, waits for them, and re-layouts: 0.04 us -> 1.84 us  [line_window(): data[v:v + 1]]
    pallas_call x2, Pallas kernels: 9.39 us -> 7.73 us  [the longest x1 4.47 us: body(): pl.pallas_call(functools.partial(last_kernel, split, late), out_shape=[ja...]
    select_n x1 -> x2, other arithmetic: 1.19 us -> 1.96 us  [line_window(): onward = jnp.where(at_end(), own, far if v == 0 else after(far, near))]
  transfers between devices with their start and end apart: 8 -> 8, of which waited for: 3 -> 3; matrix products, arithmetic and copies ran while one was open for 2% -> 7% of each run, Pallas kernels for 7% -> 6%
where the time goes in v8:
time: 51.1 us; the launch traced here: 50.8 us
  waiting for transfers between devices  22 us (43%)
  starting transfers between devices  17.2 us (34%)
  Pallas kernels  7.73 us (15%)
  other arithmetic  1.96 us (4%)
  local copies, waits for them, and re-layouts  1.85 us (4%)
    ppermute x2, waiting for transfers between devices, line_window(): far = lax.ppermute(own, 'src', [(0, 3), (1, 2), (2, 1), (3, 0)])  20.1 us
    ppermute x2, starting transfers between devices, line_window(): across = lax.ppermute(onward, 'src', [(0, 2), (2, 3), (3, 1), (1, 0)])  8.9 us
    pallas_call x1, Pallas kernels, body(): pl.pallas_call(functools.partial(last_kernel, split, late), out_shape=[ja...  4.47 us
    ppermute x2, starting transfers between devices, line_window(): far = lax.ppermute(own, 'src', [(0, 3), (1, 2), (2, 1), (3, 0)])  3.82 us
    pallas_call x1, Pallas kernels, body(): pl.pallas_call(functools.partial(first_kernel, split, [v for _, v in firs...  3.25 us
    ppermute x3, starting transfers between devices, swap(): return lax.ppermute(x, axis, [(i, i ^ bit) for i in range(peers)])  2.94 us
    select_n x2, other arithmetic, line_window(): onward = jnp.where(at_end(), own, far if v == 0 else after(far, near))  1.96 us
    slice x1, local copies, waits for them, and re-layouts, line_window(): data[v:v + 1]  1.84 us
  transfers between devices with their start and end apart: 8, of which 3 were waited for; matrix products, arithmetic and copies ran while one was open for 7% of the time, Pallas kernels for 6%

profile of v8, /device:TPU:0, one launch (start us, length us, event | category | flops | bytes accessed | tf_op | source)
XLA Modules:
  0.0 50.8 jit_solution(15659960958468587181)
XLA Ops:
  0.0 0.0 copy-start
  0.0 0.0 copy-start.2
  0.0 2.9 %collective-permute-start.1 = (bf16[2,2,256,768]{3,2,1,0:T(8,128)(2,1)}, bf16[2,2,256,768]{3,2,1,0:T(8,128)(2,1)S(1)}, u32[]{:S(2)}, u32[]{:S(2)}) collective-permute-start(bf16[2,2,256,768]{3,2,1,0:T(8,128)(2,1)} %refs_0_.3), channel_id=1, source_target_pairs={{0,2},{1,3},{2,0},{3,1},{4,6},{5,7},{6,4},{7,5},{8,10},{9,11},{10,... | collective-permute-start | bytes 4718600 | tf_op jit(solution)/shard_map/ppermute | solution.py:27
  2.9 0.0 collective-permute-start
  2.9 1.6 %collective-permute-start.2 = (bf16[2,2,256,256]{3,2,1,0:T(8,128)(2,1)}, bf16[2,2,256,256]{3,2,1,0:T(8,128)(2,1)}, u32[]{:S(2)}, u32[]{:S(2)}) collective-permute-start(bf16[2,2,256,256]{3,2,1,0:T(8,128)(2,1)} %refs_7_.1), channel_id=1, source_target_pairs={{0,4},{4,0},{8,12},{12,8},{1,5},{5,1},{9,13},{13,9},{2,6},{6,2},{1... | collective-permute-start | bytes 1572872 | tf_op jit(solution)/shard_map/ppermute | solution.py:35
  4.5 1.8 %fusion = (bf16[1,2,256,256]{3,2,1,0:T(8,128)(2,1)}, bf16[1,2,256,256]{3,2,1,0:T(8,128)(2,1)}) fusion(bf16[2,2,256,256]{3,2,1,0:T(8,128)(2,1)} %refs_7_.1), kind=kLoop, calls=%fused_computation.2 | loop fusion | bytes 1048576 | tf_op jit(solution)/shard_map/slice | solution.py:37
  6.4 2.5 %collective-permute-start.3 = (bf16[1,2,256,256]{3,2,1,0:T(8,128)(2,1)}, bf16[1,2,256,256]{3,2,1,0:T(8,128)(2,1)S(1)}, u32[]{:S(2)}, u32[]{:S(2)}) collective-permute-start(bf16[1,2,256,256]{3,2,1,0:T(8,128)(2,1)} %get-tuple-element.12), channel_id=1, source_target_pairs={{0,12},{4,8},{8,4},{12,0},{1,13},{5,9},{9,5},{13,1},{2,14},{6,10},... | collective-permute-start | bytes 786440 | tf_op jit(solution)/shard_map/ppermute | solution.py:38
  8.8 1.3 %collective-permute-start.5 = (bf16[1,2,256,256]{3,2,1,0:T(8,128)(2,1)}, bf16[1,2,256,256]{3,2,1,0:T(8,128)(2,1)}, u32[]{:S(2)}, u32[]{:S(2)}) collective-permute-start(bf16[1,2,256,256]{3,2,1,0:T(8,128)(2,1)} %get-tuple-element.13), channel_id=1, source_target_pairs={{0,12},{4,8},{8,4},{12,0},{1,13},{5,9},{9,5},{13,1},{2,14},{6,10},... | collective-permute-start | bytes 786440 | tf_op jit(solution)/shard_map/ppermute | solution.py:38
  10.2 0.0 copy-start.1
  10.2 15.4 %collective-permute-done.3.refs_6_ = bf16[1,2,256,256]{3,2,1,0:T(8,128)(2,1)S(1)} collective-permute-done((bf16[1,2,256,256]{3,2,1,0:T(8,128)(2,1)}, bf16[1,2,256,256]{3,2,1,0:T(8,128)(2,1)S(1)}, u32[]{:S(2)}, u32[]{:S(2)}) %collective-permute-start.3) | collective-permute-done | bytes 262176 | tf_op jit(solution)/shard_map/ppermute | solution.py:38
  25.6 1.0 %broadcast_select_fusion.1 = bf16[1,2,256,256]{3,2,1,0:T(8,128)(2,1)S(1)} fusion(bf16[1,2,256,256]{3,2,1,0:T(8,128)(2,1)} %get-tuple-element.12, bf16[1,2,256,256]{3,2,1,0:T(8,128)(2,1)S(1)} %collective-permute-done.3.refs_6_, pred[]{:T(512)S(6)} %lt.13), kind=kLoop, calls=%fused_computation.1 | loop fusion | flops 131072 | bytes 786433 | tf_op jit(solution)/shard_map/jit(_where)/select_n | solution.py:39
  26.6 0.1 collective-permute-start.4
  26.7 4.7 %collective-permute-done.5.refs_9_ = bf16[1,2,256,256]{3,2,1,0:T(8,128)(2,1)} collective-permute-done((bf16[1,2,256,256]{3,2,1,0:T(8,128)(2,1)}, bf16[1,2,256,256]{3,2,1,0:T(8,128)(2,1)}, u32[]{:S(2)}, u32[]{:S(2)}) %collective-permute-start.5) | collective-permute-done | bytes 262176 | tf_op jit(solution)/shard_map/ppermute | solution.py:38
  31.4 0.0 collective-permute-done.2.refs_4_.refs_8_
  31.4 1.0 %broadcast_select_fusion = bf16[1,2,256,256]{3,2,1,0:T(8,128)(2,1)S(1)} fusion(bf16[1,2,256,256]{3,2,1,0:T(8,128)(2,1)} %get-tuple-element.13, bf16[1,2,256,256]{3,2,1,0:T(8,128)(2,1)} %collective-permute-done.5.refs_9_, pred[]{:T(512)S(6)} %lt.13), kind=kLoop, calls=%fused_computation | loop fusion | flops 131072 | bytes 786433 | tf_op jit(solution)/shard_map/jit(_where)/select_n | solution.py:39
  32.4 8.8 %collective-permute-start.6 = (bf16[1,2,256,256]{3,2,1,0:T(8,128)(2,1)S(1)}, bf16[1,2,256,256]{3,2,1,0:T(8,128)(2,1)S(1)}, u32[]{:S(2)}, u32[]{:S(2)}) collective-permute-start(bf16[1,2,256,256]{3,2,1,0:T(8,128)(2,1)S(1)} %broadcast_select_fusion), channel_id=1, source_target_pairs={{0,8},{8,12},{12,4},{4,0},{1,9},{9,13},{13,5},{5,1},{2,10},{10,14}... | collective-permute-start | bytes 786440 | tf_op jit(solution)/shard_map/ppermute | solution.py:40
  41.2 0.0 collective-permute-done.1.refs_2_
  41.2 0.0 collective-permute-start.7
  41.2 0.0 collective-permute-done.4.refs_5_
  41.2 0.0 collective-permute-done.refs_1_
  41.2 0.0 copy-done
  41.3 0.0 copy-done.2
  41.3 0.0 copy-done.1
  41.3 3.3 %shard_map.37 = (bf16[4,256,512]{2,1,0:T(8,128)(2,1)S(1)}, bf16[4,256,512]{2,1,0:T(8,128)(2,1)S(1)}, f32[2,256,256]{2,1,0:T(8,128)S(1)}) custom-call(s32[4,12]{1,0:T(4,128)S(1)} %copy-done.2, bf16[2,2,256,768]{3,2,1,0:T(8,128)(2,1)S(1)} %copy-done, bf16[2,2,256,768]{3,2,1,0:T(8,128)(2,1)} %collective-permute-done.refs_1_, ...), custom_call_target="tpu_custom_call" | custom-call | flops 483183808 | bytes 1048576 | tf_op jit(solution)/shard_map/pallas_call | solution.py:152
  44.5 1.8 %collective-permute-done.6.piece_ref = bf16[1,2,256,256]{3,2,1,0:T(8,128)(2,1)S(1)} collective-permute-done((bf16[1,2,256,256]{3,2,1,0:T(8,128)(2,1)S(1)}, bf16[1,2,256,256]{3,2,1,0:T(8,128)(2,1)S(1)}, u32[]{:S(2)}, u32[]{:S(2)}) %collective-permute-start.6) | collective-permute-done | bytes 262176 | tf_op jit(solution)/shard_map/ppermute | solution.py:40
  46.4 0.0 collective-permute-done.7.refs_3_
  46.4 4.5 %shard_map.39 = (f32[2,2,256,256]{3,2,1,0:T(8,128)}, bf16[4,256,512]{2,1,0:T(8,128)(2,1)S(1)}) custom-call(s32[4,12]{1,0:T(4,128)S(1)} %copy-done.2, f32[2,256,256]{2,1,0:T(8,128)S(1)} %get-tuple-element.14.token_ref.partial, bf16[4,256,512]{2,1,0:T(8,128)(2,1)S(1)} %get-tuple-element.15.first_window, ...), custom_call_target="tpu_custom_call", output_to_operand_aliasing={{1}: (3, {})} | custom-call | flops 2013265920 | bytes 1048576 | tf_op jit(solution)/shard_map/pallas_call | solution.py:162
  (1 shorter events, 0.0 us)
Async XLA Ops:
  0.0 41.2 %copy-start = (bf16[2,2,256,768]{3,2,1,0:T(8,128)(2,1)S(1)}, bf16[2,2,256,768]{3,2,1,0:T(8,128)(2,1)}, u32[]{:S(2)}) copy-start(bf16[2,2,256,768]{3,2,1,0:T(8,128)(2,1)} %refs_0_.3) | copy-start | bytes 4718596
  0.0 41.3 %copy-start.2 = (s32[4,12]{1,0:T(4,128)S(1)}, s32[4,12]{1,0:T(4,128)}, u32[]{:S(2)}) copy-start(s32[4,12]{1,0:T(4,128)} %aperture_ref.3) | copy-start | bytes 580
  0.0 41.2 %collective-permute-start.1 = (bf16[2,2,256,768]{3,2,1,0:T(8,128)(2,1)}, bf16[2,2,256,768]{3,2,1,0:T(8,128)(2,1)S(1)}, u32[]{:S(2)}, u32[]{:S(2)}) collective-permute-start(bf16[2,2,256,768]{3,2,1,0:T(8,128)(2,1)} %refs_0_.3), channel_id=1, source_target_pairs={{0,2},{1,3},{2,0},{3,1},{4,6},{5,7},{6,4},{7,5},{8,10},{9,11},{10,... | collective-permute-start | bytes 4718600 | tf_op jit(solution)/shard_map/ppermute | solution.py:27
  2.9 38.3 %collective-permute-start = (bf16[2,2,256,768]{3,2,1,0:T(8,128)(2,1)}, bf16[2,2,256,768]{3,2,1,0:T(8,128)(2,1)}, u32[]{:S(2)}, u32[]{:S(2)}) collective-permute-start(bf16[2,2,256,768]{3,2,1,0:T(8,128)(2,1)} %refs_0_.3), channel_id=1, source_target_pairs={{0,1},{1,0},{2,3},{3,2},{4,5},{5,4},{6,7},{7,6},{8,9},{9,8},{10,11... | collective-permute-start | bytes 4718600 | tf_op jit(solution)/shard_map/ppermute | solution.py:27
  2.9 28.4 %collective-permute-start.2 = (bf16[2,2,256,256]{3,2,1,0:T(8,128)(2,1)}, bf16[2,2,256,256]{3,2,1,0:T(8,128)(2,1)}, u32[]{:S(2)}, u32[]{:S(2)}) collective-permute-start(bf16[2,2,256,256]{3,2,1,0:T(8,128)(2,1)} %refs_7_.1), channel_id=1, source_target_pairs={{0,4},{4,0},{8,12},{12,8},{1,5},{5,1},{9,13},{13,9},{2,6},{6,2},{1... | collective-permute-start | bytes 1572872 | tf_op jit(solution)/shard_map/ppermute | solution.py:35
  6.4 19.3 %collective-permute-start.3 = (bf16[1,2,256,256]{3,2,1,0:T(8,128)(2,1)}, bf16[1,2,256,256]{3,2,1,0:T(8,128)(2,1)S(1)}, u32[]{:S(2)}, u32[]{:S(2)}) collective-permute-start(bf16[1,2,256,256]{3,2,1,0:T(8,128)(2,1)} %get-tuple-element.12), channel_id=1, source_target_pairs={{0,12},{4,8},{8,4},{12,0},{1,13},{5,9},{9,5},{13,1},{2,14},{6,10},... | collective-permute-start | bytes 786440 | tf_op jit(solution)/shard_map/ppermute | solution.py:38
  8.8 22.5 %collective-permute-start.5 = (bf16[1,2,256,256]{3,2,1,0:T(8,128)(2,1)}, bf16[1,2,256,256]{3,2,1,0:T(8,128)(2,1)}, u32[]{:S(2)}, u32[]{:S(2)}) collective-permute-start(bf16[1,2,256,256]{3,2,1,0:T(8,128)(2,1)} %get-tuple-element.13), channel_id=1, source_target_pairs={{0,12},{4,8},{8,4},{12,0},{1,13},{5,9},{9,5},{13,1},{2,14},{6,10},... | collective-permute-start | bytes 786440 | tf_op jit(solution)/shard_map/ppermute | solution.py:38
  10.2 31.1 %copy-start.1 = (bf16[2,2,256,256]{3,2,1,0:T(8,128)(2,1)S(1)}, bf16[2,2,256,256]{3,2,1,0:T(8,128)(2,1)}, u32[]{:S(2)}) copy-start(bf16[2,2,256,256]{3,2,1,0:T(8,128)(2,1)} %refs_7_.1) | copy-start | bytes 1572868
  26.6 14.6 %collective-permute-start.4 = (bf16[1,2,256,256]{3,2,1,0:T(8,128)(2,1)S(1)}, bf16[1,2,256,256]{3,2,1,0:T(8,128)(2,1)S(1)}, u32[]{:S(2)}, u32[]{:S(2)}) collective-permute-start(bf16[1,2,256,256]{3,2,1,0:T(8,128)(2,1)S(1)} %broadcast_select_fusion.1), channel_id=1, source_target_pairs={{0,8},{8,12},{12,4},{4,0},{1,9},{9,13},{13,5},{5,1},{2,10},{10,14}... | collective-permute-start | bytes 786440 | tf_op jit(solution)/shard_map/ppermute | solution.py:40
  32.4 14.0 %collective-permute-start.6 = (bf16[1,2,256,256]{3,2,1,0:T(8,128)(2,1)S(1)}, bf16[1,2,256,256]{3,2,1,0:T(8,128)(2,1)S(1)}, u32[]{:S(2)}, u32[]{:S(2)}) collective-permute-start(bf16[1,2,256,256]{3,2,1,0:T(8,128)(2,1)S(1)} %broadcast_select_fusion), channel_id=1, source_target_pairs={{0,8},{8,12},{12,4},{4,0},{1,9},{9,13},{13,5},{5,1},{2,10},{10,14}... | collective-permute-start | bytes 786440 | tf_op jit(solution)/shard_map/ppermute | solution.py:40
  41.2 5.1 %collective-permute-start.7 = (bf16[2,2,256,768]{3,2,1,0:T(8,128)(2,1)S(1)}, bf16[2,2,256,768]{3,2,1,0:T(8,128)(2,1)S(1)}, u32[]{:S(2)}, u32[]{:S(2)}) collective-permute-start(bf16[2,2,256,768]{3,2,1,0:T(8,128)(2,1)S(1)} %collective-permute-done.1.refs_2_), channel_id=1, source_target_pairs={{0,1},{1,0},{2,3},{3,2},{4,5},{5,4},{6,7},{7,6},{8,9},{9,8},{10,11... | collective-permute-start | bytes 4718600 | tf_op jit(solution)/shard_map/ppermute | solution.py:27

commit v9 on v8

--- a/solution.py
+++ b/solution.py
@@ -31,12 +31,34 @@
     return (lax.axis_index("src") + 1) % lax.axis_size("src") < 2
 
 
+def split_kernel(data_ref, *refs):
+    *part_refs, sems = refs
+    copies = [pltpu.make_async_copy(data_ref.at[pl.ds(v, 1)], ref, sems.at[v]) for v, ref in enumerate(part_refs)]
+    for copy in copies:
+        copy.start()
+    for copy in copies:
+        copy.wait()
+
+
+def split_surveys(data):
+    surveys, *shape = data.shape
+    return pl.pallas_call(
+        split_kernel,
+        out_shape=[jax.ShapeDtypeStruct((1, *shape), data.dtype)] * surveys,
+        in_specs=[spec(pl.ANY)],
+        out_specs=[spec(pltpu.VMEM)] * surveys,
+        scratch_shapes=[pltpu.SemaphoreType.DMA((surveys,))],
+        compiler_params=limit(1),
+        cost_estimate=cost(0.1),
+    )(data)
+
+
 def line_window(data):
     near = lax.ppermute(data, "src", [(0, 1), (1, 0), (2, 3), (3, 2)])
     windows = []
-    for v, own in enumerate(lax.optimization_barrier([data[v : v + 1] for v in range(data.shape[0])])):
+    for v, own in enumerate(split_surveys(data)):
         far = lax.ppermute(own, "src", [(0, 3), (1, 2), (2, 1), (3, 0)])
-        onward = jnp.where(at_end(), own, far if v == 0 else after(far, near))
+        onward = jnp.where(at_end(), own, far)
         across = lax.ppermute(onward, "src", [(0, 2), (2, 3), (3, 1), (1, 0)])
         windows.append([(data, v), (near, v), (across, 0), (far, 0)])
     return windows

time: 51.1 us -> 48.6 us (0.951)
  waiting for transfers between devices: 22 us -> 13.6 us
  starting transfers between devices: 17.2 us -> 23.1 us
  Pallas kernels: 7.73 us -> 8.57 us
  local copies, waits for them, and re-layouts: 1.85 us -> 1.05 us
    ppermute x2, waiting for transfers between devices: 20.1 us -> 7.45 us  [line_window(): far = lax.ppermute(own, 'src', [(0, 3), (1, 2), (2, 1), (3, 0)])]
    ppermute x2, starting transfers between devices: 8.9 us -> 16.2 us  [line_window(): across = lax.ppermute(onward, 'src', [(0, 2), (2, 3), (3, 1), (1, 0)])]
    ppermute x3, waiting for transfers between devices: 0.01 us -> 3.19 us  [swap(): return lax.ppermute(x, axis, [(i, i ^ bit) for i in range(peers)])]
    slice x1 -> x0, local copies, waits for them, and re-layouts: 1.84 us -> none  [line_window(): data[v:v + 1]]
    ppermute x1, starting transfers between devices: 1.58 us -> 0.01 us  [line_window(): near = lax.ppermute(data, 'src', [(0, 1), (1, 0), (2, 3), (3, 2)])]
    ppermute x2, waiting for transfers between devices: 1.83 us -> 2.99 us  [line_window(): across = lax.ppermute(onward, 'src', [(0, 2), (2, 3), (3, 1), (1, 0)])]
    unnamed x6 -> x8, local copies, waits for them, and re-layouts: 0.01 us -> 1.05 us
    pallas_call x0 -> x1, Pallas kernels: none -> 0.85 us  [split_surveys(): pl.pallas_call(split_kernel, out_shape=[jax.ShapeDtypeStruct((1, *shape),...]
  transfers between devices with their start and end apart: 8 -> 8, of which waited for: 3 -> 4; matrix products, arithmetic and copies ran while one was open for 7% -> 4% of each run, Pallas kernels for 6% -> 8%
where the time goes in v9:
time: 48.6 us; the launch traced here: 48.4 us
  starting transfers between devices  23.1 us (48%)
  waiting for transfers between devices  13.6 us (28%)
  Pallas kernels  8.57 us (18%)
  other arithmetic  1.96 us (4%)
  local copies, waits for them, and re-layouts  1.05 us (2%)
    ppermute x2, starting transfers between devices, line_window(): across = lax.ppermute(onward, 'src', [(0, 2), (2, 3), (3, 1), (1, 0)])  16.2 us
    ppermute x2, waiting for transfers between devices, line_window(): far = lax.ppermute(own, 'src', [(0, 3), (1, 2), (2, 1), (3, 0)])  7.45 us
    pallas_call x1, Pallas kernels, body(): pl.pallas_call(functools.partial(last_kernel, split, late), out_shape=[ja...  4.47 us
    ppermute x2, starting transfers between devices, line_window(): far = lax.ppermute(own, 'src', [(0, 3), (1, 2), (2, 1), (3, 0)])  3.9 us
    pallas_call x1, Pallas kernels, body(): pl.pallas_call(functools.partial(first_kernel, split, [v for _, v in firs...  3.25 us
    ppermute x3, waiting for transfers between devices, swap(): return lax.ppermute(x, axis, [(i, i ^ bit) for i in range(peers)])  3.19 us
    ppermute x2, waiting for transfers between devices, line_window(): across = lax.ppermute(onward, 'src', [(0, 2), (2, 3), (3, 1), (1, 0)])  2.99 us
    ppermute x3, starting transfers between devices, swap(): return lax.ppermute(x, axis, [(i, i ^ bit) for i in range(peers)])  2.94 us
  transfers between devices with their start and end apart: 8, of which 4 were waited for; matrix products, arithmetic and copies ran while one was open for 4% of the time, Pallas kernels for 8%

profile of v9, /device:TPU:0, one launch (start us, length us, event | category | flops | bytes accessed | tf_op | source)
XLA Modules:
  0.0 48.4 jit_solution(10933525924840817893)
XLA Ops:
  0.0 0.0 copy-start
  0.0 2.9 %collective-permute-start.1 = (bf16[2,2,256,768]{3,2,1,0:T(8,128)(2,1)}, bf16[2,2,256,768]{3,2,1,0:T(8,128)(2,1)S(1)}, u32[]{:S(2)}, u32[]{:S(2)}) collective-permute-start(bf16[2,2,256,768]{3,2,1,0:T(8,128)(2,1)} %refs_0_.3), channel_id=1, source_target_pairs={{0,2},{1,3},{2,0},{3,1},{4,6},{5,7},{6,4},{7,5},{8,10},{9,11},{10,... | collective-permute-start | bytes 4718600 | tf_op jit(solution)/shard_map/ppermute | solution.py:27
  2.9 0.0 collective-permute-start
  2.9 0.0 copy-start.1
  2.9 1.0 %copy-done.1 = bf16[2,2,256,256]{3,2,1,0:T(8,128)(2,1)S(1)} copy-done((bf16[2,2,256,256]{3,2,1,0:T(8,128)(2,1)S(1)}, bf16[2,2,256,256]{3,2,1,0:T(8,128)(2,1)}, u32[]{:S(2)}) %copy-start.1) | copy-done | bytes 524312
  4.0 0.0 copy-start.3
  4.0 0.9 %shard_map.37 = (bf16[1,2,256,256]{3,2,1,0:T(8,128)(2,1)}, bf16[1,2,256,256]{3,2,1,0:T(8,128)(2,1)}) custom-call(bf16[2,2,256,256]{3,2,1,0:T(8,128)(2,1)S(1)} %copy-done.1), custom_call_target="tpu_custom_call" | custom-call | flops 161061280 | bytes 1048576 | tf_op jit(solution)/shard_map/pallas_call | solution.py:45
  4.9 3.7 %collective-permute-start.3 = (bf16[1,2,256,256]{3,2,1,0:T(8,128)(2,1)}, bf16[1,2,256,256]{3,2,1,0:T(8,128)(2,1)S(1)}, u32[]{:S(2)}, u32[]{:S(2)}) collective-permute-start(bf16[1,2,256,256]{3,2,1,0:T(8,128)(2,1)} %get-tuple-element.11), channel_id=1, source_target_pairs={{0,12},{4,8},{8,4},{12,0},{1,13},{5,9},{9,5},{13,1},{2,14},{6,10},... | collective-permute-start | bytes 786440 | tf_op jit(solution)/shard_map/ppermute | solution.py:60
  8.5 0.2 collective-permute-start.5
  8.8 0.0 collective-permute-start.2
  8.8 0.0 copy-start.2
  8.8 7.5 %collective-permute-done.3.refs_6_ = bf16[1,2,256,256]{3,2,1,0:T(8,128)(2,1)S(1)} collective-permute-done((bf16[1,2,256,256]{3,2,1,0:T(8,128)(2,1)}, bf16[1,2,256,256]{3,2,1,0:T(8,128)(2,1)S(1)}, u32[]{:S(2)}, u32[]{:S(2)}) %collective-permute-start.3) | collective-permute-done | bytes 262176 | tf_op jit(solution)/shard_map/ppermute | solution.py:60
  16.2 1.0 %broadcast_select_fusion.1 = bf16[1,2,256,256]{3,2,1,0:T(8,128)(2,1)S(1)} fusion(bf16[1,2,256,256]{3,2,1,0:T(8,128)(2,1)} %get-tuple-element.11, bf16[1,2,256,256]{3,2,1,0:T(8,128)(2,1)S(1)} %collective-permute-done.3.refs_6_, pred[]{:T(512)S(6)} %lt.13), kind=kLoop, calls=%fused_computation.1 | loop fusion | flops 131072 | bytes 786433 | tf_op jit(solution)/shard_map/jit(_where)/select_n | solution.py:61
  17.2 10.9 %collective-permute-start.4 = (bf16[1,2,256,256]{3,2,1,0:T(8,128)(2,1)S(1)}, bf16[1,2,256,256]{3,2,1,0:T(8,128)(2,1)S(1)}, u32[]{:S(2)}, u32[]{:S(2)}) collective-permute-start(bf16[1,2,256,256]{3,2,1,0:T(8,128)(2,1)S(1)} %broadcast_select_fusion.1), channel_id=1, source_target_pairs={{0,8},{8,12},{12,4},{4,0},{1,9},{9,13},{13,5},{5,1},{2,10},{10,14}... | collective-permute-start | bytes 786440 | tf_op jit(solution)/shard_map/ppermute | solution.py:62
  28.1 0.0 collective-permute-done.5.refs_9_
  28.1 1.0 %broadcast_select_fusion = bf16[1,2,256,256]{3,2,1,0:T(8,128)(2,1)S(1)} fusion(bf16[1,2,256,256]{3,2,1,0:T(8,128)(2,1)} %get-tuple-element.12, bf16[1,2,256,256]{3,2,1,0:T(8,128)(2,1)} %collective-permute-done.5.refs_9_, pred[]{:T(512)S(6)} %lt.13), kind=kLoop, calls=%fused_computation | loop fusion | flops 131072 | bytes 786433 | tf_op jit(solution)/shard_map/jit(_where)/select_n | solution.py:61
  29.1 5.3 %collective-permute-start.6 = (bf16[1,2,256,256]{3,2,1,0:T(8,128)(2,1)S(1)}, bf16[1,2,256,256]{3,2,1,0:T(8,128)(2,1)S(1)}, u32[]{:S(2)}, u32[]{:S(2)}) collective-permute-start(bf16[1,2,256,256]{3,2,1,0:T(8,128)(2,1)S(1)} %broadcast_select_fusion), channel_id=1, source_target_pairs={{0,8},{8,12},{12,4},{4,0},{1,9},{9,13},{13,5},{5,1},{2,10},{10,14}... | collective-permute-start | bytes 786440 | tf_op jit(solution)/shard_map/ppermute | solution.py:62
  34.4 3.2 %collective-permute-done.1.refs_2_ = bf16[2,2,256,768]{3,2,1,0:T(8,128)(2,1)S(1)} collective-permute-done((bf16[2,2,256,768]{3,2,1,0:T(8,128)(2,1)}, bf16[2,2,256,768]{3,2,1,0:T(8,128)(2,1)S(1)}, u32[]{:S(2)}, u32[]{:S(2)}) %collective-permute-start.1) | collective-permute-done | bytes 1572896 | tf_op jit(solution)/shard_map/ppermute | solution.py:27
  37.6 0.0 collective-permute-start.7
  37.6 0.7 %collective-permute-done.4.refs_5_ = bf16[1,2,256,256]{3,2,1,0:T(8,128)(2,1)S(1)} collective-permute-done((bf16[1,2,256,256]{3,2,1,0:T(8,128)(2,1)S(1)}, bf16[1,2,256,256]{3,2,1,0:T(8,128)(2,1)S(1)}, u32[]{:S(2)}, u32[]{:S(2)}) %collective-permute-start.4) | collective-permute-done | bytes 262176 | tf_op jit(solution)/shard_map/ppermute | solution.py:62
  38.4 0.0 collective-permute-done.2.refs_4_.refs_8_
  38.4 0.0 collective-permute-done.refs_1_
  38.4 0.0 copy-done
  38.4 0.0 copy-done.3
  38.4 0.0 copy-done.2
  38.4 3.3 %shard_map.38 = (bf16[4,256,512]{2,1,0:T(8,128)(2,1)S(1)}, bf16[4,256,512]{2,1,0:T(8,128)(2,1)S(1)}, f32[2,256,256]{2,1,0:T(8,128)S(1)}) custom-call(s32[4,12]{1,0:T(4,128)S(1)} %copy-done.3, bf16[2,2,256,768]{3,2,1,0:T(8,128)(2,1)S(1)} %copy-done, bf16[2,2,256,768]{3,2,1,0:T(8,128)(2,1)} %collective-permute-done.refs_1_, ...), custom_call_target="tpu_custom_call" | custom-call | flops 483183808 | bytes 1048576 | tf_op jit(solution)/shard_map/pallas_call | solution.py:174
  41.7 2.2 %collective-permute-done.6.piece_ref = bf16[1,2,256,256]{3,2,1,0:T(8,128)(2,1)S(1)} collective-permute-done((bf16[1,2,256,256]{3,2,1,0:T(8,128)(2,1)S(1)}, bf16[1,2,256,256]{3,2,1,0:T(8,128)(2,1)S(1)}, u32[]{:S(2)}, u32[]{:S(2)}) %collective-permute-start.6) | collective-permute-done | bytes 262176 | tf_op jit(solution)/shard_map/ppermute | solution.py:62
  43.9 0.0 collective-permute-done.7.refs_3_
  43.9 4.5 %shard_map.40 = (f32[2,2,256,256]{3,2,1,0:T(8,128)}, bf16[4,256,512]{2,1,0:T(8,128)(2,1)S(1)}) custom-call(s32[4,12]{1,0:T(4,128)S(1)} %copy-done.3, f32[2,256,256]{2,1,0:T(8,128)S(1)} %get-tuple-element.13.token_ref.partial, bf16[4,256,512]{2,1,0:T(8,128)(2,1)S(1)} %get-tuple-element.14.first_window, ...), custom_call_target="tpu_custom_call", output_to_operand_aliasing={{1}: (3, {})} | custom-call | flops 2013265920 | bytes 1048576 | tf_op jit(solution)/shard_map/pallas_call | solution.py:184
  (1 shorter events, 0.0 us)
Async XLA Ops:
  0.0 38.4 %copy-start = (bf16[2,2,256,768]{3,2,1,0:T(8,128)(2,1)S(1)}, bf16[2,2,256,768]{3,2,1,0:T(8,128)(2,1)}, u32[]{:S(2)}) copy-start(bf16[2,2,256,768]{3,2,1,0:T(8,128)(2,1)} %refs_0_.3) | copy-start | bytes 4718596
  0.0 37.6 %collective-permute-start.1 = (bf16[2,2,256,768]{3,2,1,0:T(8,128)(2,1)}, bf16[2,2,256,768]{3,2,1,0:T(8,128)(2,1)S(1)}, u32[]{:S(2)}, u32[]{:S(2)}) collective-permute-start(bf16[2,2,256,768]{3,2,1,0:T(8,128)(2,1)} %refs_0_.3), channel_id=1, source_target_pairs={{0,2},{1,3},{2,0},{3,1},{4,6},{5,7},{6,4},{7,5},{8,10},{9,11},{10,... | collective-permute-start | bytes 4718600 | tf_op jit(solution)/shard_map/ppermute | solution.py:27
  2.9 35.4 %collective-permute-start = (bf16[2,2,256,768]{3,2,1,0:T(8,128)(2,1)}, bf16[2,2,256,768]{3,2,1,0:T(8,128)(2,1)}, u32[]{:S(2)}, u32[]{:S(2)}) collective-permute-start(bf16[2,2,256,768]{3,2,1,0:T(8,128)(2,1)} %refs_0_.3), channel_id=1, source_target_pairs={{0,1},{1,0},{2,3},{3,2},{4,5},{5,4},{6,7},{7,6},{8,9},{9,8},{10,11... | collective-permute-start | bytes 4718600 | tf_op jit(solution)/shard_map/ppermute | solution.py:27
  2.9 1.0 %copy-start.1 = (bf16[2,2,256,256]{3,2,1,0:T(8,128)(2,1)S(1)}, bf16[2,2,256,256]{3,2,1,0:T(8,128)(2,1)}, u32[]{:S(2)}) copy-start(bf16[2,2,256,256]{3,2,1,0:T(8,128)(2,1)} %refs_7_.1) | copy-start | bytes 1572868
  4.0 34.4 %copy-start.3 = (s32[4,12]{1,0:T(4,128)S(1)}, s32[4,12]{1,0:T(4,128)}, u32[]{:S(2)}) copy-start(s32[4,12]{1,0:T(4,128)} %aperture_ref.3) | copy-start | bytes 580
  4.9 11.4 %collective-permute-start.3 = (bf16[1,2,256,256]{3,2,1,0:T(8,128)(2,1)}, bf16[1,2,256,256]{3,2,1,0:T(8,128)(2,1)S(1)}, u32[]{:S(2)}, u32[]{:S(2)}) collective-permute-start(bf16[1,2,256,256]{3,2,1,0:T(8,128)(2,1)} %get-tuple-element.11), channel_id=1, source_target_pairs={{0,12},{4,8},{8,4},{12,0},{1,13},{5,9},{9,5},{13,1},{2,14},{6,10},... | collective-permute-start | bytes 786440 | tf_op jit(solution)/shard_map/ppermute | solution.py:60
  8.5 19.6 %collective-permute-start.5 = (bf16[1,2,256,256]{3,2,1,0:T(8,128)(2,1)}, bf16[1,2,256,256]{3,2,1,0:T(8,128)(2,1)}, u32[]{:S(2)}, u32[]{:S(2)}) collective-permute-start(bf16[1,2,256,256]{3,2,1,0:T(8,128)(2,1)} %get-tuple-element.12), channel_id=1, source_target_pairs={{0,12},{4,8},{8,4},{12,0},{1,13},{5,9},{9,5},{13,1},{2,14},{6,10},... | collective-permute-start | bytes 786440 | tf_op jit(solution)/shard_map/ppermute | solution.py:60
  8.8 29.6 %collective-permute-start.2 = (bf16[2,2,256,256]{3,2,1,0:T(8,128)(2,1)}, bf16[2,2,256,256]{3,2,1,0:T(8,128)(2,1)}, u32[]{:S(2)}, u32[]{:S(2)}) collective-permute-start(bf16[2,2,256,256]{3,2,1,0:T(8,128)(2,1)} %refs_7_.1), channel_id=1, source_target_pairs={{0,4},{4,0},{8,12},{12,8},{1,5},{5,1},{9,13},{13,9},{2,6},{6,2},{1... | collective-permute-start | bytes 1572872 | tf_op jit(solution)/shard_map/ppermute | solution.py:57
  8.8 29.6 %copy-start.2 = (bf16[2,2,256,256]{3,2,1,0:T(8,128)(2,1)S(1)}, bf16[2,2,256,256]{3,2,1,0:T(8,128)(2,1)}, u32[]{:S(2)}) copy-start(bf16[2,2,256,256]{3,2,1,0:T(8,128)(2,1)} %refs_7_.1) | copy-start | bytes 1572868
  17.2 21.2 %collective-permute-start.4 = (bf16[1,2,256,256]{3,2,1,0:T(8,128)(2,1)S(1)}, bf16[1,2,256,256]{3,2,1,0:T(8,128)(2,1)S(1)}, u32[]{:S(2)}, u32[]{:S(2)}) collective-permute-start(bf16[1,2,256,256]{3,2,1,0:T(8,128)(2,1)S(1)} %broadcast_select_fusion.1), channel_id=1, source_target_pairs={{0,8},{8,12},{12,4},{4,0},{1,9},{9,13},{13,5},{5,1},{2,10},{10,14}... | collective-permute-start | bytes 786440 | tf_op jit(solution)/shard_map/ppermute | solution.py:62
  29.1 14.8 %collective-permute-start.6 = (bf16[1,2,256,256]{3,2,1,0:T(8,128)(2,1)S(1)}, bf16[1,2,256,256]{3,2,1,0:T(8,128)(2,1)S(1)}, u32[]{:S(2)}, u32[]{:S(2)}) collective-permute-start(bf16[1,2,256,256]{3,2,1,0:T(8,128)(2,1)S(1)} %broadcast_select_fusion), channel_id=1, source_target_pairs={{0,8},{8,12},{12,4},{4,0},{1,9},{9,13},{13,5},{5,1},{2,10},{10,14}... | collective-permute-start | bytes 786440 | tf_op jit(solution)/shard_map/ppermute | solution.py:62
  37.6 6.3 %collective-permute-start.7 = (bf16[2,2,256,768]{3,2,1,0:T(8,128)(2,1)S(1)}, bf16[2,2,256,768]{3,2,1,0:T(8,128)(2,1)S(1)}, u32[]{:S(2)}, u32[]{:S(2)}) collective-permute-start(bf16[2,2,256,768]{3,2,1,0:T(8,128)(2,1)S(1)} %collective-permute-done.1.refs_2_), channel_id=1, source_target_pairs={{0,1},{1,0},{2,3},{3,2},{4,5},{5,4},{6,7},{7,6},{8,9},{9,8},{10,11... | collective-permute-start | bytes 4718600 | tf_op jit(solution)/shard_map/ppermute | solution.py:27

commit v10 on v8

v10 whole, which is shorter than its diff:
```python
import functools

import jax
import jax.numpy as jnp
from jax import lax
from jax.experimental import pallas as pl
from jax.experimental.pallas import tpu as pltpu
from jax.sharding import PartitionSpec as P

BLK = 256
APER = 12
HW = 6


def after(value, *earlier):
    return lax.optimization_barrier((value, *earlier))[0]


def from_behind(x, axis, by):
    peers = lax.axis_size(axis)
    pairs = [(i, i + by) for i in range(peers) if 0 <= i + by < peers]
    return lax.ppermute(x, axis, pairs)


def swap(x, axis, bit):
    peers = lax.axis_size(axis)
    return lax.ppermute(x, axis, [(i, i ^ bit) for i in range(peers)])


def at_end():
    return (lax.axis_index("src") + 1) % lax.axis_size("src") < 2


def line_window(data):
    near = lax.ppermute(data, "src", [(0, 1), (1, 0), (2, 3), (3, 2)])
    windows = []
    for v, own in enumerate(lax.optimization_barrier([data[v : v + 1] for v in range(data.shape[0])])):
        far = lax.ppermute(own, "src", [(0, 3), (1, 2), (2, 1), (3, 0)])
        onward = jnp.where(at_end(), own, far)
        across = lax.ppermute(onward, "src", [(0, 2), (2, 3), (3, 1), (1, 0)])
        windows.append([(own, 0), (near, v), (across, 0), (far, 0)])
    return windows


def hop_window(data):
    reach = min(HW, lax.axis_size("src") - 1)
    window = {0: data}
    for hop in range(1, reach + 1):
        window[-hop] = from_behind(window[1 - hop], "src", 1)
        window[hop] = from_behind(window[hop - 1], "src", -1)
    return [[(window[distance], v) for distance in range(-reach, reach + 1)] for v in range(data.shape[0])]


def gather_panels(primaries):
    bit = lax.axis_size("rcv") // 2
    panels = [primaries]
    for lower in range(1, bit):
        panels.append(swap(panels[lower & (lower - 1)], "rcv", lower & -lower))
    return panels, swap(primaries, "rcv", bit)


def hand_on(panel, token):
    bit = lax.axis_size("rcv") // 2
    panels = [after(panel, token)]
    for lower in range(1, bit):
        panels.append(swap(panels[lower & (lower - 1)], "rcv", lower & -lower))
    return panels[1:]


def fill_window(window, pieces):
    width = window.shape[-1] // 2
    for k, piece in pieces.items():
        window[k, :, :width] = piece[0]
        window[k, :, width:] = piece[1]


def slot_entries(aperture_ref, m, per_shard, depth):
    src = lax.axis_index("src")
    shard = lax.bitwise_xor(lax.axis_index("rcv"), m)
    wanted = [aperture_ref[src, shard * per_shard + q] for q in range(per_shard)]
    if lax.axis_size("src") == 4:
        return [lax.bitwise_xor(src, block) for block in wanted]
    return [block - src + depth // 2 for block in wanted]


def times(values, blocks):
    both = jnp.dot(values, blocks, preferred_element_type=jnp.float32)
    rows, width = both.shape[0] // 2, both.shape[1] // 2
    return both[:rows, :width] - both[rows:, width:], both[:rows, width:] + both[rows:, :width]


def rows_of(panel):
    return panel[...].reshape(2 * panel.shape[1], panel.shape[2])


def product(window, aperture_ref, panels):
    blocks = []
    for m, panel in panels.items():
        entries = slot_entries(aperture_ref, m, panel.shape[-1] // BLK, window.shape[0])
        blocks += [window[k] for k in entries]
    values = jnp.concatenate([rows_of(panel) for panel in panels.values()], axis=1)
    return times(values, jnp.concatenate(blocks, axis=0))


def sum_of_late(aperture_ref, panels, late, depth):
    total = None
    for m, panel in panels.items():
        values = rows_of(panel)
        for q, k in enumerate(slot_entries(aperture_ref, m, panel.shape[-1] // BLK, depth)):
            term = values[:, q * BLK : (q + 1) * BLK].astype(jnp.float32) * jnp.where(k == late, 1.0, 0.0)
            total = term if total is None else total + term
    return total


def in_two(total):
    high = total.astype(jnp.bfloat16)
    low = (total - high.astype(jnp.float32)).astype(jnp.bfloat16)
    return jnp.concatenate([high, low], axis=1)


def add_late(total_in_two, window, late):
    block = window[late]
    return times(total_in_two, jnp.concatenate([block, block], axis=0))


def kernel_a(near_half, ats, late, aperture_ref, *refs):
    panel_refs = refs[:near_half]
    piece_refs = list(refs[near_half:-6])
    windows, sums, parts = refs[-6:-4], refs[-4:-2], refs[-2:]
    for v, (window, at) in enumerate(zip(windows, ats)):
        window[late] = jnp.zeros(window.shape[1:], window.dtype)
        fill_window(window, {k: piece_refs.pop(0).at[index] for k, index in at.items()})
        panels = {m: ref.at[v] for m, ref in enumerate(panel_refs)}
        parts[v][0], parts[v][1] = product(window, aperture_ref, panels)
        sums[v][...] = sum_of_late(aperture_ref, panels, late, window.shape[0])


def kernel_b(m, late, aperture_ref, late_ref, _, last_window, first_sum, last_sum, first_in, last_in, panel_ref, *refs):
    window, two, first_part, last_part = refs
    fill_window(window, {late: late_ref.at[0]})
    real, imag = product(window, aperture_ref, {m: panel_ref.at[0]})
    late_real, late_imag = add_late(in_two(first_sum[...]), window, late)
    first_part[0] = first_in[0] + (real + late_real)
    first_part[1] = first_in[1] + (imag + late_imag)
    panels = {m: panel_ref.at[1]}
    real, imag = product(last_window, aperture_ref, panels)
    last_part[0] = last_in[0] + real
    last_part[1] = last_in[1] + imag
    two[...] = in_two(last_sum[...] + sum_of_late(aperture_ref, panels, late, last_window.shape[0]))


def last_kernel(far_half, late, aperture_ref, late_ref, first_window, _, two, first_part, last_part, *refs):
    *panel_refs, out_ref, window, result, sems = refs

    def finish(v, part, real, imag):
        copies = [pltpu.make_async_copy(result.at[v, p], out_ref.at[v, p], sems.at[v, p]) for p in range(2)]
        for p, value in enumerate((real, imag)):
            result[v, p] = part[p] + value
            copies[p].start()
        return copies

    panels = [{far_half + m: ref.at[v] for m, ref in enumerate(panel_refs)} for v in range(2)]
    copies = finish(0, first_part, *product(first_window, aperture_ref, panels[0]))
    fill_window(window, {late: late_ref.at[0]})
    real, imag = product(window, aperture_ref, panels[1])
    late_real, late_imag = add_late(two[...], window, late)
    copies += finish(1, last_part, real + late_real, imag + late_imag)
    for copy in copies:
        copy.wait()


def spec(space):
    return pl.BlockSpec(memory_space=space)


def cost(share):
    return pl.CostEstimate(flops=int(share * (8 * BLK * BLK * APER * BLK)), bytes_accessed=1 << 20, transcendentals=0)


def limit(megabytes):
    return pltpu.CompilerParams(vmem_limit_bytes=megabytes << 20)


def held(piece, token):
    return pl.pallas_call(
        lambda piece_ref, token_ref, out_ref: None,
        out_shape=jax.ShapeDtypeStruct(piece.shape, piece.dtype),
        in_specs=[spec(pl.ANY)] * 2,
        out_specs=spec(pl.ANY),
        input_output_aliases={0: 0},
        compiler_params=limit(1),
        cost_estimate=cost(12),
    )(piece, token)


def body(primaries, data, aperture):
    width = data.shape[3]
    line = lax.axis_size("src") == 4
    windows = (line_window if line else hop_window)(data)
    panels, far_panel = gather_panels(primaries)
    half = len(panels)
    late = 2 if line else len(windows[0]) - 1
    late_pieces = [piece[at : at + 1] for piece, at in (window[late] for window in windows)]
    early = [{k: piece for k, piece in enumerate(window) if k != late} for window in windows]
    vmem, smem, anywhere = spec(pltpu.VMEM), spec(pltpu.SMEM), spec(pl.ANY)
    window = jax.ShapeDtypeStruct((len(windows[0]), BLK, 2 * width), jnp.bfloat16)
    total = jax.ShapeDtypeStruct((2 * BLK, BLK), jnp.float32)
    part = jax.ShapeDtypeStruct((2, BLK, width), jnp.float32)

    pieces = [piece for window_pieces in early for piece, _ in window_pieces.values()]
    first, last, first_sum, last_sum, first_part, last_part = pl.pallas_call(
        functools.partial(kernel_a, half, [{k: at for k, (_, at) in pieces.items()} for pieces in early], late),
        out_shape=[window] * 2 + [total] * 2 + [part] * 2,
        in_specs=[smem] + [vmem] * (half + len(pieces)),
        out_specs=[vmem] * 6,
        compiler_params=limit(16),
        cost_estimate=cost(0.1),
    )(aperture, *panels, *pieces)

    handed_on = hand_on(far_panel, first_part)
    first, two, first_part, last_part = pl.pallas_call(
        functools.partial(kernel_b, half, late),
        out_shape=[window, jax.ShapeDtypeStruct((2 * BLK, 2 * BLK), jnp.bfloat16), part, part],
        in_specs=[smem] + [vmem] * 8,
        out_specs=[vmem] * 4,
        input_output_aliases={2: 0, 6: 2, 7: 3},
        compiler_params=limit(16),
        cost_estimate=cost(0.1),
    )(aperture, late_pieces[0], first, last, first_sum, last_sum, first_part, last_part, far_panel)

    return pl.pallas_call(
        functools.partial(last_kernel, half + 1, late),
        out_shape=[jax.ShapeDtypeStruct((2, 2, BLK, width), jnp.float32), window],
        in_specs=[smem] + [vmem] * (6 + len(handed_on)),
        out_specs=[anywhere, vmem],
        scratch_shapes=[pltpu.VMEM((2, 2, BLK, width), jnp.float32), pltpu.SemaphoreType.DMA((2, 2))],
        input_output_aliases={3: 1},
        compiler_params=limit(16),
        cost_estimate=cost(1),
    )(aperture, held(late_pieces[1], two), first, last, two, first_part, last_part, *handed_on)[0]


def solution(mesh):
    placed = (P("freq", None, "src", "rcv"), P("freq", None, "src", "rcv"), P())
    return jax.shard_map(
        body, mesh=mesh, in_specs=placed, out_specs=P("freq", None, "src", "rcv"), check_vma=False
    )
```

time: 51.1 us -> 45.5 us (0.89)
  waiting for transfers between devices: 22 us -> 10.7 us
  starting transfers between devices: 17.2 us -> 23.6 us
  Pallas kernels: 7.73 us -> 9.84 us
  other arithmetic: 1.96 us -> 0.06 us
  local copies, waits for them, and re-layouts: 1.85 us -> 1.07 us
    ppermute x2, waiting for transfers between devices: 20.1 us -> 7.31 us  [line_window(): far = lax.ppermute(own, 'src', [(0, 3), (1, 2), (2, 1), (3, 0)])]
    ppermute x2, starting transfers between devices: 8.9 us -> 16.7 us  [line_window(): across = lax.ppermute(onward, 'src', [(0, 2), (2, 3), (3, 1), (1, 0)])]
    ppermute x3, waiting for transfers between devices: 0.01 us -> 2.18 us  [swap(): return lax.ppermute(x, axis, [(i, i ^ bit) for i in range(peers)])]
    pallas_call x2 -> x3, Pallas kernels: 7.73 us -> 9.84 us  [the longest x1 4.08 us: body(): pl.pallas_call(functools.partial(kernel_a, half, [{k: at for k, (_, at) i...]
    select_n x2, other arithmetic: 1.96 us -> 0.06 us  [line_window(): onward = jnp.where(at_end(), own, far)]
    ppermute x1, starting transfers between devices: 1.58 us -> 0.01 us  [line_window(): near = lax.ppermute(data, 'src', [(0, 1), (1, 0), (2, 3), (3, 2)])]
    slice x1, local copies, waits for them, and re-layouts: 1.84 us -> 1.06 us  [line_window(): data[v:v + 1]]
    ppermute x2, waiting for transfers between devices: 1.83 us -> 1.21 us  [line_window(): across = lax.ppermute(onward, 'src', [(0, 2), (2, 3), (3, 1), (1, 0)])]
  transfers between devices with their start and end apart: 8 -> 8, of which waited for: 3 -> 3; matrix products, arithmetic and copies ran while one was open for 7% -> 2% of each run, Pallas kernels for 6% -> 16%
where the time goes in v10:
time: 45.5 us; the launch traced here: 45.3 us
  starting transfers between devices  23.6 us (52%)
  waiting for transfers between devices  10.7 us (24%)
  Pallas kernels  9.84 us (22%)
  local copies, waits for them, and re-layouts  1.07 us (2%)
    ppermute x2, starting transfers between devices, line_window(): across = lax.ppermute(onward, 'src', [(0, 2), (2, 3), (3, 1), (1, 0)])  16.7 us
    ppermute x2, waiting for transfers between devices, line_window(): far = lax.ppermute(own, 'src', [(0, 3), (1, 2), (2, 1), (3, 0)])  7.31 us
    pallas_call x1, Pallas kernels, body(): pl.pallas_call(functools.partial(kernel_a, half, [{k: at for k, (_, at) i...  4.08 us
    ppermute x2, starting transfers between devices, line_window(): far = lax.ppermute(own, 'src', [(0, 3), (1, 2), (2, 1), (3, 0)])  3.89 us
    pallas_call x1, Pallas kernels, body(): pl.pallas_call(functools.partial(kernel_b, half, late), out_shape=[window...  3.02 us
    ppermute x3, starting transfers between devices, swap(): return lax.ppermute(x, axis, [(i, i ^ bit) for i in range(peers)])  3.02 us
    pallas_call x1, Pallas kernels, body(): pl.pallas_call(functools.partial(last_kernel, half + 1, late), out_shape=...  2.73 us
    ppermute x3, waiting for transfers between devices, swap(): return lax.ppermute(x, axis, [(i, i ^ bit) for i in range(peers)])  2.18 us
  transfers between devices with their start and end apart: 8, of which 3 were waited for; matrix products, arithmetic and copies ran while one was open for 2% of the time, Pallas kernels for 16%

profile of v10, /device:TPU:0, one launch (start us, length us, event | category | flops | bytes accessed | tf_op | source)
XLA Modules:
  0.0 45.3 jit_solution(156338554321123169)
XLA Ops:
  0.0 0.0 copy-start
  0.0 0.0 copy-start.1
  0.0 0.5 collective-permute-start.4
  0.5 2.6 %collective-permute-start.6 = (bf16[2,2,256,768]{3,2,1,0:T(8,128)(2,1)}, bf16[2,2,256,768]{3,2,1,0:T(8,128)(2,1)}, u32[]{:S(2)}, u32[]{:S(2)}) collective-permute-start(bf16[2,2,256,768]{3,2,1,0:T(8,128)(2,1)} %refs_0_.1), channel_id=1, source_target_pairs={{0,2},{1,3},{2,0},{3,1},{4,6},{5,7},{6,4},{7,5},{8,10},{9,11},{10,... | collective-permute-start | bytes 4718600 | tf_op jit(solution)/shard_map/ppermute | solution.py:27
  3.0 1.1 %fusion = (bf16[1,2,256,256]{3,2,1,0:T(8,128)(2,1)S(1)}, bf16[1,2,256,256]{3,2,1,0:T(8,128)(2,1)S(1)}) fusion(bf16[2,2,256,256]{3,2,1,0:T(8,128)(2,1)} %param.4), kind=kLoop, calls=%fused_computation.2 | loop fusion | bytes 1048576 | tf_op jit(solution)/shard_map/slice | solution.py:37
  4.1 3.7 %collective-permute-start.2 = (bf16[1,2,256,256]{3,2,1,0:T(8,128)(2,1)S(1)}, bf16[1,2,256,256]{3,2,1,0:T(8,128)(2,1)S(1)}, u32[]{:S(2)}, u32[]{:S(2)}) collective-permute-start(bf16[1,2,256,256]{3,2,1,0:T(8,128)(2,1)S(1)} %get-tuple-element.20.refs_2_), channel_id=1, source_target_pairs={{0,12},{4,8},{8,4},{12,0},{1,13},{5,9},{9,5},{13,1},{2,14},{6,10},... | collective-permute-start | bytes 786440 | tf_op jit(solution)/shard_map/ppermute | solution.py:38
  7.8 0.2 collective-permute-start
  8.0 0.0 collective-permute-start.5
  8.0 7.3 %collective-permute-done.2.refs_4_ = bf16[1,2,256,256]{3,2,1,0:T(8,128)(2,1)S(1)} collective-permute-done((bf16[1,2,256,256]{3,2,1,0:T(8,128)(2,1)S(1)}, bf16[1,2,256,256]{3,2,1,0:T(8,128)(2,1)S(1)}, u32[]{:S(2)}, u32[]{:S(2)}) %collective-permute-start.2) | collective-permute-done | bytes 262176 | tf_op jit(solution)/shard_map/ppermute | solution.py:38
  15.3 11.9 %collective-permute-start.3 = (bf16[1,2,256,256]{3,2,1,0:T(8,128)(2,1)S(1)}, bf16[1,2,256,256]{3,2,1,0:T(8,128)(2,1)S(1)}, u32[]{:S(2)}, u32[]{:S(2)}) collective-permute-start(bf16[1,2,256,256]{3,2,1,0:T(8,128)(2,1)S(1)} %broadcast_select_fusion), channel_id=1, source_target_pairs={{0,8},{8,12},{12,4},{4,0},{1,9},{9,13},{13,5},{5,1},{2,10},{10,14}... | collective-permute-start | bytes 786440 | tf_op jit(solution)/shard_map/ppermute | solution.py:40
  27.2 0.0 collective-permute-done.refs_7_
  27.2 4.8 %collective-permute-start.1 = (bf16[1,2,256,256]{3,2,1,0:T(8,128)(2,1)S(1)}, bf16[1,2,256,256]{3,2,1,0:T(8,128)(2,1)S(1)}, u32[]{:S(2)}, u32[]{:S(2)}) collective-permute-start(bf16[1,2,256,256]{3,2,1,0:T(8,128)(2,1)S(1)} %broadcast_select_fusion.1), channel_id=1, source_target_pairs={{0,8},{8,12},{12,4},{4,0},{1,9},{9,13},{13,5},{5,1},{2,10},{10,14}... | collective-permute-start | bytes 786440 | tf_op jit(solution)/shard_map/ppermute | solution.py:40
  32.0 0.0 collective-permute-done.5.refs_3_.refs_6_
  32.0 0.0 collective-permute-done.4.refs_1_
  32.1 0.0 copy-done
  32.1 0.0 copy-done.1
  32.1 4.1 %shard_map.37 = (bf16[4,256,512]{2,1,0:T(8,128)(2,1)S(1)}, bf16[4,256,512]{2,1,0:T(8,128)(2,1)S(1)}, f32[512,256]{1,0:T(8,128)S(1)}, f32[512,256]{1,0:T(8,128)S(...) custom-call(s32[4,12]{1,0:T(4,128)S(1)} %copy-done.1, bf16[2,2,256,768]{3,2,1,0:T(8,128)(2,1)S(1)} %copy-done, ...), custom_call_target="tpu_custom_call" | custom-call | flops 161061280 | bytes 1048576 | tf_op jit(solution)/shard_map/pallas_call | solution.py:211
  36.2 2.2 %collective-permute-done.6.panel_ref = bf16[2,2,256,768]{3,2,1,0:T(8,128)(2,1)} collective-permute-done((bf16[2,2,256,768]{3,2,1,0:T(8,128)(2,1)}, bf16[2,2,256,768]{3,2,1,0:T(8,128)(2,1)}, u32[]{:S(2)}, u32[]{:S(2)}) %collective-permute-start.6) | collective-permute-done | bytes 1572896 | tf_op jit(solution)/shard_map/ppermute | solution.py:27
  38.3 0.0 collective-permute-start.7
  38.3 0.0 collective-permute-done.3.late_ref
  38.3 3.0 %shard_map.38 = (bf16[4,256,512]{2,1,0:T(8,128)(2,1)S(1)}, bf16[512,512]{1,0:T(8,128)(2,1)S(1)}, f32[2,256,256]{2,1,0:T(8,128)S(1)}, f32[2,256,256]{2,1,0:T(8,128)S(1)}) custom-call(s32[4,12]{1,0:T(4,128)S(1)} %copy-done.1, bf16[1,2,256,256]{3,2,1,0:T(8,128)(2,1)S(1)} %collective-permute-done.3.late_ref, ...), custom_call_target="tpu_custom_call", output_to_operand_aliasing={{0}: (2, {}), {2}: (6, {}), {3}: (7, {})} | custom-call | flops 161061280 | bytes 1048576 | tf_op jit(solution)/shard_map/pallas_call | solution.py:221
  41.4 1.2 %collective-permute-done.1.piece_ref = bf16[1,2,256,256]{3,2,1,0:T(8,128)(2,1)S(1)} collective-permute-done((bf16[1,2,256,256]{3,2,1,0:T(8,128)(2,1)S(1)}, bf16[1,2,256,256]{3,2,1,0:T(8,128)(2,1)S(1)}, u32[]{:S(2)}, u32[]{:S(2)}) %collective-permute-start.1) | collective-permute-done | bytes 262176 | tf_op jit(solution)/shard_map/ppermute | solution.py:40
  42.6 0.0 collective-permute-done.7.refs_0_
  42.6 2.7 %shard_map.40 = (f32[2,2,256,256]{3,2,1,0:T(8,128)}, bf16[4,256,512]{2,1,0:T(8,128)(2,1)S(1)}) custom-call(s32[4,12]{1,0:T(4,128)S(1)} %copy-done.1, bf16[1,2,256,256]{3,2,1,0:T(8,128)(2,1)S(1)} %shard_map.39.late_ref, bf16[4,256,512]{2,1,0:T(8,128)(2,1)S(1)} %get-tuple-element.28.first_window, ...), custom_call_target="tpu_custom_call", output_to_operand_aliasing={{1}: (3, {})} | custom-call | flops 1610612736 | bytes 1048576 | tf_op jit(solution)/shard_map/pallas_call | solution.py:231
  (3 shorter events, 0.1 us)
Async XLA Ops:
  0.0 32.1 %copy-start = (bf16[2,2,256,768]{3,2,1,0:T(8,128)(2,1)S(1)}, bf16[2,2,256,768]{3,2,1,0:T(8,128)(2,1)}, u32[]{:S(2)}) copy-start(bf16[2,2,256,768]{3,2,1,0:T(8,128)(2,1)} %refs_0_.1) | copy-start | bytes 4718596
  0.0 32.1 %copy-start.1 = (s32[4,12]{1,0:T(4,128)S(1)}, s32[4,12]{1,0:T(4,128)}, u32[]{:S(2)}) copy-start(s32[4,12]{1,0:T(4,128)} %aperture_ref.5) | copy-start | bytes 580
  0.0 32.0 %collective-permute-start.4 = (bf16[2,2,256,768]{3,2,1,0:T(8,128)(2,1)}, bf16[2,2,256,768]{3,2,1,0:T(8,128)(2,1)}, u32[]{:S(2)}, u32[]{:S(2)}) collective-permute-start(bf16[2,2,256,768]{3,2,1,0:T(8,128)(2,1)} %refs_0_.1), channel_id=1, source_target_pairs={{0,1},{1,0},{2,3},{3,2},{4,5},{5,4},{6,7},{7,6},{8,9},{9,8},{10,11... | collective-permute-start | bytes 4718600 | tf_op jit(solution)/shard_map/ppermute | solution.py:27
  0.5 37.9 %collective-permute-start.6 = (bf16[2,2,256,768]{3,2,1,0:T(8,128)(2,1)}, bf16[2,2,256,768]{3,2,1,0:T(8,128)(2,1)}, u32[]{:S(2)}, u32[]{:S(2)}) collective-permute-start(bf16[2,2,256,768]{3,2,1,0:T(8,128)(2,1)} %refs_0_.1), channel_id=1, source_target_pairs={{0,2},{1,3},{2,0},{3,1},{4,6},{5,7},{6,4},{7,5},{8,10},{9,11},{10,... | collective-permute-start | bytes 4718600 | tf_op jit(solution)/shard_map/ppermute | solution.py:27
  4.1 11.2 %collective-permute-start.2 = (bf16[1,2,256,256]{3,2,1,0:T(8,128)(2,1)S(1)}, bf16[1,2,256,256]{3,2,1,0:T(8,128)(2,1)S(1)}, u32[]{:S(2)}, u32[]{:S(2)}) collective-permute-start(bf16[1,2,256,256]{3,2,1,0:T(8,128)(2,1)S(1)} %get-tuple-element.20.refs_2_), channel_id=1, source_target_pairs={{0,12},{4,8},{8,4},{12,0},{1,13},{5,9},{9,5},{13,1},{2,14},{6,10},... | collective-permute-start | bytes 786440 | tf_op jit(solution)/shard_map/ppermute | solution.py:38
  7.8 19.5 %collective-permute-start = (bf16[1,2,256,256]{3,2,1,0:T(8,128)(2,1)S(1)}, bf16[1,2,256,256]{3,2,1,0:T(8,128)(2,1)S(1)}, u32[]{:S(2)}, u32[]{:S(2)}) collective-permute-start(bf16[1,2,256,256]{3,2,1,0:T(8,128)(2,1)S(1)} %get-tuple-element.19.refs_5_), channel_id=1, source_target_pairs={{0,12},{4,8},{8,4},{12,0},{1,13},{5,9},{9,5},{13,1},{2,14},{6,10},... | collective-permute-start | bytes 786440 | tf_op jit(solution)/shard_map/ppermute | solution.py:38
  8.0 24.1 %collective-permute-start.5 = (bf16[2,2,256,256]{3,2,1,0:T(8,128)(2,1)}, bf16[2,2,256,256]{3,2,1,0:T(8,128)(2,1)S(1)}, u32[]{:S(2)}, u32[]{:S(2)}) collective-permute-start(bf16[2,2,256,256]{3,2,1,0:T(8,128)(2,1)} %param.4), channel_id=1, source_target_pairs={{0,4},{4,0},{8,12},{12,8},{1,5},{5,1},{9,13},{13,9},{2,6},{6,2},{1... | collective-permute-start | bytes 1572872 | tf_op jit(solution)/shard_map/ppermute | solution.py:35
  15.3 23.0 %collective-permute-start.3 = (bf16[1,2,256,256]{3,2,1,0:T(8,128)(2,1)S(1)}, bf16[1,2,256,256]{3,2,1,0:T(8,128)(2,1)S(1)}, u32[]{:S(2)}, u32[]{:S(2)}) collective-permute-start(bf16[1,2,256,256]{3,2,1,0:T(8,128)(2,1)S(1)} %broadcast_select_fusion), channel_id=1, source_target_pairs={{0,8},{8,12},{12,4},{4,0},{1,9},{9,13},{13,5},{5,1},{2,10},{10,14}... | collective-permute-start | bytes 786440 | tf_op jit(solution)/shard_map/ppermute | solution.py:40
  27.2 15.3 %collective-permute-start.1 = (bf16[1,2,256,256]{3,2,1,0:T(8,128)(2,1)S(1)}, bf16[1,2,256,256]{3,2,1,0:T(8,128)(2,1)S(1)}, u32[]{:S(2)}, u32[]{:S(2)}) collective-permute-start(bf16[1,2,256,256]{3,2,1,0:T(8,128)(2,1)S(1)} %broadcast_select_fusion.1), channel_id=1, source_target_pairs={{0,8},{8,12},{12,4},{4,0},{1,9},{9,13},{13,5},{5,1},{2,10},{10,14}... | collective-permute-start | bytes 786440 | tf_op jit(solution)/shard_map/ppermute | solution.py:40
  38.3 4.2 %collective-permute-start.7 = (bf16[2,2,256,768]{3,2,1,0:T(8,128)(2,1)}, bf16[2,2,256,768]{3,2,1,0:T(8,128)(2,1)S(1)}, u32[]{:S(2)}, u32[]{:S(2)}) collective-permute-start(bf16[2,2,256,768]{3,2,1,0:T(8,128)(2,1)} %collective-permute-done.6.panel_ref), channel_id=1, source_target_pairs={{0,1},{1,0},{2,3},{3,2},{4,5},{5,4},{6,7},{7,6},{8,9},{9,8},{10,11... | collective-permute-start | bytes 4718600 | tf_op jit(solution)/shard_map/ppermute | solution.py:27

commit v11 on v10

--- a/solution.py
+++ b/solution.py
@@ -31,18 +31,19 @@
     return (lax.axis_index("src") + 1) % lax.axis_size("src") < 2
 
 
-def line_window(data):
-    near = lax.ppermute(data, "src", [(0, 1), (1, 0), (2, 3), (3, 2)])
+def line_window(data, others):
     windows = []
     for v, own in enumerate(lax.optimization_barrier([data[v : v + 1] for v in range(data.shape[0])])):
-        far = lax.ppermute(own, "src", [(0, 3), (1, 2), (2, 1), (3, 0)])
-        onward = jnp.where(at_end(), own, far)
+        begun = own if v == 0 else after(own, *others)
+        near = lax.ppermute(begun, "src", [(0, 1), (1, 0), (2, 3), (3, 2)])
+        far = lax.ppermute(begun, "src", [(0, 3), (1, 2), (2, 1), (3, 0)])
+        onward = jnp.where(at_end(), after(own, near), far)
         across = lax.ppermute(onward, "src", [(0, 2), (2, 3), (3, 1), (1, 0)])
-        windows.append([(own, 0), (near, v), (across, 0), (far, 0)])
+        windows.append([(own, 0), (near, 0), (across, 0), (far, 0)])
     return windows
 
 
-def hop_window(data):
+def hop_window(data, others):
     reach = min(HW, lax.axis_size("src") - 1)
     window = {0: data}
     for hop in range(1, reach + 1):
@@ -135,17 +136,20 @@
         sums[v][...] = sum_of_late(aperture_ref, panels, late, window.shape[0])
 
 
-def kernel_b(m, late, aperture_ref, late_ref, _, last_window, first_sum, last_sum, first_in, last_in, panel_ref, *refs):
-    window, two, first_part, last_part = refs
+def kernel_b(late, late_ref, _, first_sum, first_in, window, first_part):
     fill_window(window, {late: late_ref.at[0]})
-    real, imag = product(window, aperture_ref, {m: panel_ref.at[0]})
-    late_real, late_imag = add_late(in_two(first_sum[...]), window, late)
-    first_part[0] = first_in[0] + (real + late_real)
-    first_part[1] = first_in[1] + (imag + late_imag)
+    real, imag = add_late(in_two(first_sum[...]), window, late)
+    first_part[0] = first_in[0] + real
+    first_part[1] = first_in[1] + imag
+
+
+def kernel_c(m, late, aperture_ref, first_window, last_window, last_sum, first_in, last_in, panel_ref, *refs):
+    two, *parts = refs
+    for v, (window, part_in, part) in enumerate(zip((first_window, last_window), (first_in, last_in), parts)):
+        real, imag = product(window, aperture_ref, {m: panel_ref.at[v]})
+        part[0] = part_in[0] + real
+        part[1] = part_in[1] + imag
     panels = {m: panel_ref.at[1]}
-    real, imag = product(last_window, aperture_ref, panels)
-    last_part[0] = last_in[0] + real
-    last_part[1] = last_in[1] + imag
     two[...] = in_two(last_sum[...] + sum_of_late(aperture_ref, panels, late, last_window.shape[0]))
 
 
@@ -196,9 +200,9 @@
 def body(primaries, data, aperture):
     width = data.shape[3]
     line = lax.axis_size("src") == 4
-    windows = (line_window if line else hop_window)(data)
     panels, far_panel = gather_panels(primaries)
     half = len(panels)
+    windows = (line_window if line else hop_window)(data, panels[1:])
     late = 2 if line else len(windows[0]) - 1
     late_pieces = [piece[at : at + 1] for piece, at in (window[late] for window in windows)]
     early = [{k: piece for k, piece in enumerate(window) if k != late} for window in windows]
@@ -217,16 +221,26 @@
         cost_estimate=cost(0.1),
     )(aperture, *panels, *pieces)
 
+    first, first_part = pl.pallas_call(
+        functools.partial(kernel_b, late),
+        out_shape=[window, part],
+        in_specs=[vmem] * 4,
+        out_specs=[vmem] * 2,
+        input_output_aliases={1: 0, 3: 1},
+        compiler_params=limit(16),
+        cost_estimate=cost(0.1),
+    )(late_pieces[0], first, first_sum, first_part)
+
     handed_on = hand_on(far_panel, first_part)
-    first, two, first_part, last_part = pl.pallas_call(
-        functools.partial(kernel_b, half, late),
-        out_shape=[window, jax.ShapeDtypeStruct((2 * BLK, 2 * BLK), jnp.bfloat16), part, part],
-        in_specs=[smem] + [vmem] * 8,
-        out_specs=[vmem] * 4,
-        input_output_aliases={2: 0, 6: 2, 7: 3},
+    two, first_part, last_part = pl.pallas_call(
+        functools.partial(kernel_c, half, late),
+        out_shape=[jax.ShapeDtypeStruct((2 * BLK, 2 * BLK), jnp.bfloat16), part, part],
+        in_specs=[smem] + [vmem] * 6,
+        out_specs=[vmem] * 3,
+        input_output_aliases={4: 1, 5: 2},
         compiler_params=limit(16),
         cost_estimate=cost(0.1),
-    )(aperture, late_pieces[0], first, last, first_sum, last_sum, first_part, last_part, far_panel)
+    )(aperture, first, last, last_sum, first_part, last_part, far_panel)
 
     return pl.pallas_call(
         functools.partial(last_kernel, half + 1, late),

time: 45.5 us -> 50.8 us (1.12)
  waiting for transfers between devices: 10.7 us -> 20 us
  starting transfers between devices: 23.6 us -> 17.6 us
  local copies, waits for them, and re-layouts: 1.07 us -> 3.62 us
  Pallas kernels: 9.84 us -> 9.2 us
    ppermute x3 -> x4, waiting for transfers between devices: 7.31 us -> 19.2 us  [the longest x2 15.5 us: line_window(): far = lax.ppermute(begun, 'src', [(0, 3), (1, 2), (2, 1), (3, 0)])]
    ppermute x2, starting transfers between devices: 16.7 us -> 8.81 us  [line_window(): across = lax.ppermute(onward, 'src', [(0, 2), (2, 3), (3, 1), (1, 0)])]
    unnamed x4 -> x8, local copies, waits for them, and re-layouts: 0.01 us -> 2.56 us
    ppermute x3 -> x4, starting transfers between devices: 3.89 us -> 5.7 us  [the longest x2 3.38 us: line_window(): far = lax.ppermute(begun, 'src', [(0, 3), (1, 2), (2, 1), (3, 0)])]
    ppermute x3, waiting for transfers between devices: 2.18 us -> 0.89 us  [swap(): return lax.ppermute(x, axis, [(i, i ^ bit) for i in range(peers)])]
    ppermute x2, waiting for transfers between devices: 1.21 us -> 0.01 us  [line_window(): across = lax.ppermute(onward, 'src', [(0, 2), (2, 3), (3, 1), (1, 0)])]
    pallas_call x1, Pallas kernels: 4.08 us -> 3.3 us  [body(): pl.pallas_call(functools.partial(kernel_a, half, [{k: at for k, (_, at) i...]
    pallas_call x1 -> x2, Pallas kernels: 3.02 us -> 3.17 us  [the longest x1 2.7 us: body(): pl.pallas_call(functools.partial(kernel_c, half, late), out_shape=[jax.Sh...]
  transfers between devices with their start and end apart: 8 -> 9, of which waited for: 3 -> 5; matrix products, arithmetic and copies ran while one was open for 2% -> 2% of each run, Pallas kernels for 16% -> 13%
where the time goes in v11:
time: 50.8 us; the launch traced here: 50.6 us
  waiting for transfers between devices  20 us (39%)
  starting transfers between devices  17.6 us (35%)
  Pallas kernels  9.2 us (18%)
  local copies, waits for them, and re-layouts  3.62 us (7%)
    ppermute x2, waiting for transfers between devices, line_window(): far = lax.ppermute(begun, 'src', [(0, 3), (1, 2), (2, 1), (3, 0)])  15.5 us
    ppermute x2, starting transfers between devices, line_window(): across = lax.ppermute(onward, 'src', [(0, 2), (2, 3), (3, 1), (1, 0)])  8.81 us
    ppermute x2, waiting for transfers between devices, line_window(): near = lax.ppermute(begun, 'src', [(0, 1), (1, 0), (2, 3), (3, 2)])  3.7 us
    ppermute x2, starting transfers between devices, line_window(): far = lax.ppermute(begun, 'src', [(0, 3), (1, 2), (2, 1), (3, 0)])  3.38 us
    pallas_call x1, Pallas kernels, body(): pl.pallas_call(functools.partial(kernel_a, half, [{k: at for k, (_, at) i...  3.3 us
    ppermute x3, starting transfers between devices, swap(): return lax.ppermute(x, axis, [(i, i ^ bit) for i in range(peers)])  3.08 us
    pallas_call x1, Pallas kernels, body(): pl.pallas_call(functools.partial(last_kernel, half + 1, late), out_shape=...  2.73 us
    pallas_call x1, Pallas kernels, body(): pl.pallas_call(functools.partial(kernel_c, half, late), out_shape=[jax.Sh...  2.7 us
  transfers between devices with their start and end apart: 9, of which 5 were waited for; matrix products, arithmetic and copies ran while one was open for 2% of the time, Pallas kernels for 13%

profile of v11, /device:TPU:0, one launch (start us, length us, event | category | flops | bytes accessed | tf_op | source)
XLA Modules:
  0.0 50.6 jit_solution(10104112344601341664)
XLA Ops:
  0.0 0.0 copy-start
  0.0 0.0 copy-start.3
  0.0 0.5 collective-permute-start
  0.5 2.6 %collective-permute-start.7 = (bf16[2,2,256,768]{3,2,1,0:T(8,128)(2,1)}, bf16[2,2,256,768]{3,2,1,0:T(8,128)(2,1)}, u32[]{:S(2)}, u32[]{:S(2)}) collective-permute-start(bf16[2,2,256,768]{3,2,1,0:T(8,128)(2,1)} %refs_0_.1), channel_id=1, source_target_pairs={{0,2},{1,3},{2,0},{3,1},{4,6},{5,7},{6,4},{7,5},{8,10},{9,11},{10,... | collective-permute-start | bytes 4718600 | tf_op jit(solution)/shard_map/ppermute | solution.py:27
  3.0 1.1 %fusion = (bf16[1,2,256,256]{3,2,1,0:T(8,128)(2,1)S(1)}, bf16[1,2,256,256]{3,2,1,0:T(8,128)(2,1)S(1)}) fusion(bf16[2,2,256,256]{3,2,1,0:T(8,128)(2,1)} %param.4), kind=kLoop, calls=%fused_computation.2 | loop fusion | bytes 1048576 | tf_op jit(solution)/shard_map/slice | solution.py:36
  4.1 1.6 %collective-permute-start.4 = (bf16[1,2,256,256]{3,2,1,0:T(8,128)(2,1)S(1)}, bf16[1,2,256,256]{3,2,1,0:T(8,128)(2,1)S(1)}, u32[]{:S(2)}, u32[]{:S(2)}) collective-permute-start(bf16[1,2,256,256]{3,2,1,0:T(8,128)(2,1)S(1)} %get-tuple-element.27.refs_2_), channel_id=1, source_target_pairs={{0,4},{4,0},{8,12},{12,8},{1,5},{5,1},{9,13},{13,9},{2,6},{6,2},{1... | collective-permute-start | bytes 786440 | tf_op jit(solution)/shard_map/ppermute | solution.py:38
  5.7 2.5 %collective-permute-start.5 = (bf16[1,2,256,256]{3,2,1,0:T(8,128)(2,1)S(1)}, bf16[1,2,256,256]{3,2,1,0:T(8,128)(2,1)S(1)}, u32[]{:S(2)}, u32[]{:S(2)}) collective-permute-start(bf16[1,2,256,256]{3,2,1,0:T(8,128)(2,1)S(1)} %get-tuple-element.27.refs_2_), channel_id=1, source_target_pairs={{0,12},{4,8},{8,4},{12,0},{1,13},{5,9},{9,5},{13,1},{2,14},{6,10},... | collective-permute-start | bytes 786440 | tf_op jit(solution)/shard_map/ppermute | solution.py:39
  8.2 0.0 collective-permute-done.refs_1_
  8.2 0.0 copy-start.1
  8.2 1.1 %copy-done.1 = bf16[2,2,256,768]{3,2,1,0:T(8,128)(2,1)} copy-done((bf16[2,2,256,768]{3,2,1,0:T(8,128)(2,1)}, bf16[2,2,256,768]{3,2,1,0:T(8,128)(2,1)S(1)}, u32[]{:S(2)}) %copy-start.1) | copy-done | bytes 1572888
  9.3 0.7 %collective-permute-start.1 = (bf16[1,2,256,256]{3,2,1,0:T(8,128)(2,1)S(1)}, bf16[1,2,256,256]{3,2,1,0:T(8,128)(2,1)S(1)}, u32[]{:S(2)}, u32[]{:S(2)}) collective-permute-start(bf16[1,2,256,256]{3,2,1,0:T(8,128)(2,1)S(1)} %get-tuple-element.25.refs_5_), channel_id=1, source_target_pairs={{0,4},{4,0},{8,12},{12,8},{1,5},{5,1},{9,13},{13,9},{2,6},{6,2},{1... | collective-permute-start | bytes 786440 | tf_op jit(solution)/shard_map/ppermute | solution.py:38
  10.0 0.9 %collective-permute-start.2 = (bf16[1,2,256,256]{3,2,1,0:T(8,128)(2,1)S(1)}, bf16[1,2,256,256]{3,2,1,0:T(8,128)(2,1)S(1)}, u32[]{:S(2)}, u32[]{:S(2)}) collective-permute-start(bf16[1,2,256,256]{3,2,1,0:T(8,128)(2,1)S(1)} %get-tuple-element.25.refs_5_), channel_id=1, source_target_pairs={{0,12},{4,8},{8,4},{12,0},{1,13},{5,9},{9,5},{13,1},{2,14},{6,10},... | collective-permute-start | bytes 786440 | tf_op jit(solution)/shard_map/ppermute | solution.py:39
  10.9 2.4 %collective-permute-done.4.refs_3_ = bf16[1,2,256,256]{3,2,1,0:T(8,128)(2,1)S(1)} collective-permute-done((bf16[1,2,256,256]{3,2,1,0:T(8,128)(2,1)S(1)}, bf16[1,2,256,256]{3,2,1,0:T(8,128)(2,1)S(1)}, u32[]{:S(2)}, u32[]{:S(2)}) %collective-permute-start.4) | collective-permute-done | bytes 262176 | tf_op jit(solution)/shard_map/ppermute | solution.py:38
  13.3 7.7 %collective-permute-done.5.refs_4_ = bf16[1,2,256,256]{3,2,1,0:T(8,128)(2,1)S(1)} collective-permute-done((bf16[1,2,256,256]{3,2,1,0:T(8,128)(2,1)S(1)}, bf16[1,2,256,256]{3,2,1,0:T(8,128)(2,1)S(1)}, u32[]{:S(2)}, u32[]{:S(2)}) %collective-permute-start.5) | collective-permute-done | bytes 262176 | tf_op jit(solution)/shard_map/ppermute | solution.py:39
  21.0 2.2 %collective-permute-start.6 = (bf16[1,2,256,256]{3,2,1,0:T(8,128)(2,1)S(1)}, bf16[1,2,256,256]{3,2,1,0:T(8,128)(2,1)S(1)}, u32[]{:S(2)}, u32[]{:S(2)}) collective-permute-start(bf16[1,2,256,256]{3,2,1,0:T(8,128)(2,1)S(1)} %broadcast_select_fusion), channel_id=1, source_target_pairs={{0,8},{8,12},{12,4},{4,0},{1,9},{9,13},{13,5},{5,1},{2,10},{10,14}... | collective-permute-start | bytes 786440 | tf_op jit(solution)/shard_map/ppermute | solution.py:41
  23.2 1.3 %collective-permute-done.1.refs_6_ = bf16[1,2,256,256]{3,2,1,0:T(8,128)(2,1)S(1)} collective-permute-done((bf16[1,2,256,256]{3,2,1,0:T(8,128)(2,1)S(1)}, bf16[1,2,256,256]{3,2,1,0:T(8,128)(2,1)S(1)}, u32[]{:S(2)}, u32[]{:S(2)}) %collective-permute-start.1) | collective-permute-done | bytes 262176 | tf_op jit(solution)/shard_map/ppermute | solution.py:38
  24.5 7.8 %collective-permute-done.2.refs_7_ = bf16[1,2,256,256]{3,2,1,0:T(8,128)(2,1)S(1)} collective-permute-done((bf16[1,2,256,256]{3,2,1,0:T(8,128)(2,1)S(1)}, bf16[1,2,256,256]{3,2,1,0:T(8,128)(2,1)S(1)}, u32[]{:S(2)}, u32[]{:S(2)}) %collective-permute-start.2) | collective-permute-done | bytes 262176 | tf_op jit(solution)/shard_map/ppermute | solution.py:39
  32.3 6.6 %collective-permute-start.3 = (bf16[1,2,256,256]{3,2,1,0:T(8,128)(2,1)S(1)}, bf16[1,2,256,256]{3,2,1,0:T(8,128)(2,1)S(1)}, u32[]{:S(2)}, u32[]{:S(2)}) collective-permute-start(bf16[1,2,256,256]{3,2,1,0:T(8,128)(2,1)S(1)} %broadcast_select_fusion.1), channel_id=1, source_target_pairs={{0,8},{8,12},{12,4},{4,0},{1,9},{9,13},{13,5},{5,1},{2,10},{10,14}... | collective-permute-start | bytes 786440 | tf_op jit(solution)/shard_map/ppermute | solution.py:41
  39.0 0.0 copy-done
  39.0 0.0 copy-done.3
  39.0 0.0 copy-start.2
  39.0 1.4 %copy-done.2 = bf16[2,2,256,768]{3,2,1,0:T(8,128)(2,1)S(1)} copy-done((bf16[2,2,256,768]{3,2,1,0:T(8,128)(2,1)S(1)}, bf16[2,2,256,768]{3,2,1,0:T(8,128)(2,1)}, u32[]{:S(2)}) %copy-start.2) | copy-done | bytes 1572888
  40.4 3.3 %shard_map.37 = (bf16[4,256,512]{2,1,0:T(8,128)(2,1)S(1)}, bf16[4,256,512]{2,1,0:T(8,128)(2,1)S(1)}, f32[512,256]{1,0:T(8,128)S(1)}, f32[512,256]{1,0:T(8,128)S(...) custom-call(s32[4,12]{1,0:T(4,128)S(1)} %copy-done.3, bf16[2,2,256,768]{3,2,1,0:T(8,128)(2,1)S(1)} %copy-done, ...), custom_call_target="tpu_custom_call" | custom-call | flops 161061280 | bytes 1048576 | tf_op jit(solution)/shard_map/pallas_call | solution.py:215
  43.7 0.0 collective-permute-done.6.late_ref
  43.7 0.5 shard_map.38
  44.2 0.0 collective-permute-done.7.panel_ref
  44.2 0.1 collective-permute-start.8
  44.3 2.7 %shard_map.39 = (bf16[512,512]{1,0:T(8,128)(2,1)S(1)}, f32[2,256,256]{2,1,0:T(8,128)S(1)}, f32[2,256,256]{2,1,0:T(8,128)S(1)}) custom-call(s32[4,12]{1,0:T(4,128)S(1)} %copy-done.3, bf16[4,256,512]{2,1,0:T(8,128)(2,1)S(1)} %get-tuple-element.31.first_window, ...), custom_call_target="tpu_custom_call", output_to_operand_aliasing={{1}: (4, {}), {2}: (5, {})} | custom-call | flops 161061280 | bytes 1048576 | tf_op jit(solution)/shard_map/pallas_call | solution.py:235
  47.0 0.0 collective-permute-done.3.piece_ref
  47.0 0.9 %collective-permute-done.8.refs_0_ = bf16[2,2,256,768]{3,2,1,0:T(8,128)(2,1)S(1)} collective-permute-done((bf16[2,2,256,768]{3,2,1,0:T(8,128)(2,1)}, bf16[2,2,256,768]{3,2,1,0:T(8,128)(2,1)S(1)}, u32[]{:S(2)}, u32[]{:S(2)}) %collective-permute-start.8) | collective-permute-done | bytes 1572896 | tf_op jit(solution)/shard_map/ppermute | solution.py:27
  47.9 2.7 %shard_map.41 = (f32[2,2,256,256]{3,2,1,0:T(8,128)}, bf16[4,256,512]{2,1,0:T(8,128)(2,1)S(1)}) custom-call(s32[4,12]{1,0:T(4,128)S(1)} %copy-done.3, bf16[1,2,256,256]{3,2,1,0:T(8,128)(2,1)S(1)} %shard_map.40.late_ref, bf16[4,256,512]{2,1,0:T(8,128)(2,1)S(1)} %get-tuple-element.31.first_window, ...), custom_call_target="tpu_custom_call", output_to_operand_aliasing={{1}: (3, {})} | custom-call | flops 1610612736 | bytes 1048576 | tf_op jit(solution)/shard_map/pallas_call | solution.py:245
  (3 shorter events, 0.1 us)
Async XLA Ops:
  0.0 39.0 %copy-start = (bf16[2,2,256,768]{3,2,1,0:T(8,128)(2,1)S(1)}, bf16[2,2,256,768]{3,2,1,0:T(8,128)(2,1)}, u32[]{:S(2)}) copy-start(bf16[2,2,256,768]{3,2,1,0:T(8,128)(2,1)} %refs_0_.1) | copy-start | bytes 4718596
  0.0 39.0 %copy-start.3 = (s32[4,12]{1,0:T(4,128)S(1)}, s32[4,12]{1,0:T(4,128)}, u32[]{:S(2)}) copy-start(s32[4,12]{1,0:T(4,128)} %aperture_ref.5) | copy-start | bytes 580
  0.0 8.2 %collective-permute-start = (bf16[2,2,256,768]{3,2,1,0:T(8,128)(2,1)}, bf16[2,2,256,768]{3,2,1,0:T(8,128)(2,1)S(1)}, u32[]{:S(2)}, u32[]{:S(2)}) collective-permute-start(bf16[2,2,256,768]{3,2,1,0:T(8,128)(2,1)} %refs_0_.1), channel_id=1, source_target_pairs={{0,1},{1,0},{2,3},{3,2},{4,5},{5,4},{6,7},{7,6},{8,9},{9,8},{10,11... | collective-permute-start | bytes 4718600 | tf_op jit(solution)/shard_map/ppermute | solution.py:27
  0.5 43.7 %collective-permute-start.7 = (bf16[2,2,256,768]{3,2,1,0:T(8,128)(2,1)}, bf16[2,2,256,768]{3,2,1,0:T(8,128)(2,1)}, u32[]{:S(2)}, u32[]{:S(2)}) collective-permute-start(bf16[2,2,256,768]{3,2,1,0:T(8,128)(2,1)} %refs_0_.1), channel_id=1, source_target_pairs={{0,2},{1,3},{2,0},{3,1},{4,6},{5,7},{6,4},{7,5},{8,10},{9,11},{10,... | collective-permute-start | bytes 4718600 | tf_op jit(solution)/shard_map/ppermute | solution.py:27
  4.1 9.2 %collective-permute-start.4 = (bf16[1,2,256,256]{3,2,1,0:T(8,128)(2,1)S(1)}, bf16[1,2,256,256]{3,2,1,0:T(8,128)(2,1)S(1)}, u32[]{:S(2)}, u32[]{:S(2)}) collective-permute-start(bf16[1,2,256,256]{3,2,1,0:T(8,128)(2,1)S(1)} %get-tuple-element.27.refs_2_), channel_id=1, source_target_pairs={{0,4},{4,0},{8,12},{12,8},{1,5},{5,1},{9,13},{13,9},{2,6},{6,2},{1... | collective-permute-start | bytes 786440 | tf_op jit(solution)/shard_map/ppermute | solution.py:38
  5.7 15.3 %collective-permute-start.5 = (bf16[1,2,256,256]{3,2,1,0:T(8,128)(2,1)S(1)}, bf16[1,2,256,256]{3,2,1,0:T(8,128)(2,1)S(1)}, u32[]{:S(2)}, u32[]{:S(2)}) collective-permute-start(bf16[1,2,256,256]{3,2,1,0:T(8,128)(2,1)S(1)} %get-tuple-element.27.refs_2_), channel_id=1, source_target_pairs={{0,12},{4,8},{8,4},{12,0},{1,13},{5,9},{9,5},{13,1},{2,14},{6,10},... | collective-permute-start | bytes 786440 | tf_op jit(solution)/shard_map/ppermute | solution.py:39
  8.2 1.1 %copy-start.1 = (bf16[2,2,256,768]{3,2,1,0:T(8,128)(2,1)}, bf16[2,2,256,768]{3,2,1,0:T(8,128)(2,1)S(1)}, u32[]{:S(2)}) copy-start(bf16[2,2,256,768]{3,2,1,0:T(8,128)(2,1)S(1)} %collective-permute-done.refs_1_) | copy-start | bytes 4718596
  9.3 15.2 %collective-permute-start.1 = (bf16[1,2,256,256]{3,2,1,0:T(8,128)(2,1)S(1)}, bf16[1,2,256,256]{3,2,1,0:T(8,128)(2,1)S(1)}, u32[]{:S(2)}, u32[]{:S(2)}) collective-permute-start(bf16[1,2,256,256]{3,2,1,0:T(8,128)(2,1)S(1)} %get-tuple-element.25.refs_5_), channel_id=1, source_target_pairs={{0,4},{4,0},{8,12},{12,8},{1,5},{5,1},{9,13},{13,9},{2,6},{6,2},{1... | collective-permute-start | bytes 786440 | tf_op jit(solution)/shard_map/ppermute | solution.py:38
  10.0 22.3 %collective-permute-start.2 = (bf16[1,2,256,256]{3,2,1,0:T(8,128)(2,1)S(1)}, bf16[1,2,256,256]{3,2,1,0:T(8,128)(2,1)S(1)}, u32[]{:S(2)}, u32[]{:S(2)}) collective-permute-start(bf16[1,2,256,256]{3,2,1,0:T(8,128)(2,1)S(1)} %get-tuple-element.25.refs_5_), channel_id=1, source_target_pairs={{0,12},{4,8},{8,4},{12,0},{1,13},{5,9},{9,5},{13,1},{2,14},{6,10},... | collective-permute-start | bytes 786440 | tf_op jit(solution)/shard_map/ppermute | solution.py:39
  21.0 22.7 %collective-permute-start.6 = (bf16[1,2,256,256]{3,2,1,0:T(8,128)(2,1)S(1)}, bf16[1,2,256,256]{3,2,1,0:T(8,128)(2,1)S(1)}, u32[]{:S(2)}, u32[]{:S(2)}) collective-permute-start(bf16[1,2,256,256]{3,2,1,0:T(8,128)(2,1)S(1)} %broadcast_select_fusion), channel_id=1, source_target_pairs={{0,8},{8,12},{12,4},{4,0},{1,9},{9,13},{13,5},{5,1},{2,10},{10,14}... | collective-permute-start | bytes 786440 | tf_op jit(solution)/shard_map/ppermute | solution.py:41
  32.3 14.6 %collective-permute-start.3 = (bf16[1,2,256,256]{3,2,1,0:T(8,128)(2,1)S(1)}, bf16[1,2,256,256]{3,2,1,0:T(8,128)(2,1)S(1)}, u32[]{:S(2)}, u32[]{:S(2)}) collective-permute-start(bf16[1,2,256,256]{3,2,1,0:T(8,128)(2,1)S(1)} %broadcast_select_fusion.1), channel_id=1, source_target_pairs={{0,8},{8,12},{12,4},{4,0},{1,9},{9,13},{13,5},{5,1},{2,10},{10,14}... | collective-permute-start | bytes 786440 | tf_op jit(solution)/shard_map/ppermute | solution.py:41
  39.0 1.4 %copy-start.2 = (bf16[2,2,256,768]{3,2,1,0:T(8,128)(2,1)S(1)}, bf16[2,2,256,768]{3,2,1,0:T(8,128)(2,1)}, u32[]{:S(2)}) copy-start(bf16[2,2,256,768]{3,2,1,0:T(8,128)(2,1)} %copy-done.1) | copy-start | bytes 4718596
  44.2 3.7 %collective-permute-start.8 = (bf16[2,2,256,768]{3,2,1,0:T(8,128)(2,1)}, bf16[2,2,256,768]{3,2,1,0:T(8,128)(2,1)S(1)}, u32[]{:S(2)}, u32[]{:S(2)}) collective-permute-start(bf16[2,2,256,768]{3,2,1,0:T(8,128)(2,1)} %collective-permute-done.7.panel_ref), channel_id=1, source_target_pairs={{0,1},{1,0},{2,3},{3,2},{4,5},{5,4},{6,7},{7,6},{8,9},{9,8},{10,11... | collective-permute-start | bytes 4718600 | tf_op jit(solution)/shard_map/ppermute | solution.py:27

commit v12 on v10

--- a/solution.py
+++ b/solution.py
@@ -10,6 +10,7 @@
 BLK = 256
 APER = 12
 HW = 6
+PIECES = 4
 
 
 def after(value, *earlier):
@@ -32,13 +33,14 @@
 
 
 def line_window(data):
+    middle = lax.ppermute(data, "src", [(0, 0), (1, 2), (2, 1), (3, 3)])
     near = lax.ppermute(data, "src", [(0, 1), (1, 0), (2, 3), (3, 2)])
+    ends = lax.ppermute(data, "src", [(0, 3), (1, 1), (2, 2), (3, 0)])
     windows = []
-    for v, own in enumerate(lax.optimization_barrier([data[v : v + 1] for v in range(data.shape[0])])):
-        far = lax.ppermute(own, "src", [(0, 3), (1, 2), (2, 1), (3, 0)])
-        onward = jnp.where(at_end(), own, far)
-        across = lax.ppermute(onward, "src", [(0, 2), (2, 3), (3, 1), (1, 0)])
-        windows.append([(own, 0), (near, v), (across, 0), (far, 0)])
+    for v in range(data.shape[0]):
+        onward = middle
+        across = lax.ppermute(onward[v : v + 1], "src", [(0, 2), (2, 3), (3, 1), (1, 0)])
+        windows.append([(data, v), (near, v), (across, 0), (middle, v), (ends, v)])
     return windows
 
 
@@ -70,8 +72,12 @@
 def fill_window(window, pieces):
     width = window.shape[-1] // 2
     for k, piece in pieces.items():
-        window[k, :, :width] = piece[0]
-        window[k, :, width:] = piece[1]
+        if k < window.shape[0]:
+            for part in range(2):
+                block = piece[part]
+                if k + 1 == window.shape[0] and k + 1 in pieces:
+                    block = jnp.where(at_end(), pieces[k + 1][part], block)
+                window[k, :, part * width : (part + 1) * width] = block
 
 
 def slot_entries(aperture_ref, m, per_shard, depth):
@@ -93,13 +99,16 @@
     return panel[...].reshape(2 * panel.shape[1], panel.shape[2])
 
 
-def product(window, aperture_ref, panels):
+def product(window, aperture_ref, panels, late_in_two=None, late=None):
     blocks = []
     for m, panel in panels.items():
         entries = slot_entries(aperture_ref, m, panel.shape[-1] // BLK, window.shape[0])
         blocks += [window[k] for k in entries]
-    values = jnp.concatenate([rows_of(panel) for panel in panels.values()], axis=1)
-    return times(values, jnp.concatenate(blocks, axis=0))
+    values = [rows_of(panel) for panel in panels.values()]
+    if late_in_two is not None:
+        values.append(late_in_two)
+        blocks += [window[late]] * 2
+    return times(jnp.concatenate(values, axis=1), jnp.concatenate(blocks, axis=0))
 
 
 def sum_of_late(aperture_ref, panels, late, depth):
@@ -116,11 +125,6 @@
     high = total.astype(jnp.bfloat16)
     low = (total - high.astype(jnp.float32)).astype(jnp.bfloat16)
     return jnp.concatenate([high, low], axis=1)
-
-
-def add_late(total_in_two, window, late):
-    block = window[late]
-    return times(total_in_two, jnp.concatenate([block, block], axis=0))
 
 
 def kernel_a(near_half, ats, late, aperture_ref, *refs):
@@ -138,10 +142,9 @@
 def kernel_b(m, late, aperture_ref, late_ref, _, last_window, first_sum, last_sum, first_in, last_in, panel_ref, *refs):
     window, two, first_part, last_part = refs
     fill_window(window, {late: late_ref.at[0]})
-    real, imag = product(window, aperture_ref, {m: panel_ref.at[0]})
-    late_real, late_imag = add_late(in_two(first_sum[...]), window, late)
-    first_part[0] = first_in[0] + (real + late_real)
-    first_part[1] = first_in[1] + (imag + late_imag)
+    real, imag = product(window, aperture_ref, {m: panel_ref.at[0]}, in_two(first_sum[...]), late)
+    first_part[0] = first_in[0] + real
+    first_part[1] = first_in[1] + imag
     panels = {m: panel_ref.at[1]}
     real, imag = product(last_window, aperture_ref, panels)
     last_part[0] = last_in[0] + real
@@ -153,18 +156,21 @@
     *panel_refs, out_ref, window, result, sems = refs
 
     def finish(v, part, real, imag):
-        copies = [pltpu.make_async_copy(result.at[v, p], out_ref.at[v, p], sems.at[v, p]) for p in range(2)]
+        copies = []
         for p, value in enumerate((real, imag)):
             result[v, p] = part[p] + value
-            copies[p].start()
+            for chunk in range(PIECES):
+                rows = pl.ds(chunk * (BLK // PIECES), BLK // PIECES)
+                copies.append(
+                    pltpu.make_async_copy(result.at[v, p, rows], out_ref.at[v, p, rows], sems.at[v, p, chunk])
+                )
+                copies[-1].start()
         return copies
 
     panels = [{far_half + m: ref.at[v] for m, ref in enumerate(panel_refs)} for v in range(2)]
     copies = finish(0, first_part, *product(first_window, aperture_ref, panels[0]))
     fill_window(window, {late: late_ref.at[0]})
-    real, imag = product(window, aperture_ref, panels[1])
-    late_real, late_imag = add_late(two[...], window, late)
-    copies += finish(1, last_part, real + late_real, imag + late_imag)
+    copies += finish(1, last_part, *product(window, aperture_ref, panels[1], two[...], late))
     for copy in copies:
         copy.wait()
 
@@ -203,7 +209,7 @@
     late_pieces = [piece[at : at + 1] for piece, at in (window[late] for window in windows)]
     early = [{k: piece for k, piece in enumerate(window) if k != late} for window in windows]
     vmem, smem, anywhere = spec(pltpu.VMEM), spec(pltpu.SMEM), spec(pl.ANY)
-    window = jax.ShapeDtypeStruct((len(windows[0]), BLK, 2 * width), jnp.bfloat16)
+    window = jax.ShapeDtypeStruct((4 if line else len(windows[0]), BLK, 2 * width), jnp.bfloat16)
     total = jax.ShapeDtypeStruct((2 * BLK, BLK), jnp.float32)
     part = jax.ShapeDtypeStruct((2, BLK, width), jnp.float32)
 
@@ -233,7 +239,7 @@
         out_shape=[jax.ShapeDtypeStruct((2, 2, BLK, width), jnp.float32), window],
         in_specs=[smem] + [vmem] * (6 + len(handed_on)),
         out_specs=[anywhere, vmem],
-        scratch_shapes=[pltpu.VMEM((2, 2, BLK, width), jnp.float32), pltpu.SemaphoreType.DMA((2, 2))],
+        scratch_shapes=[pltpu.VMEM((2, 2, BLK, width), jnp.float32), pltpu.SemaphoreType.DMA((2, 2, PIECES))],
         input_output_aliases={3: 1},
         compiler_params=limit(16),
         cost_estimate=cost(1),

time: 45.5 us -> 46.9 us (1.031)
  local copies, waits for them, and re-layouts: 1.07 us -> 3.17 us
  Pallas kernels: 9.84 us -> 8.5 us
  waiting for transfers between devices: 10.7 us -> 11.9 us
  starting transfers between devices: 23.6 us -> 23 us
    ppermute x4, starting transfers between devices: 20.6 us -> 16.5 us  [the longest x2 11.6 us: line_window(): lax.ppermute(onward[v:v + 1], 'src', [(0, 2), (2, 3), (3, 1), (1, 0)])]
    ppermute x1, starting transfers between devices: 0.01 us -> 3.43 us  [line_window(): near = lax.ppermute(data, 'src', [(0, 1), (1, 0), (2, 3), (3, 2)])]
    unnamed x4 -> x6, local copies, waits for them, and re-layouts: 0.01 us -> 3.13 us
    ppermute x4, waiting for transfers between devices: 8.52 us -> 11.2 us  [the longest x1 10.7 us: line_window(): ends = lax.ppermute(data, 'src', [(0, 3), (1, 1), (2, 2), (3, 0)])]
    ppermute x3, waiting for transfers between devices: 2.18 us -> 0.68 us  [swap(): return lax.ppermute(x, axis, [(i, i ^ bit) for i in range(peers)])]
    slice x1, local copies, waits for them, and re-layouts: 1.06 us -> 0.04 us  [line_window(): onward[v:v + 1]]
    pallas_call x1, Pallas kernels: 3.02 us -> 2.18 us  [body(): pl.pallas_call(functools.partial(kernel_b, half, late), out_shape=[window...]
    pallas_call x1, Pallas kernels: 4.08 us -> 3.52 us  [body(): pl.pallas_call(functools.partial(kernel_a, half, [{k: at for k, (_, at) i...]
  transfers between devices with their start and end apart: 8 -> 8, of which waited for: 3 -> 3; matrix products, arithmetic and copies ran while one was open for 2% -> 0% of each run, Pallas kernels for 16% -> 12%
where the time goes in v12:
time: 46.9 us; the launch traced here: 46.6 us
  starting transfers between devices  23 us (49%)
  waiting for transfers between devices  11.9 us (25%)
  Pallas kernels  8.5 us (18%)
  local copies, waits for them, and re-layouts  3.17 us (7%)
    ppermute x2, starting transfers between devices, line_window(): lax.ppermute(onward[v:v + 1], 'src', [(0, 2), (2, 3), (3, 1), (1, 0)])  11.6 us
    ppermute x1, waiting for transfers between devices, line_window(): ends = lax.ppermute(data, 'src', [(0, 3), (1, 1), (2, 2), (3, 0)])  10.7 us
    pallas_call x1, Pallas kernels, body(): pl.pallas_call(functools.partial(kernel_a, half, [{k: at for k, (_, at) i...  3.52 us
    ppermute x1, starting transfers between devices, line_window(): near = lax.ppermute(data, 'src', [(0, 1), (1, 0), (2, 3), (3, 2)])  3.43 us
    ppermute x1, starting transfers between devices, line_window(): ends = lax.ppermute(data, 'src', [(0, 3), (1, 1), (2, 2), (3, 0)])  3.25 us
    unnamed x6, local copies, waits for them, and re-layouts  3.13 us
    ppermute x3, starting transfers between devices, swap(): return lax.ppermute(x, axis, [(i, i ^ bit) for i in range(peers)])  3.01 us
    pallas_call x1, Pallas kernels, body(): pl.pallas_call(functools.partial(last_kernel, half + 1, late), out_shape=...  2.8 us
  transfers between devices with their start and end apart: 8, of which 3 were waited for; matrix products, arithmetic and copies ran while one was open for 0% of the time, Pallas kernels for 12%

profile of v12, /device:TPU:0, one launch (start us, length us, event | category | flops | bytes accessed | tf_op | source)
XLA Modules:
  0.0 46.6 jit_solution(8086038256418069086)
XLA Ops:
  0.0 0.5 collective-permute-start.3
  0.5 2.5 %collective-permute-start.6 = (bf16[2,2,256,768]{3,2,1,0:T(8,128)(2,1)}, bf16[2,2,256,768]{3,2,1,0:T(8,128)(2,1)S(1)}, u32[]{:S(2)}, u32[]{:S(2)}) collective-permute-start(bf16[2,2,256,768]{3,2,1,0:T(8,128)(2,1)} %refs_0_.1), channel_id=1, source_target_pairs={{0,2},{1,3},{2,0},{3,1},{4,6},{5,7},{6,4},{7,5},{8,10},{9,11},{10,... | collective-permute-start | bytes 4718600 | tf_op jit(solution)/shard_map/ppermute | solution.py:28
  2.9 1.7 %collective-permute-start = (bf16[2,2,256,256]{3,2,1,0:T(8,128)(2,1)}, bf16[2,2,256,256]{3,2,1,0:T(8,128)(2,1)S(1)}, u32[]{:S(2)}, u32[]{:S(2)}) collective-permute-start(bf16[2,2,256,256]{3,2,1,0:T(8,128)(2,1)} %refs_6_.1), channel_id=1, source_target_pairs={{0,0},{4,8},{8,4},{12,12},{1,1},{5,9},{9,5},{13,13},{2,2},{6,10},{... | collective-permute-start | bytes 1572872 | tf_op jit(solution)/shard_map/ppermute | solution.py:36
  4.6 3.4 %collective-permute-start.4 = (bf16[2,2,256,256]{3,2,1,0:T(8,128)(2,1)}, bf16[2,2,256,256]{3,2,1,0:T(8,128)(2,1)S(1)}, u32[]{:S(2)}, u32[]{:S(2)}) collective-permute-start(bf16[2,2,256,256]{3,2,1,0:T(8,128)(2,1)} %refs_6_.1), channel_id=1, source_target_pairs={{0,4},{4,0},{8,12},{12,8},{1,5},{5,1},{9,13},{13,9},{2,6},{6,2},{1... | collective-permute-start | bytes 1572872 | tf_op jit(solution)/shard_map/ppermute | solution.py:37
  8.1 3.2 %collective-permute-start.5 = (bf16[2,2,256,256]{3,2,1,0:T(8,128)(2,1)}, bf16[2,2,256,256]{3,2,1,0:T(8,128)(2,1)S(1)}, u32[]{:S(2)}, u32[]{:S(2)}) collective-permute-start(bf16[2,2,256,256]{3,2,1,0:T(8,128)(2,1)} %refs_6_.1), channel_id=1, source_target_pairs={{0,12},{4,4},{8,8},{12,0},{1,13},{5,5},{9,9},{13,1},{2,14},{6,6},{... | collective-permute-start | bytes 1572872 | tf_op jit(solution)/shard_map/ppermute | solution.py:38
  11.3 0.0 collective-permute-done.refs_4_.refs_8_
  11.4 10.4 %collective-permute-start.2 = (bf16[1,2,256,256]{3,2,1,0:T(8,128)(2,1)S(1)}, bf16[1,2,256,256]{3,2,1,0:T(8,128)(2,1)S(1)}, u32[]{:S(2)}, u32[]{:S(2)}) collective-permute-start(bf16[1,2,256,256]{3,2,1,0:T(8,128)(2,1)S(1)} %get-tuple-element.29), channel_id=1, source_target_pairs={{0,8},{8,12},{12,4},{4,0},{1,9},{9,13},{13,5},{5,1},{2,10},{10,14}... | collective-permute-start | bytes 786440 | tf_op jit(solution)/shard_map/ppermute | solution.py:42
  21.8 0.0 collective-permute-done.4.refs_3_.refs_7_
  21.8 1.2 %collective-permute-start.1 = (bf16[1,2,256,256]{3,2,1,0:T(8,128)(2,1)S(1)}, bf16[1,2,256,256]{3,2,1,0:T(8,128)(2,1)S(1)}, u32[]{:S(2)}, u32[]{:S(2)}) collective-permute-start(bf16[1,2,256,256]{3,2,1,0:T(8,128)(2,1)S(1)} %get-tuple-element.30), channel_id=1, source_target_pairs={{0,8},{8,12},{12,4},{4,0},{1,9},{9,13},{13,5},{5,1},{2,10},{10,14}... | collective-permute-start | bytes 786440 | tf_op jit(solution)/shard_map/ppermute | solution.py:42
  23.0 10.7 %collective-permute-done.5.refs_5_.refs_9_ = bf16[2,2,256,256]{3,2,1,0:T(8,128)(2,1)S(1)} collective-permute-done((bf16[2,2,256,256]{3,2,1,0:T(8,128)(2,1)}, bf16[2,2,256,256]{3,2,1,0:T(8,128)(2,1)S(1)}, u32[]{:S(2)}, u32[]{:S(2)}) %collective-permute-start.5) | collective-permute-done | bytes 524320 | tf_op jit(solution)/shard_map/ppermute | solution.py:38
  33.7 0.0 collective-permute-done.3.refs_1_
  33.7 0.0 copy-start
  33.7 1.0 %copy-done = bf16[2,2,256,256]{3,2,1,0:T(8,128)(2,1)S(1)} copy-done((bf16[2,2,256,256]{3,2,1,0:T(8,128)(2,1)S(1)}, bf16[2,2,256,256]{3,2,1,0:T(8,128)(2,1)}, u32[]{:S(2)}) %copy-start) | copy-done | bytes 524312
  34.7 0.0 copy-start.1
  34.7 1.4 %copy-done.1 = bf16[2,2,256,768]{3,2,1,0:T(8,128)(2,1)S(1)} copy-done((bf16[2,2,256,768]{3,2,1,0:T(8,128)(2,1)S(1)}, bf16[2,2,256,768]{3,2,1,0:T(8,128)(2,1)}, u32[]{:S(2)}) %copy-start.1) | copy-done | bytes 1572888
  36.1 0.0 copy-start.2
  36.1 0.7 %copy-done.2 = s32[4,12]{1,0:T(4,128)S(1)} copy-done((s32[4,12]{1,0:T(4,128)S(1)}, s32[4,12]{1,0:T(4,128)}, u32[]{:S(2)}) %copy-start.2) | copy-done | bytes 216
  36.8 3.5 %shard_map.37 = (bf16[4,256,512]{2,1,0:T(8,128)(2,1)S(1)}, bf16[4,256,512]{2,1,0:T(8,128)(2,1)S(1)}, f32[512,256]{1,0:T(8,128)S(1)}, f32[512,256]{1,0:T(8,128)S(...) custom-call(s32[4,12]{1,0:T(4,128)S(1)} %copy-done.2, bf16[2,2,256,768]{3,2,1,0:T(8,128)(2,1)S(1)} %copy-done.1, ...), custom_call_target="tpu_custom_call" | custom-call | flops 161061280 | bytes 1048576 | tf_op jit(solution)/shard_map/pallas_call | solution.py:217
  40.3 0.0 collective-permute-done.6.panel_ref
  40.4 0.1 collective-permute-start.7
  40.4 0.0 collective-permute-done.2.late_ref
  40.4 2.2 %shard_map.38 = (bf16[4,256,512]{2,1,0:T(8,128)(2,1)S(1)}, bf16[512,512]{1,0:T(8,128)(2,1)S(1)}, f32[2,256,256]{2,1,0:T(8,128)S(1)}, f32[2,256,256]{2,1,0:T(8,128)S(1)}) custom-call(s32[4,12]{1,0:T(4,128)S(1)} %copy-done.2, bf16[1,2,256,256]{3,2,1,0:T(8,128)(2,1)S(1)} %collective-permute-done.2.late_ref, ...), custom_call_target="tpu_custom_call", output_to_operand_aliasing={{0}: (2, {}), {2}: (6, {}), {3}: (7, {})} | custom-call | flops 161061280 | bytes 1048576 | tf_op jit(solution)/shard_map/pallas_call | solution.py:227
  42.6 0.5 %collective-permute-done.1.piece_ref = bf16[1,2,256,256]{3,2,1,0:T(8,128)(2,1)S(1)} collective-permute-done((bf16[1,2,256,256]{3,2,1,0:T(8,128)(2,1)S(1)}, bf16[1,2,256,256]{3,2,1,0:T(8,128)(2,1)S(1)}, u32[]{:S(2)}, u32[]{:S(2)}) %collective-permute-start.1) | collective-permute-done | bytes 262176 | tf_op jit(solution)/shard_map/ppermute | solution.py:42
  43.2 0.7 %collective-permute-done.7.refs_0_ = bf16[2,2,256,768]{3,2,1,0:T(8,128)(2,1)S(1)} collective-permute-done((bf16[2,2,256,768]{3,2,1,0:T(8,128)(2,1)S(1)}, bf16[2,2,256,768]{3,2,1,0:T(8,128)(2,1)S(1)}, u32[]{:S(2)}, u32[]{:S(2)}) %collective-permute-start.7) | collective-permute-done | bytes 1572896 | tf_op jit(solution)/shard_map/ppermute | solution.py:28
  43.8 2.8 %shard_map.40 = (f32[2,2,256,256]{3,2,1,0:T(8,128)}, bf16[4,256,512]{2,1,0:T(8,128)(2,1)S(1)}) custom-call(s32[4,12]{1,0:T(4,128)S(1)} %copy-done.2, bf16[1,2,256,256]{3,2,1,0:T(8,128)(2,1)S(1)} %shard_map.39.late_ref, bf16[4,256,512]{2,1,0:T(8,128)(2,1)S(1)} %get-tuple-element.24.first_window, ...), custom_call_target="tpu_custom_call", output_to_operand_aliasing={{1}: (3, {})} | custom-call | flops 1610612736 | bytes 1048576 | tf_op jit(solution)/shard_map/pallas_call | solution.py:237
  (2 shorter events, 0.0 us)
Async XLA Ops:
  0.0 33.7 %collective-permute-start.3 = (bf16[2,2,256,768]{3,2,1,0:T(8,128)(2,1)}, bf16[2,2,256,768]{3,2,1,0:T(8,128)(2,1)S(1)}, u32[]{:S(2)}, u32[]{:S(2)}) collective-permute-start(bf16[2,2,256,768]{3,2,1,0:T(8,128)(2,1)} %refs_0_.1), channel_id=1, source_target_pairs={{0,1},{1,0},{2,3},{3,2},{4,5},{5,4},{6,7},{7,6},{8,9},{9,8},{10,11... | collective-permute-start | bytes 4718600 | tf_op jit(solution)/shard_map/ppermute | solution.py:28
  0.5 39.9 %collective-permute-start.6 = (bf16[2,2,256,768]{3,2,1,0:T(8,128)(2,1)}, bf16[2,2,256,768]{3,2,1,0:T(8,128)(2,1)S(1)}, u32[]{:S(2)}, u32[]{:S(2)}) collective-permute-start(bf16[2,2,256,768]{3,2,1,0:T(8,128)(2,1)} %refs_0_.1), channel_id=1, source_target_pairs={{0,2},{1,3},{2,0},{3,1},{4,6},{5,7},{6,4},{7,5},{8,10},{9,11},{10,... | collective-permute-start | bytes 4718600 | tf_op jit(solution)/shard_map/ppermute | solution.py:28
  2.9 8.4 %collective-permute-start = (bf16[2,2,256,256]{3,2,1,0:T(8,128)(2,1)}, bf16[2,2,256,256]{3,2,1,0:T(8,128)(2,1)S(1)}, u32[]{:S(2)}, u32[]{:S(2)}) collective-permute-start(bf16[2,2,256,256]{3,2,1,0:T(8,128)(2,1)} %refs_6_.1), channel_id=1, source_target_pairs={{0,0},{4,8},{8,4},{12,12},{1,1},{5,9},{9,5},{13,13},{2,2},{6,10},{... | collective-permute-start | bytes 1572872 | tf_op jit(solution)/shard_map/ppermute | solution.py:36
  4.6 17.1 %collective-permute-start.4 = (bf16[2,2,256,256]{3,2,1,0:T(8,128)(2,1)}, bf16[2,2,256,256]{3,2,1,0:T(8,128)(2,1)S(1)}, u32[]{:S(2)}, u32[]{:S(2)}) collective-permute-start(bf16[2,2,256,256]{3,2,1,0:T(8,128)(2,1)} %refs_6_.1), channel_id=1, source_target_pairs={{0,4},{4,0},{8,12},{12,8},{1,5},{5,1},{9,13},{13,9},{2,6},{6,2},{1... | collective-permute-start | bytes 1572872 | tf_op jit(solution)/shard_map/ppermute | solution.py:37
  8.1 25.6 %collective-permute-start.5 = (bf16[2,2,256,256]{3,2,1,0:T(8,128)(2,1)}, bf16[2,2,256,256]{3,2,1,0:T(8,128)(2,1)S(1)}, u32[]{:S(2)}, u32[]{:S(2)}) collective-permute-start(bf16[2,2,256,256]{3,2,1,0:T(8,128)(2,1)} %refs_6_.1), channel_id=1, source_target_pairs={{0,12},{4,4},{8,8},{12,0},{1,13},{5,5},{9,9},{13,1},{2,14},{6,6},{... | collective-permute-start | bytes 1572872 | tf_op jit(solution)/shard_map/ppermute | solution.py:38
  11.4 29.1 %collective-permute-start.2 = (bf16[1,2,256,256]{3,2,1,0:T(8,128)(2,1)S(1)}, bf16[1,2,256,256]{3,2,1,0:T(8,128)(2,1)S(1)}, u32[]{:S(2)}, u32[]{:S(2)}) collective-permute-start(bf16[1,2,256,256]{3,2,1,0:T(8,128)(2,1)S(1)} %get-tuple-element.29), channel_id=1, source_target_pairs={{0,8},{8,12},{12,4},{4,0},{1,9},{9,13},{13,5},{5,1},{2,10},{10,14}... | collective-permute-start | bytes 786440 | tf_op jit(solution)/shard_map/ppermute | solution.py:42
  21.8 21.4 %collective-permute-start.1 = (bf16[1,2,256,256]{3,2,1,0:T(8,128)(2,1)S(1)}, bf16[1,2,256,256]{3,2,1,0:T(8,128)(2,1)S(1)}, u32[]{:S(2)}, u32[]{:S(2)}) collective-permute-start(bf16[1,2,256,256]{3,2,1,0:T(8,128)(2,1)S(1)} %get-tuple-element.30), channel_id=1, source_target_pairs={{0,8},{8,12},{12,4},{4,0},{1,9},{9,13},{13,5},{5,1},{2,10},{10,14}... | collective-permute-start | bytes 786440 | tf_op jit(solution)/shard_map/ppermute | solution.py:42
  33.7 1.0 %copy-start = (bf16[2,2,256,256]{3,2,1,0:T(8,128)(2,1)S(1)}, bf16[2,2,256,256]{3,2,1,0:T(8,128)(2,1)}, u32[]{:S(2)}) copy-start(bf16[2,2,256,256]{3,2,1,0:T(8,128)(2,1)} %refs_6_.1) | copy-start | bytes 1572868
  34.7 1.4 %copy-start.1 = (bf16[2,2,256,768]{3,2,1,0:T(8,128)(2,1)S(1)}, bf16[2,2,256,768]{3,2,1,0:T(8,128)(2,1)}, u32[]{:S(2)}) copy-start(bf16[2,2,256,768]{3,2,1,0:T(8,128)(2,1)} %refs_0_.1) | copy-start | bytes 4718596
  36.1 0.7 %copy-start.2 = (s32[4,12]{1,0:T(4,128)S(1)}, s32[4,12]{1,0:T(4,128)}, u32[]{:S(2)}) copy-start(s32[4,12]{1,0:T(4,128)} %aperture_ref.5) | copy-start | bytes 580
  40.4 3.5 %collective-permute-start.7 = (bf16[2,2,256,768]{3,2,1,0:T(8,128)(2,1)S(1)}, bf16[2,2,256,768]{3,2,1,0:T(8,128)(2,1)S(1)}, u32[]{:S(2)}, u32[]{:S(2)}) collective-permute-start(bf16[2,2,256,768]{3,2,1,0:T(8,128)(2,1)S(1)} %collective-permute-done.6.panel_ref), channel_id=1, source_target_pairs={{0,1},{1,0},{2,3},{3,2},{4,5},{5,4},{6,7},{7,6},{8,9},{9,8},{10,11... | collective-permute-start | bytes 4718600 | tf_op jit(solution)/shard_map/ppermute | solution.py:28

commit v13 on v12

--- a/solution.py
+++ b/solution.py
@@ -10,7 +10,7 @@
 BLK = 256
 APER = 12
 HW = 6
-PIECES = 4
+PIECES = 1
 
 
 def after(value, *earlier):
@@ -33,14 +33,14 @@
 
 
 def line_window(data):
-    middle = lax.ppermute(data, "src", [(0, 0), (1, 2), (2, 1), (3, 3)])
     near = lax.ppermute(data, "src", [(0, 1), (1, 0), (2, 3), (3, 2)])
-    ends = lax.ppermute(data, "src", [(0, 3), (1, 1), (2, 2), (3, 0)])
     windows = []
     for v in range(data.shape[0]):
-        onward = middle
-        across = lax.ppermute(onward[v : v + 1], "src", [(0, 2), (2, 3), (3, 1), (1, 0)])
-        windows.append([(data, v), (near, v), (across, 0), (middle, v), (ends, v)])
+        own = (after(data, windows[-1][0][0]) if windows else data)[v : v + 1]
+        far = lax.ppermute(own, "src", [(0, 3), (1, 2), (2, 1), (3, 0)])
+        onward = jnp.where(at_end(), own, far)
+        across = lax.ppermute(onward, "src", [(0, 2), (2, 3), (3, 1), (1, 0)])
+        windows.append([(own, 0), (near, v), (across, 0), (far, 0)])
     return windows
 
 
@@ -72,12 +72,8 @@
 def fill_window(window, pieces):
     width = window.shape[-1] // 2
     for k, piece in pieces.items():
-        if k < window.shape[0]:
-            for part in range(2):
-                block = piece[part]
-                if k + 1 == window.shape[0] and k + 1 in pieces:
-                    block = jnp.where(at_end(), pieces[k + 1][part], block)
-                window[k, :, part * width : (part + 1) * width] = block
+        window[k, :, :width] = piece[0]
+        window[k, :, width:] = piece[1]
 
 
 def slot_entries(aperture_ref, m, per_shard, depth):
@@ -209,7 +205,7 @@
     late_pieces = [piece[at : at + 1] for piece, at in (window[late] for window in windows)]
     early = [{k: piece for k, piece in enumerate(window) if k != late} for window in windows]
     vmem, smem, anywhere = spec(pltpu.VMEM), spec(pltpu.SMEM), spec(pl.ANY)
-    window = jax.ShapeDtypeStruct((4 if line else len(windows[0]), BLK, 2 * width), jnp.bfloat16)
+    window = jax.ShapeDtypeStruct((len(windows[0]), BLK, 2 * width), jnp.bfloat16)
     total = jax.ShapeDtypeStruct((2 * BLK, BLK), jnp.float32)
     part = jax.ShapeDtypeStruct((2, BLK, width), jnp.float32)
 

time: 46.9 us -> 45.5 us (0.970)
  waiting for transfers between devices: 11.9 us -> 8.66 us
  other arithmetic: 0 us -> 1.99 us
  Pallas kernels: 8.5 us -> 9.85 us
  local copies, waits for them, and re-layouts: 3.17 us -> 1.94 us
    ppermute x4, waiting for transfers between devices: 11.2 us -> 7.39 us  [the longest x2 6.27 us: line_window(): far = lax.ppermute(own, 'src', [(0, 3), (1, 2), (2, 1), (3, 0)])]
    ppermute x1, starting transfers between devices: 3.43 us -> 0.01 us  [line_window(): near = lax.ppermute(data, 'src', [(0, 1), (1, 0), (2, 3), (3, 2)])]
    ppermute x4, starting transfers between devices: 16.5 us -> 19.7 us  [the longest x2 15.7 us: line_window(): across = lax.ppermute(onward, 'src', [(0, 2), (2, 3), (3, 1), (1, 0)])]
    unnamed x6 -> x4, local copies, waits for them, and re-layouts: 3.13 us -> 0.01 us
    select_n x0 -> x2, other arithmetic: none -> 1.99 us  [line_window(): onward = jnp.where(at_end(), own, far)]
    slice x1 -> x2, local copies, waits for them, and re-layouts: 0.04 us -> 1.93 us  [line_window(): own = (after(data, windows[-1][0][0]) if windows else data)[v:v + 1]]
    pallas_call x1, Pallas kernels: 2.18 us -> 3.02 us  [body(): pl.pallas_call(functools.partial(kernel_b, half, late), out_shape=[window...]
    pallas_call x1, Pallas kernels: 3.52 us -> 4.13 us  [body(): pl.pallas_call(functools.partial(kernel_a, half, [{k: at for k, (_, at) i...]
  transfers between devices with their start and end apart: 8 -> 8, of which waited for: 3 -> 3; matrix products, arithmetic and copies ran while one was open for 0% -> 9% of each run, Pallas kernels for 12% -> 16%
where the time goes in v13:
time: 45.5 us; the launch traced here: 45.2 us
  starting transfers between devices  22.7 us (50%)
  Pallas kernels  9.85 us (22%)
  waiting for transfers between devices  8.66 us (19%)
  other arithmetic  1.99 us (4%)
  local copies, waits for them, and re-layouts  1.94 us (4%)
    ppermute x2, starting transfers between devices, line_window(): across = lax.ppermute(onward, 'src', [(0, 2), (2, 3), (3, 1), (1, 0)])  15.7 us
    ppermute x2, waiting for transfers between devices, line_window(): far = lax.ppermute(own, 'src', [(0, 3), (1, 2), (2, 1), (3, 0)])  6.27 us
    pallas_call x1, Pallas kernels, body(): pl.pallas_call(functools.partial(kernel_a, half, [{k: at for k, (_, at) i...  4.13 us
    ppermute x2, starting transfers between devices, line_window(): far = lax.ppermute(own, 'src', [(0, 3), (1, 2), (2, 1), (3, 0)])  3.95 us
    pallas_call x1, Pallas kernels, body(): pl.pallas_call(functools.partial(kernel_b, half, late), out_shape=[window...  3.02 us
    ppermute x3, starting transfers between devices, swap(): return lax.ppermute(x, axis, [(i, i ^ bit) for i in range(peers)])  3.02 us
    pallas_call x1, Pallas kernels, body(): pl.pallas_call(functools.partial(last_kernel, half + 1, late), out_shape=...  2.71 us
    select_n x2, other arithmetic, line_window(): onward = jnp.where(at_end(), own, far)  1.99 us
  transfers between devices with their start and end apart: 8, of which 3 were waited for; matrix products, arithmetic and copies ran while one was open for 9% of the time, Pallas kernels for 16%

profile of v13, /device:TPU:0, one launch (start us, length us, event | category | flops | bytes accessed | tf_op | source)
XLA Modules:
  0.0 45.2 jit_solution(13535289516133976168)
XLA Ops:
  0.0 0.0 copy-start
  0.0 0.0 copy-start.1
  0.0 0.5 %collective-permute-start.4 = (bf16[2,2,256,768]{3,2,1,0:T(8,128)(2,1)}, bf16[2,2,256,768]{3,2,1,0:T(8,128)(2,1)}, u32[]{:S(2)}, u32[]{:S(2)}) collective-permute-start(bf16[2,2,256,768]{3,2,1,0:T(8,128)(2,1)} %refs_0_.1), channel_id=1, source_target_pairs={{0,1},{1,0},{2,3},{3,2},{4,5},{5,4},{6,7},{7,6},{8,9},{9,8},{10,11... | collective-permute-start | bytes 4718600 | tf_op jit(solution)/shard_map/ppermute | solution.py:28
  0.5 2.6 %collective-permute-start.6 = (bf16[2,2,256,768]{3,2,1,0:T(8,128)(2,1)}, bf16[2,2,256,768]{3,2,1,0:T(8,128)(2,1)}, u32[]{:S(2)}, u32[]{:S(2)}) collective-permute-start(bf16[2,2,256,768]{3,2,1,0:T(8,128)(2,1)} %refs_0_.1), channel_id=1, source_target_pairs={{0,2},{1,3},{2,0},{3,1},{4,6},{5,7},{6,4},{7,5},{8,10},{9,11},{10,... | collective-permute-start | bytes 4718600 | tf_op jit(solution)/shard_map/ppermute | solution.py:28
  3.0 1.0 %slice.6.refs_2_ = bf16[1,2,256,256]{3,2,1,0:T(8,128)(2,1)S(1)} slice(bf16[2,2,256,256]{3,2,1,0:T(8,128)(2,1)} %param.4), slice={[0:1], [0:2], [0:256], [0:256]} | slice | bytes 524288 | tf_op jit(solution)/shard_map/slice | solution.py:39
  4.0 3.7 %collective-permute-start.2 = (bf16[1,2,256,256]{3,2,1,0:T(8,128)(2,1)S(1)}, bf16[1,2,256,256]{3,2,1,0:T(8,128)(2,1)S(1)}, u32[]{:S(2)}, u32[]{:S(2)}) collective-permute-start(bf16[1,2,256,256]{3,2,1,0:T(8,128)(2,1)S(1)} %slice.6.refs_2_), channel_id=1, source_target_pairs={{0,12},{4,8},{8,4},{12,0},{1,13},{5,9},{9,5},{13,1},{2,14},{6,10},... | collective-permute-start | bytes 786440 | tf_op jit(solution)/shard_map/ppermute | solution.py:40
  7.7 1.0 %slice.7.refs_5_ = bf16[1,2,256,256]{3,2,1,0:T(8,128)(2,1)S(1)} slice(bf16[2,2,256,256]{3,2,1,0:T(8,128)(2,1)} %param.4), slice={[1:2], [0:2], [0:256], [0:256]} | slice | bytes 524288 | tf_op jit(solution)/shard_map/slice | solution.py:39
  8.6 0.3 collective-permute-start
  8.9 0.0 collective-permute-start.5
  8.9 6.3 %collective-permute-done.2.refs_4_ = bf16[1,2,256,256]{3,2,1,0:T(8,128)(2,1)S(1)} collective-permute-done((bf16[1,2,256,256]{3,2,1,0:T(8,128)(2,1)S(1)}, bf16[1,2,256,256]{3,2,1,0:T(8,128)(2,1)S(1)}, u32[]{:S(2)}, u32[]{:S(2)}) %collective-permute-start.2) | collective-permute-done | bytes 262176 | tf_op jit(solution)/shard_map/ppermute | solution.py:40
  15.2 1.0 %broadcast_select_fusion = bf16[1,2,256,256]{3,2,1,0:T(8,128)(2,1)S(1)} fusion(bf16[1,2,256,256]{3,2,1,0:T(8,128)(2,1)S(1)} %collective-permute-done.2.refs_4_, pred[]{:T(512)S(6)} %lt.13, bf16[2,2,256,256]{3,2,1,0:T(8,128)(2,1)} %param.4), kind=kLoop, calls=%fused_computation | loop fusion | flops 131072 | bytes 786433 | tf_op jit(solution)/shard_map/jit(_where)/select_n | solution.py:41
  16.2 11.9 %collective-permute-start.3 = (bf16[1,2,256,256]{3,2,1,0:T(8,128)(2,1)S(1)}, bf16[1,2,256,256]{3,2,1,0:T(8,128)(2,1)S(1)}, u32[]{:S(2)}, u32[]{:S(2)}) collective-permute-start(bf16[1,2,256,256]{3,2,1,0:T(8,128)(2,1)S(1)} %broadcast_select_fusion), channel_id=1, source_target_pairs={{0,8},{8,12},{12,4},{4,0},{1,9},{9,13},{13,5},{5,1},{2,10},{10,14}... | collective-permute-start | bytes 786440 | tf_op jit(solution)/shard_map/ppermute | solution.py:42
  28.1 0.0 collective-permute-done.refs_7_
  28.1 1.0 %broadcast_select_fusion.1 = bf16[1,2,256,256]{3,2,1,0:T(8,128)(2,1)S(1)} fusion(bf16[1,2,256,256]{3,2,1,0:T(8,128)(2,1)S(1)} %collective-permute-done.refs_7_, pred[]{:T(512)S(6)} %lt.13, bf16[2,2,256,256]{3,2,1,0:T(8,128)(2,1)} %param.4), kind=kLoop, calls=%fused_computation.1 | loop fusion | flops 131072 | bytes 786433 | tf_op jit(solution)/shard_map/jit(_where)/select_n | solution.py:41
  29.1 3.8 %collective-permute-start.1 = (bf16[1,2,256,256]{3,2,1,0:T(8,128)(2,1)S(1)}, bf16[1,2,256,256]{3,2,1,0:T(8,128)(2,1)S(1)}, u32[]{:S(2)}, u32[]{:S(2)}) collective-permute-start(bf16[1,2,256,256]{3,2,1,0:T(8,128)(2,1)S(1)} %broadcast_select_fusion.1), channel_id=1, source_target_pairs={{0,8},{8,12},{12,4},{4,0},{1,9},{9,13},{13,5},{5,1},{2,10},{10,14}... | collective-permute-start | bytes 786440 | tf_op jit(solution)/shard_map/ppermute | solution.py:42
  32.9 0.0 collective-permute-done.5.refs_3_.refs_6_
  32.9 0.0 collective-permute-done.4.refs_1_
  32.9 0.0 copy-done
  32.9 0.0 copy-done.1
  32.9 4.1 %shard_map.37 = (bf16[4,256,512]{2,1,0:T(8,128)(2,1)S(1)}, bf16[4,256,512]{2,1,0:T(8,128)(2,1)S(1)}, f32[512,256]{1,0:T(8,128)S(1)}, f32[512,256]{1,0:T(8,128)S(...) custom-call(s32[4,12]{1,0:T(4,128)S(1)} %copy-done.1, bf16[2,2,256,768]{3,2,1,0:T(8,128)(2,1)S(1)} %copy-done, ...), custom_call_target="tpu_custom_call" | custom-call | flops 161061280 | bytes 1048576 | tf_op jit(solution)/shard_map/pallas_call | solution.py:213
  37.1 1.3 %collective-permute-done.6.panel_ref = bf16[2,2,256,768]{3,2,1,0:T(8,128)(2,1)} collective-permute-done((bf16[2,2,256,768]{3,2,1,0:T(8,128)(2,1)}, bf16[2,2,256,768]{3,2,1,0:T(8,128)(2,1)}, u32[]{:S(2)}, u32[]{:S(2)}) %collective-permute-start.6) | collective-permute-done | bytes 1572896 | tf_op jit(solution)/shard_map/ppermute | solution.py:28
  38.3 0.0 collective-permute-start.7
  38.3 0.0 collective-permute-done.3.late_ref
  38.3 3.0 %shard_map.38 = (bf16[4,256,512]{2,1,0:T(8,128)(2,1)S(1)}, bf16[512,512]{1,0:T(8,128)(2,1)S(1)}, f32[2,256,256]{2,1,0:T(8,128)S(1)}, f32[2,256,256]{2,1,0:T(8,128)S(1)}) custom-call(s32[4,12]{1,0:T(4,128)S(1)} %copy-done.1, bf16[1,2,256,256]{3,2,1,0:T(8,128)(2,1)S(1)} %collective-permute-done.3.late_ref, ...), custom_call_target="tpu_custom_call", output_to_operand_aliasing={{0}: (2, {}), {2}: (6, {}), {3}: (7, {})} | custom-call | flops 161061280 | bytes 1048576 | tf_op jit(solution)/shard_map/pallas_call | solution.py:223
  41.4 1.1 %collective-permute-done.1.piece_ref = bf16[1,2,256,256]{3,2,1,0:T(8,128)(2,1)S(1)} collective-permute-done((bf16[1,2,256,256]{3,2,1,0:T(8,128)(2,1)S(1)}, bf16[1,2,256,256]{3,2,1,0:T(8,128)(2,1)S(1)}, u32[]{:S(2)}, u32[]{:S(2)}) %collective-permute-start.1) | collective-permute-done | bytes 262176 | tf_op jit(solution)/shard_map/ppermute | solution.py:42
  42.5 0.0 collective-permute-done.7.refs_0_
  42.5 2.7 %shard_map.40 = (f32[2,2,256,256]{3,2,1,0:T(8,128)}, bf16[4,256,512]{2,1,0:T(8,128)(2,1)S(1)}) custom-call(s32[4,12]{1,0:T(4,128)S(1)} %copy-done.1, bf16[1,2,256,256]{3,2,1,0:T(8,128)(2,1)S(1)} %shard_map.39.late_ref, bf16[4,256,512]{2,1,0:T(8,128)(2,1)S(1)} %get-tuple-element.26.first_window, ...), custom_call_target="tpu_custom_call", output_to_operand_aliasing={{1}: (3, {})} | custom-call | flops 1610612736 | bytes 1048576 | tf_op jit(solution)/shard_map/pallas_call | solution.py:233
  (1 shorter events, 0.0 us)
Async XLA Ops:
  0.0 32.9 %copy-start = (bf16[2,2,256,768]{3,2,1,0:T(8,128)(2,1)S(1)}, bf16[2,2,256,768]{3,2,1,0:T(8,128)(2,1)}, u32[]{:S(2)}) copy-start(bf16[2,2,256,768]{3,2,1,0:T(8,128)(2,1)} %refs_0_.1) | copy-start | bytes 4718596
  0.0 32.9 %copy-start.1 = (s32[4,12]{1,0:T(4,128)S(1)}, s32[4,12]{1,0:T(4,128)}, u32[]{:S(2)}) copy-start(s32[4,12]{1,0:T(4,128)} %aperture_ref.5) | copy-start | bytes 580
  0.0 32.9 %collective-permute-start.4 = (bf16[2,2,256,768]{3,2,1,0:T(8,128)(2,1)}, bf16[2,2,256,768]{3,2,1,0:T(8,128)(2,1)}, u32[]{:S(2)}, u32[]{:S(2)}) collective-permute-start(bf16[2,2,256,768]{3,2,1,0:T(8,128)(2,1)} %refs_0_.1), channel_id=1, source_target_pairs={{0,1},{1,0},{2,3},{3,2},{4,5},{5,4},{6,7},{7,6},{8,9},{9,8},{10,11... | collective-permute-start | bytes 4718600 | tf_op jit(solution)/shard_map/ppermute | solution.py:28
  0.5 37.9 %collective-permute-start.6 = (bf16[2,2,256,768]{3,2,1,0:T(8,128)(2,1)}, bf16[2,2,256,768]{3,2,1,0:T(8,128)(2,1)}, u32[]{:S(2)}, u32[]{:S(2)}) collective-permute-start(bf16[2,2,256,768]{3,2,1,0:T(8,128)(2,1)} %refs_0_.1), channel_id=1, source_target_pairs={{0,2},{1,3},{2,0},{3,1},{4,6},{5,7},{6,4},{7,5},{8,10},{9,11},{10,... | collective-permute-start | bytes 4718600 | tf_op jit(solution)/shard_map/ppermute | solution.py:28
  4.0 11.2 %collective-permute-start.2 = (bf16[1,2,256,256]{3,2,1,0:T(8,128)(2,1)S(1)}, bf16[1,2,256,256]{3,2,1,0:T(8,128)(2,1)S(1)}, u32[]{:S(2)}, u32[]{:S(2)}) collective-permute-start(bf16[1,2,256,256]{3,2,1,0:T(8,128)(2,1)S(1)} %slice.6.refs_2_), channel_id=1, source_target_pairs={{0,12},{4,8},{8,4},{12,0},{1,13},{5,9},{9,5},{13,1},{2,14},{6,10},... | collective-permute-start | bytes 786440 | tf_op jit(solution)/shard_map/ppermute | solution.py:40
  8.6 19.5 %collective-permute-start = (bf16[1,2,256,256]{3,2,1,0:T(8,128)(2,1)S(1)}, bf16[1,2,256,256]{3,2,1,0:T(8,128)(2,1)S(1)}, u32[]{:S(2)}, u32[]{:S(2)}) collective-permute-start(bf16[1,2,256,256]{3,2,1,0:T(8,128)(2,1)S(1)} %slice.7.refs_5_), channel_id=1, source_target_pairs={{0,12},{4,8},{8,4},{12,0},{1,13},{5,9},{9,5},{13,1},{2,14},{6,10},... | collective-permute-start | bytes 786440 | tf_op jit(solution)/shard_map/ppermute | solution.py:40
  8.9 24.0 %collective-permute-start.5 = (bf16[2,2,256,256]{3,2,1,0:T(8,128)(2,1)}, bf16[2,2,256,256]{3,2,1,0:T(8,128)(2,1)S(1)}, u32[]{:S(2)}, u32[]{:S(2)}) collective-permute-start(bf16[2,2,256,256]{3,2,1,0:T(8,128)(2,1)} %param.4), channel_id=1, source_target_pairs={{0,4},{4,0},{8,12},{12,8},{1,5},{5,1},{9,13},{13,9},{2,6},{6,2},{1... | collective-permute-start | bytes 1572872 | tf_op jit(solution)/shard_map/ppermute | solution.py:36
  16.2 22.1 %collective-permute-start.3 = (bf16[1,2,256,256]{3,2,1,0:T(8,128)(2,1)S(1)}, bf16[1,2,256,256]{3,2,1,0:T(8,128)(2,1)S(1)}, u32[]{:S(2)}, u32[]{:S(2)}) collective-permute-start(bf16[1,2,256,256]{3,2,1,0:T(8,128)(2,1)S(1)} %broadcast_select_fusion), channel_id=1, source_target_pairs={{0,8},{8,12},{12,4},{4,0},{1,9},{9,13},{13,5},{5,1},{2,10},{10,14}... | collective-permute-start | bytes 786440 | tf_op jit(solution)/shard_map/ppermute | solution.py:42
  29.1 13.4 %collective-permute-start.1 = (bf16[1,2,256,256]{3,2,1,0:T(8,128)(2,1)S(1)}, bf16[1,2,256,256]{3,2,1,0:T(8,128)(2,1)S(1)}, u32[]{:S(2)}, u32[]{:S(2)}) collective-permute-start(bf16[1,2,256,256]{3,2,1,0:T(8,128)(2,1)S(1)} %broadcast_select_fusion.1), channel_id=1, source_target_pairs={{0,8},{8,12},{12,4},{4,0},{1,9},{9,13},{13,5},{5,1},{2,10},{10,14}... | collective-permute-start | bytes 786440 | tf_op jit(solution)/shard_map/ppermute | solution.py:42
  38.3 4.1 %collective-permute-start.7 = (bf16[2,2,256,768]{3,2,1,0:T(8,128)(2,1)}, bf16[2,2,256,768]{3,2,1,0:T(8,128)(2,1)S(1)}, u32[]{:S(2)}, u32[]{:S(2)}) collective-permute-start(bf16[2,2,256,768]{3,2,1,0:T(8,128)(2,1)} %collective-permute-done.6.panel_ref), channel_id=1, source_target_pairs={{0,1},{1,0},{2,3},{3,2},{4,5},{5,4},{6,7},{7,6},{8,9},{9,8},{10,11... | collective-permute-start | bytes 4718600 | tf_op jit(solution)/shard_map/ppermute | solution.py:28

commit v14 on v13

--- a/solution.py
+++ b/solution.py
@@ -33,14 +33,13 @@
 
 
 def line_window(data):
-    near = lax.ppermute(data, "src", [(0, 1), (1, 0), (2, 3), (3, 2)])
+    near_pairs = [(0, 1), (1, 0), (2, 3), (3, 2)]
+    far = lax.ppermute(data, "src", [(0, 3), (1, 2), (2, 1), (3, 0)])
+    near = lax.ppermute(data, "src", near_pairs)
     windows = []
     for v in range(data.shape[0]):
-        own = (after(data, windows[-1][0][0]) if windows else data)[v : v + 1]
-        far = lax.ppermute(own, "src", [(0, 3), (1, 2), (2, 1), (3, 0)])
-        onward = jnp.where(at_end(), own, far)
-        across = lax.ppermute(onward, "src", [(0, 2), (2, 3), (3, 1), (1, 0)])
-        windows.append([(own, 0), (near, v), (across, 0), (far, 0)])
+        across = lax.ppermute(far[v : v + 1], "src", near_pairs)
+        windows.append([(data, v), (near, v), (across, 0), (far, v)])
     return windows
 
 

time: 45.5 us -> 44.6 us (0.980)
  waiting for transfers between devices: 8.66 us -> 16 us
  starting transfers between devices: 22.7 us -> 16.9 us
  other arithmetic: 1.99 us -> 0 us
  Pallas kernels: 9.85 us -> 8.21 us
  local copies, waits for them, and re-layouts: 1.94 us -> 3.17 us
    ppermute x5 -> x4, waiting for transfers between devices: 7.39 us -> 14.7 us  [the longest x1 13.2 us: line_window(): far = lax.ppermute(data, 'src', [(0, 3), (1, 2), (2, 1), (3, 0)])]
    ppermute x5 -> x4, starting transfers between devices: 19.7 us -> 14 us  [the longest x2 10.4 us: line_window(): across = lax.ppermute(far[v:v + 1], 'src', near_pairs)]
    unnamed x4 -> x6, local copies, waits for them, and re-layouts: 0.01 us -> 3.13 us
    select_n x2 -> x0, other arithmetic: 1.99 us -> none  [line_window(): onward = jnp.where(at_end(), own, far)]
    slice x2 -> x1, local copies, waits for them, and re-layouts: 1.93 us -> 0.03 us  [line_window(): across = lax.ppermute(far[v:v + 1], 'src', near_pairs)]
    pallas_call x1, Pallas kernels: 3.02 us -> 2.18 us  [body(): pl.pallas_call(functools.partial(kernel_b, half, late), out_shape=[window...]
    pallas_call x1, Pallas kernels: 4.13 us -> 3.32 us  [body(): pl.pallas_call(functools.partial(kernel_a, half, [{k: at for k, (_, at) i...]
  transfers between devices with their start and end apart: 8 -> 7, of which waited for: 3 -> 4; matrix products, arithmetic and copies ran while one was open for 9% -> 0% of each run, Pallas kernels for 16% -> 12%
where the time goes in v14:
time: 44.6 us; the launch traced here: 44.4 us
  starting transfers between devices  16.9 us (38%)
  waiting for transfers between devices  16 us (36%)
  Pallas kernels  8.21 us (18%)
  local copies, waits for them, and re-layouts  3.17 us (7%)
    ppermute x1, waiting for transfers between devices, line_window(): far = lax.ppermute(data, 'src', [(0, 3), (1, 2), (2, 1), (3, 0)])  13.2 us
    ppermute x2, starting transfers between devices, line_window(): across = lax.ppermute(far[v:v + 1], 'src', near_pairs)  10.4 us
    ppermute x1, starting transfers between devices, line_window(): far = lax.ppermute(data, 'src', [(0, 3), (1, 2), (2, 1), (3, 0)])  3.6 us
    pallas_call x1, Pallas kernels, body(): pl.pallas_call(functools.partial(kernel_a, half, [{k: at for k, (_, at) i...  3.32 us
    unnamed x6, local copies, waits for them, and re-layouts  3.13 us
    ppermute x3, starting transfers between devices, swap(): return lax.ppermute(x, axis, [(i, i ^ bit) for i in range(peers)])  2.94 us
    pallas_call x1, Pallas kernels, body(): pl.pallas_call(functools.partial(last_kernel, half + 1, late), out_shape=...  2.71 us
    pallas_call x1, Pallas kernels, body(): pl.pallas_call(functools.partial(kernel_b, half, late), out_shape=[window...  2.18 us
  transfers between devices with their start and end apart: 7, of which 4 were waited for; matrix products, arithmetic and copies ran while one was open for 0% of the time, Pallas kernels for 12%

profile of v14, /device:TPU:0, one launch (start us, length us, event | category | flops | bytes accessed | tf_op | source)
XLA Modules:
  0.0 44.4 jit_solution(1413763242494159993)
XLA Ops:
  0.0 0.5 %collective-permute-start.3 = (bf16[2,2,256,768]{3,2,1,0:T(8,128)(2,1)}, bf16[2,2,256,768]{3,2,1,0:T(8,128)(2,1)S(1)}, u32[]{:S(2)}, u32[]{:S(2)}) collective-permute-start(bf16[2,2,256,768]{3,2,1,0:T(8,128)(2,1)} %refs_0_.1), channel_id=1, source_target_pairs={{0,1},{1,0},{2,3},{3,2},{4,5},{5,4},{6,7},{7,6},{8,9},{9,8},{10,11... | collective-permute-start | bytes 4718600 | tf_op jit(solution)/shard_map/ppermute | solution.py:28
  0.5 2.5 %collective-permute-start.5 = (bf16[2,2,256,768]{3,2,1,0:T(8,128)(2,1)}, bf16[2,2,256,768]{3,2,1,0:T(8,128)(2,1)S(1)}, u32[]{:S(2)}, u32[]{:S(2)}) collective-permute-start(bf16[2,2,256,768]{3,2,1,0:T(8,128)(2,1)} %refs_0_.1), channel_id=1, source_target_pairs={{0,2},{1,3},{2,0},{3,1},{4,6},{5,7},{6,4},{7,5},{8,10},{9,11},{10,... | collective-permute-start | bytes 4718600 | tf_op jit(solution)/shard_map/ppermute | solution.py:28
  2.9 3.6 %collective-permute-start = (bf16[2,2,256,256]{3,2,1,0:T(8,128)(2,1)}, bf16[2,2,256,256]{3,2,1,0:T(8,128)(2,1)S(1)}, u32[]{:S(2)}, u32[]{:S(2)}) collective-permute-start(bf16[2,2,256,256]{3,2,1,0:T(8,128)(2,1)} %refs_5_.1), channel_id=1, source_target_pairs={{0,12},{4,8},{8,4},{12,0},{1,13},{5,9},{9,5},{13,1},{2,14},{6,10},... | collective-permute-start | bytes 1572872 | tf_op jit(solution)/shard_map/ppermute | solution.py:37
  6.5 0.0 collective-permute-start.4
  6.5 13.2 %collective-permute-done.refs_4_.refs_7_ = bf16[2,2,256,256]{3,2,1,0:T(8,128)(2,1)S(1)} collective-permute-done((bf16[2,2,256,256]{3,2,1,0:T(8,128)(2,1)}, bf16[2,2,256,256]{3,2,1,0:T(8,128)(2,1)S(1)}, u32[]{:S(2)}, u32[]{:S(2)}) %collective-permute-start) | collective-permute-done | bytes 524320 | tf_op jit(solution)/shard_map/ppermute | solution.py:37
  19.8 10.3 %collective-permute-start.2 = (bf16[1,2,256,256]{3,2,1,0:T(8,128)(2,1)S(1)}, bf16[1,2,256,256]{3,2,1,0:T(8,128)(2,1)S(1)}, u32[]{:S(2)}, u32[]{:S(2)}) collective-permute-start(bf16[1,2,256,256]{3,2,1,0:T(8,128)(2,1)S(1)} %get-tuple-element.29), channel_id=1, source_target_pairs={{0,4},{4,0},{8,12},{12,8},{1,5},{5,1},{9,13},{13,9},{2,6},{6,2},{1... | collective-permute-start | bytes 786440 | tf_op jit(solution)/shard_map/ppermute | solution.py:41
  30.1 0.1 collective-permute-start.1
  30.2 0.2 collective-permute-done.4.refs_3_.refs_6_
  30.4 0.0 collective-permute-done.3.refs_1_
  30.4 0.0 copy-start
  30.4 1.0 %copy-done = bf16[2,2,256,256]{3,2,1,0:T(8,128)(2,1)S(1)} copy-done((bf16[2,2,256,256]{3,2,1,0:T(8,128)(2,1)S(1)}, bf16[2,2,256,256]{3,2,1,0:T(8,128)(2,1)}, u32[]{:S(2)}) %copy-start) | copy-done | bytes 524312
  31.5 0.0 copy-start.1
  31.5 1.4 %copy-done.1 = bf16[2,2,256,768]{3,2,1,0:T(8,128)(2,1)S(1)} copy-done((bf16[2,2,256,768]{3,2,1,0:T(8,128)(2,1)S(1)}, bf16[2,2,256,768]{3,2,1,0:T(8,128)(2,1)}, u32[]{:S(2)}) %copy-start.1) | copy-done | bytes 1572888
  32.9 0.0 copy-start.2
  32.9 0.7 %copy-done.2 = s32[4,12]{1,0:T(4,128)S(1)} copy-done((s32[4,12]{1,0:T(4,128)S(1)}, s32[4,12]{1,0:T(4,128)}, u32[]{:S(2)}) %copy-start.2) | copy-done | bytes 216
  33.5 3.3 %shard_map.37 = (bf16[4,256,512]{2,1,0:T(8,128)(2,1)S(1)}, bf16[4,256,512]{2,1,0:T(8,128)(2,1)S(1)}, f32[512,256]{1,0:T(8,128)S(1)}, f32[512,256]{1,0:T(8,128)S(...) custom-call(s32[4,12]{1,0:T(4,128)S(1)} %copy-done.2, bf16[2,2,256,768]{3,2,1,0:T(8,128)(2,1)S(1)} %copy-done.1, ...), custom_call_target="tpu_custom_call" | custom-call | flops 161061280 | bytes 1048576 | tf_op jit(solution)/shard_map/pallas_call | solution.py:212
  36.9 1.3 %collective-permute-done.5.panel_ref = bf16[2,2,256,768]{3,2,1,0:T(8,128)(2,1)S(1)} collective-permute-done((bf16[2,2,256,768]{3,2,1,0:T(8,128)(2,1)}, bf16[2,2,256,768]{3,2,1,0:T(8,128)(2,1)S(1)}, u32[]{:S(2)}, u32[]{:S(2)}) %collective-permute-start.5) | collective-permute-done | bytes 1572896 | tf_op jit(solution)/shard_map/ppermute | solution.py:28
  38.2 0.0 collective-permute-start.6
  38.2 0.0 collective-permute-done.2.late_ref
  38.2 2.2 %shard_map.38 = (bf16[4,256,512]{2,1,0:T(8,128)(2,1)S(1)}, bf16[512,512]{1,0:T(8,128)(2,1)S(1)}, f32[2,256,256]{2,1,0:T(8,128)S(1)}, f32[2,256,256]{2,1,0:T(8,128)S(1)}) custom-call(s32[4,12]{1,0:T(4,128)S(1)} %copy-done.2, bf16[1,2,256,256]{3,2,1,0:T(8,128)(2,1)S(1)} %collective-permute-done.2.late_ref, ...), custom_call_target="tpu_custom_call", output_to_operand_aliasing={{0}: (2, {}), {2}: (6, {}), {3}: (7, {})} | custom-call | flops 161061280 | bytes 1048576 | tf_op jit(solution)/shard_map/pallas_call | solution.py:222
  40.4 1.2 %collective-permute-done.1.piece_ref = bf16[1,2,256,256]{3,2,1,0:T(8,128)(2,1)S(1)} collective-permute-done((bf16[1,2,256,256]{3,2,1,0:T(8,128)(2,1)S(1)}, bf16[1,2,256,256]{3,2,1,0:T(8,128)(2,1)S(1)}, u32[]{:S(2)}, u32[]{:S(2)}) %collective-permute-start.1) | collective-permute-done | bytes 262176 | tf_op jit(solution)/shard_map/ppermute | solution.py:41
  41.6 0.0 collective-permute-done.6.refs_0_
  41.6 2.7 %shard_map.40 = (f32[2,2,256,256]{3,2,1,0:T(8,128)}, bf16[4,256,512]{2,1,0:T(8,128)(2,1)S(1)}) custom-call(s32[4,12]{1,0:T(4,128)S(1)} %copy-done.2, bf16[1,2,256,256]{3,2,1,0:T(8,128)(2,1)S(1)} %shard_map.39.late_ref, bf16[4,256,512]{2,1,0:T(8,128)(2,1)S(1)} %get-tuple-element.24.first_window, ...), custom_call_target="tpu_custom_call", output_to_operand_aliasing={{1}: (3, {})} | custom-call | flops 1610612736 | bytes 1048576 | tf_op jit(solution)/shard_map/pallas_call | solution.py:232
  (2 shorter events, 0.0 us)
Async XLA Ops:
  0.0 30.4 %collective-permute-start.3 = (bf16[2,2,256,768]{3,2,1,0:T(8,128)(2,1)}, bf16[2,2,256,768]{3,2,1,0:T(8,128)(2,1)S(1)}, u32[]{:S(2)}, u32[]{:S(2)}) collective-permute-start(bf16[2,2,256,768]{3,2,1,0:T(8,128)(2,1)} %refs_0_.1), channel_id=1, source_target_pairs={{0,1},{1,0},{2,3},{3,2},{4,5},{5,4},{6,7},{7,6},{8,9},{9,8},{10,11... | collective-permute-start | bytes 4718600 | tf_op jit(solution)/shard_map/ppermute | solution.py:28
  0.5 37.8 %collective-permute-start.5 = (bf16[2,2,256,768]{3,2,1,0:T(8,128)(2,1)}, bf16[2,2,256,768]{3,2,1,0:T(8,128)(2,1)S(1)}, u32[]{:S(2)}, u32[]{:S(2)}) collective-permute-start(bf16[2,2,256,768]{3,2,1,0:T(8,128)(2,1)} %refs_0_.1), channel_id=1, source_target_pairs={{0,2},{1,3},{2,0},{3,1},{4,6},{5,7},{6,4},{7,5},{8,10},{9,11},{10,... | collective-permute-start | bytes 4718600 | tf_op jit(solution)/shard_map/ppermute | solution.py:28
  2.9 16.8 %collective-permute-start = (bf16[2,2,256,256]{3,2,1,0:T(8,128)(2,1)}, bf16[2,2,256,256]{3,2,1,0:T(8,128)(2,1)S(1)}, u32[]{:S(2)}, u32[]{:S(2)}) collective-permute-start(bf16[2,2,256,256]{3,2,1,0:T(8,128)(2,1)} %refs_5_.1), channel_id=1, source_target_pairs={{0,12},{4,8},{8,4},{12,0},{1,13},{5,9},{9,5},{13,1},{2,14},{6,10},... | collective-permute-start | bytes 1572872 | tf_op jit(solution)/shard_map/ppermute | solution.py:37
  6.5 23.9 %collective-permute-start.4 = (bf16[2,2,256,256]{3,2,1,0:T(8,128)(2,1)}, bf16[2,2,256,256]{3,2,1,0:T(8,128)(2,1)S(1)}, u32[]{:S(2)}, u32[]{:S(2)}) collective-permute-start(bf16[2,2,256,256]{3,2,1,0:T(8,128)(2,1)} %refs_5_.1), channel_id=1, source_target_pairs={{0,4},{4,0},{8,12},{12,8},{1,5},{5,1},{9,13},{13,9},{2,6},{6,2},{1... | collective-permute-start | bytes 1572872 | tf_op jit(solution)/shard_map/ppermute | solution.py:38
  19.8 18.4 %collective-permute-start.2 = (bf16[1,2,256,256]{3,2,1,0:T(8,128)(2,1)S(1)}, bf16[1,2,256,256]{3,2,1,0:T(8,128)(2,1)S(1)}, u32[]{:S(2)}, u32[]{:S(2)}) collective-permute-start(bf16[1,2,256,256]{3,2,1,0:T(8,128)(2,1)S(1)} %get-tuple-element.29), channel_id=1, source_target_pairs={{0,4},{4,0},{8,12},{12,8},{1,5},{5,1},{9,13},{13,9},{2,6},{6,2},{1... | collective-permute-start | bytes 786440 | tf_op jit(solution)/shard_map/ppermute | solution.py:41
  30.1 11.5 %collective-permute-start.1 = (bf16[1,2,256,256]{3,2,1,0:T(8,128)(2,1)S(1)}, bf16[1,2,256,256]{3,2,1,0:T(8,128)(2,1)S(1)}, u32[]{:S(2)}, u32[]{:S(2)}) collective-permute-start(bf16[1,2,256,256]{3,2,1,0:T(8,128)(2,1)S(1)} %get-tuple-element.30), channel_id=1, source_target_pairs={{0,4},{4,0},{8,12},{12,8},{1,5},{5,1},{9,13},{13,9},{2,6},{6,2},{1... | collective-permute-start | bytes 786440 | tf_op jit(solution)/shard_map/ppermute | solution.py:41
  30.4 1.0 %copy-start = (bf16[2,2,256,256]{3,2,1,0:T(8,128)(2,1)S(1)}, bf16[2,2,256,256]{3,2,1,0:T(8,128)(2,1)}, u32[]{:S(2)}) copy-start(bf16[2,2,256,256]{3,2,1,0:T(8,128)(2,1)} %refs_5_.1) | copy-start | bytes 1572868
  31.5 1.4 %copy-start.1 = (bf16[2,2,256,768]{3,2,1,0:T(8,128)(2,1)S(1)}, bf16[2,2,256,768]{3,2,1,0:T(8,128)(2,1)}, u32[]{:S(2)}) copy-start(bf16[2,2,256,768]{3,2,1,0:T(8,128)(2,1)} %refs_0_.1) | copy-start | bytes 4718596
  32.9 0.7 %copy-start.2 = (s32[4,12]{1,0:T(4,128)S(1)}, s32[4,12]{1,0:T(4,128)}, u32[]{:S(2)}) copy-start(s32[4,12]{1,0:T(4,128)} %aperture_ref.5) | copy-start | bytes 580
  38.2 3.4 %collective-permute-start.6 = (bf16[2,2,256,768]{3,2,1,0:T(8,128)(2,1)S(1)}, bf16[2,2,256,768]{3,2,1,0:T(8,128)(2,1)S(1)}, u32[]{:S(2)}, u32[]{:S(2)}) collective-permute-start(bf16[2,2,256,768]{3,2,1,0:T(8,128)(2,1)S(1)} %collective-permute-done.5.panel_ref), channel_id=1, source_target_pairs={{0,1},{1,0},{2,3},{3,2},{4,5},{5,4},{6,7},{7,6},{8,9},{9,8},{10,11... | collective-permute-start | bytes 4718600 | tf_op jit(solution)/shard_map/ppermute | solution.py:28

commit v15 on v14

--- a/solution.py
+++ b/solution.py
@@ -34,12 +34,12 @@
 
 def line_window(data):
     near_pairs = [(0, 1), (1, 0), (2, 3), (3, 2)]
-    far = lax.ppermute(data, "src", [(0, 3), (1, 2), (2, 1), (3, 0)])
     near = lax.ppermute(data, "src", near_pairs)
     windows = []
-    for v in range(data.shape[0]):
-        across = lax.ppermute(far[v : v + 1], "src", near_pairs)
-        windows.append([(data, v), (near, v), (across, 0), (far, v)])
+    for own in lax.optimization_barrier([data[v : v + 1] for v in range(data.shape[0])]):
+        far = lax.ppermute(own, "src", [(0, 3), (1, 2), (2, 1), (3, 0)])
+        across = lax.ppermute(far, "src", near_pairs)
+        windows.append([(own, 0), (near, len(windows)), (across, 0), (far, 0)])
     return windows
 
 
@@ -162,7 +162,8 @@
                 copies[-1].start()
         return copies
 
-    panels = [{far_half + m: ref.at[v] for m, ref in enumerate(panel_refs)} for v in range(2)]
+    each = len(panel_refs) // 2
+    panels = [{far_half + m: panel_refs[v * each + m].at[0] for m in range(each)} for v in range(2)]
     copies = finish(0, first_part, *product(first_window, aperture_ref, panels[0]))
     fill_window(window, {late: late_ref.at[0]})
     copies += finish(1, last_part, *product(window, aperture_ref, panels[1], two[...], late))
@@ -218,7 +219,7 @@
         cost_estimate=cost(0.1),
     )(aperture, *panels, *pieces)
 
-    handed_on = hand_on(far_panel, first_part)
+    handed_on = [hand_on(half_panel, first_part) for half_panel in (far_panel[:1], far_panel[1:])]
     first, two, first_part, last_part = pl.pallas_call(
         functools.partial(kernel_b, half, late),
         out_shape=[window, jax.ShapeDtypeStruct((2 * BLK, 2 * BLK), jnp.bfloat16), part, part],
@@ -232,13 +233,13 @@
     return pl.pallas_call(
         functools.partial(last_kernel, half + 1, late),
         out_shape=[jax.ShapeDtypeStruct((2, 2, BLK, width), jnp.float32), window],
-        in_specs=[smem] + [vmem] * (6 + len(handed_on)),
+        in_specs=[smem] + [vmem] * (6 + 2 * len(handed_on[0])),
         out_specs=[anywhere, vmem],
         scratch_shapes=[pltpu.VMEM((2, 2, BLK, width), jnp.float32), pltpu.SemaphoreType.DMA((2, 2, PIECES))],
         input_output_aliases={3: 1},
         compiler_params=limit(16),
         cost_estimate=cost(1),
-    )(aperture, held(late_pieces[1], two), first, last, two, first_part, last_part, *handed_on)[0]
+    )(aperture, held(late_pieces[1], two), first, last, two, first_part, last_part, *handed_on[0], *handed_on[1])[0]
 
 
 def solution(mesh):

time: 44.6 us -> 46.9 us (1.052)
  waiting for transfers between devices: 16 us -> 25.4 us
  starting transfers between devices: 16.9 us -> 9.79 us
    ppermute x3 -> x4, waiting for transfers between devices: 14.5 us -> 24.7 us  [the longest x2 21.8 us: line_window(): far = lax.ppermute(own, 'src', [(0, 3), (1, 2), (2, 1), (3, 0)])]
    ppermute x3 -> x4, starting transfers between devices: 14 us -> 4.7 us  [the longest x2 3.89 us: line_window(): far = lax.ppermute(own, 'src', [(0, 3), (1, 2), (2, 1), (3, 0)])]
    ppermute x1, starting transfers between devices: 0.01 us -> 1.58 us  [line_window(): near = lax.ppermute(data, 'src', near_pairs)]
    slice x1 -> x2, local copies, waits for them, and re-layouts: 0.03 us -> 1.17 us  [the longest x1 1.06 us: line_window(): data[v:v + 1]]
    unnamed x6, local copies, waits for them, and re-layouts: 3.13 us -> 2.09 us
    ppermute x3 -> x4, waiting for transfers between devices: 1.35 us -> 0.71 us  [swap(): return lax.ppermute(x, axis, [(i, i ^ bit) for i in range(peers)])]
    ppermute x3 -> x4, starting transfers between devices: 2.94 us -> 3.51 us  [swap(): return lax.ppermute(x, axis, [(i, i ^ bit) for i in range(peers)])]
  transfers between devices with their start and end apart: 7 -> 9, of which waited for: 4 -> 4; matrix products, arithmetic and copies ran while one was open for 0% -> 2% of each run, Pallas kernels for 12% -> 12%
where the time goes in v15:
time: 46.9 us; the launch traced here: 46.7 us
  waiting for transfers between devices  25.4 us (54%)
  starting transfers between devices  9.79 us (21%)
  Pallas kernels  8.21 us (18%)
  local copies, waits for them, and re-layouts  3.26 us (7%)
    ppermute x2, waiting for transfers between devices, line_window(): far = lax.ppermute(own, 'src', [(0, 3), (1, 2), (2, 1), (3, 0)])  21.8 us
    ppermute x2, starting transfers between devices, line_window(): far = lax.ppermute(own, 'src', [(0, 3), (1, 2), (2, 1), (3, 0)])  3.89 us
    ppermute x4, starting transfers between devices, swap(): return lax.ppermute(x, axis, [(i, i ^ bit) for i in range(peers)])  3.51 us
    pallas_call x1, Pallas kernels, body(): pl.pallas_call(functools.partial(kernel_a, half, [{k: at for k, (_, at) i...  3.32 us
    ppermute x2, waiting for transfers between devices, line_window(): across = lax.ppermute(far, 'src', near_pairs)  2.91 us
    pallas_call x1, Pallas kernels, body(): pl.pallas_call(functools.partial(last_kernel, half + 1, late), out_shape=...  2.71 us
    pallas_call x1, Pallas kernels, body(): pl.pallas_call(functools.partial(kernel_b, half, late), out_shape=[window...  2.18 us
    unnamed x6, local copies, waits for them, and re-layouts  2.09 us
  transfers between devices with their start and end apart: 9, of which 4 were waited for; matrix products, arithmetic and copies ran while one was open for 2% of the time, Pallas kernels for 12%

profile of v15, /device:TPU:0, one launch (start us, length us, event | category | flops | bytes accessed | tf_op | source)
XLA Modules:
  0.0 46.7 jit_solution(5945740108191505519)
XLA Ops:
  0.0 0.5 collective-permute-start.4
  0.5 2.5 %collective-permute-start.6 = (bf16[2,2,256,768]{3,2,1,0:T(8,128)(2,1)}, bf16[2,2,256,768]{3,2,1,0:T(8,128)(2,1)S(1)}, u32[]{:S(2)}, u32[]{:S(2)}) collective-permute-start(bf16[2,2,256,768]{3,2,1,0:T(8,128)(2,1)} %refs_0_.1), channel_id=1, source_target_pairs={{0,2},{1,3},{2,0},{3,1},{4,6},{5,7},{6,4},{7,5},{8,10},{9,11},{10,... | collective-permute-start | bytes 4718600 | tf_op jit(solution)/shard_map/ppermute | solution.py:28
  2.9 1.6 %collective-permute-start.5 = (bf16[2,2,256,256]{3,2,1,0:T(8,128)(2,1)}, bf16[2,2,256,256]{3,2,1,0:T(8,128)(2,1)S(1)}, u32[]{:S(2)}, u32[]{:S(2)}) collective-permute-start(bf16[2,2,256,256]{3,2,1,0:T(8,128)(2,1)} %param.4), channel_id=1, source_target_pairs={{0,4},{4,0},{8,12},{12,8},{1,5},{5,1},{9,13},{13,9},{2,6},{6,2},{1... | collective-permute-start | bytes 1572872 | tf_op jit(solution)/shard_map/ppermute | solution.py:37
  4.5 1.1 %fusion.1 = (bf16[1,2,256,256]{3,2,1,0:T(8,128)(2,1)S(1)}, bf16[1,2,256,256]{3,2,1,0:T(8,128)(2,1)S(1)}) fusion(bf16[2,2,256,256]{3,2,1,0:T(8,128)(2,1)} %param.4), kind=kLoop, calls=%fused_computation.1 | loop fusion | bytes 1048576 | tf_op jit(solution)/shard_map/slice | solution.py:39
  5.6 2.5 %collective-permute-start = (bf16[1,2,256,256]{3,2,1,0:T(8,128)(2,1)S(1)}, bf16[1,2,256,256]{3,2,1,0:T(8,128)(2,1)S(1)}, u32[]{:S(2)}, u32[]{:S(2)}) collective-permute-start(bf16[1,2,256,256]{3,2,1,0:T(8,128)(2,1)S(1)} %get-tuple-element.20.refs_5_), channel_id=1, source_target_pairs={{0,12},{4,8},{8,4},{12,0},{1,13},{5,9},{9,5},{13,1},{2,14},{6,10},... | collective-permute-start | bytes 786440 | tf_op jit(solution)/shard_map/ppermute | solution.py:40
  8.1 1.3 %collective-permute-start.2 = (bf16[1,2,256,256]{3,2,1,0:T(8,128)(2,1)S(1)}, bf16[1,2,256,256]{3,2,1,0:T(8,128)(2,1)S(1)}, u32[]{:S(2)}, u32[]{:S(2)}) collective-permute-start(bf16[1,2,256,256]{3,2,1,0:T(8,128)(2,1)S(1)} %get-tuple-element.21.refs_2_), channel_id=1, source_target_pairs={{0,12},{4,8},{8,4},{12,0},{1,13},{5,9},{9,5},{13,1},{2,14},{6,10},... | collective-permute-start | bytes 786440 | tf_op jit(solution)/shard_map/ppermute | solution.py:40
  9.5 16.2 %collective-permute-done.refs_7_ = bf16[1,2,256,256]{3,2,1,0:T(8,128)(2,1)S(1)} collective-permute-done((bf16[1,2,256,256]{3,2,1,0:T(8,128)(2,1)S(1)}, bf16[1,2,256,256]{3,2,1,0:T(8,128)(2,1)S(1)}, u32[]{:S(2)}, u32[]{:S(2)}) %collective-permute-start) | collective-permute-done | bytes 262176 | tf_op jit(solution)/shard_map/ppermute | solution.py:40
  25.7 0.0 collective-permute-start.1
  25.7 5.6 %collective-permute-done.2.refs_4_ = bf16[1,2,256,256]{3,2,1,0:T(8,128)(2,1)S(1)} collective-permute-done((bf16[1,2,256,256]{3,2,1,0:T(8,128)(2,1)S(1)}, bf16[1,2,256,256]{3,2,1,0:T(8,128)(2,1)S(1)}, u32[]{:S(2)}, u32[]{:S(2)}) %collective-permute-start.2) | collective-permute-done | bytes 262176 | tf_op jit(solution)/shard_map/ppermute | solution.py:40
  31.3 0.8 %collective-permute-start.3 = (bf16[1,2,256,256]{3,2,1,0:T(8,128)(2,1)S(1)}, bf16[1,2,256,256]{3,2,1,0:T(8,128)(2,1)S(1)}, u32[]{:S(2)}, u32[]{:S(2)}) collective-permute-start(bf16[1,2,256,256]{3,2,1,0:T(8,128)(2,1)S(1)} %collective-permute-done.2.refs_4_), channel_id=1, source_target_pairs={{0,4},{4,0},{8,12},{12,8},{1,5},{5,1},{9,13},{13,9},{2,6},{6,2},{1... | collective-permute-start | bytes 786440 | tf_op jit(solution)/shard_map/ppermute | solution.py:41
  32.1 0.0 collective-permute-done.5.refs_3_.refs_6_
  32.1 0.0 collective-permute-done.4.refs_1_
  32.1 0.0 copy-start
  32.1 1.4 %copy-done = bf16[2,2,256,768]{3,2,1,0:T(8,128)(2,1)S(1)} copy-done((bf16[2,2,256,768]{3,2,1,0:T(8,128)(2,1)S(1)}, bf16[2,2,256,768]{3,2,1,0:T(8,128)(2,1)}, u32[]{:S(2)}) %copy-start) | copy-done | bytes 1572888
  33.5 0.0 copy-start.1
  33.5 0.7 %copy-done.1 = s32[4,12]{1,0:T(4,128)S(1)} copy-done((s32[4,12]{1,0:T(4,128)S(1)}, s32[4,12]{1,0:T(4,128)}, u32[]{:S(2)}) %copy-start.1) | copy-done | bytes 216
  34.2 3.3 %shard_map.37 = (bf16[4,256,512]{2,1,0:T(8,128)(2,1)S(1)}, bf16[4,256,512]{2,1,0:T(8,128)(2,1)S(1)}, f32[512,256]{1,0:T(8,128)S(1)}, f32[512,256]{1,0:T(8,128)S(...) custom-call(s32[4,12]{1,0:T(4,128)S(1)} %copy-done.1, bf16[2,2,256,768]{3,2,1,0:T(8,128)(2,1)S(1)} %copy-done, ...), custom_call_target="tpu_custom_call" | custom-call | flops 161061280 | bytes 1048576 | tf_op jit(solution)/shard_map/pallas_call | solution.py:213
  37.5 0.0 copy-start.2
  37.5 0.7 %collective-permute-done.6.panel_ref = bf16[2,2,256,768]{3,2,1,0:T(8,128)(2,1)S(1)} collective-permute-done((bf16[2,2,256,768]{3,2,1,0:T(8,128)(2,1)}, bf16[2,2,256,768]{3,2,1,0:T(8,128)(2,1)S(1)}, u32[]{:S(2)}, u32[]{:S(2)}) %collective-permute-start.6) | collective-permute-done | bytes 1572896 | tf_op jit(solution)/shard_map/ppermute | solution.py:28
  38.2 0.1 fusion
  38.3 0.1 collective-permute-start.7
  38.4 0.5 %collective-permute-start.8 = (bf16[1,2,256,768]{3,2,1,0:T(8,128)(2,1)S(1)}, bf16[1,2,256,768]{3,2,1,0:T(8,128)(2,1)S(1)}, u32[]{:S(2)}, u32[]{:S(2)}) collective-permute-start(bf16[1,2,256,768]{3,2,1,0:T(8,128)(2,1)S(1)} %get-tuple-element.33), channel_id=1, source_target_pairs={{0,1},{1,0},{2,3},{3,2},{4,5},{5,4},{6,7},{7,6},{8,9},{9,8},{10,11... | collective-permute-start | bytes 2359304 | tf_op jit(solution)/shard_map/ppermute | solution.py:28
  38.9 2.9 %collective-permute-done.3.late_ref = bf16[1,2,256,256]{3,2,1,0:T(8,128)(2,1)S(1)} collective-permute-done((bf16[1,2,256,256]{3,2,1,0:T(8,128)(2,1)S(1)}, bf16[1,2,256,256]{3,2,1,0:T(8,128)(2,1)S(1)}, u32[]{:S(2)}, u32[]{:S(2)}) %collective-permute-start.3) | collective-permute-done | bytes 262176 | tf_op jit(solution)/shard_map/ppermute | solution.py:41
  41.8 0.0 copy-done.2
  41.8 2.2 %shard_map.38 = (bf16[4,256,512]{2,1,0:T(8,128)(2,1)S(1)}, bf16[512,512]{1,0:T(8,128)(2,1)S(1)}, f32[2,256,256]{2,1,0:T(8,128)S(1)}, f32[2,256,256]{2,1,0:T(8,128)S(1)}) custom-call(s32[4,12]{1,0:T(4,128)S(1)} %copy-done.2, bf16[1,2,256,256]{3,2,1,0:T(8,128)(2,1)S(1)} %collective-permute-done.3.late_ref, ...), custom_call_target="tpu_custom_call", output_to_operand_aliasing={{0}: (2, {}), {2}: (6, {}), {3}: (7, {})} | custom-call | flops 161061280 | bytes 1048576 | tf_op jit(solution)/shard_map/pallas_call | solution.py:223
  44.0 0.0 collective-permute-done.1.piece_ref
  44.0 0.0 collective-permute-done.7.refs_0_
  44.0 0.0 collective-permute-done.8.refs_1_
  44.0 2.7 %shard_map.40 = (f32[2,2,256,256]{3,2,1,0:T(8,128)}, bf16[4,256,512]{2,1,0:T(8,128)(2,1)S(1)}) custom-call(s32[4,12]{1,0:T(4,128)S(1)} %copy-done.2, bf16[1,2,256,256]{3,2,1,0:T(8,128)(2,1)S(1)} %shard_map.39.late_ref, bf16[4,256,512]{2,1,0:T(8,128)(2,1)S(1)} %get-tuple-element.29.first_window, ...), custom_call_target="tpu_custom_call", output_to_operand_aliasing={{1}: (3, {})} | custom-call | flops 1610612736 | bytes 1048576 | tf_op jit(solution)/shard_map/pallas_call | solution.py:233
  (1 shorter events, 0.0 us)
Async XLA Ops:
  0.0 32.1 %collective-permute-start.4 = (bf16[2,2,256,768]{3,2,1,0:T(8,128)(2,1)}, bf16[2,2,256,768]{3,2,1,0:T(8,128)(2,1)S(1)}, u32[]{:S(2)}, u32[]{:S(2)}) collective-permute-start(bf16[2,2,256,768]{3,2,1,0:T(8,128)(2,1)} %refs_0_.1), channel_id=1, source_target_pairs={{0,1},{1,0},{2,3},{3,2},{4,5},{5,4},{6,7},{7,6},{8,9},{9,8},{10,11... | collective-permute-start | bytes 4718600 | tf_op jit(solution)/shard_map/ppermute | solution.py:28
  0.5 37.8 %collective-permute-start.6 = (bf16[2,2,256,768]{3,2,1,0:T(8,128)(2,1)}, bf16[2,2,256,768]{3,2,1,0:T(8,128)(2,1)S(1)}, u32[]{:S(2)}, u32[]{:S(2)}) collective-permute-start(bf16[2,2,256,768]{3,2,1,0:T(8,128)(2,1)} %refs_0_.1), channel_id=1, source_target_pairs={{0,2},{1,3},{2,0},{3,1},{4,6},{5,7},{6,4},{7,5},{8,10},{9,11},{10,... | collective-permute-start | bytes 4718600 | tf_op jit(solution)/shard_map/ppermute | solution.py:28
  2.9 29.1 %collective-permute-start.5 = (bf16[2,2,256,256]{3,2,1,0:T(8,128)(2,1)}, bf16[2,2,256,256]{3,2,1,0:T(8,128)(2,1)S(1)}, u32[]{:S(2)}, u32[]{:S(2)}) collective-permute-start(bf16[2,2,256,256]{3,2,1,0:T(8,128)(2,1)} %param.4), channel_id=1, source_target_pairs={{0,4},{4,0},{8,12},{12,8},{1,5},{5,1},{9,13},{13,9},{2,6},{6,2},{1... | collective-permute-start | bytes 1572872 | tf_op jit(solution)/shard_map/ppermute | solution.py:37
  5.6 20.1 %collective-permute-start = (bf16[1,2,256,256]{3,2,1,0:T(8,128)(2,1)S(1)}, bf16[1,2,256,256]{3,2,1,0:T(8,128)(2,1)S(1)}, u32[]{:S(2)}, u32[]{:S(2)}) collective-permute-start(bf16[1,2,256,256]{3,2,1,0:T(8,128)(2,1)S(1)} %get-tuple-element.20.refs_5_), channel_id=1, source_target_pairs={{0,12},{4,8},{8,4},{12,0},{1,13},{5,9},{9,5},{13,1},{2,14},{6,10},... | collective-permute-start | bytes 786440 | tf_op jit(solution)/shard_map/ppermute | solution.py:40
  8.1 23.1 %collective-permute-start.2 = (bf16[1,2,256,256]{3,2,1,0:T(8,128)(2,1)S(1)}, bf16[1,2,256,256]{3,2,1,0:T(8,128)(2,1)S(1)}, u32[]{:S(2)}, u32[]{:S(2)}) collective-permute-start(bf16[1,2,256,256]{3,2,1,0:T(8,128)(2,1)S(1)} %get-tuple-element.21.refs_2_), channel_id=1, source_target_pairs={{0,12},{4,8},{8,4},{12,0},{1,13},{5,9},{9,5},{13,1},{2,14},{6,10},... | collective-permute-start | bytes 786440 | tf_op jit(solution)/shard_map/ppermute | solution.py:40
  25.7 18.3 %collective-permute-start.1 = (bf16[1,2,256,256]{3,2,1,0:T(8,128)(2,1)S(1)}, bf16[1,2,256,256]{3,2,1,0:T(8,128)(2,1)S(1)}, u32[]{:S(2)}, u32[]{:S(2)}) collective-permute-start(bf16[1,2,256,256]{3,2,1,0:T(8,128)(2,1)S(1)} %collective-permute-done.refs_7_), channel_id=1, source_target_pairs={{0,4},{4,0},{8,12},{12,8},{1,5},{5,1},{9,13},{13,9},{2,6},{6,2},{1... | collective-permute-start | bytes 786440 | tf_op jit(solution)/shard_map/ppermute | solution.py:41
  31.3 10.5 %collective-permute-start.3 = (bf16[1,2,256,256]{3,2,1,0:T(8,128)(2,1)S(1)}, bf16[1,2,256,256]{3,2,1,0:T(8,128)(2,1)S(1)}, u32[]{:S(2)}, u32[]{:S(2)}) collective-permute-start(bf16[1,2,256,256]{3,2,1,0:T(8,128)(2,1)S(1)} %collective-permute-done.2.refs_4_), channel_id=1, source_target_pairs={{0,4},{4,0},{8,12},{12,8},{1,5},{5,1},{9,13},{13,9},{2,6},{6,2},{1... | collective-permute-start | bytes 786440 | tf_op jit(solution)/shard_map/ppermute | solution.py:41
  32.1 1.4 %copy-start = (bf16[2,2,256,768]{3,2,1,0:T(8,128)(2,1)S(1)}, bf16[2,2,256,768]{3,2,1,0:T(8,128)(2,1)}, u32[]{:S(2)}) copy-start(bf16[2,2,256,768]{3,2,1,0:T(8,128)(2,1)} %refs_0_.1) | copy-start | bytes 4718596
  33.5 0.7 %copy-start.1 = (s32[4,12]{1,0:T(4,128)S(1)}, s32[4,12]{1,0:T(4,128)}, u32[]{:S(2)}) copy-start(s32[4,12]{1,0:T(4,128)} %aperture_ref.5) | copy-start | bytes 580
  37.5 4.3 %copy-start.2 = (s32[4,12]{1,0:T(4,128)S(1)}, s32[4,12]{1,0:T(4,128)}, u32[]{:S(2)}) copy-start(s32[4,12]{1,0:T(4,128)} %aperture_ref.5) | copy-start | bytes 580
  38.3 5.7 %collective-permute-start.7 = (bf16[1,2,256,768]{3,2,1,0:T(8,128)(2,1)S(1)}, bf16[1,2,256,768]{3,2,1,0:T(8,128)(2,1)S(1)}, u32[]{:S(2)}, u32[]{:S(2)}) collective-permute-start(bf16[1,2,256,768]{3,2,1,0:T(8,128)(2,1)S(1)} %get-tuple-element.32), channel_id=1, source_target_pairs={{0,1},{1,0},{2,3},{3,2},{4,5},{5,4},{6,7},{7,6},{8,9},{9,8},{10,11... | collective-permute-start | bytes 2359304 | tf_op jit(solution)/shard_map/ppermute | solution.py:28
  38.4 5.6 %collective-permute-start.8 = (bf16[1,2,256,768]{3,2,1,0:T(8,128)(2,1)S(1)}, bf16[1,2,256,768]{3,2,1,0:T(8,128)(2,1)S(1)}, u32[]{:S(2)}, u32[]{:S(2)}) collective-permute-start(bf16[1,2,256,768]{3,2,1,0:T(8,128)(2,1)S(1)} %get-tuple-element.33), channel_id=1, source_target_pairs={{0,1},{1,0},{2,3},{3,2},{4,5},{5,4},{6,7},{7,6},{8,9},{9,8},{10,11... | collective-permute-start | bytes 2359304 | tf_op jit(solution)/shard_map/ppermute | solution.py:28

commit v16 on v14

--- a/solution.py
+++ b/solution.py
@@ -84,26 +84,24 @@
     return [block - src + depth // 2 for block in wanted]
 
 
-def times(values, blocks):
-    both = jnp.dot(values, blocks, preferred_element_type=jnp.float32)
+def rows_of(panel):
+    return panel[...].reshape(2 * panel.shape[1], panel.shape[2])
+
+
+def product(window, aperture_ref, panels, late_in_two=None, late=None):
+    terms = []
+    for m, panel in panels.items():
+        values = rows_of(panel)
+        entries = slot_entries(aperture_ref, m, panel.shape[-1] // BLK, window.shape[0])
+        terms += [(values[:, q * BLK : (q + 1) * BLK], window[k]) for q, k in enumerate(entries)]
+    if late_in_two is not None:
+        terms += [(late_in_two[:, q * BLK : (q + 1) * BLK], window[late]) for q in range(2)]
+    both = None
+    for values, block in terms:
+        term = jnp.dot(values, block, preferred_element_type=jnp.float32)
+        both = term if both is None else both + term
     rows, width = both.shape[0] // 2, both.shape[1] // 2
     return both[:rows, :width] - both[rows:, width:], both[:rows, width:] + both[rows:, :width]
-
-
-def rows_of(panel):
-    return panel[...].reshape(2 * panel.shape[1], panel.shape[2])
-
-
-def product(window, aperture_ref, panels, late_in_two=None, late=None):
-    blocks = []
-    for m, panel in panels.items():
-        entries = slot_entries(aperture_ref, m, panel.shape[-1] // BLK, window.shape[0])
-        blocks += [window[k] for k in entries]
-    values = [rows_of(panel) for panel in panels.values()]
-    if late_in_two is not None:
-        values.append(late_in_two)
-        blocks += [window[late]] * 2
-    return times(jnp.concatenate(values, axis=1), jnp.concatenate(blocks, axis=0))
 
 
 def sum_of_late(aperture_ref, panels, late, depth):

time: 44.6 us -> 44.6 us (level)
  no operation moved by 1% of the time
where the time goes in v16:
time: 44.6 us; the launch traced here: 44.4 us
  starting transfers between devices  16.9 us (38%)
  waiting for transfers between devices  16 us (36%)
  Pallas kernels  8.24 us (18%)
  local copies, waits for them, and re-layouts  3.17 us (7%)
    ppermute x1, waiting for transfers between devices, line_window(): far = lax.ppermute(data, 'src', [(0, 3), (1, 2), (2, 1), (3, 0)])  13.2 us
    ppermute x2, starting transfers between devices, line_window(): across = lax.ppermute(far[v:v + 1], 'src', near_pairs)  10.4 us
    ppermute x1, starting transfers between devices, line_window(): far = lax.ppermute(data, 'src', [(0, 3), (1, 2), (2, 1), (3, 0)])  3.6 us
    pallas_call x1, Pallas kernels, body(): pl.pallas_call(functools.partial(kernel_a, half, [{k: at for k, (_, at) i...  3.35 us
    unnamed x6, local copies, waits for them, and re-layouts  3.13 us
    ppermute x3, starting transfers between devices, swap(): return lax.ppermute(x, axis, [(i, i ^ bit) for i in range(peers)])  2.94 us
    pallas_call x1, Pallas kernels, body(): pl.pallas_call(functools.partial(last_kernel, half + 1, late), out_shape=...  2.72 us
    pallas_call x1, Pallas kernels, body(): pl.pallas_call(functools.partial(kernel_b, half, late), out_shape=[window...  2.17 us
  transfers between devices with their start and end apart: 7, of which 4 were waited for; matrix products, arithmetic and copies ran while one was open for 0% of the time, Pallas kernels for 12%

profile of v16, /device:TPU:0, one launch (start us, length us, event | category | flops | bytes accessed | tf_op | source)
XLA Modules:
  0.0 44.4 jit_solution(17992530359347659562)
XLA Ops:
  0.0 0.5 %collective-permute-start.3 = (bf16[2,2,256,768]{3,2,1,0:T(8,128)(2,1)}, bf16[2,2,256,768]{3,2,1,0:T(8,128)(2,1)S(1)}, u32[]{:S(2)}, u32[]{:S(2)}) collective-permute-start(bf16[2,2,256,768]{3,2,1,0:T(8,128)(2,1)} %refs_0_.1), channel_id=1, source_target_pairs={{0,1},{1,0},{2,3},{3,2},{4,5},{5,4},{6,7},{7,6},{8,9},{9,8},{10,11... | collective-permute-start | bytes 4718600 | tf_op jit(solution)/shard_map/ppermute | solution.py:28
  0.5 2.5 %collective-permute-start.5 = (bf16[2,2,256,768]{3,2,1,0:T(8,128)(2,1)}, bf16[2,2,256,768]{3,2,1,0:T(8,128)(2,1)S(1)}, u32[]{:S(2)}, u32[]{:S(2)}) collective-permute-start(bf16[2,2,256,768]{3,2,1,0:T(8,128)(2,1)} %refs_0_.1), channel_id=1, source_target_pairs={{0,2},{1,3},{2,0},{3,1},{4,6},{5,7},{6,4},{7,5},{8,10},{9,11},{10,... | collective-permute-start | bytes 4718600 | tf_op jit(solution)/shard_map/ppermute | solution.py:28
  2.9 3.6 %collective-permute-start = (bf16[2,2,256,256]{3,2,1,0:T(8,128)(2,1)}, bf16[2,2,256,256]{3,2,1,0:T(8,128)(2,1)S(1)}, u32[]{:S(2)}, u32[]{:S(2)}) collective-permute-start(bf16[2,2,256,256]{3,2,1,0:T(8,128)(2,1)} %refs_5_.1), channel_id=1, source_target_pairs={{0,12},{4,8},{8,4},{12,0},{1,13},{5,9},{9,5},{13,1},{2,14},{6,10},... | collective-permute-start | bytes 1572872 | tf_op jit(solution)/shard_map/ppermute | solution.py:37
  6.5 0.0 collective-permute-start.4
  6.5 13.2 %collective-permute-done.refs_4_.refs_7_ = bf16[2,2,256,256]{3,2,1,0:T(8,128)(2,1)S(1)} collective-permute-done((bf16[2,2,256,256]{3,2,1,0:T(8,128)(2,1)}, bf16[2,2,256,256]{3,2,1,0:T(8,128)(2,1)S(1)}, u32[]{:S(2)}, u32[]{:S(2)}) %collective-permute-start) | collective-permute-done | bytes 524320 | tf_op jit(solution)/shard_map/ppermute | solution.py:37
  19.8 10.3 %collective-permute-start.2 = (bf16[1,2,256,256]{3,2,1,0:T(8,128)(2,1)S(1)}, bf16[1,2,256,256]{3,2,1,0:T(8,128)(2,1)S(1)}, u32[]{:S(2)}, u32[]{:S(2)}) collective-permute-start(bf16[1,2,256,256]{3,2,1,0:T(8,128)(2,1)S(1)} %get-tuple-element.29), channel_id=1, source_target_pairs={{0,4},{4,0},{8,12},{12,8},{1,5},{5,1},{9,13},{13,9},{2,6},{6,2},{1... | collective-permute-start | bytes 786440 | tf_op jit(solution)/shard_map/ppermute | solution.py:41
  30.1 0.1 collective-permute-start.1
  30.2 0.2 collective-permute-done.4.refs_3_.refs_6_
  30.4 0.0 collective-permute-done.3.refs_1_
  30.4 0.0 copy-start
  30.4 1.0 %copy-done = bf16[2,2,256,256]{3,2,1,0:T(8,128)(2,1)S(1)} copy-done((bf16[2,2,256,256]{3,2,1,0:T(8,128)(2,1)S(1)}, bf16[2,2,256,256]{3,2,1,0:T(8,128)(2,1)}, u32[]{:S(2)}) %copy-start) | copy-done | bytes 524312
  31.5 0.0 copy-start.1
  31.5 1.4 %copy-done.1 = bf16[2,2,256,768]{3,2,1,0:T(8,128)(2,1)S(1)} copy-done((bf16[2,2,256,768]{3,2,1,0:T(8,128)(2,1)S(1)}, bf16[2,2,256,768]{3,2,1,0:T(8,128)(2,1)}, u32[]{:S(2)}) %copy-start.1) | copy-done | bytes 1572888
  32.9 0.0 copy-start.2
  32.9 0.7 %copy-done.2 = s32[4,12]{1,0:T(4,128)S(1)} copy-done((s32[4,12]{1,0:T(4,128)S(1)}, s32[4,12]{1,0:T(4,128)}, u32[]{:S(2)}) %copy-start.2) | copy-done | bytes 216
  33.5 3.3 %shard_map.37 = (bf16[4,256,512]{2,1,0:T(8,128)(2,1)S(1)}, bf16[4,256,512]{2,1,0:T(8,128)(2,1)S(1)}, f32[512,256]{1,0:T(8,128)S(1)}, f32[512,256]{1,0:T(8,128)S(...) custom-call(s32[4,12]{1,0:T(4,128)S(1)} %copy-done.2, bf16[2,2,256,768]{3,2,1,0:T(8,128)(2,1)S(1)} %copy-done.1, ...), custom_call_target="tpu_custom_call" | custom-call | flops 161061280 | bytes 1048576 | tf_op jit(solution)/shard_map/pallas_call | solution.py:210
  36.9 1.3 %collective-permute-done.5.panel_ref = bf16[2,2,256,768]{3,2,1,0:T(8,128)(2,1)S(1)} collective-permute-done((bf16[2,2,256,768]{3,2,1,0:T(8,128)(2,1)}, bf16[2,2,256,768]{3,2,1,0:T(8,128)(2,1)S(1)}, u32[]{:S(2)}, u32[]{:S(2)}) %collective-permute-start.5) | collective-permute-done | bytes 1572896 | tf_op jit(solution)/shard_map/ppermute | solution.py:28
  38.2 0.0 collective-permute-start.6
  38.2 0.0 collective-permute-done.2.late_ref
  38.2 2.2 %shard_map.38 = (bf16[4,256,512]{2,1,0:T(8,128)(2,1)S(1)}, bf16[512,512]{1,0:T(8,128)(2,1)S(1)}, f32[2,256,256]{2,1,0:T(8,128)S(1)}, f32[2,256,256]{2,1,0:T(8,128)S(1)}) custom-call(s32[4,12]{1,0:T(4,128)S(1)} %copy-done.2, bf16[1,2,256,256]{3,2,1,0:T(8,128)(2,1)S(1)} %collective-permute-done.2.late_ref, ...), custom_call_target="tpu_custom_call", output_to_operand_aliasing={{0}: (2, {}), {2}: (6, {}), {3}: (7, {})} | custom-call | flops 161061280 | bytes 1048576 | tf_op jit(solution)/shard_map/pallas_call | solution.py:220
  40.4 1.2 %collective-permute-done.1.piece_ref = bf16[1,2,256,256]{3,2,1,0:T(8,128)(2,1)S(1)} collective-permute-done((bf16[1,2,256,256]{3,2,1,0:T(8,128)(2,1)S(1)}, bf16[1,2,256,256]{3,2,1,0:T(8,128)(2,1)S(1)}, u32[]{:S(2)}, u32[]{:S(2)}) %collective-permute-start.1) | collective-permute-done | bytes 262176 | tf_op jit(solution)/shard_map/ppermute | solution.py:41
  41.6 0.0 collective-permute-done.6.refs_0_
  41.6 2.7 %shard_map.40 = (f32[2,2,256,256]{3,2,1,0:T(8,128)}, bf16[4,256,512]{2,1,0:T(8,128)(2,1)S(1)}) custom-call(s32[4,12]{1,0:T(4,128)S(1)} %copy-done.2, bf16[1,2,256,256]{3,2,1,0:T(8,128)(2,1)S(1)} %shard_map.39.late_ref, bf16[4,256,512]{2,1,0:T(8,128)(2,1)S(1)} %get-tuple-element.24.first_window, ...), custom_call_target="tpu_custom_call", output_to_operand_aliasing={{1}: (3, {})} | custom-call | flops 1610612736 | bytes 1048576 | tf_op jit(solution)/shard_map/pallas_call | solution.py:230
  (2 shorter events, 0.0 us)
Async XLA Ops:
  0.0 30.4 %collective-permute-start.3 = (bf16[2,2,256,768]{3,2,1,0:T(8,128)(2,1)}, bf16[2,2,256,768]{3,2,1,0:T(8,128)(2,1)S(1)}, u32[]{:S(2)}, u32[]{:S(2)}) collective-permute-start(bf16[2,2,256,768]{3,2,1,0:T(8,128)(2,1)} %refs_0_.1), channel_id=1, source_target_pairs={{0,1},{1,0},{2,3},{3,2},{4,5},{5,4},{6,7},{7,6},{8,9},{9,8},{10,11... | collective-permute-start | bytes 4718600 | tf_op jit(solution)/shard_map/ppermute | solution.py:28
  0.5 37.8 %collective-permute-start.5 = (bf16[2,2,256,768]{3,2,1,0:T(8,128)(2,1)}, bf16[2,2,256,768]{3,2,1,0:T(8,128)(2,1)S(1)}, u32[]{:S(2)}, u32[]{:S(2)}) collective-permute-start(bf16[2,2,256,768]{3,2,1,0:T(8,128)(2,1)} %refs_0_.1), channel_id=1, source_target_pairs={{0,2},{1,3},{2,0},{3,1},{4,6},{5,7},{6,4},{7,5},{8,10},{9,11},{10,... | collective-permute-start | bytes 4718600 | tf_op jit(solution)/shard_map/ppermute | solution.py:28
  2.9 16.8 %collective-permute-start = (bf16[2,2,256,256]{3,2,1,0:T(8,128)(2,1)}, bf16[2,2,256,256]{3,2,1,0:T(8,128)(2,1)S(1)}, u32[]{:S(2)}, u32[]{:S(2)}) collective-permute-start(bf16[2,2,256,256]{3,2,1,0:T(8,128)(2,1)} %refs_5_.1), channel_id=1, source_target_pairs={{0,12},{4,8},{8,4},{12,0},{1,13},{5,9},{9,5},{13,1},{2,14},{6,10},... | collective-permute-start | bytes 1572872 | tf_op jit(solution)/shard_map/ppermute | solution.py:37
  6.5 23.9 %collective-permute-start.4 = (bf16[2,2,256,256]{3,2,1,0:T(8,128)(2,1)}, bf16[2,2,256,256]{3,2,1,0:T(8,128)(2,1)S(1)}, u32[]{:S(2)}, u32[]{:S(2)}) collective-permute-start(bf16[2,2,256,256]{3,2,1,0:T(8,128)(2,1)} %refs_5_.1), channel_id=1, source_target_pairs={{0,4},{4,0},{8,12},{12,8},{1,5},{5,1},{9,13},{13,9},{2,6},{6,2},{1... | collective-permute-start | bytes 1572872 | tf_op jit(solution)/shard_map/ppermute | solution.py:38
  19.8 18.4 %collective-permute-start.2 = (bf16[1,2,256,256]{3,2,1,0:T(8,128)(2,1)S(1)}, bf16[1,2,256,256]{3,2,1,0:T(8,128)(2,1)S(1)}, u32[]{:S(2)}, u32[]{:S(2)}) collective-permute-start(bf16[1,2,256,256]{3,2,1,0:T(8,128)(2,1)S(1)} %get-tuple-element.29), channel_id=1, source_target_pairs={{0,4},{4,0},{8,12},{12,8},{1,5},{5,1},{9,13},{13,9},{2,6},{6,2},{1... | collective-permute-start | bytes 786440 | tf_op jit(solution)/shard_map/ppermute | solution.py:41
  30.1 11.5 %collective-permute-start.1 = (bf16[1,2,256,256]{3,2,1,0:T(8,128)(2,1)S(1)}, bf16[1,2,256,256]{3,2,1,0:T(8,128)(2,1)S(1)}, u32[]{:S(2)}, u32[]{:S(2)}) collective-permute-start(bf16[1,2,256,256]{3,2,1,0:T(8,128)(2,1)S(1)} %get-tuple-element.30), channel_id=1, source_target_pairs={{0,4},{4,0},{8,12},{12,8},{1,5},{5,1},{9,13},{13,9},{2,6},{6,2},{1... | collective-permute-start | bytes 786440 | tf_op jit(solution)/shard_map/ppermute | solution.py:41
  30.4 1.0 %copy-start = (bf16[2,2,256,256]{3,2,1,0:T(8,128)(2,1)S(1)}, bf16[2,2,256,256]{3,2,1,0:T(8,128)(2,1)}, u32[]{:S(2)}) copy-start(bf16[2,2,256,256]{3,2,1,0:T(8,128)(2,1)} %refs_5_.1) | copy-start | bytes 1572868
  31.5 1.4 %copy-start.1 = (bf16[2,2,256,768]{3,2,1,0:T(8,128)(2,1)S(1)}, bf16[2,2,256,768]{3,2,1,0:T(8,128)(2,1)}, u32[]{:S(2)}) copy-start(bf16[2,2,256,768]{3,2,1,0:T(8,128)(2,1)} %refs_0_.1) | copy-start | bytes 4718596
  32.9 0.7 %copy-start.2 = (s32[4,12]{1,0:T(4,128)S(1)}, s32[4,12]{1,0:T(4,128)}, u32[]{:S(2)}) copy-start(s32[4,12]{1,0:T(4,128)} %aperture_ref.5) | copy-start | bytes 580
  38.2 3.4 %collective-permute-start.6 = (bf16[2,2,256,768]{3,2,1,0:T(8,128)(2,1)S(1)}, bf16[2,2,256,768]{3,2,1,0:T(8,128)(2,1)S(1)}, u32[]{:S(2)}, u32[]{:S(2)}) collective-permute-start(bf16[2,2,256,768]{3,2,1,0:T(8,128)(2,1)S(1)} %collective-permute-done.5.panel_ref), channel_id=1, source_target_pairs={{0,1},{1,0},{2,3},{3,2},{4,5},{5,4},{6,7},{7,6},{8,9},{9,8},{10,11... | collective-permute-start | bytes 4718600 | tf_op jit(solution)/shard_map/ppermute | solution.py:28

commit v17 on v14

--- a/solution.py
+++ b/solution.py
@@ -77,8 +77,11 @@
 
 def slot_entries(aperture_ref, m, per_shard, depth):
     src = lax.axis_index("src")
-    shard = lax.bitwise_xor(lax.axis_index("rcv"), m)
-    wanted = [aperture_ref[src, shard * per_shard + q] for q in range(per_shard)]
+    first_slot = lax.bitwise_xor(lax.axis_index("rcv"), m) * per_shard
+    blocks = aperture_ref[...]
+    at_row = lax.broadcasted_iota(jnp.int32, blocks.shape, 0) == src
+    at_slot = lax.broadcasted_iota(jnp.int32, blocks.shape, 1)
+    wanted = [jnp.sum(jnp.where(at_row & (at_slot == first_slot + q), blocks, 0)) for q in range(per_shard)]
     if lax.axis_size("src") == 4:
         return [lax.bitwise_xor(src, block) for block in wanted]
     return [block - src + depth // 2 for block in wanted]
@@ -203,7 +206,7 @@
     late = 2 if line else len(windows[0]) - 1
     late_pieces = [piece[at : at + 1] for piece, at in (window[late] for window in windows)]
     early = [{k: piece for k, piece in enumerate(window) if k != late} for window in windows]
-    vmem, smem, anywhere = spec(pltpu.VMEM), spec(pltpu.SMEM), spec(pl.ANY)
+    vmem, anywhere = spec(pltpu.VMEM), spec(pl.ANY)
     window = jax.ShapeDtypeStruct((len(windows[0]), BLK, 2 * width), jnp.bfloat16)
     total = jax.ShapeDtypeStruct((2 * BLK, BLK), jnp.float32)
     part = jax.ShapeDtypeStruct((2, BLK, width), jnp.float32)
@@ -212,7 +215,7 @@
     first, last, first_sum, last_sum, first_part, last_part = pl.pallas_call(
         functools.partial(kernel_a, half, [{k: at for k, (_, at) in pieces.items()} for pieces in early], late),
         out_shape=[window] * 2 + [total] * 2 + [part] * 2,
-        in_specs=[smem] + [vmem] * (half + len(pieces)),
+        in_specs=[vmem] + [vmem] * (half + len(pieces)),
         out_specs=[vmem] * 6,
         compiler_params=limit(16),
         cost_estimate=cost(0.1),
@@ -222,7 +225,7 @@
     first, two, first_part, last_part = pl.pallas_call(
         functools.partial(kernel_b, half, late),
         out_shape=[window, jax.ShapeDtypeStruct((2 * BLK, 2 * BLK), jnp.bfloat16), part, part],
-        in_specs=[smem] + [vmem] * 8,
+        in_specs=[vmem] + [vmem] * 8,
         out_specs=[vmem] * 4,
         input_output_aliases={2: 0, 6: 2, 7: 3},
         compiler_params=limit(16),
@@ -232,7 +235,7 @@
     return pl.pallas_call(
         functools.partial(last_kernel, half + 1, late),
         out_shape=[jax.ShapeDtypeStruct((2, 2, BLK, width), jnp.float32), window],
-        in_specs=[smem] + [vmem] * (6 + len(handed_on)),
+        in_specs=[vmem] + [vmem] * (6 + len(handed_on)),
         out_specs=[anywhere, vmem],
         scratch_shapes=[pltpu.VMEM((2, 2, BLK, width), jnp.float32), pltpu.SemaphoreType.DMA((2, 2, PIECES))],
         input_output_aliases={3: 1},

time: 44.6 us -> 44.1 us (0.989)
  Pallas kernels: 8.21 us -> 7.15 us
  waiting for transfers between devices: 16 us -> 16.7 us
  transfers between devices with their start and end apart: 7 -> 7, of which waited for: 4 -> 4; matrix products, arithmetic and copies ran while one was open for 0% -> 0% of each run, Pallas kernels for 12% -> 11%
where the time goes in v17:
time: 44.1 us; the launch traced here: 43.9 us
  starting transfers between devices  16.9 us (38%)
  waiting for transfers between devices  16.7 us (38%)
  Pallas kernels  7.15 us (16%)
  local copies, waits for them, and re-layouts  3.17 us (7%)
    ppermute x1, waiting for transfers between devices, line_window(): far = lax.ppermute(data, 'src', [(0, 3), (1, 2), (2, 1), (3, 0)])  13.2 us
    ppermute x2, starting transfers between devices, line_window(): across = lax.ppermute(far[v:v + 1], 'src', near_pairs)  10.4 us
    ppermute x1, starting transfers between devices, line_window(): far = lax.ppermute(data, 'src', [(0, 3), (1, 2), (2, 1), (3, 0)])  3.6 us
    unnamed x6, local copies, waits for them, and re-layouts  3.13 us
    pallas_call x1, Pallas kernels, body(): pl.pallas_call(functools.partial(kernel_a, half, [{k: at for k, (_, at) i...  3.02 us
    ppermute x3, starting transfers between devices, swap(): return lax.ppermute(x, axis, [(i, i ^ bit) for i in range(peers)])  2.94 us
    pallas_call x1, Pallas kernels, body(): pl.pallas_call(functools.partial(last_kernel, half + 1, late), out_shape=...  2.26 us
    pallas_call x1, Pallas kernels, body(): pl.pallas_call(functools.partial(kernel_b, half, late), out_shape=[window...  1.86 us
  transfers between devices with their start and end apart: 7, of which 4 were waited for; matrix products, arithmetic and copies ran while one was open for 0% of the time, Pallas kernels for 11%

profile of v17, /device:TPU:0, one launch (start us, length us, event | category | flops | bytes accessed | tf_op | source)
XLA Modules:
  0.0 43.9 jit_solution(16168864924548728071)
XLA Ops:
  0.0 0.5 %collective-permute-start.3 = (bf16[2,2,256,768]{3,2,1,0:T(8,128)(2,1)}, bf16[2,2,256,768]{3,2,1,0:T(8,128)(2,1)S(1)}, u32[]{:S(2)}, u32[]{:S(2)}) collective-permute-start(bf16[2,2,256,768]{3,2,1,0:T(8,128)(2,1)} %refs_0_.1), channel_id=1, source_target_pairs={{0,1},{1,0},{2,3},{3,2},{4,5},{5,4},{6,7},{7,6},{8,9},{9,8},{10,11... | collective-permute-start | bytes 4718600 | tf_op jit(solution)/shard_map/ppermute | solution.py:28
  0.5 2.5 %collective-permute-start.5 = (bf16[2,2,256,768]{3,2,1,0:T(8,128)(2,1)}, bf16[2,2,256,768]{3,2,1,0:T(8,128)(2,1)S(1)}, u32[]{:S(2)}, u32[]{:S(2)}) collective-permute-start(bf16[2,2,256,768]{3,2,1,0:T(8,128)(2,1)} %refs_0_.1), channel_id=1, source_target_pairs={{0,2},{1,3},{2,0},{3,1},{4,6},{5,7},{6,4},{7,5},{8,10},{9,11},{10,... | collective-permute-start | bytes 4718600 | tf_op jit(solution)/shard_map/ppermute | solution.py:28
  2.9 3.6 %collective-permute-start = (bf16[2,2,256,256]{3,2,1,0:T(8,128)(2,1)}, bf16[2,2,256,256]{3,2,1,0:T(8,128)(2,1)S(1)}, u32[]{:S(2)}, u32[]{:S(2)}) collective-permute-start(bf16[2,2,256,256]{3,2,1,0:T(8,128)(2,1)} %refs_5_.1), channel_id=1, source_target_pairs={{0,12},{4,8},{8,4},{12,0},{1,13},{5,9},{9,5},{13,1},{2,14},{6,10},... | collective-permute-start | bytes 1572872 | tf_op jit(solution)/shard_map/ppermute | solution.py:37
  6.5 0.0 collective-permute-start.4
  6.5 13.2 %collective-permute-done.refs_4_.refs_7_ = bf16[2,2,256,256]{3,2,1,0:T(8,128)(2,1)S(1)} collective-permute-done((bf16[2,2,256,256]{3,2,1,0:T(8,128)(2,1)}, bf16[2,2,256,256]{3,2,1,0:T(8,128)(2,1)S(1)}, u32[]{:S(2)}, u32[]{:S(2)}) %collective-permute-start) | collective-permute-done | bytes 524320 | tf_op jit(solution)/shard_map/ppermute | solution.py:37
  19.8 10.3 %collective-permute-start.2 = (bf16[1,2,256,256]{3,2,1,0:T(8,128)(2,1)S(1)}, bf16[1,2,256,256]{3,2,1,0:T(8,128)(2,1)S(1)}, u32[]{:S(2)}, u32[]{:S(2)}) collective-permute-start(bf16[1,2,256,256]{3,2,1,0:T(8,128)(2,1)S(1)} %get-tuple-element.29), channel_id=1, source_target_pairs={{0,4},{4,0},{8,12},{12,8},{1,5},{5,1},{9,13},{13,9},{2,6},{6,2},{1... | collective-permute-start | bytes 786440 | tf_op jit(solution)/shard_map/ppermute | solution.py:41
  30.1 0.1 collective-permute-start.1
  30.2 0.2 collective-permute-done.4.refs_3_.refs_6_
  30.4 0.0 collective-permute-done.3.refs_1_
  30.4 0.0 copy-start
  30.4 1.0 %copy-done = bf16[2,2,256,256]{3,2,1,0:T(8,128)(2,1)S(1)} copy-done((bf16[2,2,256,256]{3,2,1,0:T(8,128)(2,1)S(1)}, bf16[2,2,256,256]{3,2,1,0:T(8,128)(2,1)}, u32[]{:S(2)}) %copy-start) | copy-done | bytes 524312
  31.5 0.0 copy-start.1
  31.5 1.4 %copy-done.1 = bf16[2,2,256,768]{3,2,1,0:T(8,128)(2,1)S(1)} copy-done((bf16[2,2,256,768]{3,2,1,0:T(8,128)(2,1)S(1)}, bf16[2,2,256,768]{3,2,1,0:T(8,128)(2,1)}, u32[]{:S(2)}) %copy-start.1) | copy-done | bytes 1572888
  32.9 0.0 copy-start.2
  32.9 0.7 %copy-done.2 = s32[4,12]{1,0:T(4,128)S(1)} copy-done((s32[4,12]{1,0:T(4,128)S(1)}, s32[4,12]{1,0:T(4,128)}, u32[]{:S(2)}) %copy-start.2) | copy-done | bytes 216
  33.5 3.0 %shard_map.37 = (bf16[4,256,512]{2,1,0:T(8,128)(2,1)S(1)}, bf16[4,256,512]{2,1,0:T(8,128)(2,1)S(1)}, f32[512,256]{1,0:T(8,128)S(1)}, f32[512,256]{1,0:T(8,128)S(...) custom-call(s32[4,12]{1,0:T(4,128)S(1)} %copy-done.2, bf16[2,2,256,768]{3,2,1,0:T(8,128)(2,1)S(1)} %copy-done.1, ...), custom_call_target="tpu_custom_call" | custom-call | flops 161061280 | bytes 1048576 | tf_op jit(solution)/shard_map/pallas_call | solution.py:215
  36.6 1.6 %collective-permute-done.5.panel_ref = bf16[2,2,256,768]{3,2,1,0:T(8,128)(2,1)S(1)} collective-permute-done((bf16[2,2,256,768]{3,2,1,0:T(8,128)(2,1)}, bf16[2,2,256,768]{3,2,1,0:T(8,128)(2,1)S(1)}, u32[]{:S(2)}, u32[]{:S(2)}) %collective-permute-start.5) | collective-permute-done | bytes 1572896 | tf_op jit(solution)/shard_map/ppermute | solution.py:28
  38.2 0.0 collective-permute-start.6
  38.2 0.0 collective-permute-done.2.late_ref
  38.2 1.9 %shard_map.38 = (bf16[4,256,512]{2,1,0:T(8,128)(2,1)S(1)}, bf16[512,512]{1,0:T(8,128)(2,1)S(1)}, f32[2,256,256]{2,1,0:T(8,128)S(1)}, f32[2,256,256]{2,1,0:T(8,128)S(1)}) custom-call(s32[4,12]{1,0:T(4,128)S(1)} %copy-done.2, bf16[1,2,256,256]{3,2,1,0:T(8,128)(2,1)S(1)} %collective-permute-done.2.late_ref, ...), custom_call_target="tpu_custom_call", output_to_operand_aliasing={{0}: (2, {}), {2}: (6, {}), {3}: (7, {})} | custom-call | flops 161061280 | bytes 1048576 | tf_op jit(solution)/shard_map/pallas_call | solution.py:225
  40.1 1.6 %collective-permute-done.1.piece_ref = bf16[1,2,256,256]{3,2,1,0:T(8,128)(2,1)S(1)} collective-permute-done((bf16[1,2,256,256]{3,2,1,0:T(8,128)(2,1)S(1)}, bf16[1,2,256,256]{3,2,1,0:T(8,128)(2,1)S(1)}, u32[]{:S(2)}, u32[]{:S(2)}) %collective-permute-start.1) | collective-permute-done | bytes 262176 | tf_op jit(solution)/shard_map/ppermute | solution.py:41
  41.6 0.0 collective-permute-done.6.refs_0_
  41.6 2.3 %shard_map.40 = (f32[2,2,256,256]{3,2,1,0:T(8,128)}, bf16[4,256,512]{2,1,0:T(8,128)(2,1)S(1)}) custom-call(s32[4,12]{1,0:T(4,128)S(1)} %copy-done.2, bf16[1,2,256,256]{3,2,1,0:T(8,128)(2,1)S(1)} %shard_map.39.late_ref, bf16[4,256,512]{2,1,0:T(8,128)(2,1)S(1)} %get-tuple-element.24.first_window, ...), custom_call_target="tpu_custom_call", output_to_operand_aliasing={{1}: (3, {})} | custom-call | flops 1610612736 | bytes 1048576 | tf_op jit(solution)/shard_map/pallas_call | solution.py:235
  (2 shorter events, 0.0 us)
Async XLA Ops:
  0.0 30.4 %collective-permute-start.3 = (bf16[2,2,256,768]{3,2,1,0:T(8,128)(2,1)}, bf16[2,2,256,768]{3,2,1,0:T(8,128)(2,1)S(1)}, u32[]{:S(2)}, u32[]{:S(2)}) collective-permute-start(bf16[2,2,256,768]{3,2,1,0:T(8,128)(2,1)} %refs_0_.1), channel_id=1, source_target_pairs={{0,1},{1,0},{2,3},{3,2},{4,5},{5,4},{6,7},{7,6},{8,9},{9,8},{10,11... | collective-permute-start | bytes 4718600 | tf_op jit(solution)/shard_map/ppermute | solution.py:28
  0.5 37.8 %collective-permute-start.5 = (bf16[2,2,256,768]{3,2,1,0:T(8,128)(2,1)}, bf16[2,2,256,768]{3,2,1,0:T(8,128)(2,1)S(1)}, u32[]{:S(2)}, u32[]{:S(2)}) collective-permute-start(bf16[2,2,256,768]{3,2,1,0:T(8,128)(2,1)} %refs_0_.1), channel_id=1, source_target_pairs={{0,2},{1,3},{2,0},{3,1},{4,6},{5,7},{6,4},{7,5},{8,10},{9,11},{10,... | collective-permute-start | bytes 4718600 | tf_op jit(solution)/shard_map/ppermute | solution.py:28
  2.9 16.8 %collective-permute-start = (bf16[2,2,256,256]{3,2,1,0:T(8,128)(2,1)}, bf16[2,2,256,256]{3,2,1,0:T(8,128)(2,1)S(1)}, u32[]{:S(2)}, u32[]{:S(2)}) collective-permute-start(bf16[2,2,256,256]{3,2,1,0:T(8,128)(2,1)} %refs_5_.1), channel_id=1, source_target_pairs={{0,12},{4,8},{8,4},{12,0},{1,13},{5,9},{9,5},{13,1},{2,14},{6,10},... | collective-permute-start | bytes 1572872 | tf_op jit(solution)/shard_map/ppermute | solution.py:37
  6.5 23.9 %collective-permute-start.4 = (bf16[2,2,256,256]{3,2,1,0:T(8,128)(2,1)}, bf16[2,2,256,256]{3,2,1,0:T(8,128)(2,1)S(1)}, u32[]{:S(2)}, u32[]{:S(2)}) collective-permute-start(bf16[2,2,256,256]{3,2,1,0:T(8,128)(2,1)} %refs_5_.1), channel_id=1, source_target_pairs={{0,4},{4,0},{8,12},{12,8},{1,5},{5,1},{9,13},{13,9},{2,6},{6,2},{1... | collective-permute-start | bytes 1572872 | tf_op jit(solution)/shard_map/ppermute | solution.py:38
  19.8 18.4 %collective-permute-start.2 = (bf16[1,2,256,256]{3,2,1,0:T(8,128)(2,1)S(1)}, bf16[1,2,256,256]{3,2,1,0:T(8,128)(2,1)S(1)}, u32[]{:S(2)}, u32[]{:S(2)}) collective-permute-start(bf16[1,2,256,256]{3,2,1,0:T(8,128)(2,1)S(1)} %get-tuple-element.29), channel_id=1, source_target_pairs={{0,4},{4,0},{8,12},{12,8},{1,5},{5,1},{9,13},{13,9},{2,6},{6,2},{1... | collective-permute-start | bytes 786440 | tf_op jit(solution)/shard_map/ppermute | solution.py:41
  30.1 11.5 %collective-permute-start.1 = (bf16[1,2,256,256]{3,2,1,0:T(8,128)(2,1)S(1)}, bf16[1,2,256,256]{3,2,1,0:T(8,128)(2,1)S(1)}, u32[]{:S(2)}, u32[]{:S(2)}) collective-permute-start(bf16[1,2,256,256]{3,2,1,0:T(8,128)(2,1)S(1)} %get-tuple-element.30), channel_id=1, source_target_pairs={{0,4},{4,0},{8,12},{12,8},{1,5},{5,1},{9,13},{13,9},{2,6},{6,2},{1... | collective-permute-start | bytes 786440 | tf_op jit(solution)/shard_map/ppermute | solution.py:41
  30.4 1.0 %copy-start = (bf16[2,2,256,256]{3,2,1,0:T(8,128)(2,1)S(1)}, bf16[2,2,256,256]{3,2,1,0:T(8,128)(2,1)}, u32[]{:S(2)}) copy-start(bf16[2,2,256,256]{3,2,1,0:T(8,128)(2,1)} %refs_5_.1) | copy-start | bytes 1572868
  31.5 1.4 %copy-start.1 = (bf16[2,2,256,768]{3,2,1,0:T(8,128)(2,1)S(1)}, bf16[2,2,256,768]{3,2,1,0:T(8,128)(2,1)}, u32[]{:S(2)}) copy-start(bf16[2,2,256,768]{3,2,1,0:T(8,128)(2,1)} %refs_0_.1) | copy-start | bytes 4718596
  32.9 0.7 %copy-start.2 = (s32[4,12]{1,0:T(4,128)S(1)}, s32[4,12]{1,0:T(4,128)}, u32[]{:S(2)}) copy-start(s32[4,12]{1,0:T(4,128)} %aperture_ref.5) | copy-start | bytes 580
  38.2 3.4 %collective-permute-start.6 = (bf16[2,2,256,768]{3,2,1,0:T(8,128)(2,1)S(1)}, bf16[2,2,256,768]{3,2,1,0:T(8,128)(2,1)S(1)}, u32[]{:S(2)}, u32[]{:S(2)}) collective-permute-start(bf16[2,2,256,768]{3,2,1,0:T(8,128)(2,1)S(1)} %collective-permute-done.5.panel_ref), channel_id=1, source_target_pairs={{0,1},{1,0},{2,3},{3,2},{4,5},{5,4},{6,7},{7,6},{8,9},{9,8},{10,11... | collective-permute-start | bytes 4718600 | tf_op jit(solution)/shard_map/ppermute | solution.py:28

commit v18 on v17

--- a/solution.py
+++ b/solution.py
@@ -34,8 +34,9 @@
 
 def line_window(data):
     near_pairs = [(0, 1), (1, 0), (2, 3), (3, 2)]
+    near = lax.ppermute(data, "src", near_pairs)
     far = lax.ppermute(data, "src", [(0, 3), (1, 2), (2, 1), (3, 0)])
-    near = lax.ppermute(data, "src", near_pairs)
+    near, far = lax.optimization_barrier((near, far))
     windows = []
     for v in range(data.shape[0]):
         across = lax.ppermute(far[v : v + 1], "src", near_pairs)

time: 44.1 us -> 46.3 us (1.050)
  waiting for transfers between devices: 16.7 us -> 26.6 us
  starting transfers between devices: 16.9 us -> 9.15 us
    ppermute x1, waiting for transfers between devices: 0.2 us -> 10.2 us  [line_window(): near = lax.ppermute(data, 'src', near_pairs)]
    ppermute x2, starting transfers between devices: 10.4 us -> 2.09 us  [line_window(): across = lax.ppermute(far[v:v + 1], 'src', near_pairs)]
    ppermute x3, waiting for transfers between devices: 1.65 us -> 0.01 us  [swap(): return lax.ppermute(x, axis, [(i, i ^ bit) for i in range(peers)])]
    ppermute x1, starting transfers between devices: 0.01 us -> 1.58 us  [line_window(): near = lax.ppermute(data, 'src', near_pairs)]
    ppermute x2, waiting for transfers between devices: 1.56 us -> 3.03 us  [line_window(): across = lax.ppermute(far[v:v + 1], 'src', near_pairs)]
    ppermute x1, starting transfers between devices: 3.6 us -> 2.47 us  [line_window(): far = lax.ppermute(data, 'src', [(0, 3), (1, 2), (2, 1), (3, 0)])]
where the time goes in v18:
time: 46.3 us; the launch traced here: 46.1 us
  waiting for transfers between devices  26.6 us (57%)
  starting transfers between devices  9.15 us (20%)
  Pallas kernels  7.15 us (15%)
  local copies, waits for them, and re-layouts  3.17 us (7%)
    ppermute x1, waiting for transfers between devices, line_window(): far = lax.ppermute(data, 'src', [(0, 3), (1, 2), (2, 1), (3, 0)])  13.4 us
    ppermute x1, waiting for transfers between devices, line_window(): near = lax.ppermute(data, 'src', near_pairs)  10.2 us
    unnamed x6, local copies, waits for them, and re-layouts  3.13 us
    ppermute x2, waiting for transfers between devices, line_window(): across = lax.ppermute(far[v:v + 1], 'src', near_pairs)  3.03 us
    pallas_call x1, Pallas kernels, body(): pl.pallas_call(functools.partial(kernel_a, half, [{k: at for k, (_, at) i...  3.02 us
    ppermute x3, starting transfers between devices, swap(): return lax.ppermute(x, axis, [(i, i ^ bit) for i in range(peers)])  3.01 us
    ppermute x1, starting transfers between devices, line_window(): far = lax.ppermute(data, 'src', [(0, 3), (1, 2), (2, 1), (3, 0)])  2.47 us
    pallas_call x1, Pallas kernels, body(): pl.pallas_call(functools.partial(last_kernel, half + 1, late), out_shape=...  2.26 us
  transfers between devices with their start and end apart: 7, of which 4 were waited for; matrix products, arithmetic and copies ran while one was open for 0% of the time, Pallas kernels for 11%

profile of v18, /device:TPU:0, one launch (start us, length us, event | category | flops | bytes accessed | tf_op | source)
XLA Modules:
  0.0 46.1 jit_solution(6831497505000449230)
XLA Ops:
  0.0 0.5 collective-permute-start.4
  0.5 2.5 %collective-permute-start.5 = (bf16[2,2,256,768]{3,2,1,0:T(8,128)(2,1)}, bf16[2,2,256,768]{3,2,1,0:T(8,128)(2,1)S(1)}, u32[]{:S(2)}, u32[]{:S(2)}) collective-permute-start(bf16[2,2,256,768]{3,2,1,0:T(8,128)(2,1)} %refs_0_.1), channel_id=1, source_target_pairs={{0,2},{1,3},{2,0},{3,1},{4,6},{5,7},{6,4},{7,5},{8,10},{9,11},{10,... | collective-permute-start | bytes 4718600 | tf_op jit(solution)/shard_map/ppermute | solution.py:28
  2.9 1.6 %collective-permute-start = (bf16[2,2,256,256]{3,2,1,0:T(8,128)(2,1)}, bf16[2,2,256,256]{3,2,1,0:T(8,128)(2,1)S(1)}, u32[]{:S(2)}, u32[]{:S(2)}) collective-permute-start(bf16[2,2,256,256]{3,2,1,0:T(8,128)(2,1)} %refs_5_.1), channel_id=1, source_target_pairs={{0,4},{4,0},{8,12},{12,8},{1,5},{5,1},{9,13},{13,9},{2,6},{6,2},{1... | collective-permute-start | bytes 1572872 | tf_op jit(solution)/shard_map/ppermute | solution.py:37
  4.5 2.5 %collective-permute-start.1 = (bf16[2,2,256,256]{3,2,1,0:T(8,128)(2,1)}, bf16[2,2,256,256]{3,2,1,0:T(8,128)(2,1)S(1)}, u32[]{:S(2)}, u32[]{:S(2)}) collective-permute-start(bf16[2,2,256,256]{3,2,1,0:T(8,128)(2,1)} %refs_5_.1), channel_id=1, source_target_pairs={{0,12},{4,8},{8,4},{12,0},{1,13},{5,9},{9,5},{13,1},{2,14},{6,10},... | collective-permute-start | bytes 1572872 | tf_op jit(solution)/shard_map/ppermute | solution.py:38
  7.0 10.2 %collective-permute-done.refs_3_.refs_6_ = bf16[2,2,256,256]{3,2,1,0:T(8,128)(2,1)S(1)} collective-permute-done((bf16[2,2,256,256]{3,2,1,0:T(8,128)(2,1)}, bf16[2,2,256,256]{3,2,1,0:T(8,128)(2,1)S(1)}, u32[]{:S(2)}, u32[]{:S(2)}) %collective-permute-start) | collective-permute-done | bytes 524320 | tf_op jit(solution)/shard_map/ppermute | solution.py:37
  17.2 13.4 %collective-permute-done.1.refs_4_.refs_7_ = bf16[2,2,256,256]{3,2,1,0:T(8,128)(2,1)S(1)} collective-permute-done((bf16[2,2,256,256]{3,2,1,0:T(8,128)(2,1)}, bf16[2,2,256,256]{3,2,1,0:T(8,128)(2,1)S(1)}, u32[]{:S(2)}, u32[]{:S(2)}) %collective-permute-start.1) | collective-permute-done | bytes 524320 | tf_op jit(solution)/shard_map/ppermute | solution.py:38
  30.6 0.7 %collective-permute-start.3 = (bf16[1,2,256,256]{3,2,1,0:T(8,128)(2,1)S(1)}, bf16[1,2,256,256]{3,2,1,0:T(8,128)(2,1)S(1)}, u32[]{:S(2)}, u32[]{:S(2)}) collective-permute-start(bf16[1,2,256,256]{3,2,1,0:T(8,128)(2,1)S(1)} %get-tuple-element.33), channel_id=1, source_target_pairs={{0,4},{4,0},{8,12},{12,8},{1,5},{5,1},{9,13},{13,9},{2,6},{6,2},{1... | collective-permute-start | bytes 786440 | tf_op jit(solution)/shard_map/ppermute | solution.py:42
  31.3 1.4 %collective-permute-start.2 = (bf16[1,2,256,256]{3,2,1,0:T(8,128)(2,1)S(1)}, bf16[1,2,256,256]{3,2,1,0:T(8,128)(2,1)S(1)}, u32[]{:S(2)}, u32[]{:S(2)}) collective-permute-start(bf16[1,2,256,256]{3,2,1,0:T(8,128)(2,1)S(1)} %get-tuple-element.34), channel_id=1, source_target_pairs={{0,4},{4,0},{8,12},{12,8},{1,5},{5,1},{9,13},{13,9},{2,6},{6,2},{1... | collective-permute-start | bytes 786440 | tf_op jit(solution)/shard_map/ppermute | solution.py:42
  32.7 0.0 collective-permute-done.4.refs_1_
  32.7 0.0 copy-start
  32.7 1.0 %copy-done = bf16[2,2,256,256]{3,2,1,0:T(8,128)(2,1)S(1)} copy-done((bf16[2,2,256,256]{3,2,1,0:T(8,128)(2,1)S(1)}, bf16[2,2,256,256]{3,2,1,0:T(8,128)(2,1)}, u32[]{:S(2)}) %copy-start) | copy-done | bytes 524312
  33.8 0.0 copy-start.1
  33.8 1.4 %copy-done.1 = bf16[2,2,256,768]{3,2,1,0:T(8,128)(2,1)S(1)} copy-done((bf16[2,2,256,768]{3,2,1,0:T(8,128)(2,1)S(1)}, bf16[2,2,256,768]{3,2,1,0:T(8,128)(2,1)}, u32[]{:S(2)}) %copy-start.1) | copy-done | bytes 1572888
  35.2 0.0 copy-start.2
  35.2 0.7 %copy-done.2 = s32[4,12]{1,0:T(4,128)S(1)} copy-done((s32[4,12]{1,0:T(4,128)S(1)}, s32[4,12]{1,0:T(4,128)}, u32[]{:S(2)}) %copy-start.2) | copy-done | bytes 216
  35.8 3.0 %shard_map.37 = (bf16[4,256,512]{2,1,0:T(8,128)(2,1)S(1)}, bf16[4,256,512]{2,1,0:T(8,128)(2,1)S(1)}, f32[512,256]{1,0:T(8,128)S(1)}, f32[512,256]{1,0:T(8,128)S(...) custom-call(s32[4,12]{1,0:T(4,128)S(1)} %copy-done.2, bf16[2,2,256,768]{3,2,1,0:T(8,128)(2,1)S(1)} %copy-done.1, ...), custom_call_target="tpu_custom_call" | custom-call | flops 161061280 | bytes 1048576 | tf_op jit(solution)/shard_map/pallas_call | solution.py:216
  38.9 0.0 collective-permute-done.5.panel_ref
  38.9 0.1 collective-permute-start.6
  39.0 1.0 %collective-permute-done.3.late_ref = bf16[1,2,256,256]{3,2,1,0:T(8,128)(2,1)S(1)} collective-permute-done((bf16[1,2,256,256]{3,2,1,0:T(8,128)(2,1)S(1)}, bf16[1,2,256,256]{3,2,1,0:T(8,128)(2,1)S(1)}, u32[]{:S(2)}, u32[]{:S(2)}) %collective-permute-start.3) | collective-permute-done | bytes 262176 | tf_op jit(solution)/shard_map/ppermute | solution.py:42
  39.9 1.9 %shard_map.38 = (bf16[4,256,512]{2,1,0:T(8,128)(2,1)S(1)}, bf16[512,512]{1,0:T(8,128)(2,1)S(1)}, f32[2,256,256]{2,1,0:T(8,128)S(1)}, f32[2,256,256]{2,1,0:T(8,128)S(1)}) custom-call(s32[4,12]{1,0:T(4,128)S(1)} %copy-done.2, bf16[1,2,256,256]{3,2,1,0:T(8,128)(2,1)S(1)} %collective-permute-done.3.late_ref, ...), custom_call_target="tpu_custom_call", output_to_operand_aliasing={{0}: (2, {}), {2}: (6, {}), {3}: (7, {})} | custom-call | flops 161061280 | bytes 1048576 | tf_op jit(solution)/shard_map/pallas_call | solution.py:226
  41.8 2.1 %collective-permute-done.2.piece_ref = bf16[1,2,256,256]{3,2,1,0:T(8,128)(2,1)S(1)} collective-permute-done((bf16[1,2,256,256]{3,2,1,0:T(8,128)(2,1)S(1)}, bf16[1,2,256,256]{3,2,1,0:T(8,128)(2,1)S(1)}, u32[]{:S(2)}, u32[]{:S(2)}) %collective-permute-start.2) | collective-permute-done | bytes 262176 | tf_op jit(solution)/shard_map/ppermute | solution.py:42
  43.9 0.0 collective-permute-done.6.refs_0_
  43.9 2.3 %shard_map.40 = (f32[2,2,256,256]{3,2,1,0:T(8,128)}, bf16[4,256,512]{2,1,0:T(8,128)(2,1)S(1)}) custom-call(s32[4,12]{1,0:T(4,128)S(1)} %copy-done.2, bf16[1,2,256,256]{3,2,1,0:T(8,128)(2,1)S(1)} %shard_map.39.late_ref, bf16[4,256,512]{2,1,0:T(8,128)(2,1)S(1)} %get-tuple-element.28.first_window, ...), custom_call_target="tpu_custom_call", output_to_operand_aliasing={{1}: (3, {})} | custom-call | flops 1610612736 | bytes 1048576 | tf_op jit(solution)/shard_map/pallas_call | solution.py:236
  (2 shorter events, 0.0 us)
Async XLA Ops:
  0.0 32.7 %collective-permute-start.4 = (bf16[2,2,256,768]{3,2,1,0:T(8,128)(2,1)}, bf16[2,2,256,768]{3,2,1,0:T(8,128)(2,1)S(1)}, u32[]{:S(2)}, u32[]{:S(2)}) collective-permute-start(bf16[2,2,256,768]{3,2,1,0:T(8,128)(2,1)} %refs_0_.1), channel_id=1, source_target_pairs={{0,1},{1,0},{2,3},{3,2},{4,5},{5,4},{6,7},{7,6},{8,9},{9,8},{10,11... | collective-permute-start | bytes 4718600 | tf_op jit(solution)/shard_map/ppermute | solution.py:28
  0.5 38.4 %collective-permute-start.5 = (bf16[2,2,256,768]{3,2,1,0:T(8,128)(2,1)}, bf16[2,2,256,768]{3,2,1,0:T(8,128)(2,1)S(1)}, u32[]{:S(2)}, u32[]{:S(2)}) collective-permute-start(bf16[2,2,256,768]{3,2,1,0:T(8,128)(2,1)} %refs_0_.1), channel_id=1, source_target_pairs={{0,2},{1,3},{2,0},{3,1},{4,6},{5,7},{6,4},{7,5},{8,10},{9,11},{10,... | collective-permute-start | bytes 4718600 | tf_op jit(solution)/shard_map/ppermute | solution.py:28
  2.9 14.3 %collective-permute-start = (bf16[2,2,256,256]{3,2,1,0:T(8,128)(2,1)}, bf16[2,2,256,256]{3,2,1,0:T(8,128)(2,1)S(1)}, u32[]{:S(2)}, u32[]{:S(2)}) collective-permute-start(bf16[2,2,256,256]{3,2,1,0:T(8,128)(2,1)} %refs_5_.1), channel_id=1, source_target_pairs={{0,4},{4,0},{8,12},{12,8},{1,5},{5,1},{9,13},{13,9},{2,6},{6,2},{1... | collective-permute-start | bytes 1572872 | tf_op jit(solution)/shard_map/ppermute | solution.py:37
  4.5 26.1 %collective-permute-start.1 = (bf16[2,2,256,256]{3,2,1,0:T(8,128)(2,1)}, bf16[2,2,256,256]{3,2,1,0:T(8,128)(2,1)S(1)}, u32[]{:S(2)}, u32[]{:S(2)}) collective-permute-start(bf16[2,2,256,256]{3,2,1,0:T(8,128)(2,1)} %refs_5_.1), channel_id=1, source_target_pairs={{0,12},{4,8},{8,4},{12,0},{1,13},{5,9},{9,5},{13,1},{2,14},{6,10},... | collective-permute-start | bytes 1572872 | tf_op jit(solution)/shard_map/ppermute | solution.py:38
  30.6 9.3 %collective-permute-start.3 = (bf16[1,2,256,256]{3,2,1,0:T(8,128)(2,1)S(1)}, bf16[1,2,256,256]{3,2,1,0:T(8,128)(2,1)S(1)}, u32[]{:S(2)}, u32[]{:S(2)}) collective-permute-start(bf16[1,2,256,256]{3,2,1,0:T(8,128)(2,1)S(1)} %get-tuple-element.33), channel_id=1, source_target_pairs={{0,4},{4,0},{8,12},{12,8},{1,5},{5,1},{9,13},{13,9},{2,6},{6,2},{1... | collective-permute-start | bytes 786440 | tf_op jit(solution)/shard_map/ppermute | solution.py:42
  31.3 12.6 %collective-permute-start.2 = (bf16[1,2,256,256]{3,2,1,0:T(8,128)(2,1)S(1)}, bf16[1,2,256,256]{3,2,1,0:T(8,128)(2,1)S(1)}, u32[]{:S(2)}, u32[]{:S(2)}) collective-permute-start(bf16[1,2,256,256]{3,2,1,0:T(8,128)(2,1)S(1)} %get-tuple-element.34), channel_id=1, source_target_pairs={{0,4},{4,0},{8,12},{12,8},{1,5},{5,1},{9,13},{13,9},{2,6},{6,2},{1... | collective-permute-start | bytes 786440 | tf_op jit(solution)/shard_map/ppermute | solution.py:42
  32.7 1.0 %copy-start = (bf16[2,2,256,256]{3,2,1,0:T(8,128)(2,1)S(1)}, bf16[2,2,256,256]{3,2,1,0:T(8,128)(2,1)}, u32[]{:S(2)}) copy-start(bf16[2,2,256,256]{3,2,1,0:T(8,128)(2,1)} %refs_5_.1) | copy-start | bytes 1572868
  33.8 1.4 %copy-start.1 = (bf16[2,2,256,768]{3,2,1,0:T(8,128)(2,1)S(1)}, bf16[2,2,256,768]{3,2,1,0:T(8,128)(2,1)}, u32[]{:S(2)}) copy-start(bf16[2,2,256,768]{3,2,1,0:T(8,128)(2,1)} %refs_0_.1) | copy-start | bytes 4718596
  35.2 0.7 %copy-start.2 = (s32[4,12]{1,0:T(4,128)S(1)}, s32[4,12]{1,0:T(4,128)}, u32[]{:S(2)}) copy-start(s32[4,12]{1,0:T(4,128)} %aperture_ref.5) | copy-start | bytes 580
  38.9 5.0 %collective-permute-start.6 = (bf16[2,2,256,768]{3,2,1,0:T(8,128)(2,1)S(1)}, bf16[2,2,256,768]{3,2,1,0:T(8,128)(2,1)S(1)}, u32[]{:S(2)}, u32[]{:S(2)}) collective-permute-start(bf16[2,2,256,768]{3,2,1,0:T(8,128)(2,1)S(1)} %collective-permute-done.5.panel_ref), channel_id=1, source_target_pairs={{0,1},{1,0},{2,3},{3,2},{4,5},{5,4},{6,7},{7,6},{8,9},{9,8},{10,11... | collective-permute-start | bytes 4718600 | tf_op jit(solution)/shard_map/ppermute | solution.py:28

commit v19 on v17

--- a/solution.py
+++ b/solution.py
@@ -10,7 +10,6 @@
 BLK = 256
 APER = 12
 HW = 6
-PIECES = 1
 
 
 def after(value, *earlier):
@@ -97,15 +96,18 @@
     return panel[...].reshape(2 * panel.shape[1], panel.shape[2])
 
 
-def product(window, aperture_ref, panels, late_in_two=None, late=None):
+def product(window, aperture_ref, panels, late_in_two=None, late=None, late_block=None):
     blocks = []
     for m, panel in panels.items():
         entries = slot_entries(aperture_ref, m, panel.shape[-1] // BLK, window.shape[0])
-        blocks += [window[k] for k in entries]
+        picked = [window[k] for k in entries]
+        if late_block is not None:
+            picked = [jnp.where(k == late, late_block, block) for k, block in zip(entries, picked)]
+        blocks += picked
     values = [rows_of(panel) for panel in panels.values()]
     if late_in_two is not None:
         values.append(late_in_two)
-        blocks += [window[late]] * 2
+        blocks += [window[late] if late_block is None else late_block] * 2
     return times(jnp.concatenate(values, axis=1), jnp.concatenate(blocks, axis=0))
 
 
@@ -150,25 +152,21 @@
     two[...] = in_two(last_sum[...] + sum_of_late(aperture_ref, panels, late, last_window.shape[0]))
 
 
-def last_kernel(far_half, late, aperture_ref, late_ref, first_window, _, two, first_part, last_part, *refs):
-    *panel_refs, out_ref, window, result, sems = refs
+def last_kernel(far_half, late, aperture_ref, late_ref, first_window, window, two, first_part, last_part, *refs):
+    *panel_refs, out_ref, result, sems = refs
 
     def finish(v, part, real, imag):
         copies = []
         for p, value in enumerate((real, imag)):
             result[v, p] = part[p] + value
-            for chunk in range(PIECES):
-                rows = pl.ds(chunk * (BLK // PIECES), BLK // PIECES)
-                copies.append(
-                    pltpu.make_async_copy(result.at[v, p, rows], out_ref.at[v, p, rows], sems.at[v, p, chunk])
-                )
-                copies[-1].start()
+            copies.append(pltpu.make_async_copy(result.at[v, p], out_ref.at[v, p], sems.at[v, p]))
+            copies[-1].start()
         return copies
 
     panels = [{far_half + m: ref.at[v] for m, ref in enumerate(panel_refs)} for v in range(2)]
     copies = finish(0, first_part, *product(first_window, aperture_ref, panels[0]))
-    fill_window(window, {late: late_ref.at[0]})
-    copies += finish(1, last_part, *product(window, aperture_ref, panels[1], two[...], late))
+    late_block = jnp.concatenate([late_ref[0, 0], late_ref[0, 1]], axis=1)
+    copies += finish(1, last_part, *product(window, aperture_ref, panels[1], two[...], late, late_block))
     for copy in copies:
         copy.wait()
 
@@ -234,14 +232,13 @@
 
     return pl.pallas_call(
         functools.partial(last_kernel, half + 1, late),
-        out_shape=[jax.ShapeDtypeStruct((2, 2, BLK, width), jnp.float32), window],
-        in_specs=[vmem] + [vmem] * (6 + len(handed_on)),
-        out_specs=[anywhere, vmem],
-        scratch_shapes=[pltpu.VMEM((2, 2, BLK, width), jnp.float32), pltpu.SemaphoreType.DMA((2, 2, PIECES))],
-        input_output_aliases={3: 1},
+        out_shape=jax.ShapeDtypeStruct((2, 2, BLK, width), jnp.float32),
+        in_specs=[vmem] * (7 + len(handed_on)),
+        out_specs=anywhere,
+        scratch_shapes=[pltpu.VMEM((2, 2, BLK, width), jnp.float32), pltpu.SemaphoreType.DMA((2, 2))],
         compiler_params=limit(16),
         cost_estimate=cost(1),
-    )(aperture, held(late_pieces[1], two), first, last, two, first_part, last_part, *handed_on)[0]
+    )(aperture, held(late_pieces[1], two), first, last, two, first_part, last_part, *handed_on)
 
 
 def solution(mesh):

time: 44.1 us -> 44.1 us (level)
  no operation moved by 1% of the time
where the time goes in v19:
time: 44.1 us; the launch traced here: 43.9 us
  starting transfers between devices  16.9 us (38%)
  waiting for transfers between devices  16.7 us (38%)
  Pallas kernels  7.14 us (16%)
  local copies, waits for them, and re-layouts  3.17 us (7%)
    ppermute x1, waiting for transfers between devices, line_window(): far = lax.ppermute(data, 'src', [(0, 3), (1, 2), (2, 1), (3, 0)])  13.2 us
    ppermute x2, starting transfers between devices, line_window(): across = lax.ppermute(far[v:v + 1], 'src', near_pairs)  10.4 us
    ppermute x1, starting transfers between devices, line_window(): far = lax.ppermute(data, 'src', [(0, 3), (1, 2), (2, 1), (3, 0)])  3.6 us
    unnamed x6, local copies, waits for them, and re-layouts  3.13 us
    pallas_call x1, Pallas kernels, body(): pl.pallas_call(functools.partial(kernel_a, half, [{k: at for k, (_, at) i...  3.02 us
    ppermute x3, starting transfers between devices, swap(): return lax.ppermute(x, axis, [(i, i ^ bit) for i in range(peers)])  2.94 us
    pallas_call x1, Pallas kernels, body(): pl.pallas_call(functools.partial(last_kernel, half + 1, late), out_shape=...  2.26 us
    pallas_call x1, Pallas kernels, body(): pl.pallas_call(functools.partial(kernel_b, half, late), out_shape=[window...  1.86 us
  transfers between devices with their start and end apart: 7, of which 4 were waited for; matrix products, arithmetic and copies ran while one was open for 0% of the time, Pallas kernels for 11%

profile of v19, /device:TPU:0, one launch (start us, length us, event | category | flops | bytes accessed | tf_op | source)
XLA Modules:
  0.0 43.9 jit_solution(13667462428210836379)
XLA Ops:
  0.0 0.5 %collective-permute-start.3 = (bf16[2,2,256,768]{3,2,1,0:T(8,128)(2,1)}, bf16[2,2,256,768]{3,2,1,0:T(8,128)(2,1)S(1)}, u32[]{:S(2)}, u32[]{:S(2)}) collective-permute-start(bf16[2,2,256,768]{3,2,1,0:T(8,128)(2,1)} %refs_0_.1), channel_id=1, source_target_pairs={{0,1},{1,0},{2,3},{3,2},{4,5},{5,4},{6,7},{7,6},{8,9},{9,8},{10,11... | collective-permute-start | bytes 4718600 | tf_op jit(solution)/shard_map/ppermute | solution.py:27
  0.5 2.5 %collective-permute-start.5 = (bf16[2,2,256,768]{3,2,1,0:T(8,128)(2,1)}, bf16[2,2,256,768]{3,2,1,0:T(8,128)(2,1)S(1)}, u32[]{:S(2)}, u32[]{:S(2)}) collective-permute-start(bf16[2,2,256,768]{3,2,1,0:T(8,128)(2,1)} %refs_0_.1), channel_id=1, source_target_pairs={{0,2},{1,3},{2,0},{3,1},{4,6},{5,7},{6,4},{7,5},{8,10},{9,11},{10,... | collective-permute-start | bytes 4718600 | tf_op jit(solution)/shard_map/ppermute | solution.py:27
  2.9 3.6 %collective-permute-start = (bf16[2,2,256,256]{3,2,1,0:T(8,128)(2,1)}, bf16[2,2,256,256]{3,2,1,0:T(8,128)(2,1)S(1)}, u32[]{:S(2)}, u32[]{:S(2)}) collective-permute-start(bf16[2,2,256,256]{3,2,1,0:T(8,128)(2,1)} %refs_5_.1), channel_id=1, source_target_pairs={{0,12},{4,8},{8,4},{12,0},{1,13},{5,9},{9,5},{13,1},{2,14},{6,10},... | collective-permute-start | bytes 1572872 | tf_op jit(solution)/shard_map/ppermute | solution.py:36
  6.5 0.0 collective-permute-start.4
  6.5 13.2 %collective-permute-done.refs_4_.refs_7_ = bf16[2,2,256,256]{3,2,1,0:T(8,128)(2,1)S(1)} collective-permute-done((bf16[2,2,256,256]{3,2,1,0:T(8,128)(2,1)}, bf16[2,2,256,256]{3,2,1,0:T(8,128)(2,1)S(1)}, u32[]{:S(2)}, u32[]{:S(2)}) %collective-permute-start) | collective-permute-done | bytes 524320 | tf_op jit(solution)/shard_map/ppermute | solution.py:36
  19.8 10.3 %collective-permute-start.2 = (bf16[1,2,256,256]{3,2,1,0:T(8,128)(2,1)S(1)}, bf16[1,2,256,256]{3,2,1,0:T(8,128)(2,1)S(1)}, u32[]{:S(2)}, u32[]{:S(2)}) collective-permute-start(bf16[1,2,256,256]{3,2,1,0:T(8,128)(2,1)S(1)} %get-tuple-element.27), channel_id=1, source_target_pairs={{0,4},{4,0},{8,12},{12,8},{1,5},{5,1},{9,13},{13,9},{2,6},{6,2},{1... | collective-permute-start | bytes 786440 | tf_op jit(solution)/shard_map/ppermute | solution.py:40
  30.1 0.1 collective-permute-start.1
  30.2 0.2 collective-permute-done.4.refs_3_.refs_6_
  30.4 0.0 collective-permute-done.3.refs_1_
  30.4 0.0 copy-start
  30.4 1.0 %copy-done = bf16[2,2,256,256]{3,2,1,0:T(8,128)(2,1)S(1)} copy-done((bf16[2,2,256,256]{3,2,1,0:T(8,128)(2,1)S(1)}, bf16[2,2,256,256]{3,2,1,0:T(8,128)(2,1)}, u32[]{:S(2)}) %copy-start) | copy-done | bytes 524312
  31.5 0.0 copy-start.1
  31.5 1.4 %copy-done.1 = bf16[2,2,256,768]{3,2,1,0:T(8,128)(2,1)S(1)} copy-done((bf16[2,2,256,768]{3,2,1,0:T(8,128)(2,1)S(1)}, bf16[2,2,256,768]{3,2,1,0:T(8,128)(2,1)}, u32[]{:S(2)}) %copy-start.1) | copy-done | bytes 1572888
  32.9 0.0 copy-start.2
  32.9 0.7 %copy-done.2 = s32[4,12]{1,0:T(4,128)S(1)} copy-done((s32[4,12]{1,0:T(4,128)S(1)}, s32[4,12]{1,0:T(4,128)}, u32[]{:S(2)}) %copy-start.2) | copy-done | bytes 216
  33.5 3.0 %shard_map.37 = (bf16[4,256,512]{2,1,0:T(8,128)(2,1)S(1)}, bf16[4,256,512]{2,1,0:T(8,128)(2,1)S(1)}, f32[512,256]{1,0:T(8,128)S(1)}, f32[512,256]{1,0:T(8,128)S(...) custom-call(s32[4,12]{1,0:T(4,128)S(1)} %copy-done.2, bf16[2,2,256,768]{3,2,1,0:T(8,128)(2,1)S(1)} %copy-done.1, ...), custom_call_target="tpu_custom_call" | custom-call | flops 161061280 | bytes 1048576 | tf_op jit(solution)/shard_map/pallas_call | solution.py:213
  36.6 1.6 %collective-permute-done.5.panel_ref = bf16[2,2,256,768]{3,2,1,0:T(8,128)(2,1)S(1)} collective-permute-done((bf16[2,2,256,768]{3,2,1,0:T(8,128)(2,1)}, bf16[2,2,256,768]{3,2,1,0:T(8,128)(2,1)S(1)}, u32[]{:S(2)}, u32[]{:S(2)}) %collective-permute-start.5) | collective-permute-done | bytes 1572896 | tf_op jit(solution)/shard_map/ppermute | solution.py:27
  38.2 0.0 collective-permute-start.6
  38.2 0.0 collective-permute-done.2.late_ref
  38.2 1.9 %shard_map.38 = (bf16[4,256,512]{2,1,0:T(8,128)(2,1)S(1)}, bf16[512,512]{1,0:T(8,128)(2,1)S(1)}, f32[2,256,256]{2,1,0:T(8,128)S(1)}, f32[2,256,256]{2,1,0:T(8,128)S(1)}) custom-call(s32[4,12]{1,0:T(4,128)S(1)} %copy-done.2, bf16[1,2,256,256]{3,2,1,0:T(8,128)(2,1)S(1)} %collective-permute-done.2.late_ref, ...), custom_call_target="tpu_custom_call", output_to_operand_aliasing={{0}: (2, {}), {2}: (6, {}), {3}: (7, {})} | custom-call | flops 161061280 | bytes 1048576 | tf_op jit(solution)/shard_map/pallas_call | solution.py:223
  40.1 1.6 %collective-permute-done.1.piece_ref = bf16[1,2,256,256]{3,2,1,0:T(8,128)(2,1)S(1)} collective-permute-done((bf16[1,2,256,256]{3,2,1,0:T(8,128)(2,1)S(1)}, bf16[1,2,256,256]{3,2,1,0:T(8,128)(2,1)S(1)}, u32[]{:S(2)}, u32[]{:S(2)}) %collective-permute-start.1) | collective-permute-done | bytes 262176 | tf_op jit(solution)/shard_map/ppermute | solution.py:40
  41.6 0.0 collective-permute-done.6.refs_0_
  41.6 2.3 %shard_map.40 = f32[2,2,256,256]{3,2,1,0:T(8,128)} custom-call(s32[4,12]{1,0:T(4,128)S(1)} %copy-done.2, bf16[1,2,256,256]{3,2,1,0:T(8,128)(2,1)S(1)} %shard_map.39.late_ref, bf16[4,256,512]{2,1,0:T(8,128)(2,1)S(1)} %get-tuple-element.23.first_window, bf16[4,256,512]{2,1,0:T(8,128)(2,1)S(1)} %get-tuple-element.17.last_window.window, ...), custom_call_target="tpu_custom_call" | custom-call | flops 1610612736 | bytes 1048576 | tf_op jit(solution)/shard_map/pallas_call | solution.py:233
  (2 shorter events, 0.0 us)
Async XLA Ops:
  0.0 30.4 %collective-permute-start.3 = (bf16[2,2,256,768]{3,2,1,0:T(8,128)(2,1)}, bf16[2,2,256,768]{3,2,1,0:T(8,128)(2,1)S(1)}, u32[]{:S(2)}, u32[]{:S(2)}) collective-permute-start(bf16[2,2,256,768]{3,2,1,0:T(8,128)(2,1)} %refs_0_.1), channel_id=1, source_target_pairs={{0,1},{1,0},{2,3},{3,2},{4,5},{5,4},{6,7},{7,6},{8,9},{9,8},{10,11... | collective-permute-start | bytes 4718600 | tf_op jit(solution)/shard_map/ppermute | solution.py:27
  0.5 37.8 %collective-permute-start.5 = (bf16[2,2,256,768]{3,2,1,0:T(8,128)(2,1)}, bf16[2,2,256,768]{3,2,1,0:T(8,128)(2,1)S(1)}, u32[]{:S(2)}, u32[]{:S(2)}) collective-permute-start(bf16[2,2,256,768]{3,2,1,0:T(8,128)(2,1)} %refs_0_.1), channel_id=1, source_target_pairs={{0,2},{1,3},{2,0},{3,1},{4,6},{5,7},{6,4},{7,5},{8,10},{9,11},{10,... | collective-permute-start | bytes 4718600 | tf_op jit(solution)/shard_map/ppermute | solution.py:27
  2.9 16.8 %collective-permute-start = (bf16[2,2,256,256]{3,2,1,0:T(8,128)(2,1)}, bf16[2,2,256,256]{3,2,1,0:T(8,128)(2,1)S(1)}, u32[]{:S(2)}, u32[]{:S(2)}) collective-permute-start(bf16[2,2,256,256]{3,2,1,0:T(8,128)(2,1)} %refs_5_.1), channel_id=1, source_target_pairs={{0,12},{4,8},{8,4},{12,0},{1,13},{5,9},{9,5},{13,1},{2,14},{6,10},... | collective-permute-start | bytes 1572872 | tf_op jit(solution)/shard_map/ppermute | solution.py:36
  6.5 23.9 %collective-permute-start.4 = (bf16[2,2,256,256]{3,2,1,0:T(8,128)(2,1)}, bf16[2,2,256,256]{3,2,1,0:T(8,128)(2,1)S(1)}, u32[]{:S(2)}, u32[]{:S(2)}) collective-permute-start(bf16[2,2,256,256]{3,2,1,0:T(8,128)(2,1)} %refs_5_.1), channel_id=1, source_target_pairs={{0,4},{4,0},{8,12},{12,8},{1,5},{5,1},{9,13},{13,9},{2,6},{6,2},{1... | collective-permute-start | bytes 1572872 | tf_op jit(solution)/shard_map/ppermute | solution.py:37
  19.8 18.4 %collective-permute-start.2 = (bf16[1,2,256,256]{3,2,1,0:T(8,128)(2,1)S(1)}, bf16[1,2,256,256]{3,2,1,0:T(8,128)(2,1)S(1)}, u32[]{:S(2)}, u32[]{:S(2)}) collective-permute-start(bf16[1,2,256,256]{3,2,1,0:T(8,128)(2,1)S(1)} %get-tuple-element.27), channel_id=1, source_target_pairs={{0,4},{4,0},{8,12},{12,8},{1,5},{5,1},{9,13},{13,9},{2,6},{6,2},{1... | collective-permute-start | bytes 786440 | tf_op jit(solution)/shard_map/ppermute | solution.py:40
  30.1 11.5 %collective-permute-start.1 = (bf16[1,2,256,256]{3,2,1,0:T(8,128)(2,1)S(1)}, bf16[1,2,256,256]{3,2,1,0:T(8,128)(2,1)S(1)}, u32[]{:S(2)}, u32[]{:S(2)}) collective-permute-start(bf16[1,2,256,256]{3,2,1,0:T(8,128)(2,1)S(1)} %get-tuple-element.28), channel_id=1, source_target_pairs={{0,4},{4,0},{8,12},{12,8},{1,5},{5,1},{9,13},{13,9},{2,6},{6,2},{1... | collective-permute-start | bytes 786440 | tf_op jit(solution)/shard_map/ppermute | solution.py:40
  30.4 1.0 %copy-start = (bf16[2,2,256,256]{3,2,1,0:T(8,128)(2,1)S(1)}, bf16[2,2,256,256]{3,2,1,0:T(8,128)(2,1)}, u32[]{:S(2)}) copy-start(bf16[2,2,256,256]{3,2,1,0:T(8,128)(2,1)} %refs_5_.1) | copy-start | bytes 1572868
  31.5 1.4 %copy-start.1 = (bf16[2,2,256,768]{3,2,1,0:T(8,128)(2,1)S(1)}, bf16[2,2,256,768]{3,2,1,0:T(8,128)(2,1)}, u32[]{:S(2)}) copy-start(bf16[2,2,256,768]{3,2,1,0:T(8,128)(2,1)} %refs_0_.1) | copy-start | bytes 4718596
  32.9 0.7 %copy-start.2 = (s32[4,12]{1,0:T(4,128)S(1)}, s32[4,12]{1,0:T(4,128)}, u32[]{:S(2)}) copy-start(s32[4,12]{1,0:T(4,128)} %aperture_ref.5) | copy-start | bytes 580
  38.2 3.4 %collective-permute-start.6 = (bf16[2,2,256,768]{3,2,1,0:T(8,128)(2,1)S(1)}, bf16[2,2,256,768]{3,2,1,0:T(8,128)(2,1)S(1)}, u32[]{:S(2)}, u32[]{:S(2)}) collective-permute-start(bf16[2,2,256,768]{3,2,1,0:T(8,128)(2,1)S(1)} %collective-permute-done.5.panel_ref), channel_id=1, source_target_pairs={{0,1},{1,0},{2,3},{3,2},{4,5},{5,4},{6,7},{7,6},{8,9},{9,8},{10,11... | collective-permute-start | bytes 4718600 | tf_op jit(solution)/shard_map/ppermute | solution.py:27

commit v20 on v17

--- a/solution.py
+++ b/solution.py
@@ -125,29 +125,28 @@
     return jnp.concatenate([high, low], axis=1)
 
 
-def kernel_a(near_half, ats, late, aperture_ref, *refs):
-    panel_refs = refs[:near_half]
-    piece_refs = list(refs[near_half:-6])
+def kernel_a(ats, late, aperture_ref, own_ref, *refs):
+    piece_refs = list(refs[:-6])
     windows, sums, parts = refs[-6:-4], refs[-4:-2], refs[-2:]
     for v, (window, at) in enumerate(zip(windows, ats)):
         window[late] = jnp.zeros(window.shape[1:], window.dtype)
         fill_window(window, {k: piece_refs.pop(0).at[index] for k, index in at.items()})
-        panels = {m: ref.at[v] for m, ref in enumerate(panel_refs)}
+        panels = {0: own_ref.at[v]}
         parts[v][0], parts[v][1] = product(window, aperture_ref, panels)
         sums[v][...] = sum_of_late(aperture_ref, panels, late, window.shape[0])
 
 
-def kernel_b(m, late, aperture_ref, late_ref, _, last_window, first_sum, last_sum, first_in, last_in, panel_ref, *refs):
-    window, two, first_part, last_part = refs
+def kernel_b(late, aperture_ref, late_ref, _, last_window, first_sum, last_sum, first_in, last_in, *refs):
+    *panel_refs, window, two, first_part, last_part = refs
     fill_window(window, {late: late_ref.at[0]})
-    real, imag = product(window, aperture_ref, {m: panel_ref.at[0]}, in_two(first_sum[...]), late)
+    panels = [{1 + m: ref.at[v] for m, ref in enumerate(panel_refs)} for v in range(2)]
+    real, imag = product(window, aperture_ref, panels[0], in_two(first_sum[...]), late)
     first_part[0] = first_in[0] + real
     first_part[1] = first_in[1] + imag
-    panels = {m: panel_ref.at[1]}
-    real, imag = product(last_window, aperture_ref, panels)
+    real, imag = product(last_window, aperture_ref, panels[1])
     last_part[0] = last_in[0] + real
     last_part[1] = last_in[1] + imag
-    two[...] = in_two(last_sum[...] + sum_of_late(aperture_ref, panels, late, last_window.shape[0]))
+    two[...] = in_two(last_sum[...] + sum_of_late(aperture_ref, panels[1], late, last_window.shape[0]))
 
 
 def last_kernel(far_half, late, aperture_ref, late_ref, first_window, _, two, first_part, last_part, *refs):
@@ -213,24 +212,24 @@
 
     pieces = [piece for window_pieces in early for piece, _ in window_pieces.values()]
     first, last, first_sum, last_sum, first_part, last_part = pl.pallas_call(
-        functools.partial(kernel_a, half, [{k: at for k, (_, at) in pieces.items()} for pieces in early], late),
+        functools.partial(kernel_a, [{k: at for k, (_, at) in pieces.items()} for pieces in early], late),
         out_shape=[window] * 2 + [total] * 2 + [part] * 2,
-        in_specs=[vmem] + [vmem] * (half + len(pieces)),
+        in_specs=[vmem] * (2 + len(pieces)),
         out_specs=[vmem] * 6,
         compiler_params=limit(16),
         cost_estimate=cost(0.1),
-    )(aperture, *panels, *pieces)
+    )(aperture, primaries, *pieces)
 
     handed_on = hand_on(far_panel, first_part)
     first, two, first_part, last_part = pl.pallas_call(
-        functools.partial(kernel_b, half, late),
+        functools.partial(kernel_b, late),
         out_shape=[window, jax.ShapeDtypeStruct((2 * BLK, 2 * BLK), jnp.bfloat16), part, part],
-        in_specs=[vmem] + [vmem] * 8,
+        in_specs=[vmem] * (8 + half),
         out_specs=[vmem] * 4,
         input_output_aliases={2: 0, 6: 2, 7: 3},
         compiler_params=limit(16),
         cost_estimate=cost(0.1),
-    )(aperture, late_pieces[0], first, last, first_sum, last_sum, first_part, last_part, far_panel)
+    )(aperture, late_pieces[0], first, last, first_sum, last_sum, first_part, last_part, *panels[1:], far_panel)
 
     return pl.pallas_call(
         functools.partial(last_kernel, half + 1, late),

time: 44.1 us -> 44.7 us (1.014)
  waiting for transfers between devices: 16.7 us -> 17.2 us
    ppermute x3, waiting for transfers between devices: 1.65 us -> 2.1 us  [swap(): return lax.ppermute(x, axis, [(i, i ^ bit) for i in range(peers)])]
  transfers between devices with their start and end apart: 7 -> 7, of which waited for: 4 -> 4; matrix products, arithmetic and copies ran while one was open for 0% -> 0% of each run, Pallas kernels for 11% -> 10%
where the time goes in v20:
time: 44.7 us; the launch traced here: 44.5 us
  starting transfers between devices  17.2 us (38%)
  waiting for transfers between devices  17.2 us (38%)
  Pallas kernels  6.86 us (15%)
  local copies, waits for them, and re-layouts  3.16 us (7%)
    ppermute x1, waiting for transfers between devices, line_window(): far = lax.ppermute(data, 'src', [(0, 3), (1, 2), (2, 1), (3, 0)])  13.2 us
    ppermute x2, starting transfers between devices, line_window(): across = lax.ppermute(far[v:v + 1], 'src', near_pairs)  10.7 us
    ppermute x1, starting transfers between devices, line_window(): far = lax.ppermute(data, 'src', [(0, 3), (1, 2), (2, 1), (3, 0)])  3.6 us
    unnamed x6, local copies, waits for them, and re-layouts  3.13 us
    pallas_call x1, Pallas kernels, body(): pl.pallas_call(functools.partial(kernel_b, late), out_shape=[window, jax....  2.98 us
    ppermute x3, starting transfers between devices, swap(): return lax.ppermute(x, axis, [(i, i ^ bit) for i in range(peers)])  2.94 us
    pallas_call x1, Pallas kernels, body(): pl.pallas_call(functools.partial(last_kernel, half + 1, late), out_shape=...  2.27 us
    ppermute x3, waiting for transfers between devices, swap(): return lax.ppermute(x, axis, [(i, i ^ bit) for i in range(peers)])  2.1 us
  transfers between devices with their start and end apart: 7, of which 4 were waited for; matrix products, arithmetic and copies ran while one was open for 0% of the time, Pallas kernels for 10%

profile of v20, /device:TPU:0, one launch (start us, length us, event | category | flops | bytes accessed | tf_op | source)
XLA Modules:
  0.0 44.5 jit_solution(14463921153456304599)
XLA Ops:
  0.0 2.9 %collective-permute-start.5 = (bf16[2,2,256,768]{3,2,1,0:T(8,128)(2,1)}, bf16[2,2,256,768]{3,2,1,0:T(8,128)(2,1)S(1)}, u32[]{:S(2)}, u32[]{:S(2)}) collective-permute-start(bf16[2,2,256,768]{3,2,1,0:T(8,128)(2,1)} %own_ref.1), channel_id=1, source_target_pairs={{0,2},{1,3},{2,0},{3,1},{4,6},{5,7},{6,4},{7,5},{8,10},{9,11},{10,... | collective-permute-start | bytes 4718600 | tf_op jit(solution)/shard_map/ppermute | solution.py:28
  2.9 0.0 collective-permute-start.4
  2.9 3.6 %collective-permute-start = (bf16[2,2,256,256]{3,2,1,0:T(8,128)(2,1)}, bf16[2,2,256,256]{3,2,1,0:T(8,128)(2,1)S(1)}, u32[]{:S(2)}, u32[]{:S(2)}) collective-permute-start(bf16[2,2,256,256]{3,2,1,0:T(8,128)(2,1)} %refs_3_.1), channel_id=1, source_target_pairs={{0,12},{4,8},{8,4},{12,0},{1,13},{5,9},{9,5},{13,1},{2,14},{6,10},... | collective-permute-start | bytes 1572872 | tf_op jit(solution)/shard_map/ppermute | solution.py:37
  6.5 0.0 collective-permute-start.3
  6.5 13.2 %collective-permute-done.refs_2_.refs_5_ = bf16[2,2,256,256]{3,2,1,0:T(8,128)(2,1)S(1)} collective-permute-done((bf16[2,2,256,256]{3,2,1,0:T(8,128)(2,1)}, bf16[2,2,256,256]{3,2,1,0:T(8,128)(2,1)S(1)}, u32[]{:S(2)}, u32[]{:S(2)}) %collective-permute-start) | collective-permute-done | bytes 524320 | tf_op jit(solution)/shard_map/ppermute | solution.py:37
  19.8 10.6 %collective-permute-start.2 = (bf16[1,2,256,256]{3,2,1,0:T(8,128)(2,1)S(1)}, bf16[1,2,256,256]{3,2,1,0:T(8,128)(2,1)S(1)}, u32[]{:S(2)}, u32[]{:S(2)}) collective-permute-start(bf16[1,2,256,256]{3,2,1,0:T(8,128)(2,1)S(1)} %get-tuple-element.29), channel_id=1, source_target_pairs={{0,4},{4,0},{8,12},{12,8},{1,5},{5,1},{9,13},{13,9},{2,6},{6,2},{1... | collective-permute-start | bytes 786440 | tf_op jit(solution)/shard_map/ppermute | solution.py:41
  30.4 0.1 collective-permute-start.1
  30.5 0.2 collective-permute-done.3.refs_1_.refs_4_
  30.7 0.0 copy-start
  30.7 1.0 %copy-done = bf16[2,2,256,256]{3,2,1,0:T(8,128)(2,1)S(1)} copy-done((bf16[2,2,256,256]{3,2,1,0:T(8,128)(2,1)S(1)}, bf16[2,2,256,256]{3,2,1,0:T(8,128)(2,1)}, u32[]{:S(2)}) %copy-start) | copy-done | bytes 524312
  31.7 0.0 copy-start.1
  31.7 1.4 %copy-done.1 = bf16[2,2,256,768]{3,2,1,0:T(8,128)(2,1)S(1)} copy-done((bf16[2,2,256,768]{3,2,1,0:T(8,128)(2,1)S(1)}, bf16[2,2,256,768]{3,2,1,0:T(8,128)(2,1)}, u32[]{:S(2)}) %copy-start.1) | copy-done | bytes 1572888
  33.1 0.0 copy-start.2
  33.1 0.7 %copy-done.2 = s32[4,12]{1,0:T(4,128)S(1)} copy-done((s32[4,12]{1,0:T(4,128)S(1)}, s32[4,12]{1,0:T(4,128)}, u32[]{:S(2)}) %copy-start.2) | copy-done | bytes 216
  33.8 1.6 %shard_map.37 = (bf16[4,256,512]{2,1,0:T(8,128)(2,1)S(1)}, bf16[4,256,512]{2,1,0:T(8,128)(2,1)S(1)}, f32[512,256]{1,0:T(8,128)S(1)}, f32[512,256]{1,0:T(8,128)S(...) custom-call(s32[4,12]{1,0:T(4,128)S(1)} %copy-done.2, bf16[2,2,256,768]{3,2,1,0:T(8,128)(2,1)S(1)} %copy-done.1, ...), custom_call_target="tpu_custom_call" | custom-call | flops 161061280 | bytes 1048576 | tf_op jit(solution)/shard_map/pallas_call | solution.py:214
  35.4 2.1 %collective-permute-done.5.refs_1_ = bf16[2,2,256,768]{3,2,1,0:T(8,128)(2,1)S(1)} collective-permute-done((bf16[2,2,256,768]{3,2,1,0:T(8,128)(2,1)}, bf16[2,2,256,768]{3,2,1,0:T(8,128)(2,1)S(1)}, u32[]{:S(2)}, u32[]{:S(2)}) %collective-permute-start.5) | collective-permute-done | bytes 1572896 | tf_op jit(solution)/shard_map/ppermute | solution.py:28
  37.5 0.0 collective-permute-start.6
  37.5 0.0 collective-permute-done.2.late_ref
  37.6 0.0 collective-permute-done.4.refs_0_
  37.6 3.0 %shard_map.38 = (bf16[4,256,512]{2,1,0:T(8,128)(2,1)S(1)}, bf16[512,512]{1,0:T(8,128)(2,1)S(1)}, f32[2,256,256]{2,1,0:T(8,128)S(1)}, f32[2,256,256]{2,1,0:T(8,128)S(1)}) custom-call(s32[4,12]{1,0:T(4,128)S(1)} %copy-done.2, bf16[1,2,256,256]{3,2,1,0:T(8,128)(2,1)S(1)} %collective-permute-done.2.late_ref, ...), custom_call_target="tpu_custom_call", output_to_operand_aliasing={{0}: (2, {}), {2}: (6, {}), {3}: (7, {})} | custom-call | flops 161061280 | bytes 1048576 | tf_op jit(solution)/shard_map/pallas_call | solution.py:224
  40.5 1.7 %collective-permute-done.1.piece_ref = bf16[1,2,256,256]{3,2,1,0:T(8,128)(2,1)S(1)} collective-permute-done((bf16[1,2,256,256]{3,2,1,0:T(8,128)(2,1)S(1)}, bf16[1,2,256,256]{3,2,1,0:T(8,128)(2,1)S(1)}, u32[]{:S(2)}, u32[]{:S(2)}) %collective-permute-start.1) | collective-permute-done | bytes 262176 | tf_op jit(solution)/shard_map/ppermute | solution.py:41
  42.2 0.0 collective-permute-done.6.refs_0_
  42.2 2.3 %shard_map.40 = (f32[2,2,256,256]{3,2,1,0:T(8,128)}, bf16[4,256,512]{2,1,0:T(8,128)(2,1)S(1)}) custom-call(s32[4,12]{1,0:T(4,128)S(1)} %copy-done.2, bf16[1,2,256,256]{3,2,1,0:T(8,128)(2,1)S(1)} %shard_map.39.late_ref, bf16[4,256,512]{2,1,0:T(8,128)(2,1)S(1)} %get-tuple-element.24.first_window, ...), custom_call_target="tpu_custom_call", output_to_operand_aliasing={{1}: (3, {})} | custom-call | flops 1610612736 | bytes 1048576 | tf_op jit(solution)/shard_map/pallas_call | solution.py:234
  (2 shorter events, 0.0 us)
Async XLA Ops:
  0.0 37.5 %collective-permute-start.5 = (bf16[2,2,256,768]{3,2,1,0:T(8,128)(2,1)}, bf16[2,2,256,768]{3,2,1,0:T(8,128)(2,1)S(1)}, u32[]{:S(2)}, u32[]{:S(2)}) collective-permute-start(bf16[2,2,256,768]{3,2,1,0:T(8,128)(2,1)} %own_ref.1), channel_id=1, source_target_pairs={{0,2},{1,3},{2,0},{3,1},{4,6},{5,7},{6,4},{7,5},{8,10},{9,11},{10,... | collective-permute-start | bytes 4718600 | tf_op jit(solution)/shard_map/ppermute | solution.py:28
  2.9 34.6 %collective-permute-start.4 = (bf16[2,2,256,768]{3,2,1,0:T(8,128)(2,1)}, bf16[2,2,256,768]{3,2,1,0:T(8,128)(2,1)S(1)}, u32[]{:S(2)}, u32[]{:S(2)}) collective-permute-start(bf16[2,2,256,768]{3,2,1,0:T(8,128)(2,1)} %own_ref.1), channel_id=1, source_target_pairs={{0,1},{1,0},{2,3},{3,2},{4,5},{5,4},{6,7},{7,6},{8,9},{9,8},{10,11... | collective-permute-start | bytes 4718600 | tf_op jit(solution)/shard_map/ppermute | solution.py:28
  2.9 16.8 %collective-permute-start = (bf16[2,2,256,256]{3,2,1,0:T(8,128)(2,1)}, bf16[2,2,256,256]{3,2,1,0:T(8,128)(2,1)S(1)}, u32[]{:S(2)}, u32[]{:S(2)}) collective-permute-start(bf16[2,2,256,256]{3,2,1,0:T(8,128)(2,1)} %refs_3_.1), channel_id=1, source_target_pairs={{0,12},{4,8},{8,4},{12,0},{1,13},{5,9},{9,5},{13,1},{2,14},{6,10},... | collective-permute-start | bytes 1572872 | tf_op jit(solution)/shard_map/ppermute | solution.py:37
  6.5 24.1 %collective-permute-start.3 = (bf16[2,2,256,256]{3,2,1,0:T(8,128)(2,1)}, bf16[2,2,256,256]{3,2,1,0:T(8,128)(2,1)S(1)}, u32[]{:S(2)}, u32[]{:S(2)}) collective-permute-start(bf16[2,2,256,256]{3,2,1,0:T(8,128)(2,1)} %refs_3_.1), channel_id=1, source_target_pairs={{0,4},{4,0},{8,12},{12,8},{1,5},{5,1},{9,13},{13,9},{2,6},{6,2},{1... | collective-permute-start | bytes 1572872 | tf_op jit(solution)/shard_map/ppermute | solution.py:38
  19.8 17.8 %collective-permute-start.2 = (bf16[1,2,256,256]{3,2,1,0:T(8,128)(2,1)S(1)}, bf16[1,2,256,256]{3,2,1,0:T(8,128)(2,1)S(1)}, u32[]{:S(2)}, u32[]{:S(2)}) collective-permute-start(bf16[1,2,256,256]{3,2,1,0:T(8,128)(2,1)S(1)} %get-tuple-element.29), channel_id=1, source_target_pairs={{0,4},{4,0},{8,12},{12,8},{1,5},{5,1},{9,13},{13,9},{2,6},{6,2},{1... | collective-permute-start | bytes 786440 | tf_op jit(solution)/shard_map/ppermute | solution.py:41
  30.4 11.8 %collective-permute-start.1 = (bf16[1,2,256,256]{3,2,1,0:T(8,128)(2,1)S(1)}, bf16[1,2,256,256]{3,2,1,0:T(8,128)(2,1)S(1)}, u32[]{:S(2)}, u32[]{:S(2)}) collective-permute-start(bf16[1,2,256,256]{3,2,1,0:T(8,128)(2,1)S(1)} %get-tuple-element.30), channel_id=1, source_target_pairs={{0,4},{4,0},{8,12},{12,8},{1,5},{5,1},{9,13},{13,9},{2,6},{6,2},{1... | collective-permute-start | bytes 786440 | tf_op jit(solution)/shard_map/ppermute | solution.py:41
  30.7 1.0 %copy-start = (bf16[2,2,256,256]{3,2,1,0:T(8,128)(2,1)S(1)}, bf16[2,2,256,256]{3,2,1,0:T(8,128)(2,1)}, u32[]{:S(2)}) copy-start(bf16[2,2,256,256]{3,2,1,0:T(8,128)(2,1)} %refs_3_.1) | copy-start | bytes 1572868
  31.7 1.4 %copy-start.1 = (bf16[2,2,256,768]{3,2,1,0:T(8,128)(2,1)S(1)}, bf16[2,2,256,768]{3,2,1,0:T(8,128)(2,1)}, u32[]{:S(2)}) copy-start(bf16[2,2,256,768]{3,2,1,0:T(8,128)(2,1)} %own_ref.1) | copy-start | bytes 4718596
  33.1 0.7 %copy-start.2 = (s32[4,12]{1,0:T(4,128)S(1)}, s32[4,12]{1,0:T(4,128)}, u32[]{:S(2)}) copy-start(s32[4,12]{1,0:T(4,128)} %aperture_ref.5) | copy-start | bytes 580
  37.5 4.7 %collective-permute-start.6 = (bf16[2,2,256,768]{3,2,1,0:T(8,128)(2,1)S(1)}, bf16[2,2,256,768]{3,2,1,0:T(8,128)(2,1)S(1)}, u32[]{:S(2)}, u32[]{:S(2)}) collective-permute-start(bf16[2,2,256,768]{3,2,1,0:T(8,128)(2,1)S(1)} %collective-permute-done.5.refs_1_), channel_id=1, source_target_pairs={{0,1},{1,0},{2,3},{3,2},{4,5},{5,4},{6,7},{7,6},{8,9},{9,8},{10,11... | collective-permute-start | bytes 4718600 | tf_op jit(solution)/shard_map/ppermute | solution.py:28

commit v21 on v20

--- a/solution.py
+++ b/solution.py
@@ -34,7 +34,7 @@
 
 def line_window(data):
     near_pairs = [(0, 1), (1, 0), (2, 3), (3, 2)]
-    far = lax.ppermute(data, "src", [(0, 3), (1, 2), (2, 1), (3, 0)])
+    far = held(lax.ppermute(data, "src", [(0, 3), (1, 2), (2, 1), (3, 0)]), 5)
     near = lax.ppermute(data, "src", near_pairs)
     windows = []
     for v in range(data.shape[0]):
@@ -184,16 +184,16 @@
     return pltpu.CompilerParams(vmem_limit_bytes=megabytes << 20)
 
 
-def held(piece, token):
+def held(piece, share, *tokens):
     return pl.pallas_call(
-        lambda piece_ref, token_ref, out_ref: None,
+        lambda *refs: None,
         out_shape=jax.ShapeDtypeStruct(piece.shape, piece.dtype),
-        in_specs=[spec(pl.ANY)] * 2,
+        in_specs=[spec(pl.ANY)] * (1 + len(tokens)),
         out_specs=spec(pl.ANY),
         input_output_aliases={0: 0},
         compiler_params=limit(1),
-        cost_estimate=cost(12),
-    )(piece, token)
+        cost_estimate=cost(share),
+    )(piece, *tokens)
 
 
 def body(primaries, data, aperture):
@@ -220,6 +220,7 @@
         cost_estimate=cost(0.1),
     )(aperture, primaries, *pieces)
 
+    far_panel = held(far_panel, 8, first_part)
     handed_on = hand_on(far_panel, first_part)
     first, two, first_part, last_part = pl.pallas_call(
         functools.partial(kernel_b, late),
@@ -240,7 +241,7 @@
         input_output_aliases={3: 1},
         compiler_params=limit(16),
         cost_estimate=cost(1),
-    )(aperture, held(late_pieces[1], two), first, last, two, first_part, last_part, *handed_on)[0]
+    )(aperture, held(late_pieces[1], 12, two), first, last, two, first_part, last_part, *handed_on)[0]
 
 
 def solution(mesh):

time: 44.7 us -> 43.4 us (0.971)
  local copies, waits for them, and re-layouts: 3.16 us -> 0.05 us
  waiting for transfers between devices: 17.2 us -> 20.1 us
  starting transfers between devices: 17.2 us -> 16.2 us
    ppermute x3, waiting for transfers between devices: 2.1 us -> 6.09 us  [swap(): return lax.ppermute(x, axis, [(i, i ^ bit) for i in range(peers)])]
    unnamed x6, local copies, waits for them, and re-layouts: 3.13 us -> 0.01 us
    ppermute x2, waiting for transfers between devices: 1.69 us -> 0.43 us  [line_window(): across = lax.ppermute(far[v:v + 1], 'src', near_pairs)]
    ppermute x2, starting transfers between devices: 10.7 us -> 9.65 us  [line_window(): across = lax.ppermute(far[v:v + 1], 'src', near_pairs)]
  transfers between devices with their start and end apart: 7 -> 7, of which waited for: 4 -> 4; matrix products, arithmetic and copies ran while one was open for 0% -> 0% of each run, Pallas kernels for 10% -> 11%
where the time goes in v21:
time: 43.4 us; the launch traced here: 43.2 us
  waiting for transfers between devices  20.1 us (46%)
  starting transfers between devices  16.2 us (37%)
  Pallas kernels  6.86 us (16%)
    ppermute x1, waiting for transfers between devices, line_window(): far = held(lax.ppermute(data, 'src', [(0, 3), (1, 2), (2, 1), (3, 0)]), 5)  13.3 us
    ppermute x2, starting transfers between devices, line_window(): across = lax.ppermute(far[v:v + 1], 'src', near_pairs)  9.65 us
    ppermute x3, waiting for transfers between devices, swap(): return lax.ppermute(x, axis, [(i, i ^ bit) for i in range(peers)])  6.09 us
    ppermute x1, starting transfers between devices, line_window(): far = held(lax.ppermute(data, 'src', [(0, 3), (1, 2), (2, 1), (3, 0)]), 5)  3.6 us
    pallas_call x1, Pallas kernels, body(): pl.pallas_call(functools.partial(kernel_b, late), out_shape=[window, jax....  2.98 us
    ppermute x3, starting transfers between devices, swap(): return lax.ppermute(x, axis, [(i, i ^ bit) for i in range(peers)])  2.94 us
    pallas_call x1, Pallas kernels, body(): pl.pallas_call(functools.partial(last_kernel, half + 1, late), out_shape=...  2.26 us
    pallas_call x1, Pallas kernels, body(): pl.pallas_call(functools.partial(kernel_a, [{k: at for k, (_, at) in piec...  1.62 us
  transfers between devices with their start and end apart: 7, of which 4 were waited for; matrix products, arithmetic and copies ran while one was open for 0% of the time, Pallas kernels for 11%

profile of v21, /device:TPU:0, one launch (start us, length us, event | category | flops | bytes accessed | tf_op | source)
XLA Modules:
  0.0 43.2 jit_solution(17963208461557905704)
XLA Ops:
  0.0 0.0 copy-start
  0.0 0.0 copy-start.2
  0.0 2.9 %collective-permute-start.5 = (bf16[2,2,256,768]{3,2,1,0:T(8,128)(2,1)}, bf16[2,2,256,768]{3,2,1,0:T(8,128)(2,1)S(1)}, u32[]{:S(2)}, u32[]{:S(2)}) collective-permute-start(bf16[2,2,256,768]{3,2,1,0:T(8,128)(2,1)} %own_ref.1), channel_id=1, source_target_pairs={{0,2},{1,3},{2,0},{3,1},{4,6},{5,7},{6,4},{7,5},{8,10},{9,11},{10,... | collective-permute-start | bytes 4718600 | tf_op jit(solution)/shard_map/ppermute | solution.py:28
  2.9 3.6 %collective-permute-start = (bf16[2,2,256,256]{3,2,1,0:T(8,128)(2,1)}, bf16[2,2,256,256]{3,2,1,0:T(8,128)(2,1)S(1)}, u32[]{:S(2)}, u32[]{:S(2)}) collective-permute-start(bf16[2,2,256,256]{3,2,1,0:T(8,128)(2,1)} %refs_3_.1), channel_id=1, source_target_pairs={{0,12},{4,8},{8,4},{12,0},{1,13},{5,9},{9,5},{13,1},{2,14},{6,10},... | collective-permute-start | bytes 1572872 | tf_op jit(solution)/shard_map/ppermute | solution.py:37
  6.5 0.0 collective-permute-start.3
  6.5 0.0 collective-permute-start.4
  6.6 13.3 %collective-permute-done.refs_0_ = bf16[2,2,256,256]{3,2,1,0:T(8,128)(2,1)S(1)} collective-permute-done((bf16[2,2,256,256]{3,2,1,0:T(8,128)(2,1)}, bf16[2,2,256,256]{3,2,1,0:T(8,128)(2,1)S(1)}, u32[]{:S(2)}, u32[]{:S(2)}) %collective-permute-start) | collective-permute-done | bytes 524320 | tf_op jit(solution)/shard_map/ppermute | solution.py:37
  19.8 0.0 copy-start.1
  19.9 9.6 %collective-permute-start.2 = (bf16[1,2,256,256]{3,2,1,0:T(8,128)(2,1)S(1)}, bf16[1,2,256,256]{3,2,1,0:T(8,128)(2,1)S(1)}, u32[]{:S(2)}, u32[]{:S(2)}) collective-permute-start(bf16[1,2,256,256]{3,2,1,0:T(8,128)(2,1)S(1)} %get-tuple-element.29), channel_id=1, source_target_pairs={{0,4},{4,0},{8,12},{12,8},{1,5},{5,1},{9,13},{13,9},{2,6},{6,2},{1... | collective-permute-start | bytes 786440 | tf_op jit(solution)/shard_map/ppermute | solution.py:41
  29.5 0.1 collective-permute-start.1
  29.5 0.3 collective-permute-done.3.refs_1_.refs_4_
  29.8 0.0 copy-done
  29.8 0.0 copy-done.2
  29.8 0.0 copy-done.1
  29.8 1.6 %shard_map.38 = (bf16[4,256,512]{2,1,0:T(8,128)(2,1)S(1)}, bf16[4,256,512]{2,1,0:T(8,128)(2,1)S(1)}, f32[512,256]{1,0:T(8,128)S(1)}, f32[512,256]{1,0:T(8,128)S(...) custom-call(s32[4,12]{1,0:T(4,128)S(1)} %copy-done.2, bf16[2,2,256,768]{3,2,1,0:T(8,128)(2,1)S(1)} %copy-done.1, ...), custom_call_target="tpu_custom_call" | custom-call | flops 161061280 | bytes 1048576 | tf_op jit(solution)/shard_map/pallas_call | solution.py:214
  31.5 6.1 %collective-permute-done.5.refs_0_ = bf16[2,2,256,768]{3,2,1,0:T(8,128)(2,1)S(1)} collective-permute-done((bf16[2,2,256,768]{3,2,1,0:T(8,128)(2,1)}, bf16[2,2,256,768]{3,2,1,0:T(8,128)(2,1)S(1)}, u32[]{:S(2)}, u32[]{:S(2)}) %collective-permute-start.5) | collective-permute-done | bytes 1572896 | tf_op jit(solution)/shard_map/ppermute | solution.py:28
  37.5 0.0 collective-permute-start.6
  37.5 0.0 collective-permute-done.2.late_ref
  37.6 0.0 collective-permute-done.4.refs_0_
  37.6 3.0 %shard_map.40 = (bf16[4,256,512]{2,1,0:T(8,128)(2,1)S(1)}, bf16[512,512]{1,0:T(8,128)(2,1)S(1)}, f32[2,256,256]{2,1,0:T(8,128)S(1)}, f32[2,256,256]{2,1,0:T(8,128)S(1)}) custom-call(s32[4,12]{1,0:T(4,128)S(1)} %copy-done.2, bf16[1,2,256,256]{3,2,1,0:T(8,128)(2,1)S(1)} %collective-permute-done.2.late_ref, ...), custom_call_target="tpu_custom_call", output_to_operand_aliasing={{0}: (2, {}), {2}: (6, {}), {3}: (7, {})} | custom-call | flops 161061280 | bytes 1048576 | tf_op jit(solution)/shard_map/pallas_call | solution.py:225
  40.5 0.4 collective-permute-done.1.refs_0_
  41.0 0.0 collective-permute-done.6.refs_0_
  41.0 2.3 %shard_map.42 = (f32[2,2,256,256]{3,2,1,0:T(8,128)}, bf16[4,256,512]{2,1,0:T(8,128)(2,1)S(1)}) custom-call(s32[4,12]{1,0:T(4,128)S(1)} %copy-done.2, bf16[1,2,256,256]{3,2,1,0:T(8,128)(2,1)S(1)} %shard_map.41.late_ref, bf16[4,256,512]{2,1,0:T(8,128)(2,1)S(1)} %get-tuple-element.24.first_window, ...), custom_call_target="tpu_custom_call", output_to_operand_aliasing={{1}: (3, {})} | custom-call | flops 1610612736 | bytes 1048576 | tf_op jit(solution)/shard_map/pallas_call | solution.py:235
  (4 shorter events, 0.0 us)
Async XLA Ops:
  0.0 29.8 %copy-start = (bf16[2,2,256,256]{3,2,1,0:T(8,128)(2,1)S(1)}, bf16[2,2,256,256]{3,2,1,0:T(8,128)(2,1)}, u32[]{:S(2)}) copy-start(bf16[2,2,256,256]{3,2,1,0:T(8,128)(2,1)} %refs_3_.1) | copy-start | bytes 1572868
  0.0 29.8 %copy-start.2 = (s32[4,12]{1,0:T(4,128)S(1)}, s32[4,12]{1,0:T(4,128)}, u32[]{:S(2)}) copy-start(s32[4,12]{1,0:T(4,128)} %aperture_ref.5) | copy-start | bytes 580
  0.0 37.5 %collective-permute-start.5 = (bf16[2,2,256,768]{3,2,1,0:T(8,128)(2,1)}, bf16[2,2,256,768]{3,2,1,0:T(8,128)(2,1)S(1)}, u32[]{:S(2)}, u32[]{:S(2)}) collective-permute-start(bf16[2,2,256,768]{3,2,1,0:T(8,128)(2,1)} %own_ref.1), channel_id=1, source_target_pairs={{0,2},{1,3},{2,0},{3,1},{4,6},{5,7},{6,4},{7,5},{8,10},{9,11},{10,... | collective-permute-start | bytes 4718600 | tf_op jit(solution)/shard_map/ppermute | solution.py:28
  2.9 16.9 %collective-permute-start = (bf16[2,2,256,256]{3,2,1,0:T(8,128)(2,1)}, bf16[2,2,256,256]{3,2,1,0:T(8,128)(2,1)S(1)}, u32[]{:S(2)}, u32[]{:S(2)}) collective-permute-start(bf16[2,2,256,256]{3,2,1,0:T(8,128)(2,1)} %refs_3_.1), channel_id=1, source_target_pairs={{0,12},{4,8},{8,4},{12,0},{1,13},{5,9},{9,5},{13,1},{2,14},{6,10},... | collective-permute-start | bytes 1572872 | tf_op jit(solution)/shard_map/ppermute | solution.py:37
  6.5 23.3 %collective-permute-start.3 = (bf16[2,2,256,256]{3,2,1,0:T(8,128)(2,1)}, bf16[2,2,256,256]{3,2,1,0:T(8,128)(2,1)S(1)}, u32[]{:S(2)}, u32[]{:S(2)}) collective-permute-start(bf16[2,2,256,256]{3,2,1,0:T(8,128)(2,1)} %refs_3_.1), channel_id=1, source_target_pairs={{0,4},{4,0},{8,12},{12,8},{1,5},{5,1},{9,13},{13,9},{2,6},{6,2},{1... | collective-permute-start | bytes 1572872 | tf_op jit(solution)/shard_map/ppermute | solution.py:38
  6.5 31.0 %collective-permute-start.4 = (bf16[2,2,256,768]{3,2,1,0:T(8,128)(2,1)}, bf16[2,2,256,768]{3,2,1,0:T(8,128)(2,1)S(1)}, u32[]{:S(2)}, u32[]{:S(2)}) collective-permute-start(bf16[2,2,256,768]{3,2,1,0:T(8,128)(2,1)} %own_ref.1), channel_id=1, source_target_pairs={{0,1},{1,0},{2,3},{3,2},{4,5},{5,4},{6,7},{7,6},{8,9},{9,8},{10,11... | collective-permute-start | bytes 4718600 | tf_op jit(solution)/shard_map/ppermute | solution.py:28
  19.8 10.0 %copy-start.1 = (bf16[2,2,256,768]{3,2,1,0:T(8,128)(2,1)S(1)}, bf16[2,2,256,768]{3,2,1,0:T(8,128)(2,1)}, u32[]{:S(2)}) copy-start(bf16[2,2,256,768]{3,2,1,0:T(8,128)(2,1)} %own_ref.1) | copy-start | bytes 4718596
  19.9 17.7 %collective-permute-start.2 = (bf16[1,2,256,256]{3,2,1,0:T(8,128)(2,1)S(1)}, bf16[1,2,256,256]{3,2,1,0:T(8,128)(2,1)S(1)}, u32[]{:S(2)}, u32[]{:S(2)}) collective-permute-start(bf16[1,2,256,256]{3,2,1,0:T(8,128)(2,1)S(1)} %get-tuple-element.29), channel_id=1, source_target_pairs={{0,4},{4,0},{8,12},{12,8},{1,5},{5,1},{9,13},{13,9},{2,6},{6,2},{1... | collective-permute-start | bytes 786440 | tf_op jit(solution)/shard_map/ppermute | solution.py:41
  29.5 11.5 %collective-permute-start.1 = (bf16[1,2,256,256]{3,2,1,0:T(8,128)(2,1)S(1)}, bf16[1,2,256,256]{3,2,1,0:T(8,128)(2,1)S(1)}, u32[]{:S(2)}, u32[]{:S(2)}) collective-permute-start(bf16[1,2,256,256]{3,2,1,0:T(8,128)(2,1)S(1)} %get-tuple-element.30), channel_id=1, source_target_pairs={{0,4},{4,0},{8,12},{12,8},{1,5},{5,1},{9,13},{13,9},{2,6},{6,2},{1... | collective-permute-start | bytes 786440 | tf_op jit(solution)/shard_map/ppermute | solution.py:41
  37.5 3.4 %collective-permute-start.6 = (bf16[2,2,256,768]{3,2,1,0:T(8,128)(2,1)S(1)}, bf16[2,2,256,768]{3,2,1,0:T(8,128)(2,1)S(1)}, u32[]{:S(2)}, u32[]{:S(2)}) collective-permute-start(bf16[2,2,256,768]{3,2,1,0:T(8,128)(2,1)S(1)} %shard_map.39.refs_1_), channel_id=1, source_target_pairs={{0,1},{1,0},{2,3},{3,2},{4,5},{5,4},{6,7},{7,6},{8,9},{9,8},{10,11... | collective-permute-start | bytes 4718600 | tf_op jit(solution)/shard_map/ppermute | solution.py:28

commit v22 on v21

--- a/solution.py
+++ b/solution.py
@@ -52,9 +52,9 @@
     return [[(window[distance], v) for distance in range(-reach, reach + 1)] for v in range(data.shape[0])]
 
 
-def gather_panels(primaries):
+def gather_panels(primaries, first):
     bit = lax.axis_size("rcv") // 2
-    panels = [primaries]
+    panels = [after(primaries, first)]
     for lower in range(1, bit):
         panels.append(swap(panels[lower & (lower - 1)], "rcv", lower & -lower))
     return panels, swap(primaries, "rcv", bit)
@@ -200,7 +200,7 @@
     width = data.shape[3]
     line = lax.axis_size("src") == 4
     windows = (line_window if line else hop_window)(data)
-    panels, far_panel = gather_panels(primaries)
+    panels, far_panel = gather_panels(primaries, windows[0][-1][0])
     half = len(panels)
     late = 2 if line else len(windows[0]) - 1
     late_pieces = [piece[at : at + 1] for piece, at in (window[late] for window in windows)]
@@ -220,7 +220,7 @@
         cost_estimate=cost(0.1),
     )(aperture, primaries, *pieces)
 
-    far_panel = held(far_panel, 8, first_part)
+    far_panel = held(far_panel, 12, first_part)
     handed_on = hand_on(far_panel, first_part)
     first, two, first_part, last_part = pl.pallas_call(
         functools.partial(kernel_b, late),

time: 43.4 us -> 43.5 us (level)
  no operation moved by 1% of the time
where the time goes in v22:
time: 43.5 us; the launch traced here: 43.3 us
  waiting for transfers between devices  20.1 us (46%)
  starting transfers between devices  16.3 us (37%)
  Pallas kernels  6.86 us (16%)
    ppermute x1, waiting for transfers between devices, line_window(): far = held(lax.ppermute(data, 'src', [(0, 3), (1, 2), (2, 1), (3, 0)]), 5)  13.3 us
    ppermute x2, starting transfers between devices, line_window(): across = lax.ppermute(far[v:v + 1], 'src', near_pairs)  9.65 us
    ppermute x3, waiting for transfers between devices, swap(): return lax.ppermute(x, axis, [(i, i ^ bit) for i in range(peers)])  6.09 us
    ppermute x1, starting transfers between devices, line_window(): far = held(lax.ppermute(data, 'src', [(0, 3), (1, 2), (2, 1), (3, 0)]), 5)  3.6 us
    ppermute x3, starting transfers between devices, swap(): return lax.ppermute(x, axis, [(i, i ^ bit) for i in range(peers)])  3.01 us
    pallas_call x1, Pallas kernels, body(): pl.pallas_call(functools.partial(kernel_b, late), out_shape=[window, jax....  2.98 us
    pallas_call x1, Pallas kernels, body(): pl.pallas_call(functools.partial(last_kernel, half + 1, late), out_shape=...  2.26 us
    pallas_call x1, Pallas kernels, body(): pl.pallas_call(functools.partial(kernel_a, [{k: at for k, (_, at) in piec...  1.62 us
  transfers between devices with their start and end apart: 7, of which 4 were waited for; matrix products, arithmetic and copies ran while one was open for 0% of the time, Pallas kernels for 11%

profile of v22, /device:TPU:0, one launch (start us, length us, event | category | flops | bytes accessed | tf_op | source)
XLA Modules:
  0.0 43.3 jit_solution(10967905008610144202)
XLA Ops:
  0.0 0.0 copy-start.1
  0.0 0.0 copy-start
  0.0 0.0 copy-start.2
  0.0 3.0 %collective-permute-start.5 = (bf16[2,2,256,768]{3,2,1,0:T(8,128)(2,1)}, bf16[2,2,256,768]{3,2,1,0:T(8,128)(2,1)S(1)}, u32[]{:S(2)}, u32[]{:S(2)}) collective-permute-start(bf16[2,2,256,768]{3,2,1,0:T(8,128)(2,1)} %own_ref.1), channel_id=1, source_target_pairs={{0,2},{1,3},{2,0},{3,1},{4,6},{5,7},{6,4},{7,5},{8,10},{9,11},{10,... | collective-permute-start | bytes 4718600 | tf_op jit(solution)/shard_map/ppermute | solution.py:28
  3.0 3.6 %collective-permute-start = (bf16[2,2,256,256]{3,2,1,0:T(8,128)(2,1)}, bf16[2,2,256,256]{3,2,1,0:T(8,128)(2,1)S(1)}, u32[]{:S(2)}, u32[]{:S(2)}) collective-permute-start(bf16[2,2,256,256]{3,2,1,0:T(8,128)(2,1)} %refs_3_.1), channel_id=1, source_target_pairs={{0,12},{4,8},{8,4},{12,0},{1,13},{5,9},{9,5},{13,1},{2,14},{6,10},... | collective-permute-start | bytes 1572872 | tf_op jit(solution)/shard_map/ppermute | solution.py:37
  6.6 0.0 collective-permute-start.3
  6.6 13.3 %collective-permute-done.refs_0_ = bf16[2,2,256,256]{3,2,1,0:T(8,128)(2,1)S(1)} collective-permute-done((bf16[2,2,256,256]{3,2,1,0:T(8,128)(2,1)}, bf16[2,2,256,256]{3,2,1,0:T(8,128)(2,1)S(1)}, u32[]{:S(2)}, u32[]{:S(2)}) %collective-permute-start) | collective-permute-done | bytes 524320 | tf_op jit(solution)/shard_map/ppermute | solution.py:37
  20.0 9.6 %collective-permute-start.2 = (bf16[1,2,256,256]{3,2,1,0:T(8,128)(2,1)S(1)}, bf16[1,2,256,256]{3,2,1,0:T(8,128)(2,1)S(1)}, u32[]{:S(2)}, u32[]{:S(2)}) collective-permute-start(bf16[1,2,256,256]{3,2,1,0:T(8,128)(2,1)S(1)} %get-tuple-element.31), channel_id=1, source_target_pairs={{0,4},{4,0},{8,12},{12,8},{1,5},{5,1},{9,13},{13,9},{2,6},{6,2},{1... | collective-permute-start | bytes 786440 | tf_op jit(solution)/shard_map/ppermute | solution.py:41
  29.5 0.1 collective-permute-start.1
  29.6 0.0 copy-done.1
  29.6 0.0 collective-permute-start.4
  29.6 0.3 collective-permute-done.3.refs_1_.refs_4_
  29.9 0.0 copy-done
  29.9 0.0 copy-done.2
  29.9 1.6 %shard_map.38 = (bf16[4,256,512]{2,1,0:T(8,128)(2,1)S(1)}, bf16[4,256,512]{2,1,0:T(8,128)(2,1)S(1)}, f32[512,256]{1,0:T(8,128)S(1)}, f32[512,256]{1,0:T(8,128)S(...) custom-call(s32[4,12]{1,0:T(4,128)S(1)} %copy-done.2, bf16[2,2,256,768]{3,2,1,0:T(8,128)(2,1)S(1)} %copy-done.1, ...), custom_call_target="tpu_custom_call" | custom-call | flops 161061280 | bytes 1048576 | tf_op jit(solution)/shard_map/pallas_call | solution.py:214
  31.5 6.1 %collective-permute-done.5.refs_0_ = bf16[2,2,256,768]{3,2,1,0:T(8,128)(2,1)S(1)} collective-permute-done((bf16[2,2,256,768]{3,2,1,0:T(8,128)(2,1)}, bf16[2,2,256,768]{3,2,1,0:T(8,128)(2,1)S(1)}, u32[]{:S(2)}, u32[]{:S(2)}) %collective-permute-start.5) | collective-permute-done | bytes 1572896 | tf_op jit(solution)/shard_map/ppermute | solution.py:28
  37.6 0.0 collective-permute-start.6
  37.6 0.0 collective-permute-done.2.late_ref
  37.6 0.0 collective-permute-done.4.refs_0_
  37.6 3.0 %shard_map.40 = (bf16[4,256,512]{2,1,0:T(8,128)(2,1)S(1)}, bf16[512,512]{1,0:T(8,128)(2,1)S(1)}, f32[2,256,256]{2,1,0:T(8,128)S(1)}, f32[2,256,256]{2,1,0:T(8,128)S(1)}) custom-call(s32[4,12]{1,0:T(4,128)S(1)} %copy-done.2, bf16[1,2,256,256]{3,2,1,0:T(8,128)(2,1)S(1)} %collective-permute-done.2.late_ref, ...), custom_call_target="tpu_custom_call", output_to_operand_aliasing={{0}: (2, {}), {2}: (6, {}), {3}: (7, {})} | custom-call | flops 161061280 | bytes 1048576 | tf_op jit(solution)/shard_map/pallas_call | solution.py:225
  40.6 0.4 collective-permute-done.1.refs_0_
  41.0 0.0 collective-permute-done.6.refs_0_
  41.0 2.3 %shard_map.42 = (f32[2,2,256,256]{3,2,1,0:T(8,128)}, bf16[4,256,512]{2,1,0:T(8,128)(2,1)S(1)}) custom-call(s32[4,12]{1,0:T(4,128)S(1)} %copy-done.2, bf16[1,2,256,256]{3,2,1,0:T(8,128)(2,1)S(1)} %shard_map.41.late_ref, bf16[4,256,512]{2,1,0:T(8,128)(2,1)S(1)} %get-tuple-element.26.first_window, ...), custom_call_target="tpu_custom_call", output_to_operand_aliasing={{1}: (3, {})} | custom-call | flops 1610612736 | bytes 1048576 | tf_op jit(solution)/shard_map/pallas_call | solution.py:235
  (4 shorter events, 0.0 us)
Async XLA Ops:
  0.0 29.6 %copy-start.1 = (bf16[2,2,256,768]{3,2,1,0:T(8,128)(2,1)S(1)}, bf16[2,2,256,768]{3,2,1,0:T(8,128)(2,1)}, u32[]{:S(2)}) copy-start(bf16[2,2,256,768]{3,2,1,0:T(8,128)(2,1)} %own_ref.1) | copy-start | bytes 4718596
  0.0 29.9 %copy-start = (bf16[2,2,256,256]{3,2,1,0:T(8,128)(2,1)S(1)}, bf16[2,2,256,256]{3,2,1,0:T(8,128)(2,1)}, u32[]{:S(2)}) copy-start(bf16[2,2,256,256]{3,2,1,0:T(8,128)(2,1)} %refs_3_.1) | copy-start | bytes 1572868
  0.0 29.9 %copy-start.2 = (s32[4,12]{1,0:T(4,128)S(1)}, s32[4,12]{1,0:T(4,128)}, u32[]{:S(2)}) copy-start(s32[4,12]{1,0:T(4,128)} %aperture_ref.5) | copy-start | bytes 580
  0.0 37.6 %collective-permute-start.5 = (bf16[2,2,256,768]{3,2,1,0:T(8,128)(2,1)}, bf16[2,2,256,768]{3,2,1,0:T(8,128)(2,1)S(1)}, u32[]{:S(2)}, u32[]{:S(2)}) collective-permute-start(bf16[2,2,256,768]{3,2,1,0:T(8,128)(2,1)} %own_ref.1), channel_id=1, source_target_pairs={{0,2},{1,3},{2,0},{3,1},{4,6},{5,7},{6,4},{7,5},{8,10},{9,11},{10,... | collective-permute-start | bytes 4718600 | tf_op jit(solution)/shard_map/ppermute | solution.py:28
  3.0 16.9 %collective-permute-start = (bf16[2,2,256,256]{3,2,1,0:T(8,128)(2,1)}, bf16[2,2,256,256]{3,2,1,0:T(8,128)(2,1)S(1)}, u32[]{:S(2)}, u32[]{:S(2)}) collective-permute-start(bf16[2,2,256,256]{3,2,1,0:T(8,128)(2,1)} %refs_3_.1), channel_id=1, source_target_pairs={{0,12},{4,8},{8,4},{12,0},{1,13},{5,9},{9,5},{13,1},{2,14},{6,10},... | collective-permute-start | bytes 1572872 | tf_op jit(solution)/shard_map/ppermute | solution.py:37
  6.6 23.3 %collective-permute-start.3 = (bf16[2,2,256,256]{3,2,1,0:T(8,128)(2,1)}, bf16[2,2,256,256]{3,2,1,0:T(8,128)(2,1)S(1)}, u32[]{:S(2)}, u32[]{:S(2)}) collective-permute-start(bf16[2,2,256,256]{3,2,1,0:T(8,128)(2,1)} %refs_3_.1), channel_id=1, source_target_pairs={{0,4},{4,0},{8,12},{12,8},{1,5},{5,1},{9,13},{13,9},{2,6},{6,2},{1... | collective-permute-start | bytes 1572872 | tf_op jit(solution)/shard_map/ppermute | solution.py:38
  20.0 17.7 %collective-permute-start.2 = (bf16[1,2,256,256]{3,2,1,0:T(8,128)(2,1)S(1)}, bf16[1,2,256,256]{3,2,1,0:T(8,128)(2,1)S(1)}, u32[]{:S(2)}, u32[]{:S(2)}) collective-permute-start(bf16[1,2,256,256]{3,2,1,0:T(8,128)(2,1)S(1)} %get-tuple-element.31), channel_id=1, source_target_pairs={{0,4},{4,0},{8,12},{12,8},{1,5},{5,1},{9,13},{13,9},{2,6},{6,2},{1... | collective-permute-start | bytes 786440 | tf_op jit(solution)/shard_map/ppermute | solution.py:41
  29.5 11.5 %collective-permute-start.1 = (bf16[1,2,256,256]{3,2,1,0:T(8,128)(2,1)S(1)}, bf16[1,2,256,256]{3,2,1,0:T(8,128)(2,1)S(1)}, u32[]{:S(2)}, u32[]{:S(2)}) collective-permute-start(bf16[1,2,256,256]{3,2,1,0:T(8,128)(2,1)S(1)} %get-tuple-element.32), channel_id=1, source_target_pairs={{0,4},{4,0},{8,12},{12,8},{1,5},{5,1},{9,13},{13,9},{2,6},{6,2},{1... | collective-permute-start | bytes 786440 | tf_op jit(solution)/shard_map/ppermute | solution.py:41
  29.6 8.0 %collective-permute-start.4 = (bf16[2,2,256,768]{3,2,1,0:T(8,128)(2,1)S(1)}, bf16[2,2,256,768]{3,2,1,0:T(8,128)(2,1)S(1)}, u32[]{:S(2)}, u32[]{:S(2)}) collective-permute-start(bf16[2,2,256,768]{3,2,1,0:T(8,128)(2,1)S(1)} %copy-done.1), channel_id=1, source_target_pairs={{0,1},{1,0},{2,3},{3,2},{4,5},{5,4},{6,7},{7,6},{8,9},{9,8},{10,11... | collective-permute-start | bytes 4718600 | tf_op jit(solution)/shard_map/ppermute | solution.py:28
  37.6 3.4 %collective-permute-start.6 = (bf16[2,2,256,768]{3,2,1,0:T(8,128)(2,1)S(1)}, bf16[2,2,256,768]{3,2,1,0:T(8,128)(2,1)S(1)}, u32[]{:S(2)}, u32[]{:S(2)}) collective-permute-start(bf16[2,2,256,768]{3,2,1,0:T(8,128)(2,1)S(1)} %shard_map.39.refs_1_), channel_id=1, source_target_pairs={{0,1},{1,0},{2,3},{3,2},{4,5},{5,4},{6,7},{7,6},{8,9},{9,8},{10,11... | collective-permute-start | bytes 4718600 | tf_op jit(solution)/shard_map/ppermute | solution.py:28

commit v23 on v22

--- a/solution.py
+++ b/solution.py
@@ -10,7 +10,7 @@
 BLK = 256
 APER = 12
 HW = 6
-PIECES = 1
+HALVES = 2
 
 
 def after(value, *earlier):
@@ -93,16 +93,16 @@
     return both[:rows, :width] - both[rows:, width:], both[:rows, width:] + both[rows:, :width]
 
 
-def rows_of(panel):
-    return panel[...].reshape(2 * panel.shape[1], panel.shape[2])
-
-
-def product(window, aperture_ref, panels, late_in_two=None, late=None):
+def rows_of(panel, rows=pl.ds(0, BLK)):
+    return panel[:, rows].reshape(2 * rows.size, panel.shape[2])
+
+
+def product(window, aperture_ref, panels, late_in_two=None, late=None, rows=pl.ds(0, BLK)):
     blocks = []
     for m, panel in panels.items():
         entries = slot_entries(aperture_ref, m, panel.shape[-1] // BLK, window.shape[0])
         blocks += [window[k] for k in entries]
-    values = [rows_of(panel) for panel in panels.values()]
+    values = [rows_of(panel, rows) for panel in panels.values()]
     if late_in_two is not None:
         values.append(late_in_two)
         blocks += [window[late]] * 2
@@ -152,22 +152,22 @@
 def last_kernel(far_half, late, aperture_ref, late_ref, first_window, _, two, first_part, last_part, *refs):
     *panel_refs, out_ref, window, result, sems = refs
 
-    def finish(v, part, real, imag):
+    def finish(v, rows, part, real, imag):
         copies = []
         for p, value in enumerate((real, imag)):
-            result[v, p] = part[p] + value
-            for chunk in range(PIECES):
-                rows = pl.ds(chunk * (BLK // PIECES), BLK // PIECES)
-                copies.append(
-                    pltpu.make_async_copy(result.at[v, p, rows], out_ref.at[v, p, rows], sems.at[v, p, chunk])
-                )
-                copies[-1].start()
+            result[v, p, rows] = part[p, rows] + value
+            sem = sems.at[v, p, rows.start // (BLK // HALVES)]
+            copies.append(pltpu.make_async_copy(result.at[v, p, rows], out_ref.at[v, p, rows], sem))
+            copies[-1].start()
         return copies
 
     panels = [{far_half + m: ref.at[v] for m, ref in enumerate(panel_refs)} for v in range(2)]
-    copies = finish(0, first_part, *product(first_window, aperture_ref, panels[0]))
+    copies = finish(0, pl.ds(0, BLK), first_part, *product(first_window, aperture_ref, panels[0]))
     fill_window(window, {late: late_ref.at[0]})
-    copies += finish(1, last_part, *product(window, aperture_ref, panels[1], two[...], late))
+    for half in range(HALVES):
+        rows = pl.ds(half * (BLK // HALVES), BLK // HALVES)
+        sums = jnp.concatenate([two[pl.ds(p * BLK + rows.start, rows.size)] for p in range(2)], axis=0)
+        copies += finish(1, rows, last_part, *product(window, aperture_ref, panels[1], sums, late, rows))
     for copy in copies:
         copy.wait()
 
@@ -237,7 +237,7 @@
         out_shape=[jax.ShapeDtypeStruct((2, 2, BLK, width), jnp.float32), window],
         in_specs=[vmem] + [vmem] * (6 + len(handed_on)),
         out_specs=[anywhere, vmem],
-        scratch_shapes=[pltpu.VMEM((2, 2, BLK, width), jnp.float32), pltpu.SemaphoreType.DMA((2, 2, PIECES))],
+        scratch_shapes=[pltpu.VMEM((2, 2, BLK, width), jnp.float32), pltpu.SemaphoreType.DMA((2, 2, HALVES))],
         input_output_aliases={3: 1},
         compiler_params=limit(16),
         cost_estimate=cost(1),

time: 43.5 us -> 43.5 us (level)
  no operation moved by 1% of the time
where the time goes in v23:
time: 43.5 us; the launch traced here: 43.4 us
  waiting for transfers between devices  20.1 us (46%)
  starting transfers between devices  16.3 us (37%)
  Pallas kernels  6.91 us (16%)
    ppermute x1, waiting for transfers between devices, line_window(): far = held(lax.ppermute(data, 'src', [(0, 3), (1, 2), (2, 1), (3, 0)]), 5)  13.3 us
    ppermute x2, starting transfers between devices, line_window(): across = lax.ppermute(far[v:v + 1], 'src', near_pairs)  9.65 us
    ppermute x3, waiting for transfers between devices, swap(): return lax.ppermute(x, axis, [(i, i ^ bit) for i in range(peers)])  6.09 us
    ppermute x1, starting transfers between devices, line_window(): far = held(lax.ppermute(data, 'src', [(0, 3), (1, 2), (2, 1), (3, 0)]), 5)  3.6 us
    ppermute x3, starting transfers between devices, swap(): return lax.ppermute(x, axis, [(i, i ^ bit) for i in range(peers)])  3.01 us
    pallas_call x1, Pallas kernels, body(): pl.pallas_call(functools.partial(kernel_b, late), out_shape=[window, jax....  2.98 us
    pallas_call x1, Pallas kernels, body(): pl.pallas_call(functools.partial(last_kernel, half + 1, late), out_shape=...  2.31 us
    pallas_call x1, Pallas kernels, body(): pl.pallas_call(functools.partial(kernel_a, [{k: at for k, (_, at) in piec...  1.62 us
  transfers between devices with their start and end apart: 7, of which 4 were waited for; matrix products, arithmetic and copies ran while one was open for 0% of the time, Pallas kernels for 11%

profile of v23, /device:TPU:0, one launch (start us, length us, event | category | flops | bytes accessed | tf_op | source)
XLA Modules:
  0.0 43.4 jit_solution(2375736589449389415)
XLA Ops:
  0.0 0.0 copy-start.1
  0.0 0.0 copy-start
  0.0 0.0 copy-start.2
  0.0 3.0 %collective-permute-start.5 = (bf16[2,2,256,768]{3,2,1,0:T(8,128)(2,1)}, bf16[2,2,256,768]{3,2,1,0:T(8,128)(2,1)S(1)}, u32[]{:S(2)}, u32[]{:S(2)}) collective-permute-start(bf16[2,2,256,768]{3,2,1,0:T(8,128)(2,1)} %own_ref.1), channel_id=1, source_target_pairs={{0,2},{1,3},{2,0},{3,1},{4,6},{5,7},{6,4},{7,5},{8,10},{9,11},{10,... | collective-permute-start | bytes 4718600 | tf_op jit(solution)/shard_map/ppermute | solution.py:28
  3.0 3.6 %collective-permute-start = (bf16[2,2,256,256]{3,2,1,0:T(8,128)(2,1)}, bf16[2,2,256,256]{3,2,1,0:T(8,128)(2,1)S(1)}, u32[]{:S(2)}, u32[]{:S(2)}) collective-permute-start(bf16[2,2,256,256]{3,2,1,0:T(8,128)(2,1)} %refs_3_.1), channel_id=1, source_target_pairs={{0,12},{4,8},{8,4},{12,0},{1,13},{5,9},{9,5},{13,1},{2,14},{6,10},... | collective-permute-start | bytes 1572872 | tf_op jit(solution)/shard_map/ppermute | solution.py:37
  6.6 0.0 collective-permute-start.3
  6.6 13.3 %collective-permute-done.refs_0_ = bf16[2,2,256,256]{3,2,1,0:T(8,128)(2,1)S(1)} collective-permute-done((bf16[2,2,256,256]{3,2,1,0:T(8,128)(2,1)}, bf16[2,2,256,256]{3,2,1,0:T(8,128)(2,1)S(1)}, u32[]{:S(2)}, u32[]{:S(2)}) %collective-permute-start) | collective-permute-done | bytes 524320 | tf_op jit(solution)/shard_map/ppermute | solution.py:37
  20.0 9.6 %collective-permute-start.2 = (bf16[1,2,256,256]{3,2,1,0:T(8,128)(2,1)S(1)}, bf16[1,2,256,256]{3,2,1,0:T(8,128)(2,1)S(1)}, u32[]{:S(2)}, u32[]{:S(2)}) collective-permute-start(bf16[1,2,256,256]{3,2,1,0:T(8,128)(2,1)S(1)} %get-tuple-element.31), channel_id=1, source_target_pairs={{0,4},{4,0},{8,12},{12,8},{1,5},{5,1},{9,13},{13,9},{2,6},{6,2},{1... | collective-permute-start | bytes 786440 | tf_op jit(solution)/shard_map/ppermute | solution.py:41
  29.5 0.1 collective-permute-start.1
  29.6 0.0 copy-done.1
  29.6 0.0 collective-permute-start.4
  29.6 0.3 collective-permute-done.3.refs_1_.refs_4_
  29.9 0.0 copy-done
  29.9 0.0 copy-done.2
  29.9 1.6 %shard_map.38 = (bf16[4,256,512]{2,1,0:T(8,128)(2,1)S(1)}, bf16[4,256,512]{2,1,0:T(8,128)(2,1)S(1)}, f32[512,256]{1,0:T(8,128)S(1)}, f32[512,256]{1,0:T(8,128)S(...) custom-call(s32[4,12]{1,0:T(4,128)S(1)} %copy-done.2, bf16[2,2,256,768]{3,2,1,0:T(8,128)(2,1)S(1)} %copy-done.1, ...), custom_call_target="tpu_custom_call" | custom-call | flops 161061280 | bytes 1048576 | tf_op jit(solution)/shard_map/pallas_call | solution.py:214
  31.5 6.1 %collective-permute-done.5.refs_0_ = bf16[2,2,256,768]{3,2,1,0:T(8,128)(2,1)S(1)} collective-permute-done((bf16[2,2,256,768]{3,2,1,0:T(8,128)(2,1)}, bf16[2,2,256,768]{3,2,1,0:T(8,128)(2,1)S(1)}, u32[]{:S(2)}, u32[]{:S(2)}) %collective-permute-start.5) | collective-permute-done | bytes 1572896 | tf_op jit(solution)/shard_map/ppermute | solution.py:28
  37.6 0.0 collective-permute-start.6
  37.6 0.0 collective-permute-done.2.late_ref
  37.6 0.0 collective-permute-done.4.refs_0_
  37.6 3.0 %shard_map.40 = (bf16[4,256,512]{2,1,0:T(8,128)(2,1)S(1)}, bf16[512,512]{1,0:T(8,128)(2,1)S(1)}, f32[2,256,256]{2,1,0:T(8,128)S(1)}, f32[2,256,256]{2,1,0:T(8,128)S(1)}) custom-call(s32[4,12]{1,0:T(4,128)S(1)} %copy-done.2, bf16[1,2,256,256]{3,2,1,0:T(8,128)(2,1)S(1)} %collective-permute-done.2.late_ref, ...), custom_call_target="tpu_custom_call", output_to_operand_aliasing={{0}: (2, {}), {2}: (6, {}), {3}: (7, {})} | custom-call | flops 161061280 | bytes 1048576 | tf_op jit(solution)/shard_map/pallas_call | solution.py:225
  40.6 0.4 collective-permute-done.1.refs_0_
  41.0 0.0 collective-permute-done.6.refs_0_
  41.0 2.3 %shard_map.42 = (f32[2,2,256,256]{3,2,1,0:T(8,128)}, bf16[4,256,512]{2,1,0:T(8,128)(2,1)S(1)}) custom-call(s32[4,12]{1,0:T(4,128)S(1)} %copy-done.2, bf16[1,2,256,256]{3,2,1,0:T(8,128)(2,1)S(1)} %shard_map.41.late_ref, bf16[4,256,512]{2,1,0:T(8,128)(2,1)S(1)} %get-tuple-element.26.first_window, ...), custom_call_target="tpu_custom_call", output_to_operand_aliasing={{1}: (3, {})} | custom-call | flops 1610612736 | bytes 1048576 | tf_op jit(solution)/shard_map/pallas_call | solution.py:235
  (4 shorter events, 0.0 us)
Async XLA Ops:
  0.0 29.6 %copy-start.1 = (bf16[2,2,256,768]{3,2,1,0:T(8,128)(2,1)S(1)}, bf16[2,2,256,768]{3,2,1,0:T(8,128)(2,1)}, u32[]{:S(2)}) copy-start(bf16[2,2,256,768]{3,2,1,0:T(8,128)(2,1)} %own_ref.1) | copy-start | bytes 4718596
  0.0 29.9 %copy-start = (bf16[2,2,256,256]{3,2,1,0:T(8,128)(2,1)S(1)}, bf16[2,2,256,256]{3,2,1,0:T(8,128)(2,1)}, u32[]{:S(2)}) copy-start(bf16[2,2,256,256]{3,2,1,0:T(8,128)(2,1)} %refs_3_.1) | copy-start | bytes 1572868
  0.0 29.9 %copy-start.2 = (s32[4,12]{1,0:T(4,128)S(1)}, s32[4,12]{1,0:T(4,128)}, u32[]{:S(2)}) copy-start(s32[4,12]{1,0:T(4,128)} %aperture_ref.5) | copy-start | bytes 580
  0.0 37.6 %collective-permute-start.5 = (bf16[2,2,256,768]{3,2,1,0:T(8,128)(2,1)}, bf16[2,2,256,768]{3,2,1,0:T(8,128)(2,1)S(1)}, u32[]{:S(2)}, u32[]{:S(2)}) collective-permute-start(bf16[2,2,256,768]{3,2,1,0:T(8,128)(2,1)} %own_ref.1), channel_id=1, source_target_pairs={{0,2},{1,3},{2,0},{3,1},{4,6},{5,7},{6,4},{7,5},{8,10},{9,11},{10,... | collective-permute-start | bytes 4718600 | tf_op jit(solution)/shard_map/ppermute | solution.py:28
  3.0 16.9 %collective-permute-start = (bf16[2,2,256,256]{3,2,1,0:T(8,128)(2,1)}, bf16[2,2,256,256]{3,2,1,0:T(8,128)(2,1)S(1)}, u32[]{:S(2)}, u32[]{:S(2)}) collective-permute-start(bf16[2,2,256,256]{3,2,1,0:T(8,128)(2,1)} %refs_3_.1), channel_id=1, source_target_pairs={{0,12},{4,8},{8,4},{12,0},{1,13},{5,9},{9,5},{13,1},{2,14},{6,10},... | collective-permute-start | bytes 1572872 | tf_op jit(solution)/shard_map/ppermute | solution.py:37
  6.6 23.3 %collective-permute-start.3 = (bf16[2,2,256,256]{3,2,1,0:T(8,128)(2,1)}, bf16[2,2,256,256]{3,2,1,0:T(8,128)(2,1)S(1)}, u32[]{:S(2)}, u32[]{:S(2)}) collective-permute-start(bf16[2,2,256,256]{3,2,1,0:T(8,128)(2,1)} %refs_3_.1), channel_id=1, source_target_pairs={{0,4},{4,0},{8,12},{12,8},{1,5},{5,1},{9,13},{13,9},{2,6},{6,2},{1... | collective-permute-start | bytes 1572872 | tf_op jit(solution)/shard_map/ppermute | solution.py:38
  20.0 17.7 %collective-permute-start.2 = (bf16[1,2,256,256]{3,2,1,0:T(8,128)(2,1)S(1)}, bf16[1,2,256,256]{3,2,1,0:T(8,128)(2,1)S(1)}, u32[]{:S(2)}, u32[]{:S(2)}) collective-permute-start(bf16[1,2,256,256]{3,2,1,0:T(8,128)(2,1)S(1)} %get-tuple-element.31), channel_id=1, source_target_pairs={{0,4},{4,0},{8,12},{12,8},{1,5},{5,1},{9,13},{13,9},{2,6},{6,2},{1... | collective-permute-start | bytes 786440 | tf_op jit(solution)/shard_map/ppermute | solution.py:41
  29.5 11.5 %collective-permute-start.1 = (bf16[1,2,256,256]{3,2,1,0:T(8,128)(2,1)S(1)}, bf16[1,2,256,256]{3,2,1,0:T(8,128)(2,1)S(1)}, u32[]{:S(2)}, u32[]{:S(2)}) collective-permute-start(bf16[1,2,256,256]{3,2,1,0:T(8,128)(2,1)S(1)} %get-tuple-element.32), channel_id=1, source_target_pairs={{0,4},{4,0},{8,12},{12,8},{1,5},{5,1},{9,13},{13,9},{2,6},{6,2},{1... | collective-permute-start | bytes 786440 | tf_op jit(solution)/shard_map/ppermute | solution.py:41
  29.6 8.0 %collective-permute-start.4 = (bf16[2,2,256,768]{3,2,1,0:T(8,128)(2,1)S(1)}, bf16[2,2,256,768]{3,2,1,0:T(8,128)(2,1)S(1)}, u32[]{:S(2)}, u32[]{:S(2)}) collective-permute-start(bf16[2,2,256,768]{3,2,1,0:T(8,128)(2,1)S(1)} %copy-done.1), channel_id=1, source_target_pairs={{0,1},{1,0},{2,3},{3,2},{4,5},{5,4},{6,7},{7,6},{8,9},{9,8},{10,11... | collective-permute-start | bytes 4718600 | tf_op jit(solution)/shard_map/ppermute | solution.py:28
  37.6 3.4 %collective-permute-start.6 = (bf16[2,2,256,768]{3,2,1,0:T(8,128)(2,1)S(1)}, bf16[2,2,256,768]{3,2,1,0:T(8,128)(2,1)S(1)}, u32[]{:S(2)}, u32[]{:S(2)}) collective-permute-start(bf16[2,2,256,768]{3,2,1,0:T(8,128)(2,1)S(1)} %shard_map.39.refs_1_), channel_id=1, source_target_pairs={{0,1},{1,0},{2,3},{3,2},{4,5},{5,4},{6,7},{7,6},{8,9},{9,8},{10,11... | collective-permute-start | bytes 4718600 | tf_op jit(solution)/shard_map/ppermute | solution.py:28

commit v24 on v22

--- a/solution.py
+++ b/solution.py
@@ -161,7 +161,7 @@
                 copies.append(
                     pltpu.make_async_copy(result.at[v, p, rows], out_ref.at[v, p, rows], sems.at[v, p, chunk])
                 )
-                copies[-1].start()
+                copies[-1].start(priority=v)
         return copies
 
     panels = [{far_half + m: ref.at[v] for m, ref in enumerate(panel_refs)} for v in range(2)]

time: 43.5 us -> 43.5 us (level)
  no operation moved by 1% of the time
where the time goes in v24:
time: 43.5 us; the launch traced here: 43.3 us
  waiting for transfers between devices  20.1 us (46%)
  starting transfers between devices  16.3 us (37%)
  Pallas kernels  6.86 us (16%)
    ppermute x1, waiting for transfers between devices, line_window(): far = held(lax.ppermute(data, 'src', [(0, 3), (1, 2), (2, 1), (3, 0)]), 5)  13.3 us
    ppermute x2, starting transfers between devices, line_window(): across = lax.ppermute(far[v:v + 1], 'src', near_pairs)  9.65 us
    ppermute x3, waiting for transfers between devices, swap(): return lax.ppermute(x, axis, [(i, i ^ bit) for i in range(peers)])  6.09 us
    ppermute x1, starting transfers between devices, line_window(): far = held(lax.ppermute(data, 'src', [(0, 3), (1, 2), (2, 1), (3, 0)]), 5)  3.6 us
    ppermute x3, starting transfers between devices, swap(): return lax.ppermute(x, axis, [(i, i ^ bit) for i in range(peers)])  3.01 us
    pallas_call x1, Pallas kernels, body(): pl.pallas_call(functools.partial(kernel_b, late), out_shape=[window, jax....  2.98 us
    pallas_call x1, Pallas kernels, body(): pl.pallas_call(functools.partial(last_kernel, half + 1, late), out_shape=...  2.26 us
    pallas_call x1, Pallas kernels, body(): pl.pallas_call(functools.partial(kernel_a, [{k: at for k, (_, at) in piec...  1.62 us
  transfers between devices with their start and end apart: 7, of which 4 were waited for; matrix products, arithmetic and copies ran while one was open for 0% of the time, Pallas kernels for 11%

profile of v24, /device:TPU:0, one launch (start us, length us, event | category | flops | bytes accessed | tf_op | source)
XLA Modules:
  0.0 43.3 jit_solution(8773735176485672334)
XLA Ops:
  0.0 0.0 copy-start.1
  0.0 0.0 copy-start
  0.0 0.0 copy-start.2
  0.0 3.0 %collective-permute-start.5 = (bf16[2,2,256,768]{3,2,1,0:T(8,128)(2,1)}, bf16[2,2,256,768]{3,2,1,0:T(8,128)(2,1)S(1)}, u32[]{:S(2)}, u32[]{:S(2)}) collective-permute-start(bf16[2,2,256,768]{3,2,1,0:T(8,128)(2,1)} %own_ref.1), channel_id=1, source_target_pairs={{0,2},{1,3},{2,0},{3,1},{4,6},{5,7},{6,4},{7,5},{8,10},{9,11},{10,... | collective-permute-start | bytes 4718600 | tf_op jit(solution)/shard_map/ppermute | solution.py:28
  3.0 3.6 %collective-permute-start = (bf16[2,2,256,256]{3,2,1,0:T(8,128)(2,1)}, bf16[2,2,256,256]{3,2,1,0:T(8,128)(2,1)S(1)}, u32[]{:S(2)}, u32[]{:S(2)}) collective-permute-start(bf16[2,2,256,256]{3,2,1,0:T(8,128)(2,1)} %refs_3_.1), channel_id=1, source_target_pairs={{0,12},{4,8},{8,4},{12,0},{1,13},{5,9},{9,5},{13,1},{2,14},{6,10},... | collective-permute-start | bytes 1572872 | tf_op jit(solution)/shard_map/ppermute | solution.py:37
  6.6 0.0 collective-permute-start.3
  6.6 13.3 %collective-permute-done.refs_0_ = bf16[2,2,256,256]{3,2,1,0:T(8,128)(2,1)S(1)} collective-permute-done((bf16[2,2,256,256]{3,2,1,0:T(8,128)(2,1)}, bf16[2,2,256,256]{3,2,1,0:T(8,128)(2,1)S(1)}, u32[]{:S(2)}, u32[]{:S(2)}) %collective-permute-start) | collective-permute-done | bytes 524320 | tf_op jit(solution)/shard_map/ppermute | solution.py:37
  20.0 9.6 %collective-permute-start.2 = (bf16[1,2,256,256]{3,2,1,0:T(8,128)(2,1)S(1)}, bf16[1,2,256,256]{3,2,1,0:T(8,128)(2,1)S(1)}, u32[]{:S(2)}, u32[]{:S(2)}) collective-permute-start(bf16[1,2,256,256]{3,2,1,0:T(8,128)(2,1)S(1)} %get-tuple-element.31), channel_id=1, source_target_pairs={{0,4},{4,0},{8,12},{12,8},{1,5},{5,1},{9,13},{13,9},{2,6},{6,2},{1... | collective-permute-start | bytes 786440 | tf_op jit(solution)/shard_map/ppermute | solution.py:41
  29.5 0.1 collective-permute-start.1
  29.6 0.0 copy-done.1
  29.6 0.0 collective-permute-start.4
  29.6 0.3 collective-permute-done.3.refs_1_.refs_4_
  29.9 0.0 copy-done
  29.9 0.0 copy-done.2
  29.9 1.6 %shard_map.38 = (bf16[4,256,512]{2,1,0:T(8,128)(2,1)S(1)}, bf16[4,256,512]{2,1,0:T(8,128)(2,1)S(1)}, f32[512,256]{1,0:T(8,128)S(1)}, f32[512,256]{1,0:T(8,128)S(...) custom-call(s32[4,12]{1,0:T(4,128)S(1)} %copy-done.2, bf16[2,2,256,768]{3,2,1,0:T(8,128)(2,1)S(1)} %copy-done.1, ...), custom_call_target="tpu_custom_call" | custom-call | flops 161061280 | bytes 1048576 | tf_op jit(solution)/shard_map/pallas_call | solution.py:214
  31.5 6.1 %collective-permute-done.5.refs_0_ = bf16[2,2,256,768]{3,2,1,0:T(8,128)(2,1)S(1)} collective-permute-done((bf16[2,2,256,768]{3,2,1,0:T(8,128)(2,1)}, bf16[2,2,256,768]{3,2,1,0:T(8,128)(2,1)S(1)}, u32[]{:S(2)}, u32[]{:S(2)}) %collective-permute-start.5) | collective-permute-done | bytes 1572896 | tf_op jit(solution)/shard_map/ppermute | solution.py:28
  37.6 0.0 collective-permute-start.6
  37.6 0.0 collective-permute-done.2.late_ref
  37.6 0.0 collective-permute-done.4.refs_0_
  37.6 3.0 %shard_map.40 = (bf16[4,256,512]{2,1,0:T(8,128)(2,1)S(1)}, bf16[512,512]{1,0:T(8,128)(2,1)S(1)}, f32[2,256,256]{2,1,0:T(8,128)S(1)}, f32[2,256,256]{2,1,0:T(8,128)S(1)}) custom-call(s32[4,12]{1,0:T(4,128)S(1)} %copy-done.2, bf16[1,2,256,256]{3,2,1,0:T(8,128)(2,1)S(1)} %collective-permute-done.2.late_ref, ...), custom_call_target="tpu_custom_call", output_to_operand_aliasing={{0}: (2, {}), {2}: (6, {}), {3}: (7, {})} | custom-call | flops 161061280 | bytes 1048576 | tf_op jit(solution)/shard_map/pallas_call | solution.py:225
  40.6 0.4 collective-permute-done.1.refs_0_
  41.0 0.0 collective-permute-done.6.refs_0_
  41.0 2.3 %shard_map.42 = (f32[2,2,256,256]{3,2,1,0:T(8,128)}, bf16[4,256,512]{2,1,0:T(8,128)(2,1)S(1)}) custom-call(s32[4,12]{1,0:T(4,128)S(1)} %copy-done.2, bf16[1,2,256,256]{3,2,1,0:T(8,128)(2,1)S(1)} %shard_map.41.late_ref, bf16[4,256,512]{2,1,0:T(8,128)(2,1)S(1)} %get-tuple-element.26.first_window, ...), custom_call_target="tpu_custom_call", output_to_operand_aliasing={{1}: (3, {})} | custom-call | flops 1610612736 | bytes 1048576 | tf_op jit(solution)/shard_map/pallas_call | solution.py:235
  (4 shorter events, 0.0 us)
Async XLA Ops:
  0.0 29.6 %copy-start.1 = (bf16[2,2,256,768]{3,2,1,0:T(8,128)(2,1)S(1)}, bf16[2,2,256,768]{3,2,1,0:T(8,128)(2,1)}, u32[]{:S(2)}) copy-start(bf16[2,2,256,768]{3,2,1,0:T(8,128)(2,1)} %own_ref.1) | copy-start | bytes 4718596
  0.0 29.9 %copy-start = (bf16[2,2,256,256]{3,2,1,0:T(8,128)(2,1)S(1)}, bf16[2,2,256,256]{3,2,1,0:T(8,128)(2,1)}, u32[]{:S(2)}) copy-start(bf16[2,2,256,256]{3,2,1,0:T(8,128)(2,1)} %refs_3_.1) | copy-start | bytes 1572868
  0.0 29.9 %copy-start.2 = (s32[4,12]{1,0:T(4,128)S(1)}, s32[4,12]{1,0:T(4,128)}, u32[]{:S(2)}) copy-start(s32[4,12]{1,0:T(4,128)} %aperture_ref.5) | copy-start | bytes 580
  0.0 37.6 %collective-permute-start.5 = (bf16[2,2,256,768]{3,2,1,0:T(8,128)(2,1)}, bf16[2,2,256,768]{3,2,1,0:T(8,128)(2,1)S(1)}, u32[]{:S(2)}, u32[]{:S(2)}) collective-permute-start(bf16[2,2,256,768]{3,2,1,0:T(8,128)(2,1)} %own_ref.1), channel_id=1, source_target_pairs={{0,2},{1,3},{2,0},{3,1},{4,6},{5,7},{6,4},{7,5},{8,10},{9,11},{10,... | collective-permute-start | bytes 4718600 | tf_op jit(solution)/shard_map/ppermute | solution.py:28
  3.0 16.9 %collective-permute-start = (bf16[2,2,256,256]{3,2,1,0:T(8,128)(2,1)}, bf16[2,2,256,256]{3,2,1,0:T(8,128)(2,1)S(1)}, u32[]{:S(2)}, u32[]{:S(2)}) collective-permute-start(bf16[2,2,256,256]{3,2,1,0:T(8,128)(2,1)} %refs_3_.1), channel_id=1, source_target_pairs={{0,12},{4,8},{8,4},{12,0},{1,13},{5,9},{9,5},{13,1},{2,14},{6,10},... | collective-permute-start | bytes 1572872 | tf_op jit(solution)/shard_map/ppermute | solution.py:37
  6.6 23.3 %collective-permute-start.3 = (bf16[2,2,256,256]{3,2,1,0:T(8,128)(2,1)}, bf16[2,2,256,256]{3,2,1,0:T(8,128)(2,1)S(1)}, u32[]{:S(2)}, u32[]{:S(2)}) collective-permute-start(bf16[2,2,256,256]{3,2,1,0:T(8,128)(2,1)} %refs_3_.1), channel_id=1, source_target_pairs={{0,4},{4,0},{8,12},{12,8},{1,5},{5,1},{9,13},{13,9},{2,6},{6,2},{1... | collective-permute-start | bytes 1572872 | tf_op jit(solution)/shard_map/ppermute | solution.py:38
  20.0 17.7 %collective-permute-start.2 = (bf16[1,2,256,256]{3,2,1,0:T(8,128)(2,1)S(1)}, bf16[1,2,256,256]{3,2,1,0:T(8,128)(2,1)S(1)}, u32[]{:S(2)}, u32[]{:S(2)}) collective-permute-start(bf16[1,2,256,256]{3,2,1,0:T(8,128)(2,1)S(1)} %get-tuple-element.31), channel_id=1, source_target_pairs={{0,4},{4,0},{8,12},{12,8},{1,5},{5,1},{9,13},{13,9},{2,6},{6,2},{1... | collective-permute-start | bytes 786440 | tf_op jit(solution)/shard_map/ppermute | solution.py:41
  29.5 11.5 %collective-permute-start.1 = (bf16[1,2,256,256]{3,2,1,0:T(8,128)(2,1)S(1)}, bf16[1,2,256,256]{3,2,1,0:T(8,128)(2,1)S(1)}, u32[]{:S(2)}, u32[]{:S(2)}) collective-permute-start(bf16[1,2,256,256]{3,2,1,0:T(8,128)(2,1)S(1)} %get-tuple-element.32), channel_id=1, source_target_pairs={{0,4},{4,0},{8,12},{12,8},{1,5},{5,1},{9,13},{13,9},{2,6},{6,2},{1... | collective-permute-start | bytes 786440 | tf_op jit(solution)/shard_map/ppermute | solution.py:41
  29.6 8.0 %collective-permute-start.4 = (bf16[2,2,256,768]{3,2,1,0:T(8,128)(2,1)S(1)}, bf16[2,2,256,768]{3,2,1,0:T(8,128)(2,1)S(1)}, u32[]{:S(2)}, u32[]{:S(2)}) collective-permute-start(bf16[2,2,256,768]{3,2,1,0:T(8,128)(2,1)S(1)} %copy-done.1), channel_id=1, source_target_pairs={{0,1},{1,0},{2,3},{3,2},{4,5},{5,4},{6,7},{7,6},{8,9},{9,8},{10,11... | collective-permute-start | bytes 4718600 | tf_op jit(solution)/shard_map/ppermute | solution.py:28
  37.6 3.4 %collective-permute-start.6 = (bf16[2,2,256,768]{3,2,1,0:T(8,128)(2,1)S(1)}, bf16[2,2,256,768]{3,2,1,0:T(8,128)(2,1)S(1)}, u32[]{:S(2)}, u32[]{:S(2)}) collective-permute-start(bf16[2,2,256,768]{3,2,1,0:T(8,128)(2,1)S(1)} %shard_map.39.refs_1_), channel_id=1, source_target_pairs={{0,1},{1,0},{2,3},{3,2},{4,5},{5,4},{6,7},{7,6},{8,9},{9,8},{10,11... | collective-permute-start | bytes 4718600 | tf_op jit(solution)/shard_map/ppermute | solution.py:28

commit v25 on v22

--- a/solution.py
+++ b/solution.py
@@ -34,12 +34,12 @@
 
 def line_window(data):
     near_pairs = [(0, 1), (1, 0), (2, 3), (3, 2)]
-    far = held(lax.ppermute(data, "src", [(0, 3), (1, 2), (2, 1), (3, 0)]), 5)
+    far = held(lax.ppermute(data, "src", [(0, 2), (1, 3), (2, 0), (3, 1)]), 5)
     near = lax.ppermute(data, "src", near_pairs)
     windows = []
     for v in range(data.shape[0]):
         across = lax.ppermute(far[v : v + 1], "src", near_pairs)
-        windows.append([(data, v), (near, v), (across, 0), (far, v)])
+        windows.append([(data, v), (near, v), (far, v), (across, 0)])
     return windows
 
 
@@ -200,9 +200,9 @@
     width = data.shape[3]
     line = lax.axis_size("src") == 4
     windows = (line_window if line else hop_window)(data)
-    panels, far_panel = gather_panels(primaries, windows[0][-1][0])
+    panels, far_panel = gather_panels(primaries, windows[0][-2][0])
     half = len(panels)
-    late = 2 if line else len(windows[0]) - 1
+    late = len(windows[0]) - 1
     late_pieces = [piece[at : at + 1] for piece, at in (window[late] for window in windows)]
     early = [{k: piece for k, piece in enumerate(window) if k != late} for window in windows]
     vmem, anywhere = spec(pltpu.VMEM), spec(pl.ANY)

time: 43.5 us -> 44.1 us (1.014)
  waiting for transfers between devices: 20.1 us -> 27.8 us
  starting transfers between devices: 16.3 us -> 9.27 us
    ppermute x1, waiting for transfers between devices: 13.3 us -> 21.7 us  [line_window(): far = held(lax.ppermute(data, 'src', [(0, 2), (1, 3), (2, 0), (3, 1)]), 5)]
    ppermute x2, starting transfers between devices: 9.65 us -> 2.09 us  [line_window(): across = lax.ppermute(far[v:v + 1], 'src', near_pairs)]
    ppermute x1, starting transfers between devices: 0.01 us -> 1.58 us  [line_window(): near = lax.ppermute(data, 'src', near_pairs)]
    ppermute x3, waiting for transfers between devices: 6.09 us -> 4.99 us  [swap(): return lax.ppermute(x, axis, [(i, i ^ bit) for i in range(peers)])]
    ppermute x1, starting transfers between devices: 3.6 us -> 2.59 us  [line_window(): far = held(lax.ppermute(data, 'src', [(0, 2), (1, 3), (2, 0), (3, 1)]), 5)]
    ppermute x2, waiting for transfers between devices: 0.43 us -> 1.12 us  [line_window(): across = lax.ppermute(far[v:v + 1], 'src', near_pairs)]
  transfers between devices with their start and end apart: 7 -> 7, of which waited for: 4 -> 4; matrix products, arithmetic and copies ran while one was open for 0% -> 0% of each run, Pallas kernels for 11% -> 10%
where the time goes in v25:
time: 44.1 us; the launch traced here: 44 us
  waiting for transfers between devices  27.8 us (63%)
  starting transfers between devices  9.27 us (21%)
  Pallas kernels  6.86 us (16%)
    ppermute x1, waiting for transfers between devices, line_window(): far = held(lax.ppermute(data, 'src', [(0, 2), (1, 3), (2, 0), (3, 1)]), 5)  21.7 us
    ppermute x3, waiting for transfers between devices, swap(): return lax.ppermute(x, axis, [(i, i ^ bit) for i in range(peers)])  4.99 us
    ppermute x3, starting transfers between devices, swap(): return lax.ppermute(x, axis, [(i, i ^ bit) for i in range(peers)])  3.01 us
    pallas_call x1, Pallas kernels, body(): pl.pallas_call(functools.partial(kernel_b, late), out_shape=[window, jax....  2.98 us
    ppermute x1, starting transfers between devices, line_window(): far = held(lax.ppermute(data, 'src', [(0, 2), (1, 3), (2, 0), (3, 1)]), 5)  2.59 us
    pallas_call x1, Pallas kernels, body(): pl.pallas_call(functools.partial(last_kernel, half + 1, late), out_shape=...  2.26 us
    ppermute x2, starting transfers between devices, line_window(): across = lax.ppermute(far[v:v + 1], 'src', near_pairs)  2.09 us
    pallas_call x1, Pallas kernels, body(): pl.pallas_call(functools.partial(kernel_a, [{k: at for k, (_, at) in piec...  1.62 us
  transfers between devices with their start and end apart: 7, of which 4 were waited for; matrix products, arithmetic and copies ran while one was open for 0% of the time, Pallas kernels for 10%

profile of v25, /device:TPU:0, one launch (start us, length us, event | category | flops | bytes accessed | tf_op | source)
XLA Modules:
  0.0 44.0 jit_solution(10414267023364561937)
XLA Ops:
  0.0 0.0 copy-start.1
  0.0 0.0 copy-start
  0.0 0.0 copy-start.2
  0.0 3.0 %collective-permute-start.5 = (bf16[2,2,256,768]{3,2,1,0:T(8,128)(2,1)}, bf16[2,2,256,768]{3,2,1,0:T(8,128)(2,1)S(1)}, u32[]{:S(2)}, u32[]{:S(2)}) collective-permute-start(bf16[2,2,256,768]{3,2,1,0:T(8,128)(2,1)} %own_ref.1), channel_id=1, source_target_pairs={{0,2},{1,3},{2,0},{3,1},{4,6},{5,7},{6,4},{7,5},{8,10},{9,11},{10,... | collective-permute-start | bytes 4718600 | tf_op jit(solution)/shard_map/ppermute | solution.py:28
  3.0 2.6 %collective-permute-start = (bf16[2,2,256,256]{3,2,1,0:T(8,128)(2,1)}, bf16[2,2,256,256]{3,2,1,0:T(8,128)(2,1)S(1)}, u32[]{:S(2)}, u32[]{:S(2)}) collective-permute-start(bf16[2,2,256,256]{3,2,1,0:T(8,128)(2,1)} %refs_3_.1), channel_id=1, source_target_pairs={{0,8},{4,12},{8,0},{12,4},{1,9},{5,13},{9,1},{13,5},{2,10},{6,14},... | collective-permute-start | bytes 1572872 | tf_op jit(solution)/shard_map/ppermute | solution.py:37
  5.6 1.6 %collective-permute-start.3 = (bf16[2,2,256,256]{3,2,1,0:T(8,128)(2,1)}, bf16[2,2,256,256]{3,2,1,0:T(8,128)(2,1)S(1)}, u32[]{:S(2)}, u32[]{:S(2)}) collective-permute-start(bf16[2,2,256,256]{3,2,1,0:T(8,128)(2,1)} %refs_3_.1), channel_id=1, source_target_pairs={{0,4},{4,0},{8,12},{12,8},{1,5},{5,1},{9,13},{13,9},{2,6},{6,2},{1... | collective-permute-start | bytes 1572872 | tf_op jit(solution)/shard_map/ppermute | solution.py:38
  7.2 21.7 %collective-permute-done.refs_0_ = bf16[2,2,256,256]{3,2,1,0:T(8,128)(2,1)S(1)} collective-permute-done((bf16[2,2,256,256]{3,2,1,0:T(8,128)(2,1)}, bf16[2,2,256,256]{3,2,1,0:T(8,128)(2,1)S(1)}, u32[]{:S(2)}, u32[]{:S(2)}) %collective-permute-start) | collective-permute-done | bytes 524320 | tf_op jit(solution)/shard_map/ppermute | solution.py:37
  28.9 0.7 %collective-permute-start.2 = (bf16[1,2,256,256]{3,2,1,0:T(8,128)(2,1)S(1)}, bf16[1,2,256,256]{3,2,1,0:T(8,128)(2,1)S(1)}, u32[]{:S(2)}, u32[]{:S(2)}) collective-permute-start(bf16[1,2,256,256]{3,2,1,0:T(8,128)(2,1)S(1)} %get-tuple-element.31), channel_id=1, source_target_pairs={{0,4},{4,0},{8,12},{12,8},{1,5},{5,1},{9,13},{13,9},{2,6},{6,2},{1... | collective-permute-start | bytes 786440 | tf_op jit(solution)/shard_map/ppermute | solution.py:41
  29.6 1.4 %collective-permute-start.1 = (bf16[1,2,256,256]{3,2,1,0:T(8,128)(2,1)S(1)}, bf16[1,2,256,256]{3,2,1,0:T(8,128)(2,1)S(1)}, u32[]{:S(2)}, u32[]{:S(2)}) collective-permute-start(bf16[1,2,256,256]{3,2,1,0:T(8,128)(2,1)S(1)} %get-tuple-element.32), channel_id=1, source_target_pairs={{0,4},{4,0},{8,12},{12,8},{1,5},{5,1},{9,13},{13,9},{2,6},{6,2},{1... | collective-permute-start | bytes 786440 | tf_op jit(solution)/shard_map/ppermute | solution.py:41
  31.0 0.0 copy-done.1
  31.0 0.0 collective-permute-start.4
  31.0 0.0 collective-permute-done.3.refs_1_.refs_4_
  31.0 0.0 copy-done
  31.0 0.0 copy-done.2
  31.0 1.6 %shard_map.38 = (bf16[4,256,512]{2,1,0:T(8,128)(2,1)S(1)}, bf16[4,256,512]{2,1,0:T(8,128)(2,1)S(1)}, f32[512,256]{1,0:T(8,128)S(1)}, f32[512,256]{1,0:T(8,128)S(...) custom-call(s32[4,12]{1,0:T(4,128)S(1)} %copy-done.2, bf16[2,2,256,768]{3,2,1,0:T(8,128)(2,1)S(1)} %copy-done.1, ...), custom_call_target="tpu_custom_call" | custom-call | flops 161061280 | bytes 1048576 | tf_op jit(solution)/shard_map/pallas_call | solution.py:214
  32.6 5.0 %collective-permute-done.5.refs_0_ = bf16[2,2,256,768]{3,2,1,0:T(8,128)(2,1)S(1)} collective-permute-done((bf16[2,2,256,768]{3,2,1,0:T(8,128)(2,1)}, bf16[2,2,256,768]{3,2,1,0:T(8,128)(2,1)S(1)}, u32[]{:S(2)}, u32[]{:S(2)}) %collective-permute-start.5) | collective-permute-done | bytes 1572896 | tf_op jit(solution)/shard_map/ppermute | solution.py:28
  37.6 0.0 collective-permute-start.6
  37.6 0.6 %collective-permute-done.2.late_ref = bf16[1,2,256,256]{3,2,1,0:T(8,128)(2,1)S(1)} collective-permute-done((bf16[1,2,256,256]{3,2,1,0:T(8,128)(2,1)S(1)}, bf16[1,2,256,256]{3,2,1,0:T(8,128)(2,1)S(1)}, u32[]{:S(2)}, u32[]{:S(2)}) %collective-permute-start.2) | collective-permute-done | bytes 262176 | tf_op jit(solution)/shard_map/ppermute | solution.py:41
  38.2 0.0 collective-permute-done.4.refs_0_
  38.2 3.0 %shard_map.40 = (bf16[4,256,512]{2,1,0:T(8,128)(2,1)S(1)}, bf16[512,512]{1,0:T(8,128)(2,1)S(1)}, f32[2,256,256]{2,1,0:T(8,128)S(1)}, f32[2,256,256]{2,1,0:T(8,128)S(1)}) custom-call(s32[4,12]{1,0:T(4,128)S(1)} %copy-done.2, bf16[1,2,256,256]{3,2,1,0:T(8,128)(2,1)S(1)} %collective-permute-done.2.late_ref, ...), custom_call_target="tpu_custom_call", output_to_operand_aliasing={{0}: (2, {}), {2}: (6, {}), {3}: (7, {})} | custom-call | flops 161061280 | bytes 1048576 | tf_op jit(solution)/shard_map/pallas_call | solution.py:225
  41.2 0.6 %collective-permute-done.1.refs_0_ = bf16[1,2,256,256]{3,2,1,0:T(8,128)(2,1)S(1)} collective-permute-done((bf16[1,2,256,256]{3,2,1,0:T(8,128)(2,1)S(1)}, bf16[1,2,256,256]{3,2,1,0:T(8,128)(2,1)S(1)}, u32[]{:S(2)}, u32[]{:S(2)}) %collective-permute-start.1) | collective-permute-done | bytes 262176 | tf_op jit(solution)/shard_map/ppermute | solution.py:41
  41.7 0.0 collective-permute-done.6.refs_0_
  41.7 2.3 %shard_map.42 = (f32[2,2,256,256]{3,2,1,0:T(8,128)}, bf16[4,256,512]{2,1,0:T(8,128)(2,1)S(1)}) custom-call(s32[4,12]{1,0:T(4,128)S(1)} %copy-done.2, bf16[1,2,256,256]{3,2,1,0:T(8,128)(2,1)S(1)} %shard_map.41.late_ref, bf16[4,256,512]{2,1,0:T(8,128)(2,1)S(1)} %get-tuple-element.26.first_window, ...), custom_call_target="tpu_custom_call", output_to_operand_aliasing={{1}: (3, {})} | custom-call | flops 1610612736 | bytes 1048576 | tf_op jit(solution)/shard_map/pallas_call | solution.py:235
  (4 shorter events, 0.0 us)
Async XLA Ops:
  0.0 31.0 %copy-start.1 = (bf16[2,2,256,768]{3,2,1,0:T(8,128)(2,1)S(1)}, bf16[2,2,256,768]{3,2,1,0:T(8,128)(2,1)}, u32[]{:S(2)}) copy-start(bf16[2,2,256,768]{3,2,1,0:T(8,128)(2,1)} %own_ref.1) | copy-start | bytes 4718596
  0.0 31.0 %copy-start = (bf16[2,2,256,256]{3,2,1,0:T(8,128)(2,1)S(1)}, bf16[2,2,256,256]{3,2,1,0:T(8,128)(2,1)}, u32[]{:S(2)}) copy-start(bf16[2,2,256,256]{3,2,1,0:T(8,128)(2,1)} %refs_3_.1) | copy-start | bytes 1572868
  0.0 31.0 %copy-start.2 = (s32[4,12]{1,0:T(4,128)S(1)}, s32[4,12]{1,0:T(4,128)}, u32[]{:S(2)}) copy-start(s32[4,12]{1,0:T(4,128)} %aperture_ref.5) | copy-start | bytes 580
  0.0 37.6 %collective-permute-start.5 = (bf16[2,2,256,768]{3,2,1,0:T(8,128)(2,1)}, bf16[2,2,256,768]{3,2,1,0:T(8,128)(2,1)S(1)}, u32[]{:S(2)}, u32[]{:S(2)}) collective-permute-start(bf16[2,2,256,768]{3,2,1,0:T(8,128)(2,1)} %own_ref.1), channel_id=1, source_target_pairs={{0,2},{1,3},{2,0},{3,1},{4,6},{5,7},{6,4},{7,5},{8,10},{9,11},{10,... | collective-permute-start | bytes 4718600 | tf_op jit(solution)/shard_map/ppermute | solution.py:28
  3.0 25.8 %collective-permute-start = (bf16[2,2,256,256]{3,2,1,0:T(8,128)(2,1)}, bf16[2,2,256,256]{3,2,1,0:T(8,128)(2,1)S(1)}, u32[]{:S(2)}, u32[]{:S(2)}) collective-permute-start(bf16[2,2,256,256]{3,2,1,0:T(8,128)(2,1)} %refs_3_.1), channel_id=1, source_target_pairs={{0,8},{4,12},{8,0},{12,4},{1,9},{5,13},{9,1},{13,5},{2,10},{6,14},... | collective-permute-start | bytes 1572872 | tf_op jit(solution)/shard_map/ppermute | solution.py:37
  5.6 25.4 %collective-permute-start.3 = (bf16[2,2,256,256]{3,2,1,0:T(8,128)(2,1)}, bf16[2,2,256,256]{3,2,1,0:T(8,128)(2,1)S(1)}, u32[]{:S(2)}, u32[]{:S(2)}) collective-permute-start(bf16[2,2,256,256]{3,2,1,0:T(8,128)(2,1)} %refs_3_.1), channel_id=1, source_target_pairs={{0,4},{4,0},{8,12},{12,8},{1,5},{5,1},{9,13},{13,9},{2,6},{6,2},{1... | collective-permute-start | bytes 1572872 | tf_op jit(solution)/shard_map/ppermute | solution.py:38
  28.9 9.3 %collective-permute-start.2 = (bf16[1,2,256,256]{3,2,1,0:T(8,128)(2,1)S(1)}, bf16[1,2,256,256]{3,2,1,0:T(8,128)(2,1)S(1)}, u32[]{:S(2)}, u32[]{:S(2)}) collective-permute-start(bf16[1,2,256,256]{3,2,1,0:T(8,128)(2,1)S(1)} %get-tuple-element.31), channel_id=1, source_target_pairs={{0,4},{4,0},{8,12},{12,8},{1,5},{5,1},{9,13},{13,9},{2,6},{6,2},{1... | collective-permute-start | bytes 786440 | tf_op jit(solution)/shard_map/ppermute | solution.py:41
  29.6 12.1 %collective-permute-start.1 = (bf16[1,2,256,256]{3,2,1,0:T(8,128)(2,1)S(1)}, bf16[1,2,256,256]{3,2,1,0:T(8,128)(2,1)S(1)}, u32[]{:S(2)}, u32[]{:S(2)}) collective-permute-start(bf16[1,2,256,256]{3,2,1,0:T(8,128)(2,1)S(1)} %get-tuple-element.32), channel_id=1, source_target_pairs={{0,4},{4,0},{8,12},{12,8},{1,5},{5,1},{9,13},{13,9},{2,6},{6,2},{1... | collective-permute-start | bytes 786440 | tf_op jit(solution)/shard_map/ppermute | solution.py:41
  31.0 7.2 %collective-permute-start.4 = (bf16[2,2,256,768]{3,2,1,0:T(8,128)(2,1)S(1)}, bf16[2,2,256,768]{3,2,1,0:T(8,128)(2,1)S(1)}, u32[]{:S(2)}, u32[]{:S(2)}) collective-permute-start(bf16[2,2,256,768]{3,2,1,0:T(8,128)(2,1)S(1)} %copy-done.1), channel_id=1, source_target_pairs={{0,1},{1,0},{2,3},{3,2},{4,5},{5,4},{6,7},{7,6},{8,9},{9,8},{10,11... | collective-permute-start | bytes 4718600 | tf_op jit(solution)/shard_map/ppermute | solution.py:28
  37.6 4.1 %collective-permute-start.6 = (bf16[2,2,256,768]{3,2,1,0:T(8,128)(2,1)S(1)}, bf16[2,2,256,768]{3,2,1,0:T(8,128)(2,1)S(1)}, u32[]{:S(2)}, u32[]{:S(2)}) collective-permute-start(bf16[2,2,256,768]{3,2,1,0:T(8,128)(2,1)S(1)} %shard_map.39.refs_1_), channel_id=1, source_target_pairs={{0,1},{1,0},{2,3},{3,2},{4,5},{5,4},{6,7},{7,6},{8,9},{9,8},{10,11... | collective-permute-start | bytes 4718600 | tf_op jit(solution)/shard_map/ppermute | solution.py:28

commit v26 on v25

--- a/solution.py
+++ b/solution.py
@@ -34,8 +34,10 @@
 
 def line_window(data):
     near_pairs = [(0, 1), (1, 0), (2, 3), (3, 2)]
-    far = held(lax.ppermute(data, "src", [(0, 2), (1, 3), (2, 0), (3, 1)]), 5)
     near = lax.ppermute(data, "src", near_pairs)
+    far = lax.ppermute(data, "src", [(0, 2), (1, 3), (2, 0), (3, 1)])
+    near, far = lax.optimization_barrier((near, far))
+    far = held(far, 5)
     windows = []
     for v in range(data.shape[0]):
         across = lax.ppermute(far[v : v + 1], "src", near_pairs)

time: 44.1 us -> 44 us (level)
    ppermute x1, waiting for transfers between devices: 0.01 us -> 20.5 us  [line_window(): near = lax.ppermute(data, 'src', near_pairs)]
    ppermute x1, waiting for transfers between devices: 21.7 us -> 2.39 us  [line_window(): far = lax.ppermute(data, 'src', [(0, 2), (1, 3), (2, 0), (3, 1)])]
    ppermute x3, waiting for transfers between devices: 4.99 us -> 3.74 us  [swap(): return lax.ppermute(x, axis, [(i, i ^ bit) for i in range(peers)])]
  transfers between devices with their start and end apart: 7 -> 7, of which waited for: 4 -> 4; matrix products, arithmetic and copies ran while one was open for 0% -> 0% of each run, Pallas kernels for 10% -> 11%
where the time goes in v26:
time: 44 us; the launch traced here: 43.8 us
  waiting for transfers between devices  27.6 us (63%)
  starting transfers between devices  9.27 us (21%)
  Pallas kernels  6.86 us (16%)
    ppermute x1, waiting for transfers between devices, line_window(): near = lax.ppermute(data, 'src', near_pairs)  20.5 us
    ppermute x3, waiting for transfers between devices, swap(): return lax.ppermute(x, axis, [(i, i ^ bit) for i in range(peers)])  3.74 us
    ppermute x3, starting transfers between devices, swap(): return lax.ppermute(x, axis, [(i, i ^ bit) for i in range(peers)])  3.01 us
    pallas_call x1, Pallas kernels, body(): pl.pallas_call(functools.partial(kernel_b, late), out_shape=[window, jax....  2.98 us
    ppermute x1, starting transfers between devices, line_window(): far = lax.ppermute(data, 'src', [(0, 2), (1, 3), (2, 0), (3, 1)])  2.59 us
    ppermute x1, waiting for transfers between devices, line_window(): far = lax.ppermute(data, 'src', [(0, 2), (1, 3), (2, 0), (3, 1)])  2.39 us
    pallas_call x1, Pallas kernels, body(): pl.pallas_call(functools.partial(last_kernel, half + 1, late), out_shape=...  2.26 us
    ppermute x2, starting transfers between devices, line_window(): across = lax.ppermute(far[v:v + 1], 'src', near_pairs)  2.09 us
  transfers between devices with their start and end apart: 7, of which 4 were waited for; matrix products, arithmetic and copies ran while one was open for 0% of the time, Pallas kernels for 11%

profile of v26, /device:TPU:0, one launch (start us, length us, event | category | flops | bytes accessed | tf_op | source)
XLA Modules:
  0.0 43.8 jit_solution(2296162136540744307)
XLA Ops:
  0.0 0.0 copy-start.1
  0.0 0.0 copy-start
  0.0 0.0 copy-start.2
  0.0 3.0 %collective-permute-start.5 = (bf16[2,2,256,768]{3,2,1,0:T(8,128)(2,1)}, bf16[2,2,256,768]{3,2,1,0:T(8,128)(2,1)S(1)}, u32[]{:S(2)}, u32[]{:S(2)}) collective-permute-start(bf16[2,2,256,768]{3,2,1,0:T(8,128)(2,1)} %own_ref.1), channel_id=1, source_target_pairs={{0,2},{1,3},{2,0},{3,1},{4,6},{5,7},{6,4},{7,5},{8,10},{9,11},{10,... | collective-permute-start | bytes 4718600 | tf_op jit(solution)/shard_map/ppermute | solution.py:28
  3.0 1.6 %collective-permute-start = (bf16[2,2,256,256]{3,2,1,0:T(8,128)(2,1)}, bf16[2,2,256,256]{3,2,1,0:T(8,128)(2,1)S(1)}, u32[]{:S(2)}, u32[]{:S(2)}) collective-permute-start(bf16[2,2,256,256]{3,2,1,0:T(8,128)(2,1)} %refs_3_.1), channel_id=1, source_target_pairs={{0,4},{4,0},{8,12},{12,8},{1,5},{5,1},{9,13},{13,9},{2,6},{6,2},{1... | collective-permute-start | bytes 1572872 | tf_op jit(solution)/shard_map/ppermute | solution.py:37
  4.6 2.6 %collective-permute-start.1 = (bf16[2,2,256,256]{3,2,1,0:T(8,128)(2,1)}, bf16[2,2,256,256]{3,2,1,0:T(8,128)(2,1)S(1)}, u32[]{:S(2)}, u32[]{:S(2)}) collective-permute-start(bf16[2,2,256,256]{3,2,1,0:T(8,128)(2,1)} %refs_3_.1), channel_id=1, source_target_pairs={{0,8},{4,12},{8,0},{12,4},{1,9},{5,13},{9,1},{13,5},{2,10},{6,14},... | collective-permute-start | bytes 1572872 | tf_op jit(solution)/shard_map/ppermute | solution.py:38
  7.2 20.5 %collective-permute-done.refs_1_.refs_4_ = bf16[2,2,256,256]{3,2,1,0:T(8,128)(2,1)S(1)} collective-permute-done((bf16[2,2,256,256]{3,2,1,0:T(8,128)(2,1)}, bf16[2,2,256,256]{3,2,1,0:T(8,128)(2,1)S(1)}, u32[]{:S(2)}, u32[]{:S(2)}) %collective-permute-start) | collective-permute-done | bytes 524320 | tf_op jit(solution)/shard_map/ppermute | solution.py:37
  27.7 2.4 %collective-permute-done.1.refs_0_ = bf16[2,2,256,256]{3,2,1,0:T(8,128)(2,1)S(1)} collective-permute-done((bf16[2,2,256,256]{3,2,1,0:T(8,128)(2,1)}, bf16[2,2,256,256]{3,2,1,0:T(8,128)(2,1)S(1)}, u32[]{:S(2)}, u32[]{:S(2)}) %collective-permute-start.1) | collective-permute-done | bytes 524320 | tf_op jit(solution)/shard_map/ppermute | solution.py:38
  30.1 0.5 %collective-permute-start.3 = (bf16[1,2,256,256]{3,2,1,0:T(8,128)(2,1)S(1)}, bf16[1,2,256,256]{3,2,1,0:T(8,128)(2,1)S(1)}, u32[]{:S(2)}, u32[]{:S(2)}) collective-permute-start(bf16[1,2,256,256]{3,2,1,0:T(8,128)(2,1)S(1)} %get-tuple-element.35), channel_id=1, source_target_pairs={{0,4},{4,0},{8,12},{12,8},{1,5},{5,1},{9,13},{13,9},{2,6},{6,2},{1... | collective-permute-start | bytes 786440 | tf_op jit(solution)/shard_map/ppermute | solution.py:43
  30.6 1.6 %collective-permute-start.2 = (bf16[1,2,256,256]{3,2,1,0:T(8,128)(2,1)S(1)}, bf16[1,2,256,256]{3,2,1,0:T(8,128)(2,1)S(1)}, u32[]{:S(2)}, u32[]{:S(2)}) collective-permute-start(bf16[1,2,256,256]{3,2,1,0:T(8,128)(2,1)S(1)} %get-tuple-element.36), channel_id=1, source_target_pairs={{0,4},{4,0},{8,12},{12,8},{1,5},{5,1},{9,13},{13,9},{2,6},{6,2},{1... | collective-permute-start | bytes 786440 | tf_op jit(solution)/shard_map/ppermute | solution.py:43
  32.2 0.0 copy-done.1
  32.2 0.0 collective-permute-start.4
  32.2 0.0 copy-done
  32.2 0.0 copy-done.2
  32.3 1.6 %shard_map.38 = (bf16[4,256,512]{2,1,0:T(8,128)(2,1)S(1)}, bf16[4,256,512]{2,1,0:T(8,128)(2,1)S(1)}, f32[512,256]{1,0:T(8,128)S(1)}, f32[512,256]{1,0:T(8,128)S(...) custom-call(s32[4,12]{1,0:T(4,128)S(1)} %copy-done.2, bf16[2,2,256,768]{3,2,1,0:T(8,128)(2,1)S(1)} %copy-done.1, ...), custom_call_target="tpu_custom_call" | custom-call | flops 161061280 | bytes 1048576 | tf_op jit(solution)/shard_map/pallas_call | solution.py:216
  33.9 3.7 %collective-permute-done.5.refs_0_ = bf16[2,2,256,768]{3,2,1,0:T(8,128)(2,1)S(1)} collective-permute-done((bf16[2,2,256,768]{3,2,1,0:T(8,128)(2,1)}, bf16[2,2,256,768]{3,2,1,0:T(8,128)(2,1)S(1)}, u32[]{:S(2)}, u32[]{:S(2)}) %collective-permute-start.5) | collective-permute-done | bytes 1572896 | tf_op jit(solution)/shard_map/ppermute | solution.py:28
  37.6 0.0 collective-permute-start.6
  37.6 0.9 %collective-permute-done.3.late_ref = bf16[1,2,256,256]{3,2,1,0:T(8,128)(2,1)S(1)} collective-permute-done((bf16[1,2,256,256]{3,2,1,0:T(8,128)(2,1)S(1)}, bf16[1,2,256,256]{3,2,1,0:T(8,128)(2,1)S(1)}, u32[]{:S(2)}, u32[]{:S(2)}) %collective-permute-start.3) | collective-permute-done | bytes 262176 | tf_op jit(solution)/shard_map/ppermute | solution.py:43
  38.5 0.0 collective-permute-done.4.refs_0_
  38.5 3.0 %shard_map.40 = (bf16[4,256,512]{2,1,0:T(8,128)(2,1)S(1)}, bf16[512,512]{1,0:T(8,128)(2,1)S(1)}, f32[2,256,256]{2,1,0:T(8,128)S(1)}, f32[2,256,256]{2,1,0:T(8,128)S(1)}) custom-call(s32[4,12]{1,0:T(4,128)S(1)} %copy-done.2, bf16[1,2,256,256]{3,2,1,0:T(8,128)(2,1)S(1)} %collective-permute-done.3.late_ref, ...), custom_call_target="tpu_custom_call", output_to_operand_aliasing={{0}: (2, {}), {2}: (6, {}), {3}: (7, {})} | custom-call | flops 161061280 | bytes 1048576 | tf_op jit(solution)/shard_map/pallas_call | solution.py:227
  41.5 0.0 collective-permute-done.2.refs_0_
  41.5 0.0 collective-permute-done.6.refs_0_
  41.5 2.3 %shard_map.42 = (f32[2,2,256,256]{3,2,1,0:T(8,128)}, bf16[4,256,512]{2,1,0:T(8,128)(2,1)S(1)}) custom-call(s32[4,12]{1,0:T(4,128)S(1)} %copy-done.2, bf16[1,2,256,256]{3,2,1,0:T(8,128)(2,1)S(1)} %shard_map.41.late_ref, bf16[4,256,512]{2,1,0:T(8,128)(2,1)S(1)} %get-tuple-element.30.first_window, ...), custom_call_target="tpu_custom_call", output_to_operand_aliasing={{1}: (3, {})} | custom-call | flops 1610612736 | bytes 1048576 | tf_op jit(solution)/shard_map/pallas_call | solution.py:237
  (4 shorter events, 0.0 us)
Async XLA Ops:
  0.0 32.2 %copy-start.1 = (bf16[2,2,256,768]{3,2,1,0:T(8,128)(2,1)S(1)}, bf16[2,2,256,768]{3,2,1,0:T(8,128)(2,1)}, u32[]{:S(2)}) copy-start(bf16[2,2,256,768]{3,2,1,0:T(8,128)(2,1)} %own_ref.1) | copy-start | bytes 4718596
  0.0 32.2 %copy-start = (bf16[2,2,256,256]{3,2,1,0:T(8,128)(2,1)S(1)}, bf16[2,2,256,256]{3,2,1,0:T(8,128)(2,1)}, u32[]{:S(2)}) copy-start(bf16[2,2,256,256]{3,2,1,0:T(8,128)(2,1)} %refs_3_.1) | copy-start | bytes 1572868
  0.0 32.2 %copy-start.2 = (s32[4,12]{1,0:T(4,128)S(1)}, s32[4,12]{1,0:T(4,128)}, u32[]{:S(2)}) copy-start(s32[4,12]{1,0:T(4,128)} %aperture_ref.5) | copy-start | bytes 580
  0.0 37.6 %collective-permute-start.5 = (bf16[2,2,256,768]{3,2,1,0:T(8,128)(2,1)}, bf16[2,2,256,768]{3,2,1,0:T(8,128)(2,1)S(1)}, u32[]{:S(2)}, u32[]{:S(2)}) collective-permute-start(bf16[2,2,256,768]{3,2,1,0:T(8,128)(2,1)} %own_ref.1), channel_id=1, source_target_pairs={{0,2},{1,3},{2,0},{3,1},{4,6},{5,7},{6,4},{7,5},{8,10},{9,11},{10,... | collective-permute-start | bytes 4718600 | tf_op jit(solution)/shard_map/ppermute | solution.py:28
  3.0 24.7 %collective-permute-start = (bf16[2,2,256,256]{3,2,1,0:T(8,128)(2,1)}, bf16[2,2,256,256]{3,2,1,0:T(8,128)(2,1)S(1)}, u32[]{:S(2)}, u32[]{:S(2)}) collective-permute-start(bf16[2,2,256,256]{3,2,1,0:T(8,128)(2,1)} %refs_3_.1), channel_id=1, source_target_pairs={{0,4},{4,0},{8,12},{12,8},{1,5},{5,1},{9,13},{13,9},{2,6},{6,2},{1... | collective-permute-start | bytes 1572872 | tf_op jit(solution)/shard_map/ppermute | solution.py:37
  4.6 25.5 %collective-permute-start.1 = (bf16[2,2,256,256]{3,2,1,0:T(8,128)(2,1)}, bf16[2,2,256,256]{3,2,1,0:T(8,128)(2,1)S(1)}, u32[]{:S(2)}, u32[]{:S(2)}) collective-permute-start(bf16[2,2,256,256]{3,2,1,0:T(8,128)(2,1)} %refs_3_.1), channel_id=1, source_target_pairs={{0,8},{4,12},{8,0},{12,4},{1,9},{5,13},{9,1},{13,5},{2,10},{6,14},... | collective-permute-start | bytes 1572872 | tf_op jit(solution)/shard_map/ppermute | solution.py:38
  30.1 8.4 %collective-permute-start.3 = (bf16[1,2,256,256]{3,2,1,0:T(8,128)(2,1)S(1)}, bf16[1,2,256,256]{3,2,1,0:T(8,128)(2,1)S(1)}, u32[]{:S(2)}, u32[]{:S(2)}) collective-permute-start(bf16[1,2,256,256]{3,2,1,0:T(8,128)(2,1)S(1)} %get-tuple-element.35), channel_id=1, source_target_pairs={{0,4},{4,0},{8,12},{12,8},{1,5},{5,1},{9,13},{13,9},{2,6},{6,2},{1... | collective-permute-start | bytes 786440 | tf_op jit(solution)/shard_map/ppermute | solution.py:43
  30.6 10.9 %collective-permute-start.2 = (bf16[1,2,256,256]{3,2,1,0:T(8,128)(2,1)S(1)}, bf16[1,2,256,256]{3,2,1,0:T(8,128)(2,1)S(1)}, u32[]{:S(2)}, u32[]{:S(2)}) collective-permute-start(bf16[1,2,256,256]{3,2,1,0:T(8,128)(2,1)S(1)} %get-tuple-element.36), channel_id=1, source_target_pairs={{0,4},{4,0},{8,12},{12,8},{1,5},{5,1},{9,13},{13,9},{2,6},{6,2},{1... | collective-permute-start | bytes 786440 | tf_op jit(solution)/shard_map/ppermute | solution.py:43
  32.2 6.3 %collective-permute-start.4 = (bf16[2,2,256,768]{3,2,1,0:T(8,128)(2,1)S(1)}, bf16[2,2,256,768]{3,2,1,0:T(8,128)(2,1)S(1)}, u32[]{:S(2)}, u32[]{:S(2)}) collective-permute-start(bf16[2,2,256,768]{3,2,1,0:T(8,128)(2,1)S(1)} %copy-done.1), channel_id=1, source_target_pairs={{0,1},{1,0},{2,3},{3,2},{4,5},{5,4},{6,7},{7,6},{8,9},{9,8},{10,11... | collective-permute-start | bytes 4718600 | tf_op jit(solution)/shard_map/ppermute | solution.py:28
  37.6 3.9 %collective-permute-start.6 = (bf16[2,2,256,768]{3,2,1,0:T(8,128)(2,1)S(1)}, bf16[2,2,256,768]{3,2,1,0:T(8,128)(2,1)S(1)}, u32[]{:S(2)}, u32[]{:S(2)}) collective-permute-start(bf16[2,2,256,768]{3,2,1,0:T(8,128)(2,1)S(1)} %shard_map.39.refs_1_), channel_id=1, source_target_pairs={{0,1},{1,0},{2,3},{3,2},{4,5},{5,4},{6,7},{7,6},{8,9},{9,8},{10,11... | collective-permute-start | bytes 4718600 | tf_op jit(solution)/shard_map/ppermute | solution.py:28

commit v27 on v26

--- a/solution.py
+++ b/solution.py
@@ -138,17 +138,22 @@
         sums[v][...] = sum_of_late(aperture_ref, panels, late, window.shape[0])
 
 
-def kernel_b(late, aperture_ref, late_ref, _, last_window, first_sum, last_sum, first_in, last_in, *refs):
-    *panel_refs, window, two, first_part, last_part = refs
+def kernel_b(late, aperture_ref, last_window, last_sum, last_in, *refs):
+    *panel_refs, two, last_part = refs
+    panels = {1 + m: ref.at[1] for m, ref in enumerate(panel_refs)}
+    real, imag = product(last_window, aperture_ref, panels)
+    last_part[0] = last_in[0] + real
+    last_part[1] = last_in[1] + imag
+    two[...] = in_two(last_sum[...] + sum_of_late(aperture_ref, panels, late, last_window.shape[0]))
+
+
+def kernel_c(late, aperture_ref, late_ref, _, first_sum, first_in, *refs):
+    *panel_refs, window, first_part = refs
     fill_window(window, {late: late_ref.at[0]})
-    panels = [{1 + m: ref.at[v] for m, ref in enumerate(panel_refs)} for v in range(2)]
-    real, imag = product(window, aperture_ref, panels[0], in_two(first_sum[...]), late)
+    panels = {1 + m: ref.at[0] for m, ref in enumerate(panel_refs)}
+    real, imag = product(window, aperture_ref, panels, in_two(first_sum[...]), late)
     first_part[0] = first_in[0] + real
     first_part[1] = first_in[1] + imag
-    real, imag = product(last_window, aperture_ref, panels[1])
-    last_part[0] = last_in[0] + real
-    last_part[1] = last_in[1] + imag
-    two[...] = in_two(last_sum[...] + sum_of_late(aperture_ref, panels[1], late, last_window.shape[0]))
 
 
 def last_kernel(far_half, late, aperture_ref, late_ref, first_window, _, two, first_part, last_part, *refs):
@@ -224,15 +229,25 @@
 
     far_panel = held(far_panel, 12, first_part)
     handed_on = hand_on(far_panel, first_part)
-    first, two, first_part, last_part = pl.pallas_call(
+    two, last_part = pl.pallas_call(
         functools.partial(kernel_b, late),
-        out_shape=[window, jax.ShapeDtypeStruct((2 * BLK, 2 * BLK), jnp.bfloat16), part, part],
-        in_specs=[vmem] * (8 + half),
-        out_specs=[vmem] * 4,
-        input_output_aliases={2: 0, 6: 2, 7: 3},
-        compiler_params=limit(16),
-        cost_estimate=cost(0.1),
-    )(aperture, late_pieces[0], first, last, first_sum, last_sum, first_part, last_part, *panels[1:], far_panel)
+        out_shape=[jax.ShapeDtypeStruct((2 * BLK, 2 * BLK), jnp.bfloat16), part],
+        in_specs=[vmem] * (4 + half),
+        out_specs=[vmem] * 2,
+        input_output_aliases={3: 1},
+        compiler_params=limit(16),
+        cost_estimate=cost(0.05),
+    )(aperture, last, last_sum, last_part, *panels[1:], far_panel)
+
+    first, first_part = pl.pallas_call(
+        functools.partial(kernel_c, late),
+        out_shape=[window, part],
+        in_specs=[vmem] * (5 + half),
+        out_specs=[vmem] * 2,
+        input_output_aliases={2: 0, 4: 1},
+        compiler_params=limit(16),
+        cost_estimate=cost(0.05),
+    )(aperture, after(late_pieces[0], two), first, first_sum, first_part, *panels[1:], far_panel)
 
     return pl.pallas_call(
         functools.partial(last_kernel, half + 1, late),
@@ -243,7 +258,7 @@
         input_output_aliases={3: 1},
         compiler_params=limit(16),
         cost_estimate=cost(1),
-    )(aperture, held(late_pieces[1], 12, two), first, last, two, first_part, last_part, *handed_on)[0]
+    )(aperture, held(late_pieces[1], 12, first_part), first, last, two, first_part, last_part, *handed_on)[0]
 
 
 def solution(mesh):

time: 44 us -> 43.7 us (level)
  waiting for transfers between devices: 27.6 us -> 27.1 us
    ppermute x2, waiting for transfers between devices: 0.91 us -> 0.42 us  [line_window(): across = lax.ppermute(far[v:v + 1], 'src', near_pairs)]
    pallas_call x1 -> x2, Pallas kernels: 2.98 us -> 3.28 us  [the longest x1 1.85 us: body(): pl.pallas_call(functools.partial(kernel_b, late), out_shape=[jax.ShapeDty...]
where the time goes in v27:
time: 43.7 us; the launch traced here: 43.6 us
  waiting for transfers between devices  27.1 us (62%)
  starting transfers between devices  9.27 us (21%)
  Pallas kernels  7.16 us (16%)
    ppermute x1, waiting for transfers between devices, line_window(): near = lax.ppermute(data, 'src', near_pairs)  20.5 us
    ppermute x3, waiting for transfers between devices, swap(): return lax.ppermute(x, axis, [(i, i ^ bit) for i in range(peers)])  3.74 us
    ppermute x3, starting transfers between devices, swap(): return lax.ppermute(x, axis, [(i, i ^ bit) for i in range(peers)])  3.01 us
    ppermute x1, starting transfers between devices, line_window(): far = lax.ppermute(data, 'src', [(0, 2), (1, 3), (2, 0), (3, 1)])  2.59 us
    ppermute x1, waiting for transfers between devices, line_window(): far = lax.ppermute(data, 'src', [(0, 2), (1, 3), (2, 0), (3, 1)])  2.39 us
    pallas_call x1, Pallas kernels, body(): pl.pallas_call(functools.partial(last_kernel, half + 1, late), out_shape=...  2.26 us
    ppermute x2, starting transfers between devices, line_window(): across = lax.ppermute(far[v:v + 1], 'src', near_pairs)  2.09 us
    pallas_call x1, Pallas kernels, body(): pl.pallas_call(functools.partial(kernel_b, late), out_shape=[jax.ShapeDty...  1.85 us
  transfers between devices with their start and end apart: 7, of which 4 were waited for; matrix products, arithmetic and copies ran while one was open for 0% of the time, Pallas kernels for 11%

profile of v27, /device:TPU:0, one launch (start us, length us, event | category | flops | bytes accessed | tf_op | source)
XLA Modules:
  0.0 43.6 jit_solution(12343985673005657564)
XLA Ops:
  0.0 0.0 copy-start.1
  0.0 0.0 copy-start
  0.0 0.0 copy-start.2
  0.0 3.0 %collective-permute-start.5 = (bf16[2,2,256,768]{3,2,1,0:T(8,128)(2,1)}, bf16[2,2,256,768]{3,2,1,0:T(8,128)(2,1)S(1)}, u32[]{:S(2)}, u32[]{:S(2)}) collective-permute-start(bf16[2,2,256,768]{3,2,1,0:T(8,128)(2,1)} %own_ref.1), channel_id=1, source_target_pairs={{0,2},{1,3},{2,0},{3,1},{4,6},{5,7},{6,4},{7,5},{8,10},{9,11},{10,... | collective-permute-start | bytes 4718600 | tf_op jit(solution)/shard_map/ppermute | solution.py:28
  3.0 1.6 %collective-permute-start = (bf16[2,2,256,256]{3,2,1,0:T(8,128)(2,1)}, bf16[2,2,256,256]{3,2,1,0:T(8,128)(2,1)S(1)}, u32[]{:S(2)}, u32[]{:S(2)}) collective-permute-start(bf16[2,2,256,256]{3,2,1,0:T(8,128)(2,1)} %refs_3_.1), channel_id=1, source_target_pairs={{0,4},{4,0},{8,12},{12,8},{1,5},{5,1},{9,13},{13,9},{2,6},{6,2},{1... | collective-permute-start | bytes 1572872 | tf_op jit(solution)/shard_map/ppermute | solution.py:37
  4.6 2.6 %collective-permute-start.1 = (bf16[2,2,256,256]{3,2,1,0:T(8,128)(2,1)}, bf16[2,2,256,256]{3,2,1,0:T(8,128)(2,1)S(1)}, u32[]{:S(2)}, u32[]{:S(2)}) collective-permute-start(bf16[2,2,256,256]{3,2,1,0:T(8,128)(2,1)} %refs_3_.1), channel_id=1, source_target_pairs={{0,8},{4,12},{8,0},{12,4},{1,9},{5,13},{9,1},{13,5},{2,10},{6,14},... | collective-permute-start | bytes 1572872 | tf_op jit(solution)/shard_map/ppermute | solution.py:38
  7.2 20.5 %collective-permute-done.refs_1_.refs_4_ = bf16[2,2,256,256]{3,2,1,0:T(8,128)(2,1)S(1)} collective-permute-done((bf16[2,2,256,256]{3,2,1,0:T(8,128)(2,1)}, bf16[2,2,256,256]{3,2,1,0:T(8,128)(2,1)S(1)}, u32[]{:S(2)}, u32[]{:S(2)}) %collective-permute-start) | collective-permute-done | bytes 524320 | tf_op jit(solution)/shard_map/ppermute | solution.py:37
  27.7 2.4 %collective-permute-done.1.refs_0_ = bf16[2,2,256,256]{3,2,1,0:T(8,128)(2,1)S(1)} collective-permute-done((bf16[2,2,256,256]{3,2,1,0:T(8,128)(2,1)}, bf16[2,2,256,256]{3,2,1,0:T(8,128)(2,1)S(1)}, u32[]{:S(2)}, u32[]{:S(2)}) %collective-permute-start.1) | collective-permute-done | bytes 524320 | tf_op jit(solution)/shard_map/ppermute | solution.py:38
  30.1 0.5 %collective-permute-start.3 = (bf16[1,2,256,256]{3,2,1,0:T(8,128)(2,1)S(1)}, bf16[1,2,256,256]{3,2,1,0:T(8,128)(2,1)S(1)}, u32[]{:S(2)}, u32[]{:S(2)}) collective-permute-start(bf16[1,2,256,256]{3,2,1,0:T(8,128)(2,1)S(1)} %get-tuple-element.37), channel_id=1, source_target_pairs={{0,4},{4,0},{8,12},{12,8},{1,5},{5,1},{9,13},{13,9},{2,6},{6,2},{1... | collective-permute-start | bytes 786440 | tf_op jit(solution)/shard_map/ppermute | solution.py:43
  30.6 1.6 %collective-permute-start.2 = (bf16[1,2,256,256]{3,2,1,0:T(8,128)(2,1)S(1)}, bf16[1,2,256,256]{3,2,1,0:T(8,128)(2,1)S(1)}, u32[]{:S(2)}, u32[]{:S(2)}) collective-permute-start(bf16[1,2,256,256]{3,2,1,0:T(8,128)(2,1)S(1)} %get-tuple-element.38), channel_id=1, source_target_pairs={{0,4},{4,0},{8,12},{12,8},{1,5},{5,1},{9,13},{13,9},{2,6},{6,2},{1... | collective-permute-start | bytes 786440 | tf_op jit(solution)/shard_map/ppermute | solution.py:43
  32.2 0.0 copy-done.1
  32.2 0.0 collective-permute-start.4
  32.2 0.0 copy-done
  32.2 0.0 copy-done.2
  32.3 1.6 %shard_map.38 = (bf16[4,256,512]{2,1,0:T(8,128)(2,1)S(1)}, bf16[4,256,512]{2,1,0:T(8,128)(2,1)S(1)}, f32[512,256]{1,0:T(8,128)S(1)}, f32[512,256]{1,0:T(8,128)S(...) custom-call(s32[4,12]{1,0:T(4,128)S(1)} %copy-done.2, bf16[2,2,256,768]{3,2,1,0:T(8,128)(2,1)S(1)} %copy-done.1, ...), custom_call_target="tpu_custom_call" | custom-call | flops 161061280 | bytes 1048576 | tf_op jit(solution)/shard_map/pallas_call | solution.py:221
  33.9 3.7 %collective-permute-done.5.refs_0_ = bf16[2,2,256,768]{3,2,1,0:T(8,128)(2,1)S(1)} collective-permute-done((bf16[2,2,256,768]{3,2,1,0:T(8,128)(2,1)}, bf16[2,2,256,768]{3,2,1,0:T(8,128)(2,1)S(1)}, u32[]{:S(2)}, u32[]{:S(2)}) %collective-permute-start.5) | collective-permute-done | bytes 1572896 | tf_op jit(solution)/shard_map/ppermute | solution.py:28
  37.6 0.0 collective-permute-start.6
  37.6 0.0 collective-permute-done.4.refs_0_
  37.6 1.9 %shard_map.40 = (bf16[512,512]{1,0:T(8,128)(2,1)S(1)}, f32[2,256,256]{2,1,0:T(8,128)S(1)}) custom-call(s32[4,12]{1,0:T(4,128)S(1)} %copy-done.2, bf16[4,256,512]{2,1,0:T(8,128)(2,1)S(1)} %get-tuple-element.23.last_window._, f32[512,256]{1,0:T(8,128)S(1)} %get-tuple-element.24.last_sum, ...), custom_call_target="tpu_custom_call", output_to_operand_aliasing={{1}: (3, {})} | custom-call | flops 80530640 | bytes 1048576 | tf_op jit(solution)/shard_map/pallas_call | solution.py:232
  39.5 0.0 collective-permute-done.3.late_ref
  39.5 1.4 %shard_map.41 = (bf16[4,256,512]{2,1,0:T(8,128)(2,1)S(1)}, f32[2,256,256]{2,1,0:T(8,128)S(1)}) custom-call(s32[4,12]{1,0:T(4,128)S(1)} %copy-done.2, bf16[1,2,256,256]{3,2,1,0:T(8,128)(2,1)S(1)} %collective-permute-done.3.late_ref, bf16[4,256,512]{2,1,0:T(8,128)(2,1)S(1)} %get-tuple-element.30._, ...), custom_call_target="tpu_custom_call", output_to_operand_aliasing={{0}: (2, {}), {1}: (4, {})} | custom-call | flops 80530640 | bytes 1048576 | tf_op jit(solution)/shard_map/pallas_call | solution.py:242
  40.9 0.4 collective-permute-done.2.refs_0_
  41.3 0.0 collective-permute-done.6.refs_0_
  41.3 2.3 %shard_map.43 = (f32[2,2,256,256]{3,2,1,0:T(8,128)}, bf16[4,256,512]{2,1,0:T(8,128)(2,1)S(1)}) custom-call(s32[4,12]{1,0:T(4,128)S(1)} %copy-done.2, bf16[1,2,256,256]{3,2,1,0:T(8,128)(2,1)S(1)} %shard_map.42.late_ref, bf16[4,256,512]{2,1,0:T(8,128)(2,1)S(1)} %get-tuple-element.33.first_window, ...), custom_call_target="tpu_custom_call", output_to_operand_aliasing={{1}: (3, {})} | custom-call | flops 1610612736 | bytes 1048576 | tf_op jit(solution)/shard_map/pallas_call | solution.py:252
  (4 shorter events, 0.0 us)
Async XLA Ops:
  0.0 32.2 %copy-start.1 = (bf16[2,2,256,768]{3,2,1,0:T(8,128)(2,1)S(1)}, bf16[2,2,256,768]{3,2,1,0:T(8,128)(2,1)}, u32[]{:S(2)}) copy-start(bf16[2,2,256,768]{3,2,1,0:T(8,128)(2,1)} %own_ref.1) | copy-start | bytes 4718596
  0.0 32.2 %copy-start = (bf16[2,2,256,256]{3,2,1,0:T(8,128)(2,1)S(1)}, bf16[2,2,256,256]{3,2,1,0:T(8,128)(2,1)}, u32[]{:S(2)}) copy-start(bf16[2,2,256,256]{3,2,1,0:T(8,128)(2,1)} %refs_3_.1) | copy-start | bytes 1572868
  0.0 32.2 %copy-start.2 = (s32[4,12]{1,0:T(4,128)S(1)}, s32[4,12]{1,0:T(4,128)}, u32[]{:S(2)}) copy-start(s32[4,12]{1,0:T(4,128)} %aperture_ref.7) | copy-start | bytes 580
  0.0 37.6 %collective-permute-start.5 = (bf16[2,2,256,768]{3,2,1,0:T(8,128)(2,1)}, bf16[2,2,256,768]{3,2,1,0:T(8,128)(2,1)S(1)}, u32[]{:S(2)}, u32[]{:S(2)}) collective-permute-start(bf16[2,2,256,768]{3,2,1,0:T(8,128)(2,1)} %own_ref.1), channel_id=1, source_target_pairs={{0,2},{1,3},{2,0},{3,1},{4,6},{5,7},{6,4},{7,5},{8,10},{9,11},{10,... | collective-permute-start | bytes 4718600 | tf_op jit(solution)/shard_map/ppermute | solution.py:28
  3.0 24.7 %collective-permute-start = (bf16[2,2,256,256]{3,2,1,0:T(8,128)(2,1)}, bf16[2,2,256,256]{3,2,1,0:T(8,128)(2,1)S(1)}, u32[]{:S(2)}, u32[]{:S(2)}) collective-permute-start(bf16[2,2,256,256]{3,2,1,0:T(8,128)(2,1)} %refs_3_.1), channel_id=1, source_target_pairs={{0,4},{4,0},{8,12},{12,8},{1,5},{5,1},{9,13},{13,9},{2,6},{6,2},{1... | collective-permute-start | bytes 1572872 | tf_op jit(solution)/shard_map/ppermute | solution.py:37
  4.6 25.5 %collective-permute-start.1 = (bf16[2,2,256,256]{3,2,1,0:T(8,128)(2,1)}, bf16[2,2,256,256]{3,2,1,0:T(8,128)(2,1)S(1)}, u32[]{:S(2)}, u32[]{:S(2)}) collective-permute-start(bf16[2,2,256,256]{3,2,1,0:T(8,128)(2,1)} %refs_3_.1), channel_id=1, source_target_pairs={{0,8},{4,12},{8,0},{12,4},{1,9},{5,13},{9,1},{13,5},{2,10},{6,14},... | collective-permute-start | bytes 1572872 | tf_op jit(solution)/shard_map/ppermute | solution.py:38
  30.1 9.3 %collective-permute-start.3 = (bf16[1,2,256,256]{3,2,1,0:T(8,128)(2,1)S(1)}, bf16[1,2,256,256]{3,2,1,0:T(8,128)(2,1)S(1)}, u32[]{:S(2)}, u32[]{:S(2)}) collective-permute-start(bf16[1,2,256,256]{3,2,1,0:T(8,128)(2,1)S(1)} %get-tuple-element.37), channel_id=1, source_target_pairs={{0,4},{4,0},{8,12},{12,8},{1,5},{5,1},{9,13},{13,9},{2,6},{6,2},{1... | collective-permute-start | bytes 786440 | tf_op jit(solution)/shard_map/ppermute | solution.py:43
  30.6 10.7 %collective-permute-start.2 = (bf16[1,2,256,256]{3,2,1,0:T(8,128)(2,1)S(1)}, bf16[1,2,256,256]{3,2,1,0:T(8,128)(2,1)S(1)}, u32[]{:S(2)}, u32[]{:S(2)}) collective-permute-start(bf16[1,2,256,256]{3,2,1,0:T(8,128)(2,1)S(1)} %get-tuple-element.38), channel_id=1, source_target_pairs={{0,4},{4,0},{8,12},{12,8},{1,5},{5,1},{9,13},{13,9},{2,6},{6,2},{1... | collective-permute-start | bytes 786440 | tf_op jit(solution)/shard_map/ppermute | solution.py:43
  32.2 5.4 %collective-permute-start.4 = (bf16[2,2,256,768]{3,2,1,0:T(8,128)(2,1)S(1)}, bf16[2,2,256,768]{3,2,1,0:T(8,128)(2,1)S(1)}, u32[]{:S(2)}, u32[]{:S(2)}) collective-permute-start(bf16[2,2,256,768]{3,2,1,0:T(8,128)(2,1)S(1)} %copy-done.1), channel_id=1, source_target_pairs={{0,1},{1,0},{2,3},{3,2},{4,5},{5,4},{6,7},{7,6},{8,9},{9,8},{10,11... | collective-permute-start | bytes 4718600 | tf_op jit(solution)/shard_map/ppermute | solution.py:28
  37.6 3.7 %collective-permute-start.6 = (bf16[2,2,256,768]{3,2,1,0:T(8,128)(2,1)S(1)}, bf16[2,2,256,768]{3,2,1,0:T(8,128)(2,1)S(1)}, u32[]{:S(2)}, u32[]{:S(2)}) collective-permute-start(bf16[2,2,256,768]{3,2,1,0:T(8,128)(2,1)S(1)} %shard_map.39.refs_1_), channel_id=1, source_target_pairs={{0,1},{1,0},{2,3},{3,2},{4,5},{5,4},{6,7},{7,6},{8,9},{9,8},{10,11... | collective-permute-start | bytes 4718600 | tf_op jit(solution)/shard_map/ppermute | solution.py:28

commit v28 on v27

--- a/solution.py
+++ b/solution.py
@@ -54,9 +54,9 @@
     return [[(window[distance], v) for distance in range(-reach, reach + 1)] for v in range(data.shape[0])]
 
 
-def gather_panels(primaries, first):
+def gather_panels(primaries):
     bit = lax.axis_size("rcv") // 2
-    panels = [after(primaries, first)]
+    panels = [primaries]
     for lower in range(1, bit):
         panels.append(swap(panels[lower & (lower - 1)], "rcv", lower & -lower))
     return panels, swap(primaries, "rcv", bit)
@@ -207,7 +207,7 @@
     width = data.shape[3]
     line = lax.axis_size("src") == 4
     windows = (line_window if line else hop_window)(data)
-    panels, far_panel = gather_panels(primaries, windows[0][-2][0])
+    panels, far_panel = gather_panels(primaries)
     half = len(panels)
     late = len(windows[0]) - 1
     late_pieces = [piece[at : at + 1] for piece, at in (window[late] for window in windows)]

time: 43.7 us -> 45.3 us (1.037)
  waiting for transfers between devices: 27.1 us -> 28.6 us
    ppermute x3, waiting for transfers between devices: 3.74 us -> 5.37 us  [swap(): return lax.ppermute(x, axis, [(i, i ^ bit) for i in range(peers)])]
  transfers between devices with their start and end apart: 7 -> 7, of which waited for: 4 -> 5; matrix products, arithmetic and copies ran while one was open for 0% -> 0% of each run, Pallas kernels for 11% -> 11%
where the time goes in v28:
time: 45.3 us; the launch traced here: 45.2 us
  waiting for transfers between devices  28.6 us (63%)
  starting transfers between devices  9.27 us (20%)
  Pallas kernels  7.15 us (16%)
    ppermute x1, waiting for transfers between devices, line_window(): near = lax.ppermute(data, 'src', near_pairs)  20.5 us
    ppermute x3, waiting for transfers between devices, swap(): return lax.ppermute(x, axis, [(i, i ^ bit) for i in range(peers)])  5.37 us
    ppermute x3, starting transfers between devices, swap(): return lax.ppermute(x, axis, [(i, i ^ bit) for i in range(peers)])  3.01 us
    ppermute x1, starting transfers between devices, line_window(): far = lax.ppermute(data, 'src', [(0, 2), (1, 3), (2, 0), (3, 1)])  2.59 us
    ppermute x1, waiting for transfers between devices, line_window(): far = lax.ppermute(data, 'src', [(0, 2), (1, 3), (2, 0), (3, 1)])  2.39 us
    pallas_call x1, Pallas kernels, body(): pl.pallas_call(functools.partial(last_kernel, half + 1, late), out_shape=...  2.26 us
    ppermute x2, starting transfers between devices, line_window(): across = lax.ppermute(far[v:v + 1], 'src', near_pairs)  2.09 us
    pallas_call x1, Pallas kernels, body(): pl.pallas_call(functools.partial(kernel_b, late), out_shape=[jax.ShapeDty...  1.85 us
  transfers between devices with their start and end apart: 7, of which 5 were waited for; matrix products, arithmetic and copies ran while one was open for 0% of the time, Pallas kernels for 11%

profile of v28, /device:TPU:0, one launch (start us, length us, event | category | flops | bytes accessed | tf_op | source)
XLA Modules:
  0.0 45.2 jit_solution(15010911313334920205)
XLA Ops:
  0.0 0.0 copy-start
  0.0 0.0 copy-start.2
  0.0 2.9 %collective-permute-start.5 = (bf16[2,2,256,768]{3,2,1,0:T(8,128)(2,1)}, bf16[2,2,256,768]{3,2,1,0:T(8,128)(2,1)S(1)}, u32[]{:S(2)}, u32[]{:S(2)}) collective-permute-start(bf16[2,2,256,768]{3,2,1,0:T(8,128)(2,1)} %own_ref.1), channel_id=1, source_target_pairs={{0,2},{1,3},{2,0},{3,1},{4,6},{5,7},{6,4},{7,5},{8,10},{9,11},{10,... | collective-permute-start | bytes 4718600 | tf_op jit(solution)/shard_map/ppermute | solution.py:28
  2.9 1.6 %collective-permute-start = (bf16[2,2,256,256]{3,2,1,0:T(8,128)(2,1)}, bf16[2,2,256,256]{3,2,1,0:T(8,128)(2,1)S(1)}, u32[]{:S(2)}, u32[]{:S(2)}) collective-permute-start(bf16[2,2,256,256]{3,2,1,0:T(8,128)(2,1)} %refs_3_.1), channel_id=1, source_target_pairs={{0,4},{4,0},{8,12},{12,8},{1,5},{5,1},{9,13},{13,9},{2,6},{6,2},{1... | collective-permute-start | bytes 1572872 | tf_op jit(solution)/shard_map/ppermute | solution.py:37
  4.5 2.6 %collective-permute-start.1 = (bf16[2,2,256,256]{3,2,1,0:T(8,128)(2,1)}, bf16[2,2,256,256]{3,2,1,0:T(8,128)(2,1)S(1)}, u32[]{:S(2)}, u32[]{:S(2)}) collective-permute-start(bf16[2,2,256,256]{3,2,1,0:T(8,128)(2,1)} %refs_3_.1), channel_id=1, source_target_pairs={{0,8},{4,12},{8,0},{12,4},{1,9},{5,13},{9,1},{13,5},{2,10},{6,14},... | collective-permute-start | bytes 1572872 | tf_op jit(solution)/shard_map/ppermute | solution.py:38
  7.1 0.0 collective-permute-start.4
  7.1 20.5 %collective-permute-done.refs_1_.refs_4_ = bf16[2,2,256,256]{3,2,1,0:T(8,128)(2,1)S(1)} collective-permute-done((bf16[2,2,256,256]{3,2,1,0:T(8,128)(2,1)}, bf16[2,2,256,256]{3,2,1,0:T(8,128)(2,1)S(1)}, u32[]{:S(2)}, u32[]{:S(2)}) %collective-permute-start) | collective-permute-done | bytes 524320 | tf_op jit(solution)/shard_map/ppermute | solution.py:37
  27.6 2.4 %collective-permute-done.1.refs_0_ = bf16[2,2,256,256]{3,2,1,0:T(8,128)(2,1)S(1)} collective-permute-done((bf16[2,2,256,256]{3,2,1,0:T(8,128)(2,1)}, bf16[2,2,256,256]{3,2,1,0:T(8,128)(2,1)S(1)}, u32[]{:S(2)}, u32[]{:S(2)}) %collective-permute-start.1) | collective-permute-done | bytes 524320 | tf_op jit(solution)/shard_map/ppermute | solution.py:38
  30.0 0.0 copy-start.1
  30.1 0.5 %collective-permute-start.3 = (bf16[1,2,256,256]{3,2,1,0:T(8,128)(2,1)S(1)}, bf16[1,2,256,256]{3,2,1,0:T(8,128)(2,1)S(1)}, u32[]{:S(2)}, u32[]{:S(2)}) collective-permute-start(bf16[1,2,256,256]{3,2,1,0:T(8,128)(2,1)S(1)} %get-tuple-element.35), channel_id=1, source_target_pairs={{0,4},{4,0},{8,12},{12,8},{1,5},{5,1},{9,13},{13,9},{2,6},{6,2},{1... | collective-permute-start | bytes 786440 | tf_op jit(solution)/shard_map/ppermute | solution.py:43
  30.6 1.6 %collective-permute-start.2 = (bf16[1,2,256,256]{3,2,1,0:T(8,128)(2,1)S(1)}, bf16[1,2,256,256]{3,2,1,0:T(8,128)(2,1)S(1)}, u32[]{:S(2)}, u32[]{:S(2)}) collective-permute-start(bf16[1,2,256,256]{3,2,1,0:T(8,128)(2,1)S(1)} %get-tuple-element.36), channel_id=1, source_target_pairs={{0,4},{4,0},{8,12},{12,8},{1,5},{5,1},{9,13},{13,9},{2,6},{6,2},{1... | collective-permute-start | bytes 786440 | tf_op jit(solution)/shard_map/ppermute | solution.py:43
  32.2 0.0 copy-done
  32.2 0.0 copy-done.2
  32.2 0.0 copy-done.1
  32.2 1.6 %shard_map.38 = (bf16[4,256,512]{2,1,0:T(8,128)(2,1)S(1)}, bf16[4,256,512]{2,1,0:T(8,128)(2,1)S(1)}, f32[512,256]{1,0:T(8,128)S(1)}, f32[512,256]{1,0:T(8,128)S(...) custom-call(s32[4,12]{1,0:T(4,128)S(1)} %copy-done.2, bf16[2,2,256,768]{3,2,1,0:T(8,128)(2,1)S(1)} %copy-done.1, ...), custom_call_target="tpu_custom_call" | custom-call | flops 161061280 | bytes 1048576 | tf_op jit(solution)/shard_map/pallas_call | solution.py:221
  33.8 3.7 %collective-permute-done.5.refs_0_ = bf16[2,2,256,768]{3,2,1,0:T(8,128)(2,1)S(1)} collective-permute-done((bf16[2,2,256,768]{3,2,1,0:T(8,128)(2,1)}, bf16[2,2,256,768]{3,2,1,0:T(8,128)(2,1)S(1)}, u32[]{:S(2)}, u32[]{:S(2)}) %collective-permute-start.5) | collective-permute-done | bytes 1572896 | tf_op jit(solution)/shard_map/ppermute | solution.py:28
  37.5 0.0 collective-permute-done.4.refs_0_
  37.5 1.8 %shard_map.40 = (bf16[512,512]{1,0:T(8,128)(2,1)S(1)}, f32[2,256,256]{2,1,0:T(8,128)S(1)}) custom-call(s32[4,12]{1,0:T(4,128)S(1)} %copy-done.2, bf16[4,256,512]{2,1,0:T(8,128)(2,1)S(1)} %get-tuple-element.22.last_window._, f32[512,256]{1,0:T(8,128)S(1)} %get-tuple-element.23.last_sum, ...), custom_call_target="tpu_custom_call", output_to_operand_aliasing={{1}: (3, {})} | custom-call | flops 80530640 | bytes 1048576 | tf_op jit(solution)/shard_map/pallas_call | solution.py:232
  39.4 0.0 collective-permute-done.3.late_ref
  39.4 0.1 collective-permute-start.6
  39.5 1.4 %shard_map.41 = (bf16[4,256,512]{2,1,0:T(8,128)(2,1)S(1)}, f32[2,256,256]{2,1,0:T(8,128)S(1)}) custom-call(s32[4,12]{1,0:T(4,128)S(1)} %copy-done.2, bf16[1,2,256,256]{3,2,1,0:T(8,128)(2,1)S(1)} %collective-permute-done.3.late_ref, bf16[4,256,512]{2,1,0:T(8,128)(2,1)S(1)} %get-tuple-element.28._, ...), custom_call_target="tpu_custom_call", output_to_operand_aliasing={{0}: (2, {}), {1}: (4, {})} | custom-call | flops 80530640 | bytes 1048576 | tf_op jit(solution)/shard_map/pallas_call | solution.py:242
  40.9 0.3 collective-permute-done.2.refs_0_
  41.3 1.6 %collective-permute-done.6.refs_0_ = bf16[2,2,256,768]{3,2,1,0:T(8,128)(2,1)S(1)} collective-permute-done((bf16[2,2,256,768]{3,2,1,0:T(8,128)(2,1)S(1)}, bf16[2,2,256,768]{3,2,1,0:T(8,128)(2,1)S(1)}, u32[]{:S(2)}, u32[]{:S(2)}) %collective-permute-start.6) | collective-permute-done | bytes 1572896 | tf_op jit(solution)/shard_map/ppermute | solution.py:28
  42.9 2.3 %shard_map.43 = (f32[2,2,256,256]{3,2,1,0:T(8,128)}, bf16[4,256,512]{2,1,0:T(8,128)(2,1)S(1)}) custom-call(s32[4,12]{1,0:T(4,128)S(1)} %copy-done.2, bf16[1,2,256,256]{3,2,1,0:T(8,128)(2,1)S(1)} %shard_map.42.late_ref, bf16[4,256,512]{2,1,0:T(8,128)(2,1)S(1)} %get-tuple-element.31.first_window, ...), custom_call_target="tpu_custom_call", output_to_operand_aliasing={{1}: (3, {})} | custom-call | flops 1610612736 | bytes 1048576 | tf_op jit(solution)/shard_map/pallas_call | solution.py:252
  (4 shorter events, 0.0 us)
Async XLA Ops:
  0.0 32.2 %copy-start = (bf16[2,2,256,256]{3,2,1,0:T(8,128)(2,1)S(1)}, bf16[2,2,256,256]{3,2,1,0:T(8,128)(2,1)}, u32[]{:S(2)}) copy-start(bf16[2,2,256,256]{3,2,1,0:T(8,128)(2,1)} %refs_3_.1) | copy-start | bytes 1572868
  0.0 32.2 %copy-start.2 = (s32[4,12]{1,0:T(4,128)S(1)}, s32[4,12]{1,0:T(4,128)}, u32[]{:S(2)}) copy-start(s32[4,12]{1,0:T(4,128)} %aperture_ref.7) | copy-start | bytes 580
  0.0 37.5 %collective-permute-start.5 = (bf16[2,2,256,768]{3,2,1,0:T(8,128)(2,1)}, bf16[2,2,256,768]{3,2,1,0:T(8,128)(2,1)S(1)}, u32[]{:S(2)}, u32[]{:S(2)}) collective-permute-start(bf16[2,2,256,768]{3,2,1,0:T(8,128)(2,1)} %own_ref.1), channel_id=1, source_target_pairs={{0,2},{1,3},{2,0},{3,1},{4,6},{5,7},{6,4},{7,5},{8,10},{9,11},{10,... | collective-permute-start | bytes 4718600 | tf_op jit(solution)/shard_map/ppermute | solution.py:28
  2.9 24.7 %collective-permute-start = (bf16[2,2,256,256]{3,2,1,0:T(8,128)(2,1)}, bf16[2,2,256,256]{3,2,1,0:T(8,128)(2,1)S(1)}, u32[]{:S(2)}, u32[]{:S(2)}) collective-permute-start(bf16[2,2,256,256]{3,2,1,0:T(8,128)(2,1)} %refs_3_.1), channel_id=1, source_target_pairs={{0,4},{4,0},{8,12},{12,8},{1,5},{5,1},{9,13},{13,9},{2,6},{6,2},{1... | collective-permute-start | bytes 1572872 | tf_op jit(solution)/shard_map/ppermute | solution.py:37
  4.5 25.5 %collective-permute-start.1 = (bf16[2,2,256,256]{3,2,1,0:T(8,128)(2,1)}, bf16[2,2,256,256]{3,2,1,0:T(8,128)(2,1)S(1)}, u32[]{:S(2)}, u32[]{:S(2)}) collective-permute-start(bf16[2,2,256,256]{3,2,1,0:T(8,128)(2,1)} %refs_3_.1), channel_id=1, source_target_pairs={{0,8},{4,12},{8,0},{12,4},{1,9},{5,13},{9,1},{13,5},{2,10},{6,14},... | collective-permute-start | bytes 1572872 | tf_op jit(solution)/shard_map/ppermute | solution.py:38
  7.1 30.4 %collective-permute-start.4 = (bf16[2,2,256,768]{3,2,1,0:T(8,128)(2,1)}, bf16[2,2,256,768]{3,2,1,0:T(8,128)(2,1)S(1)}, u32[]{:S(2)}, u32[]{:S(2)}) collective-permute-start(bf16[2,2,256,768]{3,2,1,0:T(8,128)(2,1)} %own_ref.1), channel_id=1, source_target_pairs={{0,1},{1,0},{2,3},{3,2},{4,5},{5,4},{6,7},{7,6},{8,9},{9,8},{10,11... | collective-permute-start | bytes 4718600 | tf_op jit(solution)/shard_map/ppermute | solution.py:28
  30.0 2.1 %copy-start.1 = (bf16[2,2,256,768]{3,2,1,0:T(8,128)(2,1)S(1)}, bf16[2,2,256,768]{3,2,1,0:T(8,128)(2,1)}, u32[]{:S(2)}) copy-start(bf16[2,2,256,768]{3,2,1,0:T(8,128)(2,1)} %own_ref.1) | copy-start | bytes 4718596
  30.1 9.3 %collective-permute-start.3 = (bf16[1,2,256,256]{3,2,1,0:T(8,128)(2,1)S(1)}, bf16[1,2,256,256]{3,2,1,0:T(8,128)(2,1)S(1)}, u32[]{:S(2)}, u32[]{:S(2)}) collective-permute-start(bf16[1,2,256,256]{3,2,1,0:T(8,128)(2,1)S(1)} %get-tuple-element.35), channel_id=1, source_target_pairs={{0,4},{4,0},{8,12},{12,8},{1,5},{5,1},{9,13},{13,9},{2,6},{6,2},{1... | collective-permute-start | bytes 786440 | tf_op jit(solution)/shard_map/ppermute | solution.py:43
  30.6 10.7 %collective-permute-start.2 = (bf16[1,2,256,256]{3,2,1,0:T(8,128)(2,1)S(1)}, bf16[1,2,256,256]{3,2,1,0:T(8,128)(2,1)S(1)}, u32[]{:S(2)}, u32[]{:S(2)}) collective-permute-start(bf16[1,2,256,256]{3,2,1,0:T(8,128)(2,1)S(1)} %get-tuple-element.36), channel_id=1, source_target_pairs={{0,4},{4,0},{8,12},{12,8},{1,5},{5,1},{9,13},{13,9},{2,6},{6,2},{1... | collective-permute-start | bytes 786440 | tf_op jit(solution)/shard_map/ppermute | solution.py:43
  39.4 3.5 %collective-permute-start.6 = (bf16[2,2,256,768]{3,2,1,0:T(8,128)(2,1)S(1)}, bf16[2,2,256,768]{3,2,1,0:T(8,128)(2,1)S(1)}, u32[]{:S(2)}, u32[]{:S(2)}) collective-permute-start(bf16[2,2,256,768]{3,2,1,0:T(8,128)(2,1)S(1)} %shard_map.39.refs_1_), channel_id=1, source_target_pairs={{0,1},{1,0},{2,3},{3,2},{4,5},{5,4},{6,7},{7,6},{8,9},{9,8},{10,11... | collective-permute-start | bytes 4718600 | tf_op jit(solution)/shard_map/ppermute | solution.py:28

commit v29 on v22

--- a/solution.py
+++ b/solution.py
@@ -165,9 +165,9 @@
         return copies
 
     panels = [{far_half + m: ref.at[v] for m, ref in enumerate(panel_refs)} for v in range(2)]
-    copies = finish(0, first_part, *product(first_window, aperture_ref, panels[0]))
     fill_window(window, {late: late_ref.at[0]})
-    copies += finish(1, last_part, *product(window, aperture_ref, panels[1], two[...], late))
+    copies = finish(1, last_part, *product(window, aperture_ref, panels[1], two[...], late))
+    copies += finish(0, first_part, *product(first_window, aperture_ref, panels[0]))
     for copy in copies:
         copy.wait()
 

time: 43.5 us -> 43.7 us (level)
  no operation moved by 1% of the time
where the time goes in v29:
time: 43.7 us; the launch traced here: 43.5 us
  waiting for transfers between devices  20.1 us (46%)
  starting transfers between devices  16.3 us (37%)
  Pallas kernels  7.08 us (16%)
    ppermute x1, waiting for transfers between devices, line_window(): far = held(lax.ppermute(data, 'src', [(0, 3), (1, 2), (2, 1), (3, 0)]), 5)  13.3 us
    ppermute x2, starting transfers between devices, line_window(): across = lax.ppermute(far[v:v + 1], 'src', near_pairs)  9.65 us
    ppermute x3, waiting for transfers between devices, swap(): return lax.ppermute(x, axis, [(i, i ^ bit) for i in range(peers)])  6.09 us
    ppermute x1, starting transfers between devices, line_window(): far = held(lax.ppermute(data, 'src', [(0, 3), (1, 2), (2, 1), (3, 0)]), 5)  3.6 us
    ppermute x3, starting transfers between devices, swap(): return lax.ppermute(x, axis, [(i, i ^ bit) for i in range(peers)])  3.01 us
    pallas_call x1, Pallas kernels, body(): pl.pallas_call(functools.partial(kernel_b, late), out_shape=[window, jax....  2.98 us
    pallas_call x1, Pallas kernels, body(): pl.pallas_call(functools.partial(last_kernel, half + 1, late), out_shape=...  2.48 us
    pallas_call x1, Pallas kernels, body(): pl.pallas_call(functools.partial(kernel_a, [{k: at for k, (_, at) in piec...  1.62 us
  transfers between devices with their start and end apart: 7, of which 4 were waited for; matrix products, arithmetic and copies ran while one was open for 0% of the time, Pallas kernels for 11%

profile of v29, /device:TPU:0, one launch (start us, length us, event | category | flops | bytes accessed | tf_op | source)
XLA Modules:
  0.0 43.5 jit_solution(11759393359477070912)
XLA Ops:
  0.0 0.0 copy-start.1
  0.0 0.0 copy-start
  0.0 0.0 copy-start.2
  0.0 3.0 %collective-permute-start.5 = (bf16[2,2,256,768]{3,2,1,0:T(8,128)(2,1)}, bf16[2,2,256,768]{3,2,1,0:T(8,128)(2,1)S(1)}, u32[]{:S(2)}, u32[]{:S(2)}) collective-permute-start(bf16[2,2,256,768]{3,2,1,0:T(8,128)(2,1)} %own_ref.1), channel_id=1, source_target_pairs={{0,2},{1,3},{2,0},{3,1},{4,6},{5,7},{6,4},{7,5},{8,10},{9,11},{10,... | collective-permute-start | bytes 4718600 | tf_op jit(solution)/shard_map/ppermute | solution.py:28
  3.0 3.6 %collective-permute-start = (bf16[2,2,256,256]{3,2,1,0:T(8,128)(2,1)}, bf16[2,2,256,256]{3,2,1,0:T(8,128)(2,1)S(1)}, u32[]{:S(2)}, u32[]{:S(2)}) collective-permute-start(bf16[2,2,256,256]{3,2,1,0:T(8,128)(2,1)} %refs_3_.1), channel_id=1, source_target_pairs={{0,12},{4,8},{8,4},{12,0},{1,13},{5,9},{9,5},{13,1},{2,14},{6,10},... | collective-permute-start | bytes 1572872 | tf_op jit(solution)/shard_map/ppermute | solution.py:37
  6.6 0.0 collective-permute-start.3
  6.6 13.3 %collective-permute-done.refs_0_ = bf16[2,2,256,256]{3,2,1,0:T(8,128)(2,1)S(1)} collective-permute-done((bf16[2,2,256,256]{3,2,1,0:T(8,128)(2,1)}, bf16[2,2,256,256]{3,2,1,0:T(8,128)(2,1)S(1)}, u32[]{:S(2)}, u32[]{:S(2)}) %collective-permute-start) | collective-permute-done | bytes 524320 | tf_op jit(solution)/shard_map/ppermute | solution.py:37
  20.0 9.6 %collective-permute-start.2 = (bf16[1,2,256,256]{3,2,1,0:T(8,128)(2,1)S(1)}, bf16[1,2,256,256]{3,2,1,0:T(8,128)(2,1)S(1)}, u32[]{:S(2)}, u32[]{:S(2)}) collective-permute-start(bf16[1,2,256,256]{3,2,1,0:T(8,128)(2,1)S(1)} %get-tuple-element.31), channel_id=1, source_target_pairs={{0,4},{4,0},{8,12},{12,8},{1,5},{5,1},{9,13},{13,9},{2,6},{6,2},{1... | collective-permute-start | bytes 786440 | tf_op jit(solution)/shard_map/ppermute | solution.py:41
  29.5 0.1 collective-permute-start.1
  29.6 0.0 copy-done.1
  29.6 0.0 collective-permute-start.4
  29.6 0.3 collective-permute-done.3.refs_1_.refs_4_
  29.9 0.0 copy-done
  29.9 0.0 copy-done.2
  29.9 1.6 %shard_map.38 = (bf16[4,256,512]{2,1,0:T(8,128)(2,1)S(1)}, bf16[4,256,512]{2,1,0:T(8,128)(2,1)S(1)}, f32[512,256]{1,0:T(8,128)S(1)}, f32[512,256]{1,0:T(8,128)S(...) custom-call(s32[4,12]{1,0:T(4,128)S(1)} %copy-done.2, bf16[2,2,256,768]{3,2,1,0:T(8,128)(2,1)S(1)} %copy-done.1, ...), custom_call_target="tpu_custom_call" | custom-call | flops 161061280 | bytes 1048576 | tf_op jit(solution)/shard_map/pallas_call | solution.py:214
  31.5 6.1 %collective-permute-done.5.refs_0_ = bf16[2,2,256,768]{3,2,1,0:T(8,128)(2,1)S(1)} collective-permute-done((bf16[2,2,256,768]{3,2,1,0:T(8,128)(2,1)}, bf16[2,2,256,768]{3,2,1,0:T(8,128)(2,1)S(1)}, u32[]{:S(2)}, u32[]{:S(2)}) %collective-permute-start.5) | collective-permute-done | bytes 1572896 | tf_op jit(solution)/shard_map/ppermute | solution.py:28
  37.6 0.0 collective-permute-start.6
  37.6 0.0 collective-permute-done.2.late_ref
  37.6 0.0 collective-permute-done.4.refs_0_
  37.6 3.0 %shard_map.40 = (bf16[4,256,512]{2,1,0:T(8,128)(2,1)S(1)}, bf16[512,512]{1,0:T(8,128)(2,1)S(1)}, f32[2,256,256]{2,1,0:T(8,128)S(1)}, f32[2,256,256]{2,1,0:T(8,128)S(1)}) custom-call(s32[4,12]{1,0:T(4,128)S(1)} %copy-done.2, bf16[1,2,256,256]{3,2,1,0:T(8,128)(2,1)S(1)} %collective-permute-done.2.late_ref, ...), custom_call_target="tpu_custom_call", output_to_operand_aliasing={{0}: (2, {}), {2}: (6, {}), {3}: (7, {})} | custom-call | flops 161061280 | bytes 1048576 | tf_op jit(solution)/shard_map/pallas_call | solution.py:225
  40.6 0.4 collective-permute-done.1.refs_0_
  41.0 0.0 collective-permute-done.6.refs_0_
  41.0 2.5 %shard_map.42 = (f32[2,2,256,256]{3,2,1,0:T(8,128)}, bf16[4,256,512]{2,1,0:T(8,128)(2,1)S(1)}) custom-call(s32[4,12]{1,0:T(4,128)S(1)} %copy-done.2, bf16[1,2,256,256]{3,2,1,0:T(8,128)(2,1)S(1)} %shard_map.41.late_ref, bf16[4,256,512]{2,1,0:T(8,128)(2,1)S(1)} %get-tuple-element.26.first_window, ...), custom_call_target="tpu_custom_call", output_to_operand_aliasing={{1}: (3, {})} | custom-call | flops 1610612736 | bytes 1048576 | tf_op jit(solution)/shard_map/pallas_call | solution.py:235
  (4 shorter events, 0.0 us)
Async XLA Ops:
  0.0 29.6 %copy-start.1 = (bf16[2,2,256,768]{3,2,1,0:T(8,128)(2,1)S(1)}, bf16[2,2,256,768]{3,2,1,0:T(8,128)(2,1)}, u32[]{:S(2)}) copy-start(bf16[2,2,256,768]{3,2,1,0:T(8,128)(2,1)} %own_ref.1) | copy-start | bytes 4718596
  0.0 29.9 %copy-start = (bf16[2,2,256,256]{3,2,1,0:T(8,128)(2,1)S(1)}, bf16[2,2,256,256]{3,2,1,0:T(8,128)(2,1)}, u32[]{:S(2)}) copy-start(bf16[2,2,256,256]{3,2,1,0:T(8,128)(2,1)} %refs_3_.1) | copy-start | bytes 1572868
  0.0 29.9 %copy-start.2 = (s32[4,12]{1,0:T(4,128)S(1)}, s32[4,12]{1,0:T(4,128)}, u32[]{:S(2)}) copy-start(s32[4,12]{1,0:T(4,128)} %aperture_ref.5) | copy-start | bytes 580
  0.0 37.6 %collective-permute-start.5 = (bf16[2,2,256,768]{3,2,1,0:T(8,128)(2,1)}, bf16[2,2,256,768]{3,2,1,0:T(8,128)(2,1)S(1)}, u32[]{:S(2)}, u32[]{:S(2)}) collective-permute-start(bf16[2,2,256,768]{3,2,1,0:T(8,128)(2,1)} %own_ref.1), channel_id=1, source_target_pairs={{0,2},{1,3},{2,0},{3,1},{4,6},{5,7},{6,4},{7,5},{8,10},{9,11},{10,... | collective-permute-start | bytes 4718600 | tf_op jit(solution)/shard_map/ppermute | solution.py:28
  3.0 16.9 %collective-permute-start = (bf16[2,2,256,256]{3,2,1,0:T(8,128)(2,1)}, bf16[2,2,256,256]{3,2,1,0:T(8,128)(2,1)S(1)}, u32[]{:S(2)}, u32[]{:S(2)}) collective-permute-start(bf16[2,2,256,256]{3,2,1,0:T(8,128)(2,1)} %refs_3_.1), channel_id=1, source_target_pairs={{0,12},{4,8},{8,4},{12,0},{1,13},{5,9},{9,5},{13,1},{2,14},{6,10},... | collective-permute-start | bytes 1572872 | tf_op jit(solution)/shard_map/ppermute | solution.py:37
  6.6 23.3 %collective-permute-start.3 = (bf16[2,2,256,256]{3,2,1,0:T(8,128)(2,1)}, bf16[2,2,256,256]{3,2,1,0:T(8,128)(2,1)S(1)}, u32[]{:S(2)}, u32[]{:S(2)}) collective-permute-start(bf16[2,2,256,256]{3,2,1,0:T(8,128)(2,1)} %refs_3_.1), channel_id=1, source_target_pairs={{0,4},{4,0},{8,12},{12,8},{1,5},{5,1},{9,13},{13,9},{2,6},{6,2},{1... | collective-permute-start | bytes 1572872 | tf_op jit(solution)/shard_map/ppermute | solution.py:38
  20.0 17.7 %collective-permute-start.2 = (bf16[1,2,256,256]{3,2,1,0:T(8,128)(2,1)S(1)}, bf16[1,2,256,256]{3,2,1,0:T(8,128)(2,1)S(1)}, u32[]{:S(2)}, u32[]{:S(2)}) collective-permute-start(bf16[1,2,256,256]{3,2,1,0:T(8,128)(2,1)S(1)} %get-tuple-element.31), channel_id=1, source_target_pairs={{0,4},{4,0},{8,12},{12,8},{1,5},{5,1},{9,13},{13,9},{2,6},{6,2},{1... | collective-permute-start | bytes 786440 | tf_op jit(solution)/shard_map/ppermute | solution.py:41
  29.5 11.5 %collective-permute-start.1 = (bf16[1,2,256,256]{3,2,1,0:T(8,128)(2,1)S(1)}, bf16[1,2,256,256]{3,2,1,0:T(8,128)(2,1)S(1)}, u32[]{:S(2)}, u32[]{:S(2)}) collective-permute-start(bf16[1,2,256,256]{3,2,1,0:T(8,128)(2,1)S(1)} %get-tuple-element.32), channel_id=1, source_target_pairs={{0,4},{4,0},{8,12},{12,8},{1,5},{5,1},{9,13},{13,9},{2,6},{6,2},{1... | collective-permute-start | bytes 786440 | tf_op jit(solution)/shard_map/ppermute | solution.py:41
  29.6 8.0 %collective-permute-start.4 = (bf16[2,2,256,768]{3,2,1,0:T(8,128)(2,1)S(1)}, bf16[2,2,256,768]{3,2,1,0:T(8,128)(2,1)S(1)}, u32[]{:S(2)}, u32[]{:S(2)}) collective-permute-start(bf16[2,2,256,768]{3,2,1,0:T(8,128)(2,1)S(1)} %copy-done.1), channel_id=1, source_target_pairs={{0,1},{1,0},{2,3},{3,2},{4,5},{5,4},{6,7},{7,6},{8,9},{9,8},{10,11... | collective-permute-start | bytes 4718600 | tf_op jit(solution)/shard_map/ppermute | solution.py:28
  37.6 3.4 %collective-permute-start.6 = (bf16[2,2,256,768]{3,2,1,0:T(8,128)(2,1)S(1)}, bf16[2,2,256,768]{3,2,1,0:T(8,128)(2,1)S(1)}, u32[]{:S(2)}, u32[]{:S(2)}) collective-permute-start(bf16[2,2,256,768]{3,2,1,0:T(8,128)(2,1)S(1)} %shard_map.39.refs_1_), channel_id=1, source_target_pairs={{0,1},{1,0},{2,3},{3,2},{4,5},{5,4},{6,7},{7,6},{8,9},{9,8},{10,11... | collective-permute-start | bytes 4718600 | tf_op jit(solution)/shard_map/ppermute | solution.py:28

commit v30 on v29

--- a/solution.py
+++ b/solution.py
@@ -161,7 +161,7 @@
                 copies.append(
                     pltpu.make_async_copy(result.at[v, p, rows], out_ref.at[v, p, rows], sems.at[v, p, chunk])
                 )
-                copies[-1].start()
+                copies[-1].start(priority=1 - v)
         return copies
 
     panels = [{far_half + m: ref.at[v] for m, ref in enumerate(panel_refs)} for v in range(2)]

time: 43.7 us -> 43.7 us (level)
  no operation moved by 1% of the time
where the time goes in v30:
time: 43.7 us; the launch traced here: 43.5 us
  waiting for transfers between devices  20.1 us (46%)
  starting transfers between devices  16.3 us (37%)
  Pallas kernels  7.08 us (16%)
    ppermute x1, waiting for transfers between devices, line_window(): far = held(lax.ppermute(data, 'src', [(0, 3), (1, 2), (2, 1), (3, 0)]), 5)  13.3 us
    ppermute x2, starting transfers between devices, line_window(): across = lax.ppermute(far[v:v + 1], 'src', near_pairs)  9.65 us
    ppermute x3, waiting for transfers between devices, swap(): return lax.ppermute(x, axis, [(i, i ^ bit) for i in range(peers)])  6.09 us
    ppermute x1, starting transfers between devices, line_window(): far = held(lax.ppermute(data, 'src', [(0, 3), (1, 2), (2, 1), (3, 0)]), 5)  3.6 us
    ppermute x3, starting transfers between devices, swap(): return lax.ppermute(x, axis, [(i, i ^ bit) for i in range(peers)])  3.01 us
    pallas_call x1, Pallas kernels, body(): pl.pallas_call(functools.partial(kernel_b, late), out_shape=[window, jax....  2.98 us
    pallas_call x1, Pallas kernels, body(): pl.pallas_call(functools.partial(last_kernel, half + 1, late), out_shape=...  2.48 us
    pallas_call x1, Pallas kernels, body(): pl.pallas_call(functools.partial(kernel_a, [{k: at for k, (_, at) in piec...  1.62 us
  transfers between devices with their start and end apart: 7, of which 4 were waited for; matrix products, arithmetic and copies ran while one was open for 0% of the time, Pallas kernels for 11%

profile of v30, /device:TPU:0, one launch (start us, length us, event | category | flops | bytes accessed | tf_op | source)
XLA Modules:
  0.0 43.5 jit_solution(5380097405368710511)
XLA Ops:
  0.0 0.0 copy-start.1
  0.0 0.0 copy-start
  0.0 0.0 copy-start.2
  0.0 3.0 %collective-permute-start.5 = (bf16[2,2,256,768]{3,2,1,0:T(8,128)(2,1)}, bf16[2,2,256,768]{3,2,1,0:T(8,128)(2,1)S(1)}, u32[]{:S(2)}, u32[]{:S(2)}) collective-permute-start(bf16[2,2,256,768]{3,2,1,0:T(8,128)(2,1)} %own_ref.1), channel_id=1, source_target_pairs={{0,2},{1,3},{2,0},{3,1},{4,6},{5,7},{6,4},{7,5},{8,10},{9,11},{10,... | collective-permute-start | bytes 4718600 | tf_op jit(solution)/shard_map/ppermute | solution.py:28
  3.0 3.6 %collective-permute-start = (bf16[2,2,256,256]{3,2,1,0:T(8,128)(2,1)}, bf16[2,2,256,256]{3,2,1,0:T(8,128)(2,1)S(1)}, u32[]{:S(2)}, u32[]{:S(2)}) collective-permute-start(bf16[2,2,256,256]{3,2,1,0:T(8,128)(2,1)} %refs_3_.1), channel_id=1, source_target_pairs={{0,12},{4,8},{8,4},{12,0},{1,13},{5,9},{9,5},{13,1},{2,14},{6,10},... | collective-permute-start | bytes 1572872 | tf_op jit(solution)/shard_map/ppermute | solution.py:37
  6.6 0.0 collective-permute-start.3
  6.6 13.3 %collective-permute-done.refs_0_ = bf16[2,2,256,256]{3,2,1,0:T(8,128)(2,1)S(1)} collective-permute-done((bf16[2,2,256,256]{3,2,1,0:T(8,128)(2,1)}, bf16[2,2,256,256]{3,2,1,0:T(8,128)(2,1)S(1)}, u32[]{:S(2)}, u32[]{:S(2)}) %collective-permute-start) | collective-permute-done | bytes 524320 | tf_op jit(solution)/shard_map/ppermute | solution.py:37
  20.0 9.6 %collective-permute-start.2 = (bf16[1,2,256,256]{3,2,1,0:T(8,128)(2,1)S(1)}, bf16[1,2,256,256]{3,2,1,0:T(8,128)(2,1)S(1)}, u32[]{:S(2)}, u32[]{:S(2)}) collective-permute-start(bf16[1,2,256,256]{3,2,1,0:T(8,128)(2,1)S(1)} %get-tuple-element.31), channel_id=1, source_target_pairs={{0,4},{4,0},{8,12},{12,8},{1,5},{5,1},{9,13},{13,9},{2,6},{6,2},{1... | collective-permute-start | bytes 786440 | tf_op jit(solution)/shard_map/ppermute | solution.py:41
  29.5 0.1 collective-permute-start.1
  29.6 0.0 copy-done.1
  29.6 0.0 collective-permute-start.4
  29.6 0.3 collective-permute-done.3.refs_1_.refs_4_
  29.9 0.0 copy-done
  29.9 0.0 copy-done.2
  29.9 1.6 %shard_map.38 = (bf16[4,256,512]{2,1,0:T(8,128)(2,1)S(1)}, bf16[4,256,512]{2,1,0:T(8,128)(2,1)S(1)}, f32[512,256]{1,0:T(8,128)S(1)}, f32[512,256]{1,0:T(8,128)S(...) custom-call(s32[4,12]{1,0:T(4,128)S(1)} %copy-done.2, bf16[2,2,256,768]{3,2,1,0:T(8,128)(2,1)S(1)} %copy-done.1, ...), custom_call_target="tpu_custom_call" | custom-call | flops 161061280 | bytes 1048576 | tf_op jit(solution)/shard_map/pallas_call | solution.py:214
  31.5 6.1 %collective-permute-done.5.refs_0_ = bf16[2,2,256,768]{3,2,1,0:T(8,128)(2,1)S(1)} collective-permute-done((bf16[2,2,256,768]{3,2,1,0:T(8,128)(2,1)}, bf16[2,2,256,768]{3,2,1,0:T(8,128)(2,1)S(1)}, u32[]{:S(2)}, u32[]{:S(2)}) %collective-permute-start.5) | collective-permute-done | bytes 1572896 | tf_op jit(solution)/shard_map/ppermute | solution.py:28
  37.6 0.0 collective-permute-start.6
  37.6 0.0 collective-permute-done.2.late_ref
  37.6 0.0 collective-permute-done.4.refs_0_
  37.6 3.0 %shard_map.40 = (bf16[4,256,512]{2,1,0:T(8,128)(2,1)S(1)}, bf16[512,512]{1,0:T(8,128)(2,1)S(1)}, f32[2,256,256]{2,1,0:T(8,128)S(1)}, f32[2,256,256]{2,1,0:T(8,128)S(1)}) custom-call(s32[4,12]{1,0:T(4,128)S(1)} %copy-done.2, bf16[1,2,256,256]{3,2,1,0:T(8,128)(2,1)S(1)} %collective-permute-done.2.late_ref, ...), custom_call_target="tpu_custom_call", output_to_operand_aliasing={{0}: (2, {}), {2}: (6, {}), {3}: (7, {})} | custom-call | flops 161061280 | bytes 1048576 | tf_op jit(solution)/shard_map/pallas_call | solution.py:225
  40.6 0.4 collective-permute-done.1.refs_0_
  41.0 0.0 collective-permute-done.6.refs_0_
  41.0 2.5 %shard_map.42 = (f32[2,2,256,256]{3,2,1,0:T(8,128)}, bf16[4,256,512]{2,1,0:T(8,128)(2,1)S(1)}) custom-call(s32[4,12]{1,0:T(4,128)S(1)} %copy-done.2, bf16[1,2,256,256]{3,2,1,0:T(8,128)(2,1)S(1)} %shard_map.41.late_ref, bf16[4,256,512]{2,1,0:T(8,128)(2,1)S(1)} %get-tuple-element.26.first_window, ...), custom_call_target="tpu_custom_call", output_to_operand_aliasing={{1}: (3, {})} | custom-call | flops 1610612736 | bytes 1048576 | tf_op jit(solution)/shard_map/pallas_call | solution.py:235
  (4 shorter events, 0.0 us)
Async XLA Ops:
  0.0 29.6 %copy-start.1 = (bf16[2,2,256,768]{3,2,1,0:T(8,128)(2,1)S(1)}, bf16[2,2,256,768]{3,2,1,0:T(8,128)(2,1)}, u32[]{:S(2)}) copy-start(bf16[2,2,256,768]{3,2,1,0:T(8,128)(2,1)} %own_ref.1) | copy-start | bytes 4718596
  0.0 29.9 %copy-start = (bf16[2,2,256,256]{3,2,1,0:T(8,128)(2,1)S(1)}, bf16[2,2,256,256]{3,2,1,0:T(8,128)(2,1)}, u32[]{:S(2)}) copy-start(bf16[2,2,256,256]{3,2,1,0:T(8,128)(2,1)} %refs_3_.1) | copy-start | bytes 1572868
  0.0 29.9 %copy-start.2 = (s32[4,12]{1,0:T(4,128)S(1)}, s32[4,12]{1,0:T(4,128)}, u32[]{:S(2)}) copy-start(s32[4,12]{1,0:T(4,128)} %aperture_ref.5) | copy-start | bytes 580
  0.0 37.6 %collective-permute-start.5 = (bf16[2,2,256,768]{3,2,1,0:T(8,128)(2,1)}, bf16[2,2,256,768]{3,2,1,0:T(8,128)(2,1)S(1)}, u32[]{:S(2)}, u32[]{:S(2)}) collective-permute-start(bf16[2,2,256,768]{3,2,1,0:T(8,128)(2,1)} %own_ref.1), channel_id=1, source_target_pairs={{0,2},{1,3},{2,0},{3,1},{4,6},{5,7},{6,4},{7,5},{8,10},{9,11},{10,... | collective-permute-start | bytes 4718600 | tf_op jit(solution)/shard_map/ppermute | solution.py:28
  3.0 16.9 %collective-permute-start = (bf16[2,2,256,256]{3,2,1,0:T(8,128)(2,1)}, bf16[2,2,256,256]{3,2,1,0:T(8,128)(2,1)S(1)}, u32[]{:S(2)}, u32[]{:S(2)}) collective-permute-start(bf16[2,2,256,256]{3,2,1,0:T(8,128)(2,1)} %refs_3_.1), channel_id=1, source_target_pairs={{0,12},{4,8},{8,4},{12,0},{1,13},{5,9},{9,5},{13,1},{2,14},{6,10},... | collective-permute-start | bytes 1572872 | tf_op jit(solution)/shard_map/ppermute | solution.py:37
  6.6 23.3 %collective-permute-start.3 = (bf16[2,2,256,256]{3,2,1,0:T(8,128)(2,1)}, bf16[2,2,256,256]{3,2,1,0:T(8,128)(2,1)S(1)}, u32[]{:S(2)}, u32[]{:S(2)}) collective-permute-start(bf16[2,2,256,256]{3,2,1,0:T(8,128)(2,1)} %refs_3_.1), channel_id=1, source_target_pairs={{0,4},{4,0},{8,12},{12,8},{1,5},{5,1},{9,13},{13,9},{2,6},{6,2},{1... | collective-permute-start | bytes 1572872 | tf_op jit(solution)/shard_map/ppermute | solution.py:38
  20.0 17.7 %collective-permute-start.2 = (bf16[1,2,256,256]{3,2,1,0:T(8,128)(2,1)S(1)}, bf16[1,2,256,256]{3,2,1,0:T(8,128)(2,1)S(1)}, u32[]{:S(2)}, u32[]{:S(2)}) collective-permute-start(bf16[1,2,256,256]{3,2,1,0:T(8,128)(2,1)S(1)} %get-tuple-element.31), channel_id=1, source_target_pairs={{0,4},{4,0},{8,12},{12,8},{1,5},{5,1},{9,13},{13,9},{2,6},{6,2},{1... | collective-permute-start | bytes 786440 | tf_op jit(solution)/shard_map/ppermute | solution.py:41
  29.5 11.5 %collective-permute-start.1 = (bf16[1,2,256,256]{3,2,1,0:T(8,128)(2,1)S(1)}, bf16[1,2,256,256]{3,2,1,0:T(8,128)(2,1)S(1)}, u32[]{:S(2)}, u32[]{:S(2)}) collective-permute-start(bf16[1,2,256,256]{3,2,1,0:T(8,128)(2,1)S(1)} %get-tuple-element.32), channel_id=1, source_target_pairs={{0,4},{4,0},{8,12},{12,8},{1,5},{5,1},{9,13},{13,9},{2,6},{6,2},{1... | collective-permute-start | bytes 786440 | tf_op jit(solution)/shard_map/ppermute | solution.py:41
  29.6 8.0 %collective-permute-start.4 = (bf16[2,2,256,768]{3,2,1,0:T(8,128)(2,1)S(1)}, bf16[2,2,256,768]{3,2,1,0:T(8,128)(2,1)S(1)}, u32[]{:S(2)}, u32[]{:S(2)}) collective-permute-start(bf16[2,2,256,768]{3,2,1,0:T(8,128)(2,1)S(1)} %copy-done.1), channel_id=1, source_target_pairs={{0,1},{1,0},{2,3},{3,2},{4,5},{5,4},{6,7},{7,6},{8,9},{9,8},{10,11... | collective-permute-start | bytes 4718600 | tf_op jit(solution)/shard_map/ppermute | solution.py:28
  37.6 3.4 %collective-permute-start.6 = (bf16[2,2,256,768]{3,2,1,0:T(8,128)(2,1)S(1)}, bf16[2,2,256,768]{3,2,1,0:T(8,128)(2,1)S(1)}, u32[]{:S(2)}, u32[]{:S(2)}) collective-permute-start(bf16[2,2,256,768]{3,2,1,0:T(8,128)(2,1)S(1)} %shard_map.39.refs_1_), channel_id=1, source_target_pairs={{0,1},{1,0},{2,3},{3,2},{4,5},{5,4},{6,7},{7,6},{8,9},{9,8},{10,11... | collective-permute-start | bytes 4718600 | tf_op jit(solution)/shard_map/ppermute | solution.py:28
